TPU v7x, 32 devices: a whole 2x2x4 slice. The times are simulated.
32 devices in a mesh: row: 8 (over y, x, core), col: 4 (over z).
Axes of the slice: x: 2, y: 2, z: 4, core: 2. Of those that a mesh axis runs over, the one named last changes fastest.
Arguments:
- front_inverse: bfloat16 [24576, 24576], P('row', 'col'), may hold values from -0.0390625 to 0.0390625
- coupling_tiles: bfloat16 [768, 128, 128], P('col'), may hold values from -12 to 12
- tile_row: int32 [768], P('col'), may hold values from 0 to 191, as said below
- tile_col: int32 [768], P('col'), may hold values from 0 to 15
- surface_map: int32 [2, 8192], P(None, 'row'), may hold values from 0 to 24575, as said below
- bem_entries: bfloat16 [2, 8192, 2048], P(None, 'row', 'col'), may hold values from -6 to 6
- pivot_inverse: bfloat16 [8192, 8192], P('row'), may hold values from -0.0625 to 0.0625
- slab_below: bfloat16 [8192, 8192], P('row'), may hold values from -0.0625 to 0.0625
Outputs:
- panel_out: bfloat16 [2, 8192, 2048], P(None, 'row', 'col')
Inputs may be any that keep to these rules, and one draw needn't show every extreme that they name: `tile_row`: tiles at positions c * 192 to (c + 1) * 192 - 1 lie in block rows c * 48 to (c + 1) * 48 - 1; no two tiles share both block row and block column. `surface_map`: all entries differ; of the entries in the columns of one index of row, at most 384 lie in any one block of 3072 front rows that starts at a multiple of 3072, and for every index of row some block holds exactly 384 of them.
All inputs are finite; a program needn't handle non-finite values.
Results may differ from a plain program's by a relative error of at most 0.0058.
Values may be sent and summed in bfloat16 or wider, within the bound.
No kernel may reach another device: no remote copies, remote signals or barrier semaphores. Data moves between devices by JAX's collectives and lax.ppermute only.
A program may use at most 384 MiB of HBM per device.

v0:
```python
import jax
import jax.numpy as jnp
from jax import lax
from jax.sharding import PartitionSpec as P

COLS = 2048


def fold_with(matrix, shard_piece):
    return jnp.dot(matrix, shard_piece, preferred_element_type=jnp.float32)


def per_device(
    front_inverse,
    coupling_tiles,
    tile_row,
    tile_col,
    surface_map,
    bem_entries,
    pivot_inverse,
    slab_below,
):
    row_width = front_inverse.shape[0]
    front_width = front_inverse.shape[1]
    block_count = front_width // 128
    col_blocks = COLS // 128
    tile_count = coupling_tiles.shape[0]
    group_size = min(48, tile_count)
    group_count = tile_count // group_size
    local_rows = tile_row - lax.axis_index("col") * block_count
    blocks_view = front_inverse.reshape(row_width, block_count, 128)
    block_ids = jnp.arange(col_blocks, dtype=jnp.int32)

    def group_step(total, inputs):
        tiles, rows_here, cols_here = inputs
        picked = jnp.take(blocks_view, rows_here, axis=1)
        products = jnp.einsum("tkn,rtk->tnr", tiles, picked, preferred_element_type=jnp.float32)
        placing = (cols_here[:, None] == block_ids[None, :]).astype(jnp.float32)
        placed = jnp.einsum("tb,tnr->bnr", placing, products, precision=lax.Precision.HIGHEST)
        return (total + placed.reshape(COLS, row_width), None)

    grouped = (
        coupling_tiles.reshape(group_count, group_size, 128, 128),
        local_rows.reshape(group_count, group_size),
        tile_col.reshape(group_count, group_size),
    )
    partial_all, _ = lax.scan(group_step, jnp.zeros((COLS, row_width), jnp.float32), grouped)
    col_width = COLS // lax.axis_size("col")
    mine = lax.psum_scatter(partial_all, "col", scatter_dimension=0, tiled=True)
    solved = mine.astype(jnp.bfloat16)
    pivot_count = surface_map.shape[1]
    initial = jnp.zeros((col_width, 2, pivot_count), jnp.bfloat16)
    shard_piece = lax.all_gather(solved, "row", axis=1, tiled=True)
    width = shard_piece.shape[1]
    inside = (surface_map >= 0) & (surface_map < width)
    taken = jnp.take(shard_piece, jnp.clip(surface_map, 0, width - 1), axis=1)
    schur_part = jnp.where(inside[None], taken, initial)
    schur_part = schur_part.transpose(1, 2, 0)
    assembled = (bem_entries.astype(jnp.float32) - schur_part.astype(jnp.float32)).astype(
        jnp.bfloat16
    )
    pivot_solved = fold_with(pivot_inverse, lax.all_gather(assembled[0], "row", axis=0, tiled=True))
    pivot_solved = pivot_solved.astype(jnp.bfloat16)
    update = fold_with(slab_below, lax.all_gather(pivot_solved, "row", axis=0, tiled=True))
    below = (assembled[1].astype(jnp.float32) - update).astype(jnp.bfloat16)
    return jnp.stack([pivot_solved, below])


def solution(mesh):
    placed = (
        P("row", "col"),
        P("col", None, None),
        P("col"),
        P("col"),
        P(None, "row"),
        P(None, "row", "col"),
        P("row", None),
        P("row", None),
    )
    return jax.shard_map(
        per_device, mesh=mesh, in_specs=placed, out_specs=P(None, "row", "col"), check_vma=False
    )
```

profile of v0, /device:TPU:0, one launch (start us, length us, event | category | flops | bytes accessed | tf_op | source)
XLA Modules:
  0.0 1635.2 jit_solution(10672358274168685016)
XLA Ops:
  6.5 0.0 reduce-scatter.2.cloned.1.call-start
  6.5 48.7 %copy.21 = bf16[3072,6144]{0,1:T(8,128)(2,1)} copy(bf16[3072,6144]{1,0:T(8,128)(2,1)} %param.10) | data formatting | bytes 75497472 | tf_op args[0]
  55.2 43.6 %copy.22 = bf16[3072,48,128]{2,0,1:T(8,128)(2,1)} copy(bf16[3072,48,128]{0,2,1:T(8,128)(2,1)} %bitcast.64) | data formatting | bytes 75497472
  98.8 0.0 copy-start.4
  98.8 0.0 copy-start.3
  98.8 8.7 copy.20
  107.5 0.0 copy-done.4
  107.5 0.1 reshape.62
  107.6 0.0 copy-done.3
  107.6 0.1 reshape.60
  107.6 779.2 %while.11 = (s32[]{:T(128)}, f32[2048,3072]{1,0:T(8,128)}, s32[4,48]{1,0:T(4,128)S(1)}, bf16[4,48,128,128]{2,3,1,0:T(8,128)(2,1)}, s32[4,48]{1,0:T(4,128)S(1)}, ...) while((s32[]{:T(128)}, f32[2048,3072]{1,0:T(8,128)}, s32[4,48]{1,0:T(4,128)S(1)}, ...), condition=%wide.region_1.2_spmd.clone, body=%wide.region_0.1_spmd.clone.sunk | while | flops 8487176192 | bytes 416815296 | solution.py:47
  107.7 25.8 %gather_fusion = bf16[48,3072,128]{2,1,0:T(8,128)(2,1)} fusion(bf16[3072,48,128]{2,0,1:T(8,128)(2,1)} %get-tuple-element.144, s32[1024]{0:T(1024)S(1)} %pad_clamp_fusion.2), kind=kCustom, calls=%fused_computation.clone.clone.1 | custom fusion | bytes 75497664 | tf_op jit(solution)/shard_map/while/body/eval_jaxpr/jit(_take)/gather | solution.py:36
  133.5 38.5 %fusion.43 = f32[48,128,3072]{2,1,0:T(8,128)} fusion(bf16[48,3072,128]{2,1,0:T(8,128)(2,1)} %gather_fusion, pred[48]{0:T(512)(128)(4,1)S(1)} %compare_and_fusion.4, bf16[4,48,128,128]{2,3,1,0:T(8,128)(2,1)} %get-tuple-element.142, s32[]{:T(128)} %get-tuple-element.131), kind=kOutput, calls=%fused_computation.5.clone.1 | convolution fusion | flops 4850712576 | bytes 114819632 | tf_op jit(solution)/shard_map/while/body/eval_jaxpr/tkn,rtk->tnr/dot_general | solution.py:37
  172.0 80.8 %fusion.45 = f32[16,128,3072]{2,0,1:T(8,128)} fusion(f32[48,128,3072]{2,1,0:T(8,128)} %fusion.43, s32[48]{0:T(128)S(1)} %fusion.44), kind=kOutput, calls=%fused_computation.3.clone.1 | convolution fusion | flops 3623879424 | bytes 100663488 | tf_op jit(solution)/shard_map/while/body/eval_jaxpr/tb,tnr->bnr/dot_general | solution.py:39
  252.8 24.9 %copy.33 = f32[16,128,3072]{2,1,0:T(8,128)} copy(f32[16,128,3072]{2,0,1:T(8,128)} %fusion.45) | data formatting | bytes 50331648 | tf_op jit(solution)/shard_map/while/body/eval_jaxpr/tb,tnr->bnr/dot_general | solution.py:39
  277.6 20.3 %bitcast_add_fusion.2 = f32[2048,3072]{1,0:T(8,128)} fusion(f32[16,128,3072]{2,1,0:T(8,128)} %copy.33, f32[2048,3072]{1,0:T(8,128)} %get-tuple-element.132, pred[]{:T(512)S(6)} %compare.3), kind=kLoop, calls=%fused_computation.9.clone.1 | loop fusion | flops 12582912 | bytes 75497472 | tf_op jit(solution)/shard_map/while/body/eval_jaxpr/add | solution.py:40
  297.9 26.7 %gather_fusion = bf16[48,3072,128]{2,1,0:T(8,128)(2,1)} fusion(bf16[3072,48,128]{2,0,1:T(8,128)(2,1)} %get-tuple-element.144, s32[1024]{0:T(1024)S(1)} %pad_clamp_fusion.2), kind=kCustom, calls=%fused_computation.clone.clone.1 | custom fusion | bytes 75497664 | tf_op jit(solution)/shard_map/while/body/eval_jaxpr/jit(_take)/gather | solution.py:36
  324.6 38.5 %fusion.43 = f32[48,128,3072]{2,1,0:T(8,128)} fusion(bf16[48,3072,128]{2,1,0:T(8,128)(2,1)} %gather_fusion, pred[48]{0:T(512)(128)(4,1)S(1)} %compare_and_fusion.4, bf16[4,48,128,128]{2,3,1,0:T(8,128)(2,1)} %get-tuple-element.142, s32[]{:T(128)} %get-tuple-element.131), kind=kOutput, calls=%fused_computation.5.clone.1 | convolution fusion | flops 4850712576 | bytes 114819632 | tf_op jit(solution)/shard_map/while/body/eval_jaxpr/tkn,rtk->tnr/dot_general | solution.py:37
  363.1 80.8 %fusion.45 = f32[16,128,3072]{2,0,1:T(8,128)} fusion(f32[48,128,3072]{2,1,0:T(8,128)} %fusion.43, s32[48]{0:T(128)S(1)} %fusion.44), kind=kOutput, calls=%fused_computation.3.clone.1 | convolution fusion | flops 3623879424 | bytes 100663488 | tf_op jit(solution)/shard_map/while/body/eval_jaxpr/tb,tnr->bnr/dot_general | solution.py:39
  443.9 24.9 %copy.33 = f32[16,128,3072]{2,1,0:T(8,128)} copy(f32[16,128,3072]{2,0,1:T(8,128)} %fusion.45) | data formatting | bytes 50331648 | tf_op jit(solution)/shard_map/while/body/eval_jaxpr/tb,tnr->bnr/dot_general | solution.py:39
  468.8 25.4 %bitcast_add_fusion.2 = f32[2048,3072]{1,0:T(8,128)} fusion(f32[16,128,3072]{2,1,0:T(8,128)} %copy.33, f32[2048,3072]{1,0:T(8,128)} %get-tuple-element.132, pred[]{:T(512)S(6)} %compare.3), kind=kLoop, calls=%fused_computation.9.clone.1 | loop fusion | flops 12582912 | bytes 75497472 | tf_op jit(solution)/shard_map/while/body/eval_jaxpr/add | solution.py:40
  494.2 26.8 %gather_fusion = bf16[48,3072,128]{2,1,0:T(8,128)(2,1)} fusion(bf16[3072,48,128]{2,0,1:T(8,128)(2,1)} %get-tuple-element.144, s32[1024]{0:T(1024)S(1)} %pad_clamp_fusion.2), kind=kCustom, calls=%fused_computation.clone.clone.1 | custom fusion | bytes 75497664 | tf_op jit(solution)/shard_map/while/body/eval_jaxpr/jit(_take)/gather | solution.py:36
  520.9 38.5 %fusion.43 = f32[48,128,3072]{2,1,0:T(8,128)} fusion(bf16[48,3072,128]{2,1,0:T(8,128)(2,1)} %gather_fusion, pred[48]{0:T(512)(128)(4,1)S(1)} %compare_and_fusion.4, bf16[4,48,128,128]{2,3,1,0:T(8,128)(2,1)} %get-tuple-element.142, s32[]{:T(128)} %get-tuple-element.131), kind=kOutput, calls=%fused_computation.5.clone.1 | convolution fusion | flops 4850712576 | bytes 114819632 | tf_op jit(solution)/shard_map/while/body/eval_jaxpr/tkn,rtk->tnr/dot_general | solution.py:37
  559.4 80.8 %fusion.45 = f32[16,128,3072]{2,0,1:T(8,128)} fusion(f32[48,128,3072]{2,1,0:T(8,128)} %fusion.43, s32[48]{0:T(128)S(1)} %fusion.44), kind=kOutput, calls=%fused_computation.3.clone.1 | convolution fusion | flops 3623879424 | bytes 100663488 | tf_op jit(solution)/shard_map/while/body/eval_jaxpr/tb,tnr->bnr/dot_general | solution.py:39
  640.2 24.9 %copy.33 = f32[16,128,3072]{2,1,0:T(8,128)} copy(f32[16,128,3072]{2,0,1:T(8,128)} %fusion.45) | data formatting | bytes 50331648 | tf_op jit(solution)/shard_map/while/body/eval_jaxpr/tb,tnr->bnr/dot_general | solution.py:39
  665.1 25.4 %bitcast_add_fusion.2 = f32[2048,3072]{1,0:T(8,128)} fusion(f32[16,128,3072]{2,1,0:T(8,128)} %copy.33, f32[2048,3072]{1,0:T(8,128)} %get-tuple-element.132, pred[]{:T(512)S(6)} %compare.3), kind=kLoop, calls=%fused_computation.9.clone.1 | loop fusion | flops 12582912 | bytes 75497472 | tf_op jit(solution)/shard_map/while/body/eval_jaxpr/add | solution.py:40
  690.5 26.8 %gather_fusion = bf16[48,3072,128]{2,1,0:T(8,128)(2,1)} fusion(bf16[3072,48,128]{2,0,1:T(8,128)(2,1)} %get-tuple-element.144, s32[1024]{0:T(1024)S(1)} %pad_clamp_fusion.2), kind=kCustom, calls=%fused_computation.clone.clone.1 | custom fusion | bytes 75497664 | tf_op jit(solution)/shard_map/while/body/eval_jaxpr/jit(_take)/gather | solution.py:36
  717.3 38.5 %fusion.43 = f32[48,128,3072]{2,1,0:T(8,128)} fusion(bf16[48,3072,128]{2,1,0:T(8,128)(2,1)} %gather_fusion, pred[48]{0:T(512)(128)(4,1)S(1)} %compare_and_fusion.4, bf16[4,48,128,128]{2,3,1,0:T(8,128)(2,1)} %get-tuple-element.142, s32[]{:T(128)} %get-tuple-element.131), kind=kOutput, calls=%fused_computation.5.clone.1 | convolution fusion | flops 4850712576 | bytes 114819632 | tf_op jit(solution)/shard_map/while/body/eval_jaxpr/tkn,rtk->tnr/dot_general | solution.py:37
  755.8 80.8 %fusion.45 = f32[16,128,3072]{2,0,1:T(8,128)} fusion(f32[48,128,3072]{2,1,0:T(8,128)} %fusion.43, s32[48]{0:T(128)S(1)} %fusion.44), kind=kOutput, calls=%fused_computation.3.clone.1 | convolution fusion | flops 3623879424 | bytes 100663488 | tf_op jit(solution)/shard_map/while/body/eval_jaxpr/tb,tnr->bnr/dot_general | solution.py:39
  836.6 24.9 %copy.33 = f32[16,128,3072]{2,1,0:T(8,128)} copy(f32[16,128,3072]{2,0,1:T(8,128)} %fusion.45) | data formatting | bytes 50331648 | tf_op jit(solution)/shard_map/while/body/eval_jaxpr/tb,tnr->bnr/dot_general | solution.py:39
  861.5 25.4 %bitcast_add_fusion.2 = f32[2048,3072]{1,0:T(8,128)} fusion(f32[16,128,3072]{2,1,0:T(8,128)} %copy.33, f32[2048,3072]{1,0:T(8,128)} %get-tuple-element.132, pred[]{:T(512)S(6)} %compare.3), kind=kLoop, calls=%fused_computation.9.clone.1 | loop fusion | flops 12582912 | bytes 75497472 | tf_op jit(solution)/shard_map/while/body/eval_jaxpr/add | solution.py:40
  886.9 24.8 %copy.23 = f32[2048,3072]{0,1:T(8,128)} copy(f32[2048,3072]{1,0:T(8,128)} %get-tuple-element.42) | data formatting | bytes 50331648 | tf_op jit(solution)/shard_map/while | solution.py:47
  911.7 0.0 reduce-scatter.2.cloned.1.call-update
  911.7 0.0 copy-start.1
  911.7 0.0 copy-start.2
  911.8 0.0 all-gather.5.cloned.1.call-start
  911.8 416.5 %reduce-scatter.2.cloned.1.call-done = f32[512,3072]{0,1:T(8,128)} async-done(((f32[2048,3072]{0,1:T(8,128)}), f32[512,3072]{0,1:T(8,128)}) %reduce-scatter.2.cloned.1.call-update) | async-done | bytes 6291472 | tf_op jit(solution)/shard_map/reduce_scatter | solution.py:49
  1328.3 4.9 convert_element_type.32
  1333.2 0.0 all-gather.5.cloned.1.call-update
  1333.2 0.0 all-gather.9.cloned.1.call-start
  1333.2 0.0 copy-done.1
  1333.2 2.4 copy.19
  1335.6 0.0 copy-done.2
  1335.7 124.8 %all-gather.5.cloned.1.call-done = bf16[512,24576]{0,1:T(8,128)(2,1)} async-done(((bf16[512,3072]{0,1:T(8,128)(2,1)}), bf16[512,24576]{0,1:T(8,128)(2,1)}) %all-gather.5.cloned.1.call-update) | async-done | bytes 25165840 | tf_op jit(solution)/shard_map/all_gather | solution.py:53
  1460.5 19.0 %gather_fusion.1 = bf16[2048,512]{1,0:T(8,128)(2,1)S(1)} fusion(bf16[512,24576]{0,1:T(8,128)(2,1)} %all-gather.5.cloned.1.call-done, s32[2048]{0:T(1024)S(1)} %bitcast_clamp_fusion), kind=kCustom, calls=%fused_computation.1 | custom fusion | bytes 4202496 | tf_op jit(solution)/shard_map/jit(_take)/gather | solution.py:56
  1479.5 2.5 copy.24
  1482.0 3.3 fusion.20
  1485.3 1.0 slice.12
  1486.3 0.0 all-gather.9.cloned.1.call-update
  1486.3 0.0 all-gather.7.cloned.1.call-start
  1486.4 54.5 %all-gather.9.cloned.1.call-done = bf16[1,8192,512]{1,2,0:T(8,128)(2,1)} async-done(((bf16[1,1024,512]{1,2,0:T(8,128)(2,1)}), bf16[1,8192,512]{1,2,0:T(8,128)(2,1)}) %all-gather.9.cloned.1.call-update) | async-done | bytes 8388624 | tf_op jit(solution)/shard_map/all_gather | solution.py:62
  1540.9 15.6 fusion.22
  1556.5 0.0 all-gather.7.cloned.1.call-update
  1556.5 0.0 copy-start
  1556.5 54.5 %all-gather.7.cloned.1.call-done = bf16[8192,512]{0,1:T(8,128)(2,1)} async-done(((bf16[1024,512]{0,1:T(8,128)(2,1)}), bf16[8192,512]{0,1:T(8,128)(2,1)}) %all-gather.7.cloned.1.call-update) | async-done | bytes 8388624 | tf_op jit(solution)/shard_map/all_gather | solution.py:64
  1611.0 14.8 fusion.25
  1625.9 0.0 copy-done
  1625.9 0.2 pad_maximum_fusion
  1626.1 2.6 copy.25
  (21 shorter events, 0.2 us)
Async XLA Ops:
  6.5 1321.7 %reduce-scatter.2.cloned.1.call-start = ((), (), s32[]{:S(2)}) async-start(), calls=%async_computation.1 | async-start | bytes 31457280 | tf_op jit(solution)/shard_map/reduce_scatter | solution.py:49
  98.8 8.7 copy-start.4
  98.8 8.8 copy-start.3
  911.7 421.5 %copy-start.1 = (bf16[2,1024,512]{2,1,0:T(8,128)(2,1)S(1)}, bf16[2,1024,512]{2,1,0:T(8,128)(2,1)}, u32[]{:S(2)}) copy-start(bf16[2,1024,512]{2,1,0:T(8,128)(2,1)} %param.15) | copy-start | bytes 6291460
  911.7 423.9 %copy-start.2 = (s32[2,1024]{1,0:T(2,128)S(1)}, s32[2,1024]{1,0:T(2,128)}, u32[]{:S(2)}) copy-start(s32[2,1024]{1,0:T(2,128)} %param.14) | copy-start | bytes 24580
  911.8 548.7 %all-gather.5.cloned.1.call-start = ((), (), s32[]{:S(2)}) async-start(), calls=%async_computation.2 | async-start | bytes 28311552 | tf_op jit(solution)/shard_map/all_gather | solution.py:53
  1333.2 207.7 %all-gather.9.cloned.1.call-start = ((), (), s32[]{:S(2)}) async-start(), calls=%async_computation.4 | async-start | bytes 9437184 | tf_op jit(solution)/shard_map/all_gather | solution.py:62
  1486.3 124.7 %all-gather.7.cloned.1.call-start = ((), (), s32[]{:S(2)}) async-start(), calls=%async_computation.3 | async-start | bytes 9437184 | tf_op jit(solution)/shard_map/all_gather | solution.py:64
  1556.5 69.4 %copy-start = (bf16[512,1024]{1,0:T(8,128)(2,1)S(1)}, bf16[512,1024]{1,0:T(8,128)(2,1)}, u32[]{:S(2)}) copy-start(bf16[512,1024]{1,0:T(8,128)(2,1)} %fusion.22) | copy-start | bytes 3145732
Sparse Core Ops, SparseCore 0:
  911.9 416.3 reduce-scatter.1
  1333.3 127.1 all-gather.4
  1486.4 54.3 all-gather.8
  1556.6 54.3 all-gather.6
where the time goes:
time: 1640 us
  waiting for transfers between devices  650 us (40%)
  matrix products  508 us (31%)
  local copies, waits for them, and re-layouts  359 us (22%)
  other arithmetic  105 us (6%)
    reduce_scatter x1, waiting for transfers between devices, per_device(): mine = lax.psum_scatter(partial_all, 'col', scatter_dimension=0, tiled=True)  416 us
    dot_general x4, matrix products, group_step(): jnp.einsum('tb,tnr->bnr', placing, products, precision=lax.Precision.HIGH...  323 us
    dot_general x4, matrix products, group_step(): jnp.einsum('tkn,rtk->tnr', tiles, picked, preferred_element_type=jnp.floa...  154 us
    all_gather x1, waiting for transfers between devices, per_device(): shard_piece = lax.all_gather(solved, 'row', axis=1, tiled=True)  125 us
    gather x4, local copies, waits for them, and re-layouts, group_step(): picked = jnp.take(blocks_view, rows_here, axis=1)  106 us
    unnamed x14, local copies, waits for them, and re-layouts  103 us
    dot_general x4, local copies, waits for them, and re-layouts, group_step(): jnp.einsum('tb,tnr->bnr', placing, products, precision=lax.Precision.HIGH...  99.5 us
    add x4, other arithmetic, group_step(): return (total + placed.reshape(COLS, row_width), None)  96.5 us
  transfers between devices with their start and end apart: 4, of which 4 were waited for; matrix products, arithmetic and copies ran while one was open for 0% of the time, Pallas kernels for 0%

commit v1 on v0

v1 whole, which is shorter than its diff:
```python
import functools

import jax
import jax.numpy as jnp
from jax import lax
from jax.experimental import pallas as pl
from jax.experimental.pallas import tpu as pltpu
from jax.sharding import PartitionSpec as P

TILE = 128
VMEM_BYTES = 56 * 1024 * 1024


def largest_tile(total, most):
    best = None
    for size in range(16, most + 1, 16):
        if total % size == 0:
            best = size
    return best if best is not None else total


def front_kernel(chunk, ends, per_dest, n_col, meta_ref, tiles_ref, front_ref, *refs):
    outs, dense = refs[:n_col], refs[n_col]
    width = outs[0].shape[1]
    tile_count = tiles_ref.shape[0]
    start, stop = ends

    @pl.when(pl.program_id(0) == 0)
    def build():
        step = 512

        @pl.loop(0, dense.shape[0] // step)
        def clear(i):
            dense[pl.ds(pl.multiple_of(i * step, step), step), :] = jnp.zeros(
                (step, dense.shape[1]), dense.dtype
            )

        @pl.loop(0, tile_count)
        def place(t):
            row = meta_ref[0, t]
            dest = meta_ref[1, t]
            sub = meta_ref[2, t]

            @pl.when((sub >= start) & (sub < stop))
            def _():
                left = dest * width + (sub - start) * TILE
                dense[
                    pl.ds(pl.multiple_of(row * TILE, TILE), TILE),
                    pl.ds(pl.multiple_of(left, TILE), TILE),
                ] = tiles_ref[t]

    total = jnp.dot(front_ref[...], dense[...], preferred_element_type=jnp.float32)
    for e in range(n_col):
        outs[e][...] = total[:, e * width : (e + 1) * width].astype(outs[e].dtype)


def front_products(front, tiles, meta, start, stop, per_dest, n_col):
    rows, depth = front.shape
    width = (stop - start) * TILE
    block = largest_tile(rows, 256)
    kernel = functools.partial(front_kernel, start, (start, stop), per_dest, n_col)
    return pl.pallas_call(
        kernel,
        grid_spec=pltpu.PrefetchScalarGridSpec(
            num_scalar_prefetch=1,
            grid=(rows // block,),
            in_specs=[
                pl.BlockSpec(tiles.shape, lambda i, m: (0, 0, 0), pipeline_mode=pl.Buffered(1)),
                pl.BlockSpec((block, depth), lambda i, m: (i, 0)),
            ],
            out_specs=[pl.BlockSpec((block, width), lambda i, m: (i, 0))] * n_col,
            scratch_shapes=[pltpu.VMEM((depth, n_col * width), front.dtype)],
        ),
        out_shape=[jax.ShapeDtypeStruct((rows, width), front.dtype)] * n_col,
        compiler_params=pltpu.CompilerParams(vmem_limit_bytes=VMEM_BYTES),
        cost_estimate=pl.CostEstimate(
            flops=2 * rows * depth * n_col * width,
            bytes_accessed=2 * (rows * depth + tiles.size + rows * n_col * width),
            transcendentals=0,
        ),
        name="front_products",
    )(meta, tiles, front)


def pack_kernel(n_row, index_ref, solved_ref, *outs):
    depth = solved_ref.shape[0]
    cap = outs[0].shape[0]
    step = largest_tile(cap, 128)
    for k in range(n_row):
        for s in range(cap // step):
            want = index_ref[k * cap + s * step : k * cap + (s + 1) * step, :]
            places = lax.broadcasted_iota(jnp.int32, (step, depth), 1)
            picks = (places == want).astype(jnp.float32).astype(solved_ref.dtype)
            got = jnp.dot(picks, solved_ref[...], preferred_element_type=jnp.float32)
            outs[k][s * step : (s + 1) * step, :] = got.astype(outs[k].dtype)


def pack_rows(index, solved, n_row, cap):
    depth, width = solved.shape
    return pl.pallas_call(
        functools.partial(pack_kernel, n_row),
        out_shape=[jax.ShapeDtypeStruct((cap, width), solved.dtype)] * n_row,
        compiler_params=pltpu.CompilerParams(vmem_limit_bytes=VMEM_BYTES),
        cost_estimate=pl.CostEstimate(
            flops=2 * n_row * cap * depth * max(width, 256),
            bytes_accessed=4 * n_row * cap * width,
            transcendentals=0,
        ),
        name="pack_rows",
    )(index, solved)


def assemble_kernel(n_row, index_ref, bem_ref, *refs):
    pieces, pivot_ref, lower_ref = refs[:n_row], refs[n_row], refs[n_row + 1]
    cap = pieces[0].shape[0]
    count = pivot_ref.shape[0]
    step = largest_tile(count, 128)
    for half, out in enumerate((pivot_ref, lower_ref)):

        @pl.loop(0, count // step)
        def part(i):
            begin = pl.multiple_of(i * step, step)
            want = index_ref[pl.ds(half * count + begin, step), :]
            places = lax.broadcasted_iota(jnp.int32, (step, cap), 1)
            taken = jnp.zeros((step, out.shape[1]), jnp.float32)
            for k in range(n_row):
                picks = (places + k * cap == want).astype(jnp.float32).astype(out.dtype)
                taken = taken + jnp.dot(picks, pieces[k][...], preferred_element_type=jnp.float32)
            entries = bem_ref[half, pl.ds(begin, step), :].astype(jnp.float32)
            out[pl.ds(begin, step), :] = (entries - taken).astype(out.dtype)


def assemble(index, bem, pieces, place, n_row):
    cap, width = pieces[0].shape
    count = bem.shape[1]
    whole = lambda *shape: pl.BlockSpec(shape, lambda i: (0,) * len(shape))
    return pl.pallas_call(
        functools.partial(assemble_kernel, n_row),
        grid=(1,),
        in_specs=[
            whole(*index.shape),
            pl.BlockSpec((2, count, width), lambda i: (0, 0, place)),
        ]
        + [whole(cap, width)] * n_row,
        out_specs=[whole(count, width)] * 2,
        out_shape=[jax.ShapeDtypeStruct((count, width), bem.dtype)] * 2,
        compiler_params=pltpu.CompilerParams(vmem_limit_bytes=VMEM_BYTES),
        cost_estimate=pl.CostEstimate(
            flops=2 * 2 * count * n_row * cap * max(width, 256),
            bytes_accessed=2 * (n_row * cap + 4 * count) * width,
            transcendentals=0,
        ),
        name="assemble",
    )(index, bem, *pieces)


def route_tables(surface_map, rows, n_row, cap):
    me = lax.axis_index("row")
    mine = surface_map.reshape(-1)
    count = mine.shape[0]
    every = lax.all_gather(mine, "row")
    partners = me ^ jnp.arange(n_row, dtype=jnp.int32)
    local = every[partners] - me * rows
    asked = (local >= 0) & (local < rows)
    rank = jnp.cumsum(asked.astype(jnp.int32), axis=1) - 1
    slots = jnp.arange(cap, dtype=jnp.int32)
    hit = asked[:, None, :] & (rank[:, None, :] == slots[None, :, None])
    wanted = jnp.sum(jnp.where(hit, local[:, None, :] + 1, 0), axis=2) - 1
    owner = mine // rows
    held = owner[None, :] == jnp.arange(n_row, dtype=jnp.int32)[:, None]
    place = jnp.cumsum(held.astype(jnp.int32), axis=1) - 1
    slot = jnp.sum(jnp.where(held, place, 0), axis=0)
    lands = (owner ^ me) * cap + slot
    return wanted.reshape(n_row * cap, 1), lands.reshape(count, 1)


def add_rounded(*terms):
    total = terms[0].astype(jnp.float32)
    for term in terms[1:]:
        total = total + term.astype(jnp.float32)
    return total.astype(terms[0].dtype)


def sum_over_chain(parts, n_col):
    where = lax.axis_index("col")
    received = {}
    finals = []
    for k in range(n_col - 1):
        pairs = [(k, k + 1), (n_col - 1 - k, n_col - 2 - k)]
        for d in range(n_col - 1, k, -1):
            own = parts[d if k < n_col // 2 else n_col - 1 - d]
            value = own if k == 0 else add_rounded(own, received[k - 1, d])
            received[k, d] = lax.ppermute(value, "col", pairs)
        finals.append(received[k, k + 1])
    own = parts[0]
    for e in range(1, n_col // 2):
        own = jnp.where(jnp.minimum(where, n_col - 1 - where) == e, parts[e], own)
    return add_rounded(own, *finals)


def per_device(
    front_inverse,
    coupling_tiles,
    tile_row,
    tile_col,
    surface_map,
    bem_entries,
    pivot_inverse,
    slab_below,
):
    n_row, n_col = lax.axis_size("row"), lax.axis_size("col")
    assert n_row & (n_row - 1) == 0 and n_col % 2 == 0
    rows, depth = front_inverse.shape
    per_dest = bem_entries.shape[2] // TILE
    cap = rows // n_row
    col_at = lax.axis_index("col")

    dest = tile_col // per_dest
    mirrored = jnp.where(col_at < n_col // 2, dest, n_col - 1 - dest)
    meta = jnp.stack([tile_row - col_at * (depth // TILE), mirrored, tile_col % per_dest])
    wanted, lands = route_tables(surface_map, rows, n_row, cap)

    pivots, belows = [], []
    for chunk in range(per_dest):
        parts = front_products(
            front_inverse, coupling_tiles, meta, chunk, chunk + 1, per_dest, n_col
        )
        solved = sum_over_chain(parts, n_col)
        packed = pack_rows(wanted, solved, n_row, cap)
        pieces = [packed[0]]
        for k in range(1, n_row):
            pairs = [(i, i ^ k) for i in range(n_row)]
            pieces.append(lax.ppermute(packed[k], "row", pairs))
        upper, lower = assemble(lands, bem_entries, pieces, chunk, n_row)
        gathered = lax.all_gather(upper, "row", axis=0, tiled=True)
        pivot = jnp.dot(pivot_inverse, gathered, preferred_element_type=jnp.float32)
        pivot = pivot.astype(jnp.bfloat16)
        update = jnp.dot(
            slab_below,
            lax.all_gather(pivot, "row", axis=0, tiled=True),
            preferred_element_type=jnp.float32,
        )
        pivots.append(pivot)
        belows.append((lower.astype(jnp.float32) - update).astype(jnp.bfloat16))
    return jnp.stack([jnp.concatenate(pivots, axis=1), jnp.concatenate(belows, axis=1)])


def solution(mesh):
    placed = (
        P("row", "col"),
        P("col", None, None),
        P("col"),
        P("col"),
        P(None, "row"),
        P(None, "row", "col"),
        P("row", None),
        P("row", None),
    )
    return jax.shard_map(
        per_device, mesh=mesh, in_specs=placed, out_specs=P(None, "row", "col"), check_vma=False
    )
```

time: 1640 us -> 662 us (0.40)
  waiting for transfers between devices: 650 us -> 197 us
  matrix products: 508 us -> 80.8 us
  local copies, waits for them, and re-layouts: 359 us -> 6.77 us
  Pallas kernels: 0 us -> 193 us
  starting transfers between devices: 0.13 us -> 111 us
  other arithmetic: 105 us -> 42.8 us
    dot_general x10 -> x8, matrix products: 508 us -> 80.8 us  [the longest x4 45.9 us: per_device(): pivot = jnp.dot(pivot_inverse, gathered, preferred_element_type=jnp.float32)]
    reduce_scatter x1 -> x0, waiting for transfers between devices: 416 us -> none  [per_device(): mine = lax.psum_scatter(partial_all, 'col', scatter_dimension=0, tiled=True)]
    pallas_call x0 -> x12, Pallas kernels: none -> 193 us  [the longest x4 127 us: front_products(): pl.pallas_call(kernel, grid_spec=pltpu.PrefetchScalarGridSpec(num_scalar_...]
    all_gather x3 -> x8, waiting for transfers between devices: 234 us -> 73.8 us  [the longest x4 73.8 us: per_device(): lax.all_gather(pivot, 'row', axis=0, tiled=True)]
    gather x6 -> x1, local copies, waits for them, and re-layouts: 128 us -> 0.58 us  [route_tables(): local = every[partners] - me * rows]
    ppermute x0 -> x52, waiting for transfers between devices: none -> 123 us  [the longest x24 105 us: sum_over_chain(): received[k, d] = lax.ppermute(value, 'col', pairs)]
    ppermute x0 -> x52, starting transfers between devices: none -> 110 us  [the longest x24 86.2 us: sum_over_chain(): received[k, d] = lax.ppermute(value, 'col', pairs)]
    dot_general x4 -> x0, local copies, waits for them, and re-layouts: 99.5 us -> none  [group_step(): jnp.einsum('tb,tnr->bnr', placing, products, precision=lax.Precision.HIGH...]
  transfers between devices with their start and end apart: 4 -> 60, of which waited for: 4 -> 23; matrix products, arithmetic and copies ran while one was open for 0% -> 18% of each run, Pallas kernels for 0% -> 25%
where the time goes in v1:
time: 662 us; the launch traced here: 656 us
  waiting for transfers between devices  197 us (30%)
  Pallas kernels  193 us (29%)
  starting transfers between devices  111 us (17%)
  matrix products  80.8 us (12%)
  other arithmetic  42.8 us (6%)
  between operations  15 us (2%)
  blocking collectives  9.45 us (1%)
  local copies, waits for them, and re-layouts  6.77 us (1%)
    pallas_call x4, Pallas kernels, front_products(): pl.pallas_call(kernel, grid_spec=pltpu.PrefetchScalarGridSpec(num_scalar_...  127 us
    ppermute x24, waiting for transfers between devices, sum_over_chain(): received[k, d] = lax.ppermute(value, 'col', pairs)  105 us
    ppermute x24, starting transfers between devices, sum_over_chain(): received[k, d] = lax.ppermute(value, 'col', pairs)  86.2 us
    all_gather x4, waiting for transfers between devices, per_device(): lax.all_gather(pivot, 'row', axis=0, tiled=True)  73.8 us
    dot_general x4, matrix products, per_device(): pivot = jnp.dot(pivot_inverse, gathered, preferred_element_type=jnp.float32)  45.9 us
    pallas_call x4, Pallas kernels, assemble(): pl.pallas_call(functools.partial(assemble_kernel, n_row), grid=(1,), in_s...  36.2 us
    dot_general x4, matrix products, per_device(): jnp.dot(slab_below, lax.all_gather(pivot, 'row', axis=0, tiled=True), pre...  34.8 us
    pallas_call x4, Pallas kernels, pack_rows(): pl.pallas_call(functools.partial(pack_kernel, n_row), out_shape=[jax.Shap...  29.6 us
  transfers between devices with their start and end apart: 60, of which 23 were waited for; matrix products, arithmetic and copies ran while one was open for 18% of the time, Pallas kernels for 25%

profile of v1, /device:TPU:0, one launch (start us, length us, event | category | flops | bytes accessed | tf_op | source)
XLA Modules:
  0.0 656.0 jit_solution(17447106043206026075)
XLA Ops:
  8.5 31.7 %front_products.7 = (bf16[3072,128]{1,0:T(8,128)(2,1)}, bf16[3072,128]{1,0:T(8,128)(2,1)}, bf16[3072,128]{1,0:T(8,128)(2,1)}, bf16[3072,128]{1,0:T(8,128)(2,1)}) custom-call(s32[3,192]{1,0:T(4,128)} %pad_add_fusion.meta_ref, bf16[192,128,128]{2,1,0:T(8,128)(2,1)} %tiles_ref.7, bf16[3072,6144]{1,0:T(8,128)(2,1)} %front_ref.7), custom_call_target="tpu_custom_call" | custom-call | flops 19327352832 | bytes 47185920 | tf_op jit(solution)/shard_map/front_products/pallas_call | solution.py:62
  40.2 5.1 collective-permute-start.39
  45.3 2.2 collective-permute-start.40
  47.5 2.3 collective-permute-start.42
  49.8 31.8 %front_products.6 = (bf16[3072,128]{1,0:T(8,128)(2,1)}, bf16[3072,128]{1,0:T(8,128)(2,1)}, bf16[3072,128]{1,0:T(8,128)(2,1)}, bf16[3072,128]{1,0:T(8,128)(2,1)}) custom-call(s32[3,192]{1,0:T(4,128)} %pad_add_fusion.meta_ref, bf16[192,128,128]{2,1,0:T(8,128)(2,1)} %tiles_ref.7, bf16[3072,6144]{1,0:T(8,128)(2,1)} %front_ref.7), custom_call_target="tpu_custom_call" | custom-call | flops 19327352832 | bytes 47185920 | tf_op jit(solution)/shard_map/front_products/pallas_call | solution.py:62
  81.7 2.2 collective-permute-start.26
  85.3 9.5 %all-gather = s32[8,1,2048]{2,1,0:T(1,128)S(1)} all-gather(s32[1,1,2048]{2,1,0:T(1,128)S(1)} %reshape.212), channel_id=1, replica_groups=mesh['row'=8,'col'=4] {'row'}, dimensions={0}, use_global_device_ids=true | all-gather | bytes 73728 | tf_op jit(solution)/shard_map/all_gather | solution.py:161
  95.4 31.9 %front_products.5 = (bf16[3072,128]{1,0:T(8,128)(2,1)}, bf16[3072,128]{1,0:T(8,128)(2,1)}, bf16[3072,128]{1,0:T(8,128)(2,1)}, bf16[3072,128]{1,0:T(8,128)(2,1)}) custom-call(s32[3,192]{1,0:T(4,128)} %pad_add_fusion.meta_ref, bf16[192,128,128]{2,1,0:T(8,128)(2,1)} %tiles_ref.7, bf16[3072,6144]{1,0:T(8,128)(2,1)} %front_ref.7), custom_call_target="tpu_custom_call" | custom-call | flops 19327352832 | bytes 47185920 | tf_op jit(solution)/shard_map/front_products/pallas_call | solution.py:62
  127.3 31.9 %front_products.4 = (bf16[3072,128]{1,0:T(8,128)(2,1)}, bf16[3072,128]{1,0:T(8,128)(2,1)}, bf16[3072,128]{1,0:T(8,128)(2,1)}, bf16[3072,128]{1,0:T(8,128)(2,1)}) custom-call(s32[3,192]{1,0:T(4,128)} %pad_add_fusion.meta_ref, bf16[192,128,128]{2,1,0:T(8,128)(2,1)} %tiles_ref.7, bf16[3072,6144]{1,0:T(8,128)(2,1)} %front_ref.7), custom_call_target="tpu_custom_call" | custom-call | flops 19327352832 | bytes 47185920 | tf_op jit(solution)/shard_map/front_products/pallas_call | solution.py:62
  159.2 2.3 reduce-window.16
  162.1 6.2 select_reduce_fusion
  169.8 2.5 add_convert_fusion.3
  172.3 1.7 collective-permute-start.41
  175.4 11.9 %collective-permute-done.29 = bf16[3072,128]{1,0:T(8,128)(2,1)S(1)} collective-permute-done((bf16[3072,128]{1,0:T(8,128)(2,1)S(1)}, bf16[3072,128]{1,0:T(8,128)(2,1)S(1)}, u32[]{:S(2)}, u32[]{:S(2)}) %collective-permute-start.29) | collective-permute-done | bytes 786464 | tf_op jit(solution)/shard_map/ppermute | solution.py:193
  190.2 1.6 collective-permute-start.28
  192.9 1.5 collective-permute-start.44
  196.9 2.3 reduce-window.14
  200.1 1.7 copy.84
  201.8 40.6 %collective-permute-start.16 = (bf16[3072,128]{1,0:T(8,128)(2,1)}, bf16[3072,128]{1,0:T(8,128)(2,1)}, u32[]{:S(2)}, u32[]{:S(2)}) collective-permute-start(bf16[3072,128]{1,0:T(8,128)(2,1)} %get-tuple-element.77), channel_id=1, source_target_pairs={{0,1},{3,2},{4,5},{7,6},{8,9},{11,10},{12,13},{15,14},{16,17},{19,... | collective-permute-start | bytes 2359304 | tf_op jit(solution)/shard_map/ppermute | solution.py:193
  242.4 6.5 collective-permute-done.44
  249.0 14.2 %collective-permute-done.31 = bf16[3072,128]{1,0:T(8,128)(2,1)} collective-permute-done((bf16[3072,128]{1,0:T(8,128)(2,1)}, bf16[3072,128]{1,0:T(8,128)(2,1)}, u32[]{:S(2)}, u32[]{:S(2)}) %collective-permute-start.31) | collective-permute-done | bytes 786464 | tf_op jit(solution)/shard_map/ppermute | solution.py:193
  263.2 4.2 add_convert_fusion
  267.4 7.4 %pack_rows.7 = (bf16[384,128]{1,0:T(8,128)(2,1)}, bf16[384,128]{1,0:T(8,128)(2,1)}, bf16[384,128]{1,0:T(8,128)(2,1)}, bf16[384,128]{1,0:T(8,128)(2,1)}, bf16[384...) custom-call(s32[3072,1]{1,0:T(8,128)} %bitcast.72, ...), custom_call_target="tpu_custom_call" | custom-call | flops 4831838208 | bytes 1572864 | tf_op jit(solution)/shard_map/pack_rows/pallas_call | solution.py:100
  274.8 1.6 collective-permute-start.46
  277.5 1.6 collective-permute-start.48
  284.7 2.6 collective-permute-start.14
  288.6 1.7 collective-permute-start.1
  292.4 9.1 %assemble.7 = (bf16[1024,128]{1,0:T(8,128)(2,1)}, bf16[1024,128]{1,0:T(8,128)(2,1)}) custom-call(s32[2048,1]{1,0:T(8,128)} %fusion.7.index_ref, bf16[2,1024,512]{2,1,0:T(8,128)(2,1)} %bem_ref.7, bf16[384,128]{1,0:T(8,128)(2,1)} %get-tuple-element.104.refs_0_, bf16[384,128]{1,0:T(8,128)(2,1)} %copy-done.23, bf16[384,128]{1,0:T(8,128)(2,1)} %collective-permute-done.46.refs_2_, ...), custom_call_target="tpu_custom_call" | custom-call | flops 3221225472 | bytes 1835008 | tf_op jit(solution)/shard_map/assemble/pallas_call | solution.py:137
  301.6 2.2 add_convert_fusion.10
  303.8 2.0 collective-permute-start.17
  305.9 2.5 add_convert_fusion.11
  308.4 7.5 %pack_rows.6 = (bf16[384,128]{1,0:T(8,128)(2,1)}, bf16[384,128]{1,0:T(8,128)(2,1)}, bf16[384,128]{1,0:T(8,128)(2,1)}, bf16[384,128]{1,0:T(8,128)(2,1)}, bf16[384...) custom-call(s32[3072,1]{1,0:T(8,128)} %bitcast.73, ...), custom_call_target="tpu_custom_call" | custom-call | flops 4831838208 | bytes 1572864 | tf_op jit(solution)/shard_map/pack_rows/pallas_call | solution.py:100
  316.0 1.5 collective-permute-start.33
  317.5 3.8 collective-permute-done.1
  322.5 15.2 %collective-permute-done.3 = bf16[3072,128]{1,0:T(8,128)(2,1)S(1)} collective-permute-done((bf16[3072,128]{1,0:T(8,128)(2,1)}, bf16[3072,128]{1,0:T(8,128)(2,1)S(1)}, u32[]{:S(2)}, u32[]{:S(2)}) %collective-permute-start.3) | collective-permute-done | bytes 786464 | tf_op jit(solution)/shard_map/ppermute | solution.py:193
  339.3 1.5 collective-permute-start.37
  342.3 2.3 add_convert_fusion.14
  344.6 5.2 collective-permute-start.13
  349.8 4.0 collective-permute-start
  353.8 1.5 collective-permute-start.15
  355.3 1.5 collective-permute-start.4
  356.9 9.1 %assemble.6 = (bf16[1024,128]{1,0:T(8,128)(2,1)}, bf16[1024,128]{1,0:T(8,128)(2,1)}) custom-call(s32[2048,1]{1,0:T(8,128)} %fusion.7.index_ref, bf16[2,1024,512]{2,1,0:T(8,128)(2,1)} %bem_ref.7, bf16[384,128]{1,0:T(8,128)(2,1)} %get-tuple-element.91.refs_0_, bf16[384,128]{1,0:T(8,128)(2,1)} %copy-done.22, bf16[384,128]{1,0:T(8,128)(2,1)} %copy-done.24, ...), custom_call_target="tpu_custom_call" | custom-call | flops 3221225472 | bytes 1835008 | tf_op jit(solution)/shard_map/assemble/pallas_call | solution.py:137
  372.4 10.4 %collective-permute-done = bf16[3072,128]{1,0:T(8,128)(2,1)} collective-permute-done((bf16[3072,128]{1,0:T(8,128)(2,1)S(1)}, bf16[3072,128]{1,0:T(8,128)(2,1)}, u32[]{:S(2)}, u32[]{:S(2)}) %collective-permute-start) | collective-permute-done | bytes 786464 | tf_op jit(solution)/shard_map/ppermute | solution.py:193
  382.9 28.6 %collective-permute-done.18 = bf16[3072,128]{1,0:T(8,128)(2,1)S(1)} collective-permute-done((bf16[3072,128]{1,0:T(8,128)(2,1)S(1)}, bf16[3072,128]{1,0:T(8,128)(2,1)S(1)}, u32[]{:S(2)}, u32[]{:S(2)}) %collective-permute-start.18) | collective-permute-done | bytes 786464 | tf_op jit(solution)/shard_map/ppermute | solution.py:193
  411.4 14.6 %collective-permute-done.5 = bf16[3072,128]{1,0:T(8,128)(2,1)S(1)} collective-permute-done((bf16[3072,128]{1,0:T(8,128)(2,1)S(1)}, bf16[3072,128]{1,0:T(8,128)(2,1)S(1)}, u32[]{:S(2)}, u32[]{:S(2)}) %collective-permute-start.5) | collective-permute-done | bytes 786464 | tf_op jit(solution)/shard_map/ppermute | solution.py:193
  426.0 3.8 add_convert_fusion.8
  429.8 7.4 %pack_rows.5 = (bf16[384,128]{1,0:T(8,128)(2,1)}, bf16[384,128]{1,0:T(8,128)(2,1)}, bf16[384,128]{1,0:T(8,128)(2,1)}, bf16[384,128]{1,0:T(8,128)(2,1)}, bf16[384...) custom-call(s32[3072,1]{1,0:T(8,128)} %bitcast.74, ...), custom_call_target="tpu_custom_call" | custom-call | flops 4831838208 | bytes 1572864 | tf_op jit(solution)/shard_map/pack_rows/pallas_call | solution.py:100
  444.9 5.0 collective-permute-done.23.refs_5_
  450.7 9.0 %assemble.5 = (bf16[1024,128]{1,0:T(8,128)(2,1)}, bf16[1024,128]{1,0:T(8,128)(2,1)}) custom-call(s32[2048,1]{1,0:T(8,128)} %fusion.7.index_ref, bf16[2,1024,512]{2,1,0:T(8,128)(2,1)} %bem_ref.7, bf16[384,128]{1,0:T(8,128)(2,1)} %get-tuple-element.78.refs_0_, bf16[384,128]{1,0:T(8,128)(2,1)} %copy-done.37, bf16[384,128]{1,0:T(8,128)(2,1)} %copy-done.39, ...), custom_call_target="tpu_custom_call" | custom-call | flops 3221225472 | bytes 1835008 | tf_op jit(solution)/shard_map/assemble/pallas_call | solution.py:137
  460.0 7.4 %pack_rows.4 = (bf16[384,128]{1,0:T(8,128)(2,1)}, bf16[384,128]{1,0:T(8,128)(2,1)}, bf16[384,128]{1,0:T(8,128)(2,1)}, bf16[384,128]{1,0:T(8,128)(2,1)}, bf16[384...) custom-call(s32[3072,1]{1,0:T(8,128)} %bitcast.75, ...), custom_call_target="tpu_custom_call" | custom-call | flops 4831838208 | bytes 1572864 | tf_op jit(solution)/shard_map/pack_rows/pallas_call | solution.py:100
  476.9 2.5 collective-permute-done.11.refs_6_
  481.4 9.0 %assemble.4 = (bf16[1024,128]{1,0:T(8,128)(2,1)}, bf16[1024,128]{1,0:T(8,128)(2,1)}) custom-call(s32[2048,1]{1,0:T(8,128)} %fusion.7.index_ref, bf16[2,1024,512]{2,1,0:T(8,128)(2,1)} %bem_ref.7, bf16[384,128]{1,0:T(8,128)(2,1)} %get-tuple-element.65.refs_0_, bf16[384,128]{1,0:T(8,128)(2,1)} %copy-done.36, bf16[384,128]{1,0:T(8,128)(2,1)} %copy-done.38, ...), custom_call_target="tpu_custom_call" | custom-call | flops 3221225472 | bytes 1835008 | tf_op jit(solution)/shard_map/assemble/pallas_call | solution.py:137
  490.5 11.6 %fusion.4 = bf16[1024,128]{1,0:T(8,128)(2,1)} fusion(bf16[1024,8192]{1,0:T(8,128)(2,1)} %param.14, bf16[8192,128]{1,0:T(8,128)(2,1)} %all-gather.16.cloned.1.call-done), kind=kOutput, calls=%fused_computation.33 | convolution fusion | flops 2147614720 | bytes 19136512 | tf_op jit(solution)/shard_map/dot_general | solution.py:236
  502.4 11.5 %fusion.3 = bf16[1024,128]{1,0:T(8,128)(2,1)} fusion(bf16[1024,8192]{1,0:T(8,128)(2,1)} %param.14, bf16[8192,128]{1,0:T(8,128)(2,1)} %all-gather.14.cloned.1.call-done), kind=kOutput, calls=%fused_computation.32 | convolution fusion | flops 2147614720 | bytes 19136512 | tf_op jit(solution)/shard_map/dot_general | solution.py:236
  514.1 11.7 %fusion.2 = bf16[1024,128]{1,0:T(8,128)(2,1)} fusion(bf16[1024,8192]{1,0:T(8,128)(2,1)} %param.14, bf16[8192,128]{1,0:T(8,128)(2,1)} %all-gather.12.cloned.1.call-done), kind=kOutput, calls=%fused_computation.31 | convolution fusion | flops 2147614720 | bytes 19136512 | tf_op jit(solution)/shard_map/dot_general | solution.py:236
  526.2 11.1 %fusion.1 = bf16[1024,128]{1,0:T(8,128)(2,1)S(1)} fusion(bf16[1024,8192]{1,0:T(8,128)(2,1)} %param.14, bf16[8192,128]{1,0:T(8,128)(2,1)} %all-gather.10.cloned.1.call-done), kind=kOutput, calls=%fused_computation.30 | convolution fusion | flops 2147614720 | bytes 19136512 | tf_op jit(solution)/shard_map/dot_general | solution.py:236
  538.1 10.9 %all-gather.24.cloned.1.call-done = bf16[8192,128]{1,0:T(8,128)(2,1)} async-done(((bf16[1024,128]{1,0:T(8,128)(2,1)}), bf16[8192,128]{1,0:T(8,128)(2,1)}) %all-gather.24.cloned.1.call-update) | async-done | bytes 2097168 | tf_op jit(solution)/shard_map/all_gather | solution.py:240
  549.0 8.7 %convolution_bitcast_fusion = f32[1024,128]{1,0:T(8,128)S(1)} fusion(bf16[1024,8192]{1,0:T(8,128)(2,1)} %param.15, bf16[8192,128]{1,0:T(8,128)(2,1)} %all-gather.24.cloned.1.call-done), kind=kOutput, calls=%fused_computation.22 | convolution fusion | flops 2147483648 | bytes 19398656 | tf_op jit(solution)/shard_map/dot_general | solution.py:238
  557.8 20.9 %all-gather.22.cloned.1.call-done = bf16[8192,128]{1,0:T(8,128)(2,1)} async-done(((bf16[1024,128]{1,0:T(8,128)(2,1)}), bf16[8192,128]{1,0:T(8,128)(2,1)}) %all-gather.22.cloned.1.call-update) | async-done | bytes 2097168 | tf_op jit(solution)/shard_map/all_gather | solution.py:240
  578.6 8.7 %convolution_bitcast_fusion.1 = f32[1024,128]{1,0:T(8,128)S(1)} fusion(bf16[1024,8192]{1,0:T(8,128)(2,1)} %param.15, bf16[8192,128]{1,0:T(8,128)(2,1)} %all-gather.22.cloned.1.call-done), kind=kOutput, calls=%fused_computation.23 | convolution fusion | flops 2147483648 | bytes 19398656 | tf_op jit(solution)/shard_map/dot_general | solution.py:238
  587.4 21.0 %all-gather.20.cloned.1.call-done = bf16[8192,128]{1,0:T(8,128)(2,1)} async-done(((bf16[1024,128]{1,0:T(8,128)(2,1)}), bf16[8192,128]{1,0:T(8,128)(2,1)}) %all-gather.20.cloned.1.call-update) | async-done | bytes 2097168 | tf_op jit(solution)/shard_map/all_gather | solution.py:240
  608.5 8.7 %convolution_bitcast_fusion.2 = f32[1024,128]{1,0:T(8,128)S(1)} fusion(bf16[1024,8192]{1,0:T(8,128)(2,1)} %param.15, bf16[8192,128]{1,0:T(8,128)(2,1)} %all-gather.20.cloned.1.call-done), kind=kOutput, calls=%fused_computation.24 | convolution fusion | flops 2147483648 | bytes 19398656 | tf_op jit(solution)/shard_map/dot_general | solution.py:238
  617.3 21.0 %all-gather.18.cloned.1.call-done = bf16[8192,128]{1,0:T(8,128)(2,1)} async-done(((bf16[1024,128]{1,0:T(8,128)(2,1)}), bf16[8192,128]{1,0:T(8,128)(2,1)}) %all-gather.18.cloned.1.call-update) | async-done | bytes 2097168 | tf_op jit(solution)/shard_map/all_gather | solution.py:240
  638.3 8.7 %convolution_bitcast_fusion.3 = f32[1024,128]{1,0:T(8,128)S(1)} fusion(bf16[1024,8192]{1,0:T(8,128)(2,1)} %param.15, bf16[8192,128]{1,0:T(8,128)(2,1)} %all-gather.18.cloned.1.call-done), kind=kOutput, calls=%fused_computation.25 | convolution fusion | flops 2147483648 | bytes 19398656 | tf_op jit(solution)/shard_map/dot_general | solution.py:238
  (252 shorter events, 59.1 us)
Async XLA Ops:
  6.5 484.0 %all-gather.16.cloned.1.call-start = ((), (), s32[]{:S(2)}) async-start(), calls=%async_computation.3 | async-start | bytes 2359296 | tf_op jit(solution)/shard_map/all_gather | solution.py:235
  40.2 155.3 %collective-permute-start.39 = (bf16[3072,128]{1,0:T(8,128)(2,1)}, bf16[3072,128]{1,0:T(8,128)(2,1)S(1)}, u32[]{:S(2)}, u32[]{:S(2)}) collective-permute-start(bf16[3072,128]{1,0:T(8,128)(2,1)} %get-tuple-element.100), channel_id=1, source_target_pairs={{0,1},{3,2},{4,5},{7,6},{8,9},{11,10},{12,13},{15,14},{16,17},{19,... | collective-permute-start | bytes 2359304 | tf_op jit(solution)/shard_map/ppermute | solution.py:193
  45.3 123.1 %collective-permute-start.40 = (bf16[3072,128]{1,0:T(8,128)(2,1)}, bf16[3072,128]{1,0:T(8,128)(2,1)}, u32[]{:S(2)}, u32[]{:S(2)}) collective-permute-start(bf16[3072,128]{1,0:T(8,128)(2,1)} %get-tuple-element.102), channel_id=1, source_target_pairs={{0,1},{3,2},{4,5},{7,6},{8,9},{11,10},{12,13},{15,14},{16,17},{19,... | collective-permute-start | bytes 2359304 | tf_op jit(solution)/shard_map/ppermute | solution.py:193
  47.5 37.7 %copy-start.21 = (s32[2,1024]{1,0:T(2,128)S(1)}, s32[2,1024]{1,0:T(2,128)}, u32[]{:S(2)}) copy-start(s32[2,1024]{1,0:T(2,128)} %param.12) | copy-start | bytes 24580
  47.5 124.8 %collective-permute-start.42 = (bf16[3072,128]{1,0:T(8,128)(2,1)}, bf16[3072,128]{1,0:T(8,128)(2,1)}, u32[]{:S(2)}, u32[]{:S(2)}) collective-permute-start(bf16[3072,128]{1,0:T(8,128)(2,1)} %get-tuple-element.103), channel_id=1, source_target_pairs={{0,1},{3,2},{4,5},{7,6},{8,9},{11,10},{12,13},{15,14},{16,17},{19,... | collective-permute-start | bytes 2359304 | tf_op jit(solution)/shard_map/ppermute | solution.py:193
  81.7 120.1 %collective-permute-start.26 = (bf16[3072,128]{1,0:T(8,128)(2,1)}, bf16[3072,128]{1,0:T(8,128)(2,1)}, u32[]{:S(2)}, u32[]{:S(2)}) collective-permute-start(bf16[3072,128]{1,0:T(8,128)(2,1)} %get-tuple-element.87), channel_id=1, source_target_pairs={{0,1},{3,2},{4,5},{7,6},{8,9},{11,10},{12,13},{15,14},{16,17},{19,... | collective-permute-start | bytes 2359304 | tf_op jit(solution)/shard_map/ppermute | solution.py:193
  83.8 104.4 %collective-permute-start.27 = (bf16[3072,128]{1,0:T(8,128)(2,1)}, bf16[3072,128]{1,0:T(8,128)(2,1)S(1)}, u32[]{:S(2)}, u32[]{:S(2)}) collective-permute-start(bf16[3072,128]{1,0:T(8,128)(2,1)} %get-tuple-element.89), channel_id=1, source_target_pairs={{0,1},{3,2},{4,5},{7,6},{8,9},{11,10},{12,13},{15,14},{16,17},{19,... | collective-permute-start | bytes 2359304 | tf_op jit(solution)/shard_map/ppermute | solution.py:193
  127.3 41.2 %copy-start.16 = (bf16[3072,128]{1,0:T(8,128)(2,1)S(1)}, bf16[3072,128]{1,0:T(8,128)(2,1)}, u32[]{:S(2)}) copy-start(bf16[3072,128]{1,0:T(8,128)(2,1)} %get-tuple-element.90) | copy-start | bytes 2359300
  168.5 18.9 %collective-permute-start.29 = (bf16[3072,128]{1,0:T(8,128)(2,1)S(1)}, bf16[3072,128]{1,0:T(8,128)(2,1)S(1)}, u32[]{:S(2)}, u32[]{:S(2)}) collective-permute-start(bf16[3072,128]{1,0:T(8,128)(2,1)S(1)} %copy-done.16), channel_id=1, source_target_pairs={{0,1},{3,2},{4,5},{7,6},{8,9},{11,10},{12,13},{15,14},{16,17},{19,... | collective-permute-start | bytes 2359304 | tf_op jit(solution)/shard_map/ppermute | solution.py:193
  172.3 70.1 %collective-permute-start.41 = (bf16[3072,128]{1,0:T(8,128)(2,1)}, bf16[3072,128]{1,0:T(8,128)(2,1)}, u32[]{:S(2)}, u32[]{:S(2)}) collective-permute-start(bf16[3072,128]{1,0:T(8,128)(2,1)} %add_convert_fusion.3), channel_id=1, source_target_pairs={{1,2},{2,1},{5,6},{6,5},{9,10},{10,9},{13,14},{14,13},{17,18},{18,... | collective-permute-start | bytes 2359304 | tf_op jit(solution)/shard_map/ppermute | solution.py:193
  187.3 2.9 collective-permute-start.43
  188.3 4.6 collective-permute-start.30
  190.2 52.2 %collective-permute-start.28 = (bf16[3072,128]{1,0:T(8,128)(2,1)}, bf16[3072,128]{1,0:T(8,128)(2,1)}, u32[]{:S(2)}, u32[]{:S(2)}) collective-permute-start(bf16[3072,128]{1,0:T(8,128)(2,1)} %add_convert_fusion.7), channel_id=1, source_target_pairs={{1,2},{2,1},{5,6},{6,5},{9,10},{10,9},{13,14},{14,13},{17,18},{18,... | collective-permute-start | bytes 2359304 | tf_op jit(solution)/shard_map/ppermute | solution.py:193
  192.9 56.1 %collective-permute-start.44 = (bf16[3072,128]{1,0:T(8,128)(2,1)}, bf16[3072,128]{1,0:T(8,128)(2,1)}, u32[]{:S(2)}, u32[]{:S(2)}) collective-permute-start(bf16[3072,128]{1,0:T(8,128)(2,1)} %add_convert_fusion.1), channel_id=1, source_target_pairs={{2,3},{1,0},{6,7},{5,4},{10,11},{9,8},{14,15},{13,12},{18,19},{17,... | collective-permute-start | bytes 2359304 | tf_op jit(solution)/shard_map/ppermute | solution.py:193
  194.4 68.7 %copy-start.10 = (bf16[3072,128]{1,0:T(8,128)(2,1)S(1)}, bf16[3072,128]{1,0:T(8,128)(2,1)}, u32[]{:S(2)}) copy-start(bf16[3072,128]{1,0:T(8,128)(2,1)} %get-tuple-element.100) | copy-start | bytes 2359300
  195.5 67.6 %collective-permute-start.31 = (bf16[3072,128]{1,0:T(8,128)(2,1)}, bf16[3072,128]{1,0:T(8,128)(2,1)}, u32[]{:S(2)}, u32[]{:S(2)}) collective-permute-start(bf16[3072,128]{1,0:T(8,128)(2,1)} %add_convert_fusion.5), channel_id=1, source_target_pairs={{2,3},{1,0},{6,7},{5,4},{10,11},{9,8},{14,15},{13,12},{18,19},{17,... | collective-permute-start | bytes 2359304 | tf_op jit(solution)/shard_map/ppermute | solution.py:193
  201.8 99.8 %collective-permute-start.16 = (bf16[3072,128]{1,0:T(8,128)(2,1)}, bf16[3072,128]{1,0:T(8,128)(2,1)}, u32[]{:S(2)}, u32[]{:S(2)}) collective-permute-start(bf16[3072,128]{1,0:T(8,128)(2,1)} %get-tuple-element.77), channel_id=1, source_target_pairs={{0,1},{3,2},{4,5},{7,6},{8,9},{11,10},{12,13},{15,14},{16,17},{19,... | collective-permute-start | bytes 2359304 | tf_op jit(solution)/shard_map/ppermute | solution.py:193
  274.8 4.3 collective-permute-start.45
  274.8 6.0 collective-permute-start.46
  276.4 5.9 collective-permute-start.47
  277.5 7.2 %collective-permute-start.48 = (bf16[384,128]{1,0:T(8,128)(2,1)}, bf16[384,128]{1,0:T(8,128)(2,1)S(1)}, u32[]{:S(2)}, u32[]{:S(2)}) collective-permute-start(bf16[384,128]{1,0:T(8,128)(2,1)} %get-tuple-element.108), channel_id=1, source_target_pairs={{0,16},{4,20},{8,24},{12,28},{16,0},{20,4},{24,8},{28,12},{1,17},{... | collective-permute-start | bytes 294920 | tf_op jit(solution)/shard_map/ppermute | solution.py:233
  279.1 9.5 %collective-permute-start.49 = (bf16[384,128]{1,0:T(8,128)(2,1)}, bf16[384,128]{1,0:T(8,128)(2,1)S(1)}, u32[]{:S(2)}, u32[]{:S(2)}) collective-permute-start(bf16[384,128]{1,0:T(8,128)(2,1)} %get-tuple-element.109), channel_id=1, source_target_pairs={{0,20},{4,16},{8,28},{12,24},{16,4},{20,0},{24,12},{28,8},{1,21},{... | collective-permute-start | bytes 294920 | tf_op jit(solution)/shard_map/ppermute | solution.py:233
  280.8 9.6 %collective-permute-start.50 = (bf16[384,128]{1,0:T(8,128)(2,1)S(1)}, bf16[384,128]{1,0:T(8,128)(2,1)S(1)}, u32[]{:S(2)}, u32[]{:S(2)}) collective-permute-start(bf16[384,128]{1,0:T(8,128)(2,1)S(1)} %copy-done.28), channel_id=1, source_target_pairs={{0,24},{4,28},{8,16},{12,20},{16,8},{20,12},{24,0},{28,4},{1,25},{... | collective-permute-start | bytes 294920 | tf_op jit(solution)/shard_map/ppermute | solution.py:233
  282.3 9.5 %collective-permute-start.51 = (bf16[384,128]{1,0:T(8,128)(2,1)S(1)}, bf16[384,128]{1,0:T(8,128)(2,1)S(1)}, u32[]{:S(2)}, u32[]{:S(2)}) collective-permute-start(bf16[384,128]{1,0:T(8,128)(2,1)S(1)} %copy-done.25), channel_id=1, source_target_pairs={{0,28},{4,24},{8,20},{12,16},{16,12},{20,8},{24,4},{28,0},{1,29},{... | collective-permute-start | bytes 294920 | tf_op jit(solution)/shard_map/ppermute | solution.py:233
  284.7 21.1 %collective-permute-start.14 = (bf16[3072,128]{1,0:T(8,128)(2,1)}, bf16[3072,128]{1,0:T(8,128)(2,1)}, u32[]{:S(2)}, u32[]{:S(2)}) collective-permute-start(bf16[3072,128]{1,0:T(8,128)(2,1)} %get-tuple-element.76), channel_id=1, source_target_pairs={{0,1},{3,2},{4,5},{7,6},{8,9},{11,10},{12,13},{15,14},{16,17},{19,... | collective-permute-start | bytes 2359304 | tf_op jit(solution)/shard_map/ppermute | solution.py:193
  288.6 32.7 %collective-permute-start.1 = (bf16[3072,128]{1,0:T(8,128)(2,1)S(1)}, bf16[3072,128]{1,0:T(8,128)(2,1)S(1)}, u32[]{:S(2)}, u32[]{:S(2)}) collective-permute-start(bf16[3072,128]{1,0:T(8,128)(2,1)S(1)} %copy-done.11), channel_id=1, source_target_pairs={{0,1},{3,2},{4,5},{7,6},{8,9},{11,10},{12,13},{15,14},{16,17},{19,... | collective-permute-start | bytes 2359304 | tf_op jit(solution)/shard_map/ppermute | solution.py:193
  290.4 47.3 %collective-permute-start.3 = (bf16[3072,128]{1,0:T(8,128)(2,1)}, bf16[3072,128]{1,0:T(8,128)(2,1)S(1)}, u32[]{:S(2)}, u32[]{:S(2)}) collective-permute-start(bf16[3072,128]{1,0:T(8,128)(2,1)} %get-tuple-element.64), channel_id=1, source_target_pairs={{0,1},{3,2},{4,5},{7,6},{8,9},{11,10},{12,13},{15,14},{16,17},{19,... | collective-permute-start | bytes 2359304 | tf_op jit(solution)/shard_map/ppermute | solution.py:193
  301.5 200.9 %all-gather.14.cloned.1.call-start = ((), (), s32[]{:S(2)}) async-start(), calls=%async_computation.2 | async-start | bytes 2359296 | tf_op jit(solution)/shard_map/all_gather | solution.py:235
  303.8 62.3 %collective-permute-start.17 = (bf16[3072,128]{1,0:T(8,128)(2,1)}, bf16[3072,128]{1,0:T(8,128)(2,1)}, u32[]{:S(2)}, u32[]{:S(2)}) collective-permute-start(bf16[3072,128]{1,0:T(8,128)(2,1)} %add_convert_fusion.10), channel_id=1, source_target_pairs={{1,2},{2,1},{5,6},{6,5},{9,10},{10,9},{13,14},{14,13},{17,18},{18,... | collective-permute-start | bytes 2359304 | tf_op jit(solution)/shard_map/ppermute | solution.py:193
  315.9 23.4 %collective-permute-start.32 = (bf16[384,128]{1,0:T(8,128)(2,1)}, bf16[384,128]{1,0:T(8,128)(2,1)S(1)}, u32[]{:S(2)}, u32[]{:S(2)}) collective-permute-start(bf16[384,128]{1,0:T(8,128)(2,1)} %get-tuple-element.92), channel_id=1, source_target_pairs={{0,4},{4,0},{8,12},{12,8},{16,20},{20,16},{24,28},{28,24},{1,5},{5... | collective-permute-start | bytes 294920 | tf_op jit(solution)/shard_map/ppermute | solution.py:233
  316.0 23.3 %collective-permute-start.33 = (bf16[384,128]{1,0:T(8,128)(2,1)}, bf16[384,128]{1,0:T(8,128)(2,1)S(1)}, u32[]{:S(2)}, u32[]{:S(2)}) collective-permute-start(bf16[384,128]{1,0:T(8,128)(2,1)} %get-tuple-element.93), channel_id=1, source_target_pairs={{0,8},{4,12},{8,0},{12,4},{16,24},{20,28},{24,16},{28,20},{1,9},{5... | collective-permute-start | bytes 294920 | tf_op jit(solution)/shard_map/ppermute | solution.py:233
  321.3 19.5 %collective-permute-start.34 = (bf16[384,128]{1,0:T(8,128)(2,1)}, bf16[384,128]{1,0:T(8,128)(2,1)S(1)}, u32[]{:S(2)}, u32[]{:S(2)}) collective-permute-start(bf16[384,128]{1,0:T(8,128)(2,1)} %get-tuple-element.94), channel_id=1, source_target_pairs={{0,12},{4,8},{8,4},{12,0},{16,28},{20,24},{24,20},{28,16},{1,13},{... | collective-permute-start | bytes 294920 | tf_op jit(solution)/shard_map/ppermute | solution.py:233
  337.7 6.9 %collective-permute-start.35 = (bf16[384,128]{1,0:T(8,128)(2,1)S(1)}, bf16[384,128]{1,0:T(8,128)(2,1)S(1)}, u32[]{:S(2)}, u32[]{:S(2)}) collective-permute-start(bf16[384,128]{1,0:T(8,128)(2,1)S(1)} %copy-done.35), channel_id=1, source_target_pairs={{0,16},{4,20},{8,24},{12,28},{16,0},{20,4},{24,8},{28,12},{1,17},{... | collective-permute-start | bytes 294920 | tf_op jit(solution)/shard_map/ppermute | solution.py:233
  339.2 10.5 %collective-permute-start.36 = (bf16[384,128]{1,0:T(8,128)(2,1)S(1)}, bf16[384,128]{1,0:T(8,128)(2,1)S(1)}, u32[]{:S(2)}, u32[]{:S(2)}) collective-permute-start(bf16[384,128]{1,0:T(8,128)(2,1)S(1)} %copy-done.32), channel_id=1, source_target_pairs={{0,20},{4,16},{8,28},{12,24},{16,4},{20,0},{24,12},{28,8},{1,21},{... | collective-permute-start | bytes 294920 | tf_op jit(solution)/shard_map/ppermute | solution.py:233
  339.3 14.4 %collective-permute-start.37 = (bf16[384,128]{1,0:T(8,128)(2,1)S(1)}, bf16[384,128]{1,0:T(8,128)(2,1)S(1)}, u32[]{:S(2)}, u32[]{:S(2)}) collective-permute-start(bf16[384,128]{1,0:T(8,128)(2,1)S(1)} %copy-done.29), channel_id=1, source_target_pairs={{0,24},{4,28},{8,16},{12,20},{16,8},{20,12},{24,0},{28,4},{1,25},{... | collective-permute-start | bytes 294920 | tf_op jit(solution)/shard_map/ppermute | solution.py:233
  340.9 14.5 %collective-permute-start.38 = (bf16[384,128]{1,0:T(8,128)(2,1)S(1)}, bf16[384,128]{1,0:T(8,128)(2,1)S(1)}, u32[]{:S(2)}, u32[]{:S(2)}) collective-permute-start(bf16[384,128]{1,0:T(8,128)(2,1)S(1)} %copy-done.26), channel_id=1, source_target_pairs={{0,28},{4,24},{8,20},{12,16},{16,12},{20,8},{24,4},{28,0},{1,29},{... | collective-permute-start | bytes 294920 | tf_op jit(solution)/shard_map/ppermute | solution.py:233
  344.6 26.4 %collective-permute-start.13 = (bf16[3072,128]{1,0:T(8,128)(2,1)S(1)}, bf16[3072,128]{1,0:T(8,128)(2,1)}, u32[]{:S(2)}, u32[]{:S(2)}) collective-permute-start(bf16[3072,128]{1,0:T(8,128)(2,1)S(1)} %copy-done.8), channel_id=1, source_target_pairs={{0,1},{3,2},{4,5},{7,6},{8,9},{11,10},{12,13},{15,14},{16,17},{19,... | collective-permute-start | bytes 2359304 | tf_op jit(solution)/shard_map/ppermute | solution.py:193
  349.8 33.1 %collective-permute-start = (bf16[3072,128]{1,0:T(8,128)(2,1)S(1)}, bf16[3072,128]{1,0:T(8,128)(2,1)}, u32[]{:S(2)}, u32[]{:S(2)}) collective-permute-start(bf16[3072,128]{1,0:T(8,128)(2,1)S(1)} %copy-done.9), channel_id=1, source_target_pairs={{0,1},{3,2},{4,5},{7,6},{8,9},{11,10},{12,13},{15,14},{16,17},{19,... | collective-permute-start | bytes 2359304 | tf_op jit(solution)/shard_map/ppermute | solution.py:193
  353.8 29.1 %collective-permute-start.15 = (bf16[3072,128]{1,0:T(8,128)(2,1)}, bf16[3072,128]{1,0:T(8,128)(2,1)}, u32[]{:S(2)}, u32[]{:S(2)}) collective-permute-start(bf16[3072,128]{1,0:T(8,128)(2,1)} %add_convert_fusion.11), channel_id=1, source_target_pairs={{1,2},{2,1},{5,6},{6,5},{9,10},{10,9},{13,14},{14,13},{17,18},{18,... | collective-permute-start | bytes 2359304 | tf_op jit(solution)/shard_map/ppermute | solution.py:193
  355.3 13.0 %collective-permute-start.4 = (bf16[3072,128]{1,0:T(8,128)(2,1)}, bf16[3072,128]{1,0:T(8,128)(2,1)}, u32[]{:S(2)}, u32[]{:S(2)}) collective-permute-start(bf16[3072,128]{1,0:T(8,128)(2,1)} %add_convert_fusion.14), channel_id=1, source_target_pairs={{1,2},{2,1},{5,6},{6,5},{9,10},{10,9},{13,14},{14,13},{17,18},{18,... | collective-permute-start | bytes 2359304 | tf_op jit(solution)/shard_map/ppermute | solution.py:193
  366.0 148.0 %all-gather.12.cloned.1.call-start = ((), (), s32[]{:S(2)}) async-start(), calls=%async_computation.1 | async-start | bytes 2359296 | tf_op jit(solution)/shard_map/all_gather | solution.py:235
  366.1 16.8 %collective-permute-start.2 = (bf16[3072,128]{1,0:T(8,128)(2,1)}, bf16[3072,128]{1,0:T(8,128)(2,1)S(1)}, u32[]{:S(2)}, u32[]{:S(2)}) collective-permute-start(bf16[3072,128]{1,0:T(8,128)(2,1)} %add_convert_fusion.15), channel_id=1, source_target_pairs={{1,2},{2,1},{5,6},{6,5},{9,10},{10,9},{13,14},{14,13},{17,18},{18,... | collective-permute-start | bytes 2359304 | tf_op jit(solution)/shard_map/ppermute | solution.py:193
  368.3 43.1 %collective-permute-start.18 = (bf16[3072,128]{1,0:T(8,128)(2,1)S(1)}, bf16[3072,128]{1,0:T(8,128)(2,1)S(1)}, u32[]{:S(2)}, u32[]{:S(2)}) collective-permute-start(bf16[3072,128]{1,0:T(8,128)(2,1)S(1)} %add_convert_fusion.9), channel_id=1, source_target_pairs={{2,3},{1,0},{6,7},{5,4},{10,11},{9,8},{14,15},{13,12},{18,19},{17,... | collective-permute-start | bytes 2359304 | tf_op jit(solution)/shard_map/ppermute | solution.py:193
  371.0 55.0 %collective-permute-start.5 = (bf16[3072,128]{1,0:T(8,128)(2,1)S(1)}, bf16[3072,128]{1,0:T(8,128)(2,1)S(1)}, u32[]{:S(2)}, u32[]{:S(2)}) collective-permute-start(bf16[3072,128]{1,0:T(8,128)(2,1)S(1)} %add_convert_fusion.13), channel_id=1, source_target_pairs={{2,3},{1,0},{6,7},{5,4},{10,11},{9,8},{14,15},{13,12},{18,19},{17,... | collective-permute-start | bytes 2359304 | tf_op jit(solution)/shard_map/ppermute | solution.py:193
  437.2 3.5 collective-permute-start.19
  437.2 5.8 collective-permute-start.20
  437.9 6.5 collective-permute-start.21
  439.1 5.8 collective-permute-start.22
  439.7 10.2 %collective-permute-start.23 = (bf16[384,128]{1,0:T(8,128)(2,1)}, bf16[384,128]{1,0:T(8,128)(2,1)S(1)}, u32[]{:S(2)}, u32[]{:S(2)}) collective-permute-start(bf16[384,128]{1,0:T(8,128)(2,1)} %get-tuple-element.83), channel_id=1, source_target_pairs={{0,20},{4,16},{8,28},{12,24},{16,4},{20,0},{24,12},{28,8},{1,21},{... | collective-permute-start | bytes 294920 | tf_op jit(solution)/shard_map/ppermute | solution.py:233
  440.7 9.2 %collective-permute-start.24 = (bf16[384,128]{1,0:T(8,128)(2,1)}, bf16[384,128]{1,0:T(8,128)(2,1)S(1)}, u32[]{:S(2)}, u32[]{:S(2)}) collective-permute-start(bf16[384,128]{1,0:T(8,128)(2,1)} %get-tuple-element.84), channel_id=1, source_target_pairs={{0,24},{4,28},{8,16},{12,20},{16,8},{20,12},{24,0},{28,4},{1,25},{... | collective-permute-start | bytes 294920 | tf_op jit(solution)/shard_map/ppermute | solution.py:233
  443.0 6.9 %collective-permute-start.25 = (bf16[384,128]{1,0:T(8,128)(2,1)}, bf16[384,128]{1,0:T(8,128)(2,1)S(1)}, u32[]{:S(2)}, u32[]{:S(2)}) collective-permute-start(bf16[384,128]{1,0:T(8,128)(2,1)} %get-tuple-element.85), channel_id=1, source_target_pairs={{0,28},{4,24},{8,20},{12,16},{16,12},{20,8},{24,4},{28,0},{1,29},{... | collective-permute-start | bytes 294920 | tf_op jit(solution)/shard_map/ppermute | solution.py:233
  459.7 66.5 %all-gather.10.cloned.1.call-start = ((), (), s32[]{:S(2)}) async-start(), calls=%async_computation | async-start | bytes 2359296 | tf_op jit(solution)/shard_map/all_gather | solution.py:235
  467.3 4.0 collective-permute-start.6
  467.8 6.5 collective-permute-start.7
  468.5 7.2 %collective-permute-start.8 = (bf16[384,128]{1,0:T(8,128)(2,1)}, bf16[384,128]{1,0:T(8,128)(2,1)S(1)}, u32[]{:S(2)}, u32[]{:S(2)}) collective-permute-start(bf16[384,128]{1,0:T(8,128)(2,1)} %get-tuple-element.68), channel_id=1, source_target_pairs={{0,12},{4,8},{8,4},{12,0},{16,28},{20,24},{24,20},{28,16},{1,13},{... | collective-permute-start | bytes 294920 | tf_op jit(solution)/shard_map/ppermute | solution.py:233
  469.2 6.5 collective-permute-start.9
  469.9 7.0 %collective-permute-start.10 = (bf16[384,128]{1,0:T(8,128)(2,1)}, bf16[384,128]{1,0:T(8,128)(2,1)S(1)}, u32[]{:S(2)}, u32[]{:S(2)}) collective-permute-start(bf16[384,128]{1,0:T(8,128)(2,1)} %get-tuple-element.70), channel_id=1, source_target_pairs={{0,20},{4,16},{8,28},{12,24},{16,4},{20,0},{24,12},{28,8},{1,21},{... | collective-permute-start | bytes 294920 | tf_op jit(solution)/shard_map/ppermute | solution.py:233
  471.3 8.2 %collective-permute-start.11 = (bf16[384,128]{1,0:T(8,128)(2,1)}, bf16[384,128]{1,0:T(8,128)(2,1)S(1)}, u32[]{:S(2)}, u32[]{:S(2)}) collective-permute-start(bf16[384,128]{1,0:T(8,128)(2,1)} %get-tuple-element.71), channel_id=1, source_target_pairs={{0,24},{4,28},{8,16},{12,20},{16,8},{20,12},{24,0},{28,4},{1,25},{... | collective-permute-start | bytes 294920 | tf_op jit(solution)/shard_map/ppermute | solution.py:233
  474.3 6.5 collective-permute-start.12
  490.5 58.5 %all-gather.24.cloned.1.call-start = ((), (), s32[]{:S(2)}) async-start(), calls=%async_computation.7 | async-start | bytes 2359296 | tf_op jit(solution)/shard_map/all_gather | solution.py:240
  502.1 76.5 %all-gather.22.cloned.1.call-start = ((), (), s32[]{:S(2)}) async-start(), calls=%async_computation.6 | async-start | bytes 2359296 | tf_op jit(solution)/shard_map/all_gather | solution.py:240
  514.0 94.5 %all-gather.20.cloned.1.call-start = ((), (), s32[]{:S(2)}) async-start(), calls=%async_computation.5 | async-start | bytes 2359296 | tf_op jit(solution)/shard_map/all_gather | solution.py:240
  525.9 112.4 %all-gather.18.cloned.1.call-start = ((), (), s32[]{:S(2)}) async-start(), calls=%async_computation.4 | async-start | bytes 2359296 | tf_op jit(solution)/shard_map/all_gather | solution.py:240
  587.4 29.7 %copy-start.19 = (bf16[1024,128]{1,0:T(8,128)(2,1)S(1)}, bf16[1024,128]{1,0:T(8,128)(2,1)}, u32[]{:S(2)}) copy-start(bf16[1024,128]{1,0:T(8,128)(2,1)} %get-tuple-element.114) | copy-start | bytes 786436
  (50 other events, 534.0 us)
Sparse Core Ops, SparseCore 0:
  301.6 28.9 all-gather.15
  366.2 28.0 all-gather.13
  459.8 29.7 all-gather.11
  491.4 27.9 all-gather.9
  521.0 27.8 all-gather.23
  550.7 27.8 all-gather.21
  580.5 27.8 all-gather.19
  610.3 27.8 all-gather.17

commit v2 on v1

v2 whole, which is shorter than its diff:
```python
import functools

import jax
import jax.numpy as jnp
from jax import lax
from jax.experimental import pallas as pl
from jax.experimental.pallas import tpu as pltpu
from jax.sharding import PartitionSpec as P

TILE = 128
STACK = 4
VMEM_BYTES = 56 * 1024 * 1024


def largest_tile(total, most):
    best = total
    for size in range(16, most + 1, 16):
        if total % size == 0:
            best = size
    return best


def kernel_params():
    return pltpu.CompilerParams(vmem_limit_bytes=VMEM_BYTES)


def whole_block(*shape):
    return pl.BlockSpec(shape, lambda *_: (0,) * len(shape))


def dot32(left, right):
    return jnp.dot(left, right, preferred_element_type=jnp.float32)


def front_kernel(start, stop, n_col, flat, meta_ref, tiles_ref, front_ref, out_ref, stack, acc, rows_of, count):
    span = stop - start
    groups = n_col * span

    @pl.when(pl.program_id(0) == 0)
    def build():
        for g in range(groups):
            count[g] = 0

        @pl.loop(0, tiles_ref.shape[0])
        def place(t):
            sub = meta_ref[2, t]

            @pl.when((sub >= start) & (sub < stop))
            def _():
                g = meta_ref[1, t] * span + sub - start
                at = count[g]
                rows_of[g, at] = meta_ref[0, t]
                stack[g, pl.ds(pl.multiple_of(at * TILE, TILE), TILE), :] = tiles_ref[t]
                count[g] = at + 1

        for g in range(groups):
            used = count[g]
            padded = (used + STACK - 1) // STACK * STACK

            @pl.loop(used, padded)
            def fill(at):
                rows_of[g, at] = 0
                stack[g, pl.ds(pl.multiple_of(at * TILE, TILE), TILE), :] = jnp.zeros(
                    (TILE, TILE), stack.dtype
                )

    for g in range(groups):
        acc[...] = jnp.zeros_like(acc)

        @pl.loop(0, (count[g] + STACK - 1) // STACK)
        def add(s):
            pieces = []
            for j in range(STACK):
                left = pl.multiple_of(rows_of[g, s * STACK + j] * TILE, TILE)
                pieces.append(front_ref[:, pl.ds(left, TILE)])
            deep = STACK * TILE
            tiles = stack[g, pl.ds(pl.multiple_of(s * deep, deep), deep), :]
            acc[...] += dot32(jnp.concatenate(pieces, axis=1), tiles)

        dest, sub = g // span, g % span
        if flat:
            out_ref[:, g * TILE : (g + 1) * TILE] = acc[...].astype(out_ref.dtype)
        else:
            out_ref[dest, :, sub * TILE : (sub + 1) * TILE] = acc[...].astype(out_ref.dtype)


def front_products(front, tiles, meta, start, stop, n_col, flat):
    rows, depth = front.shape
    span = stop - start
    width = span * TILE
    block = largest_tile(rows, 512)
    deepest = -(-depth // (TILE * STACK)) * STACK
    if flat:
        shape, spec = (rows, n_col * width), pl.BlockSpec((block, n_col * width), lambda i, m: (i, 0))
    else:
        shape, spec = (n_col, rows, width), pl.BlockSpec((n_col, block, width), lambda i, m: (0, i, 0))
    return pl.pallas_call(
        functools.partial(front_kernel, start, stop, n_col, flat),
        grid_spec=pltpu.PrefetchScalarGridSpec(
            num_scalar_prefetch=1,
            grid=(rows // block,),
            in_specs=[
                pl.BlockSpec(tiles.shape, lambda i, m: (0, 0, 0), pipeline_mode=pl.Buffered(1)),
                pl.BlockSpec((block, depth), lambda i, m: (i, 0)),
            ],
            out_specs=spec,
            scratch_shapes=[
                pltpu.VMEM((n_col * span, deepest * TILE, TILE), front.dtype),
                pltpu.VMEM((block, TILE), jnp.float32),
                pltpu.SMEM((n_col * span, deepest), jnp.int32),
                pltpu.SMEM((n_col * span,), jnp.int32),
            ],
        ),
        out_shape=jax.ShapeDtypeStruct(shape, front.dtype),
        compiler_params=kernel_params(),
        cost_estimate=pl.CostEstimate(
            flops=rows * depth * n_col * width,
            bytes_accessed=2 * (rows * depth + tiles.size + rows * n_col * width),
            transcendentals=0,
        ),
        name="front_products",
    )(meta, tiles, front)


def one_hot(want, depth, kind):
    places = lax.broadcasted_iota(jnp.int32, (want.shape[0], depth), 1)
    return (places == want).astype(jnp.float32).astype(kind)


def pack_kernel(n_row, index_ref, solved_ref, *outs):
    cap = outs[0].shape[0]
    for k in range(n_row):
        picks = one_hot(index_ref[k * cap : (k + 1) * cap, :], solved_ref.shape[0], solved_ref.dtype)
        outs[k][...] = dot32(picks, solved_ref[...]).astype(outs[k].dtype)


def pack_rows(index, solved, n_row, cap):
    depth, width = solved.shape
    return pl.pallas_call(
        functools.partial(pack_kernel, n_row),
        out_shape=[jax.ShapeDtypeStruct((cap, width), solved.dtype)] * n_row,
        compiler_params=kernel_params(),
        cost_estimate=pl.CostEstimate(
            flops=2 * n_row * cap * depth * max(width, 256),
            bytes_accessed=4 * n_row * cap * width,
            transcendentals=0,
        ),
        name="pack_rows",
    )(index, solved)


def join_pieces(pieces, joined):
    cap = pieces[0].shape[0]
    for k, piece in enumerate(pieces):
        joined[k * cap : (k + 1) * cap, :] = piece[...]


def assemble_kernel(n_row, index_ref, bem_ref, *refs):
    outs, joined = refs[n_row : n_row + 2], refs[n_row + 2]
    join_pieces(refs[:n_row], joined)
    count = outs[0].shape[0]
    step = largest_tile(count, 512)
    for half, out in enumerate(outs):
        for i in range(0, count, step):
            want = index_ref[half * count + i : half * count + i + step, :]
            taken = dot32(one_hot(want, joined.shape[0], joined.dtype), joined[...])
            entries = bem_ref[half, i : i + step, :].astype(jnp.float32)
            out[i : i + step, :] = (entries - taken).astype(out.dtype)


def assemble(index, bem, pieces, start, n_row):
    cap, width = pieces[0].shape
    count = bem.shape[1]
    place = start * TILE // width
    return pl.pallas_call(
        functools.partial(assemble_kernel, n_row),
        grid=(1,),
        in_specs=[
            whole_block(*index.shape),
            pl.BlockSpec((2, count, width), lambda i: (0, 0, place)),
        ]
        + [whole_block(cap, width)] * n_row,
        out_specs=[whole_block(count, width)] * 2,
        out_shape=[jax.ShapeDtypeStruct((count, width), bem.dtype)] * 2,
        scratch_shapes=[pltpu.VMEM((n_row * cap, width), bem.dtype)],
        compiler_params=kernel_params(),
        cost_estimate=pl.CostEstimate(
            flops=2 * 2 * count * n_row * cap * max(width, 256),
            bytes_accessed=2 * (n_row * cap + 4 * count) * width,
            transcendentals=0,
        ),
        name="assemble",
    )(index, bem, *pieces)


def unpack_kernel(n_row, index_ref, *refs):
    out, joined = refs[n_row], refs[n_row + 1]
    join_pieces(refs[:n_row], joined)
    n_col, count, width = out.shape
    step = largest_tile(count, 512)
    for i in range(0, count, step):
        taken = dot32(one_hot(index_ref[i : i + step, :], joined.shape[0], joined.dtype), joined[...])
        for d in range(n_col):
            out[d, i : i + step, :] = taken[:, d * width : (d + 1) * width].astype(out.dtype)


def unpack(index, pieces, n_row, n_col):
    cap, wide = pieces[0].shape
    count, width = index.shape[0], wide // n_col
    return pl.pallas_call(
        functools.partial(unpack_kernel, n_row),
        out_shape=jax.ShapeDtypeStruct((n_col, count, width), pieces[0].dtype),
        scratch_shapes=[pltpu.VMEM((n_row * cap, wide), pieces[0].dtype)],
        compiler_params=kernel_params(),
        cost_estimate=pl.CostEstimate(
            flops=2 * count * n_row * cap * wide,
            bytes_accessed=2 * (n_row * cap + count) * wide,
            transcendentals=0,
        ),
        name="unpack",
    )(index, *pieces)


def product_kernel(minus, order_ref, matrix_ref, near_ref, far_ref, *refs):
    base_ref, out_ref, acc = refs if minus else (None, *refs)
    k = pl.program_id(0)
    steps = pl.num_programs(0)
    half = steps // 2
    deep = matrix_ref.shape[1]

    @pl.when(k == 0)
    def _():
        acc[...] = dot32(matrix_ref[...], near_ref[pl.ds(0, deep), :])

    @pl.when((k > 0) & (k < half))
    def _():
        at = pl.multiple_of(k * deep, deep)
        acc[...] += dot32(matrix_ref[...], near_ref[pl.ds(at, deep), :])

    @pl.when(k >= half)
    def _():
        at = pl.multiple_of((k - half) * deep, deep)
        acc[...] += dot32(matrix_ref[...], far_ref[pl.ds(at, deep), :])

    @pl.when(k == steps - 1)
    def _():
        total = acc[...]
        if minus:
            total = base_ref[...].astype(jnp.float32) - total
        out_ref[...] = total.astype(out_ref.dtype)


def product(matrix, order, near, far, base=None):
    rows, depth = matrix.shape
    width = near.shape[1]
    n_row = order.shape[0]
    deep = depth // n_row
    bases = [] if base is None else [base]
    return pl.pallas_call(
        functools.partial(product_kernel, bool(bases)),
        grid_spec=pltpu.PrefetchScalarGridSpec(
            num_scalar_prefetch=1,
            grid=(n_row,),
            in_specs=[pl.BlockSpec((rows, deep), lambda k, order: (0, order[k]))]
            + [whole_block(*near.shape)] * 2
            + [whole_block(rows, width)] * len(bases),
            out_specs=whole_block(rows, width),
            scratch_shapes=[pltpu.VMEM((rows, width), jnp.float32)],
        ),
        out_shape=jax.ShapeDtypeStruct((rows, width), near.dtype),
        compiler_params=kernel_params(),
        cost_estimate=pl.CostEstimate(
            flops=2 * rows * depth * max(width, 256),
            bytes_accessed=2 * (rows * depth + (depth + 2 * rows) * width),
            transcendentals=0,
        ),
        name="product",
    )(order, matrix, near, far, *bases)


def exchange(value, distance, n_row):
    return lax.ppermute(value, "row", [(i, i ^ distance) for i in range(n_row)])


def route(packed, n_row):
    return [packed[0]] + [exchange(packed[k], k, n_row) for k in range(1, n_row)]


def gather_rows(block, n_row):
    near = [block] + [exchange(block, k, n_row) for k in range(2, n_row, 2)]
    near = jnp.concatenate(near, axis=0)
    return near, exchange(near, 1, n_row)


def route_tables(surface_map, rows, n_row, cap, slots):
    me = lax.axis_index("row")
    mine = surface_map.reshape(-1)
    every = lax.all_gather(mine, "row")
    partners = me ^ jnp.arange(n_row, dtype=jnp.int32)
    local = every[partners] - me * rows
    asked = (local >= 0) & (local < rows)
    rank = jnp.cumsum(asked.astype(jnp.int32), axis=1) - 1
    numbers = jnp.arange(slots, dtype=jnp.int32)
    hit = asked[:, None, :] & (rank[:, None, :] == numbers[None, :, None])
    wanted = jnp.sum(jnp.where(hit, local[:, None, :] + 1, 0), axis=2) - 1
    owner = mine // rows
    held = owner[None, :] == jnp.arange(n_row, dtype=jnp.int32)[:, None]
    place = jnp.cumsum(held.astype(jnp.int32), axis=1) - 1
    slot = jnp.sum(jnp.where(held, place, 0), axis=0)
    lands = (owner ^ me) * slots + slot
    return wanted.reshape(-1, 1), lands.reshape(-1, 1)


def per_device(
    front_inverse,
    coupling_tiles,
    tile_row,
    tile_col,
    surface_map,
    bem_entries,
    pivot_inverse,
    slab_below,
):
    n_row, n_col = lax.axis_size("row"), lax.axis_size("col")
    assert n_row > 1 and n_row & (n_row - 1) == 0
    rows, depth = front_inverse.shape
    count = bem_entries.shape[1]
    per_dest = bem_entries.shape[2] // TILE
    cap = rows // n_row
    slots = -(-cap // 16) * 16
    me = lax.axis_index("row")

    meta = jnp.stack(
        [tile_row - lax.axis_index("col") * (depth // TILE), tile_col // per_dest, tile_col % per_dest]
    )
    order = me ^ jnp.concatenate(
        [jnp.arange(0, n_row, 2, dtype=jnp.int32), jnp.arange(1, n_row, 2, dtype=jnp.int32)]
    )
    half = per_dest // 2
    first = front_products(front_inverse, coupling_tiles, meta, 0, half, n_col, False)
    first = lax.psum_scatter(first, "col", scatter_dimension=0)
    wanted, lands = route_tables(surface_map, rows, n_row, cap, slots)

    later = []
    for start in range(half, per_dest):
        parts = front_products(
            front_inverse, coupling_tiles, meta, start, start + 1, n_col, True
        )
        pieces = route(pack_rows(wanted, parts, n_row, slots), n_row)
        parts = unpack(lands, pieces, n_row, n_col)
        later.append(lax.psum_scatter(parts, "col", scatter_dimension=0))

    pieces = route(pack_rows(wanted, first, n_row, slots), n_row)
    assembled = [assemble(lands, bem_entries, pieces, 0, n_row)]
    for start, schur in zip(range(half, per_dest), later):
        entries = bem_entries[:, :, start * TILE : (start + 1) * TILE].astype(jnp.float32)
        both = entries - schur.reshape(2, count, TILE).astype(jnp.float32)
        both = both.astype(bem_entries.dtype)
        assembled.append((both[0], both[1]))

    pivots, belows = [], []
    for upper, lower in assembled:
        pivot = product(pivot_inverse, order, *gather_rows(upper, n_row))
        pivots.append(pivot)
        belows.append(product(slab_below, order, *gather_rows(pivot, n_row), lower))
    return jnp.stack([jnp.concatenate(pivots, axis=1), jnp.concatenate(belows, axis=1)])


def solution(mesh):
    placed = (
        P("row", "col"),
        P("col", None, None),
        P("col"),
        P("col"),
        P(None, "row"),
        P(None, "row", "col"),
        P("row", None),
        P("row", None),
    )
    return jax.shard_map(
        per_device, mesh=mesh, in_specs=placed, out_specs=P(None, "row", "col"), check_vma=False
    )
```

time: 662 us -> 508 us (0.77)
  matrix products: 80.8 us -> 0 us
  Pallas kernels: 193 us -> 271 us
  starting transfers between devices: 111 us -> 36.7 us
  waiting for transfers between devices: 197 us -> 132 us
  other arithmetic: 42.8 us -> 21.5 us
  local copies, waits for them, and re-layouts: 6.77 us -> 14.2 us
    pallas_call x4 -> x11, Pallas kernels: 127 us -> 231 us  [the longest x3 133 us: front_products(): pl.pallas_call(functools.partial(front_kernel, start, stop, n_col, flat),...]
    dot_general x8 -> x0, matrix products: 80.8 us -> none  [the longest x4 45.9 us: per_device(): pivot = jnp.dot(pivot_inverse, gathered, preferred_element_type=jnp.float32)]
    all_gather x8 -> x0, waiting for transfers between devices: 73.8 us -> none  [the longest x4 73.8 us: per_device(): lax.all_gather(pivot, 'row', axis=0, tiled=True)]
    ppermute x52 -> x45, starting transfers between devices: 110 us -> 36.6 us  [exchange(): return lax.ppermute(value, 'row', [(i, i ^ distance) for i in range(n_row)])]
    pallas_call x4 -> x1, Pallas kernels: 36.2 us -> 6.28 us  [assemble(): pl.pallas_call(functools.partial(assemble_kernel, n_row), grid=(1,), in_s...]
    convert_element_type x18 -> x1, other arithmetic: 26.4 us -> 2.44 us  [per_device(): both = both.astype(bem_entries.dtype)]
    ppermute x52 -> x45, waiting for transfers between devices: 123 us -> 132 us  [exchange(): return lax.ppermute(value, 'row', [(i, i ^ distance) for i in range(n_row)])]
    pallas_call x4 -> x3, Pallas kernels: 29.6 us -> 34.1 us  [pack_rows(): pl.pallas_call(functools.partial(pack_kernel, n_row), out_shape=[jax.Shap...]
  transfers between devices with their start and end apart: 60 -> 48, of which waited for: 23 -> 20; matrix products, arithmetic and copies ran while one was open for 18% -> 5% of each run, Pallas kernels for 25% -> 39%
where the time goes in v2:
time: 508 us; the launch traced here: 500 us
  Pallas kernels  271 us (53%)
  waiting for transfers between devices  132 us (26%)
  starting transfers between devices  36.7 us (7%)
  other arithmetic  21.5 us (4%)
  local copies, waits for them, and re-layouts  14.2 us (3%)
  between operations  14.2 us (3%)
  blocking collectives  10.9 us (2%)
    pallas_call x3, Pallas kernels, front_products(): pl.pallas_call(functools.partial(front_kernel, start, stop, n_col, flat),...  133 us
    ppermute x45, waiting for transfers between devices, exchange(): return lax.ppermute(value, 'row', [(i, i ^ distance) for i in range(n_row)])  132 us
    pallas_call x6, Pallas kernels, product(): pl.pallas_call(functools.partial(product_kernel, bool(bases)), grid_spec=...  77.3 us
    ppermute x45, starting transfers between devices, exchange(): return lax.ppermute(value, 'row', [(i, i ^ distance) for i in range(n_row)])  36.6 us
    pallas_call x3, Pallas kernels, pack_rows(): pl.pallas_call(functools.partial(pack_kernel, n_row), out_shape=[jax.Shap...  34.1 us
    pallas_call x2, Pallas kernels, unpack(): pl.pallas_call(functools.partial(unpack_kernel, n_row), out_shape=jax.Sha...  20.3 us
    unnamed x82, local copies, waits for them, and re-layouts  11.1 us
    all_gather x1, blocking collectives, route_tables(): every = lax.all_gather(mine, 'row')  10.9 us
  transfers between devices with their start and end apart: 48, of which 20 were waited for; matrix products, arithmetic and copies ran while one was open for 5% of the time, Pallas kernels for 39%

profile of v2, /device:TPU:0, one launch (start us, length us, event | category | flops | bytes accessed | tf_op | source)
XLA Modules:
  0.0 500.4 jit_solution(8162664111744008411)
XLA Ops:
  8.5 60.9 %front_products.3 = bf16[4,3072,256]{2,1,0:T(8,128)(2,1)} custom-call(s32[3,192]{1,0:T(4,128)} %pad_add_fusion.meta_ref, bf16[192,128,128]{2,1,0:T(8,128)(2,1)} %tiles_ref.5, bf16[3072,6144]{1,0:T(8,128)(2,1)} %front_ref.5), custom_call_target="tpu_custom_call" | custom-call | flops 19327352832 | bytes 50331648 | tf_op jit(solution)/shard_map/front_products/pallas_call | solution.py:97
  70.1 10.9 %all-gather = s32[8,1,2048]{2,1,0:T(1,128)S(1)} all-gather(s32[1,1,2048]{2,1,0:T(1,128)S(1)} %reshape.218), channel_id=1, replica_groups=mesh['row'=8,'col'=4] {'row'}, dimensions={0}, use_global_device_ids=true | all-gather | bytes 73728 | tf_op jit(solution)/shard_map/all_gather | solution.py:298
  81.7 2.3 reduce-window.16
  84.6 6.2 %select_reduce_fusion = s32[8,384]{1,0:T(8,128)S(1)} fusion(s32[8,2048]{1,0:T(8,128)S(1)} %subtract_add_fusion, s32[8,2048]{1,0:T(8,128)S(1)} %bitcast.58, pred[8,2048]{1,0:T(8,128)(4,1)S(1)} %get-tuple-element.58), kind=kLoop, calls=%fused_computation.1 | loop fusion | flops 25162752 | bytes 159744 | tf_op jit(solution)/shard_map/reduce_sum | solution.py:305
  90.8 1.7 copy.41
  92.5 37.1 %front_products.5.solved_ref = bf16[3072,512]{1,0:T(8,128)(2,1)} custom-call(s32[3,192]{1,0:T(4,128)} %pad_add_fusion.meta_ref, bf16[192,128,128]{2,1,0:T(8,128)(2,1)} %tiles_ref.5, bf16[3072,6144]{1,0:T(8,128)(2,1)} %front_ref.5), custom_call_target="tpu_custom_call" | custom-call | flops 9663676416 | bytes 47185920 | tf_op jit(solution)/shard_map/front_products/pallas_call | solution.py:97
  129.6 13.1 %pack_rows.5 = (bf16[384,512]{1,0:T(8,128)(2,1)}, bf16[384,512]{1,0:T(8,128)(2,1)}, bf16[384,512]{1,0:T(8,128)(2,1)}, bf16[384,512]{1,0:T(8,128)(2,1)}, bf16[384...) custom-call(s32[3072,1]{1,0:T(8,128)} %bitcast.53, ...), custom_call_target="tpu_custom_call" | custom-call | flops 9663676416 | bytes 6291456 | tf_op jit(solution)/shard_map/pack_rows/pallas_call | solution.py:139
  143.0 1.5 collective-permute-start.23
  144.5 1.5 collective-permute-start.25
  146.6 2.7 reduce-window.14
  151.2 1.5 collective-permute-start.27
  152.7 2.5 collective-permute-done.23.refs_2_
  155.2 1.2 fusion.3.index_ref
  156.5 6.2 %collective-permute-done.24.refs_3_ = bf16[384,512]{1,0:T(8,128)(2,1)} collective-permute-done((bf16[384,512]{1,0:T(8,128)(2,1)}, bf16[384,512]{1,0:T(8,128)(2,1)}, u32[]{:S(2)}, u32[]{:S(2)}) %collective-permute-start.24) | collective-permute-done | bytes 393248 | tf_op jit(solution)/shard_map/ppermute | solution.py:282
  162.7 18.8 %collective-permute-done.26.refs_5_ = bf16[384,512]{1,0:T(8,128)(2,1)} collective-permute-done((bf16[384,512]{1,0:T(8,128)(2,1)}, bf16[384,512]{1,0:T(8,128)(2,1)}, u32[]{:S(2)}, u32[]{:S(2)}) %collective-permute-start.26) | collective-permute-done | bytes 393248 | tf_op jit(solution)/shard_map/ppermute | solution.py:282
  182.3 10.1 %unpack.3 = bf16[4,2048,128]{2,1,0:T(8,128)(2,1)} custom-call(s32[2048,1]{1,0:T(8,128)} %fusion.3.index_ref, bf16[384,512]{1,0:T(8,128)(2,1)} %get-tuple-element.48.refs_0_, bf16[384,512]{1,0:T(8,128)(2,1)} %copy-done.17, bf16[384,512]{1,0:T(8,128)(2,1)} %collective-permute-done.23.refs_2_, bf16[384,512]{1,0:T(8,128)(2,1)} %collective-permute-done.24.refs_3_, ...), custom_call_target="tpu_custom_call" | custom-call | flops 6442450944 | bytes 5242880 | tf_op jit(solution)/shard_map/unpack/pallas_call | solution.py:210
  192.5 35.0 %front_products.4.solved_ref = bf16[3072,512]{1,0:T(8,128)(2,1)} custom-call(s32[3,192]{1,0:T(4,128)} %pad_add_fusion.meta_ref, bf16[192,128,128]{2,1,0:T(8,128)(2,1)} %tiles_ref.5, bf16[3072,6144]{1,0:T(8,128)(2,1)} %front_ref.5), custom_call_target="tpu_custom_call" | custom-call | flops 9663676416 | bytes 47185920 | tf_op jit(solution)/shard_map/front_products/pallas_call | solution.py:97
  227.6 13.1 %pack_rows.4 = (bf16[384,512]{1,0:T(8,128)(2,1)}, bf16[384,512]{1,0:T(8,128)(2,1)}, bf16[384,512]{1,0:T(8,128)(2,1)}, bf16[384,512]{1,0:T(8,128)(2,1)}, bf16[384...) custom-call(s32[3072,1]{1,0:T(8,128)} %bitcast.54, ...), custom_call_target="tpu_custom_call" | custom-call | flops 9663676416 | bytes 6291456 | tf_op jit(solution)/shard_map/pack_rows/pallas_call | solution.py:139
  241.1 1.5 collective-permute-start.12
  242.6 1.4 collective-permute-start.14
  244.6 1.5 collective-permute-start.16
  246.0 7.2 %collective-permute-done.12.refs_2_ = bf16[384,512]{1,0:T(8,128)(2,1)S(1)} collective-permute-done((bf16[384,512]{1,0:T(8,128)(2,1)}, bf16[384,512]{1,0:T(8,128)(2,1)S(1)}, u32[]{:S(2)}, u32[]{:S(2)}) %collective-permute-start.12) | collective-permute-done | bytes 393248 | tf_op jit(solution)/shard_map/ppermute | solution.py:282
  253.2 7.5 %collective-permute-done.13.refs_3_ = bf16[384,512]{1,0:T(8,128)(2,1)S(1)} collective-permute-done((bf16[384,512]{1,0:T(8,128)(2,1)}, bf16[384,512]{1,0:T(8,128)(2,1)S(1)}, u32[]{:S(2)}, u32[]{:S(2)}) %collective-permute-start.13) | collective-permute-done | bytes 393248 | tf_op jit(solution)/shard_map/ppermute | solution.py:282
  260.8 18.7 %collective-permute-done.15.refs_5_ = bf16[384,512]{1,0:T(8,128)(2,1)S(1)} collective-permute-done((bf16[384,512]{1,0:T(8,128)(2,1)}, bf16[384,512]{1,0:T(8,128)(2,1)S(1)}, u32[]{:S(2)}, u32[]{:S(2)}) %collective-permute-start.15) | collective-permute-done | bytes 393248 | tf_op jit(solution)/shard_map/ppermute | solution.py:282
  280.5 10.2 %unpack.2 = bf16[4,2048,128]{2,1,0:T(8,128)(2,1)} custom-call(s32[2048,1]{1,0:T(8,128)} %fusion.3.index_ref, bf16[384,512]{1,0:T(8,128)(2,1)} %get-tuple-element.40.refs_0_, bf16[384,512]{1,0:T(8,128)(2,1)} %copy-done.19, bf16[384,512]{1,0:T(8,128)(2,1)} %copy-done.20, bf16[384,512]{1,0:T(8,128)(2,1)} %copy-done.21, bf16[384,512]{1,0:T(8,128)(2,1)} %copy-done.22, ...), custom_call_target="tpu_custom_call" | custom-call | flops 6442450944 | bytes 5242880 | tf_op jit(solution)/shard_map/unpack/pallas_call | solution.py:210
  290.7 7.9 %pack_rows.3 = (bf16[384,256]{1,0:T(8,128)(2,1)}, bf16[384,256]{1,0:T(8,128)(2,1)}, bf16[384,256]{1,0:T(8,128)(2,1)}, bf16[384,256]{1,0:T(8,128)(2,1)}, bf16[384...) custom-call(s32[3072,1]{1,0:T(8,128)} %bitcast.55, ...), custom_call_target="tpu_custom_call" | custom-call | flops 4831838208 | bytes 3145728 | tf_op jit(solution)/shard_map/pack_rows/pallas_call | solution.py:139
  298.8 1.5 collective-permute-start.1
  300.5 1.6 collective-permute-start.3
  302.3 1.5 collective-permute-start.5
  303.7 2.9 collective-permute-done.1.refs_2_
  307.0 3.0 collective-permute-done.2.refs_3_
  310.0 9.9 %collective-permute-done.4.refs_5_ = bf16[384,256]{1,0:T(8,128)(2,1)S(1)} collective-permute-done((bf16[384,256]{1,0:T(8,128)(2,1)}, bf16[384,256]{1,0:T(8,128)(2,1)S(1)}, u32[]{:S(2)}, u32[]{:S(2)}) %collective-permute-start.4) | collective-permute-done | bytes 196640 | tf_op jit(solution)/shard_map/ppermute | solution.py:282
  320.8 6.3 %assemble.1 = (bf16[1024,256]{1,0:T(8,128)(2,1)}, bf16[1024,256]{1,0:T(8,128)(2,1)}) custom-call(s32[2048,1]{1,0:T(8,128)} %fusion.3.index_ref, bf16[2,1024,512]{2,1,0:T(8,128)(2,1)} %bem_ref.1, bf16[384,256]{1,0:T(8,128)(2,1)} %get-tuple-element.31.refs_0_, bf16[384,256]{1,0:T(8,128)(2,1)} %copy-done.28, bf16[384,256]{1,0:T(8,128)(2,1)} %copy-done.29, ...), custom_call_target="tpu_custom_call" | custom-call | flops 3221225472 | bytes 3670016 | tf_op jit(solution)/shard_map/assemble/pallas_call | solution.py:175
  327.1 1.6 collective-permute-start.7
  329.1 1.4 collective-permute-start.9
  330.6 1.1 constant_dynamic-update-slice_fusion.3
  331.7 10.4 %collective-permute-done.7 = bf16[1024,256]{1,0:T(8,128)(2,1)S(1)} collective-permute-done((bf16[1024,256]{1,0:T(8,128)(2,1)}, bf16[1024,256]{1,0:T(8,128)(2,1)S(1)}, u32[]{:S(2)}, u32[]{:S(2)}) %collective-permute-start.7) | collective-permute-done | bytes 524320 | tf_op jit(solution)/shard_map/ppermute | solution.py:282
  342.1 12.3 %collective-permute-done.8 = bf16[1024,256]{1,0:T(8,128)(2,1)S(1)} collective-permute-done((bf16[1024,256]{1,0:T(8,128)(2,1)}, bf16[1024,256]{1,0:T(8,128)(2,1)S(1)}, u32[]{:S(2)}, u32[]{:S(2)}) %collective-permute-start.8) | collective-permute-done | bytes 524320 | tf_op jit(solution)/shard_map/ppermute | solution.py:282
  354.7 2.4 fusion.5
  358.4 1.5 collective-permute-start.19
  359.9 1.5 collective-permute-start.20
  362.6 4.5 collective-permute-done.18
  367.6 3.4 collective-permute-done.19
  371.0 1.6 collective-permute-start.31
  372.8 5.5 %collective-permute-done.29 = bf16[1024,128]{1,0:T(8,128)(2,1)S(1)} collective-permute-done((bf16[1024,128]{1,0:T(8,128)(2,1)S(1)}, bf16[1024,128]{1,0:T(8,128)(2,1)S(1)}, u32[]{:S(2)}, u32[]{:S(2)}) %collective-permute-start.29) | collective-permute-done | bytes 262176 | tf_op jit(solution)/shard_map/ppermute | solution.py:282
  378.4 4.6 collective-permute-done.30
  383.9 13.3 %product.6 = bf16[1024,256]{1,0:T(8,128)(2,1)} custom-call(s32[8]{0:T(128)} %add_xor_fusion.order_ref, bf16[1024,8192]{1,0:T(8,128)(2,1)} %matrix_ref.8, bf16[4096,256]{1,0:T(8,128)(2,1)} %copy-done.6, bf16[4096,256]{1,0:T(8,128)(2,1)} %collective-permute-done.10.far_ref), custom_call_target="tpu_custom_call" | custom-call | flops 4294967296 | bytes 22020096 | tf_op jit(solution)/shard_map/product/pallas_call | solution.py:259
  397.2 1.6 collective-permute-start.33
  399.3 1.5 collective-permute-start.35
  401.8 12.8 %product.7 = bf16[1024,128]{1,0:T(8,128)(2,1)} custom-call(s32[8]{0:T(128)} %add_xor_fusion.order_ref, bf16[1024,8192]{1,0:T(8,128)(2,1)} %matrix_ref.8, bf16[4096,128]{1,0:T(8,128)(2,1)} %copy-done.2, bf16[4096,128]{1,0:T(8,128)(2,1)} %copy-done.12), custom_call_target="tpu_custom_call" | custom-call | flops 4294967296 | bytes 19398656 | tf_op jit(solution)/shard_map/product/pallas_call | solution.py:259
  414.5 1.5 collective-permute-start.37
  417.1 12.5 %product.8 = bf16[1024,128]{1,0:T(8,128)(2,1)} custom-call(s32[8]{0:T(128)} %add_xor_fusion.order_ref, bf16[1024,8192]{1,0:T(8,128)(2,1)} %matrix_ref.8, bf16[4096,128]{1,0:T(8,128)(2,1)} %copy-done.3, bf16[4096,128]{1,0:T(8,128)(2,1)} %copy-done.13), custom_call_target="tpu_custom_call" | custom-call | flops 4294967296 | bytes 19398656 | tf_op jit(solution)/shard_map/product/pallas_call | solution.py:259
  429.6 1.5 collective-permute-start.39
  433.4 1.5 collective-permute-start.43
  434.9 5.0 collective-permute-done.39
  440.0 5.0 %collective-permute-done.41 = bf16[1024,128]{1,0:T(8,128)(2,1)S(1)} collective-permute-done((bf16[1024,128]{1,0:T(8,128)(2,1)}, bf16[1024,128]{1,0:T(8,128)(2,1)S(1)}, u32[]{:S(2)}, u32[]{:S(2)}) %collective-permute-start.41) | collective-permute-done | bytes 262176 | tf_op jit(solution)/shard_map/ppermute | solution.py:282
  445.4 3.9 collective-permute-done.43
  449.5 1.1 copy-done.14
  450.6 12.6 %product.10 = bf16[1024,128]{1,0:T(8,128)(2,1)} custom-call(s32[8]{0:T(128)} %add_xor_fusion.order_ref, bf16[1024,8192]{1,0:T(8,128)(2,1)} %matrix_ref.11, bf16[4096,128]{1,0:T(8,128)(2,1)} %copy-done.4, bf16[4096,128]{1,0:T(8,128)(2,1)} %copy-done.14, bf16[1024,128]{1,0:T(8,128)(2,1)} %get-tuple-element.61.refs_0_), custom_call_target="tpu_custom_call" | custom-call | flops 4294967296 | bytes 19398656 | tf_op jit(solution)/shard_map/product/pallas_call | solution.py:259
  463.2 12.6 %product.11 = bf16[1024,128]{1,0:T(8,128)(2,1)} custom-call(s32[8]{0:T(128)} %add_xor_fusion.order_ref, bf16[1024,8192]{1,0:T(8,128)(2,1)} %matrix_ref.11, bf16[4096,128]{1,0:T(8,128)(2,1)} %copy-done.5, bf16[4096,128]{1,0:T(8,128)(2,1)} %collective-permute-done.44.far_ref, bf16[1024,128]{1,0:T(8,128)(2,1)} %get-tuple-element.63.refs_0_), custom_call_target="tpu_custom_call" | custom-call | flops 4294967296 | bytes 19398656 | tf_op jit(solution)/shard_map/product/pallas_call | solution.py:259
  475.9 1.3 copy-done.9
  477.2 13.5 %product.9 = bf16[1024,256]{1,0:T(8,128)(2,1)} custom-call(s32[8]{0:T(128)} %add_xor_fusion.order_ref, bf16[1024,8192]{1,0:T(8,128)(2,1)} %matrix_ref.11, bf16[4096,256]{1,0:T(8,128)(2,1)} %copy-done, bf16[4096,256]{1,0:T(8,128)(2,1)} %copy-done.9, bf16[1024,256]{1,0:T(8,128)(2,1)} %get-tuple-element.56.refs_0_), custom_call_target="tpu_custom_call" | custom-call | flops 4294967296 | bytes 22020096 | tf_op jit(solution)/shard_map/product/pallas_call | solution.py:259
  490.8 1.1 maximum_bitcast_fusion.1
  491.9 1.5 pad_maximum_fusion.1
  (176 shorter events, 21.5 us)
Async XLA Ops:
  6.5 284.2 %reduce-scatter.4.cloned.1.call-start = ((), (), s32[]{:S(2)}) async-start(), calls=%async_computation.3 | async-start | bytes 7864320 | tf_op jit(solution)/shard_map/reduce_scatter | solution.py:341
  69.4 285.2 %reduce-scatter.8.cloned.1.call-start = ((), (), s32[]{:S(2)}) async-start(), calls=%async_computation.5 | async-start | bytes 2621440 | tf_op jit(solution)/shard_map/reduce_scatter | solution.py:351
  142.6 12.6 %copy-start.16 = (bf16[384,512]{1,0:T(8,128)(2,1)S(1)}, bf16[384,512]{1,0:T(8,128)(2,1)}, u32[]{:S(2)}) copy-start(bf16[384,512]{1,0:T(8,128)(2,1)} %get-tuple-element.55) | copy-start | bytes 1179652
  142.6 8.6 %collective-permute-start.22 = (bf16[384,512]{1,0:T(8,128)(2,1)}, bf16[384,512]{1,0:T(8,128)(2,1)S(1)}, u32[]{:S(2)}, u32[]{:S(2)}) collective-permute-start(bf16[384,512]{1,0:T(8,128)(2,1)} %get-tuple-element.49), channel_id=1, source_target_pairs={{0,4},{4,0},{8,12},{12,8},{16,20},{20,16},{24,28},{28,24},{1,5},{5... | collective-permute-start | bytes 1179656 | tf_op jit(solution)/shard_map/ppermute | solution.py:282
  143.0 12.3 %collective-permute-start.23 = (bf16[384,512]{1,0:T(8,128)(2,1)}, bf16[384,512]{1,0:T(8,128)(2,1)}, u32[]{:S(2)}, u32[]{:S(2)}) collective-permute-start(bf16[384,512]{1,0:T(8,128)(2,1)} %get-tuple-element.50), channel_id=1, source_target_pairs={{0,8},{4,12},{8,0},{12,4},{16,24},{20,28},{24,16},{28,20},{1,9},{5... | collective-permute-start | bytes 1179656 | tf_op jit(solution)/shard_map/ppermute | solution.py:282
  144.4 18.2 %collective-permute-start.24 = (bf16[384,512]{1,0:T(8,128)(2,1)}, bf16[384,512]{1,0:T(8,128)(2,1)}, u32[]{:S(2)}, u32[]{:S(2)}) collective-permute-start(bf16[384,512]{1,0:T(8,128)(2,1)} %get-tuple-element.51), channel_id=1, source_target_pairs={{0,12},{4,8},{8,4},{12,0},{16,28},{20,24},{24,20},{28,16},{1,13},{... | collective-permute-start | bytes 1179656 | tf_op jit(solution)/shard_map/ppermute | solution.py:282
  144.5 18.2 %collective-permute-start.25 = (bf16[384,512]{1,0:T(8,128)(2,1)}, bf16[384,512]{1,0:T(8,128)(2,1)}, u32[]{:S(2)}, u32[]{:S(2)}) collective-permute-start(bf16[384,512]{1,0:T(8,128)(2,1)} %get-tuple-element.52), channel_id=1, source_target_pairs={{0,16},{4,20},{8,24},{12,28},{16,0},{20,4},{24,8},{28,12},{1,17},{... | collective-permute-start | bytes 1179656 | tf_op jit(solution)/shard_map/ppermute | solution.py:282
  146.0 35.5 %collective-permute-start.26 = (bf16[384,512]{1,0:T(8,128)(2,1)}, bf16[384,512]{1,0:T(8,128)(2,1)}, u32[]{:S(2)}, u32[]{:S(2)}) collective-permute-start(bf16[384,512]{1,0:T(8,128)(2,1)} %get-tuple-element.53), channel_id=1, source_target_pairs={{0,20},{4,16},{8,28},{12,24},{16,4},{20,0},{24,12},{28,8},{1,21},{... | collective-permute-start | bytes 1179656 | tf_op jit(solution)/shard_map/ppermute | solution.py:282
  151.2 30.3 %copy-start.17 = (bf16[384,512]{1,0:T(8,128)(2,1)}, bf16[384,512]{1,0:T(8,128)(2,1)S(1)}, u32[]{:S(2)}) copy-start(bf16[384,512]{1,0:T(8,128)(2,1)S(1)} %collective-permute-done.22.refs_1_) | copy-start | bytes 1179652
  151.2 30.2 %collective-permute-start.27 = (bf16[384,512]{1,0:T(8,128)(2,1)S(1)}, bf16[384,512]{1,0:T(8,128)(2,1)S(1)}, u32[]{:S(2)}, u32[]{:S(2)}) collective-permute-start(bf16[384,512]{1,0:T(8,128)(2,1)S(1)} %copy-done.18), channel_id=1, source_target_pairs={{0,24},{4,28},{8,16},{12,20},{16,8},{20,12},{24,0},{28,4},{1,25},{... | collective-permute-start | bytes 1179656 | tf_op jit(solution)/shard_map/ppermute | solution.py:282
  155.2 26.2 %collective-permute-start.28 = (bf16[384,512]{1,0:T(8,128)(2,1)S(1)}, bf16[384,512]{1,0:T(8,128)(2,1)S(1)}, u32[]{:S(2)}, u32[]{:S(2)}) collective-permute-start(bf16[384,512]{1,0:T(8,128)(2,1)S(1)} %copy-done.16), channel_id=1, source_target_pairs={{0,28},{4,24},{8,20},{12,16},{16,12},{20,8},{24,4},{28,0},{1,29},{... | collective-permute-start | bytes 1179656 | tf_op jit(solution)/shard_map/ppermute | solution.py:282
  192.5 162.2 %reduce-scatter.6.cloned.1.call-start = ((), (), s32[]{:S(2)}) async-start(), calls=%async_computation.4 | async-start | bytes 2621440 | tf_op jit(solution)/shard_map/reduce_scatter | solution.py:351
  240.7 3.9 collective-permute-start.11
  241.1 12.2 %collective-permute-start.12 = (bf16[384,512]{1,0:T(8,128)(2,1)}, bf16[384,512]{1,0:T(8,128)(2,1)S(1)}, u32[]{:S(2)}, u32[]{:S(2)}) collective-permute-start(bf16[384,512]{1,0:T(8,128)(2,1)} %get-tuple-element.42), channel_id=1, source_target_pairs={{0,8},{4,12},{8,0},{12,4},{16,24},{20,28},{24,16},{28,20},{1,9},{5... | collective-permute-start | bytes 1179656 | tf_op jit(solution)/shard_map/ppermute | solution.py:282
  242.6 18.2 %collective-permute-start.13 = (bf16[384,512]{1,0:T(8,128)(2,1)}, bf16[384,512]{1,0:T(8,128)(2,1)S(1)}, u32[]{:S(2)}, u32[]{:S(2)}) collective-permute-start(bf16[384,512]{1,0:T(8,128)(2,1)} %get-tuple-element.43), channel_id=1, source_target_pairs={{0,12},{4,8},{8,4},{12,0},{16,28},{20,24},{24,20},{28,16},{1,13},{... | collective-permute-start | bytes 1179656 | tf_op jit(solution)/shard_map/ppermute | solution.py:282
  242.6 18.2 %collective-permute-start.14 = (bf16[384,512]{1,0:T(8,128)(2,1)}, bf16[384,512]{1,0:T(8,128)(2,1)S(1)}, u32[]{:S(2)}, u32[]{:S(2)}) collective-permute-start(bf16[384,512]{1,0:T(8,128)(2,1)} %get-tuple-element.44), channel_id=1, source_target_pairs={{0,16},{4,20},{8,24},{12,28},{16,0},{20,4},{24,8},{28,12},{1,17},{... | collective-permute-start | bytes 1179656 | tf_op jit(solution)/shard_map/ppermute | solution.py:282
  244.0 35.4 %collective-permute-start.15 = (bf16[384,512]{1,0:T(8,128)(2,1)}, bf16[384,512]{1,0:T(8,128)(2,1)S(1)}, u32[]{:S(2)}, u32[]{:S(2)}) collective-permute-start(bf16[384,512]{1,0:T(8,128)(2,1)} %get-tuple-element.45), channel_id=1, source_target_pairs={{0,20},{4,16},{8,28},{12,24},{16,4},{20,0},{24,12},{28,8},{1,21},{... | collective-permute-start | bytes 1179656 | tf_op jit(solution)/shard_map/ppermute | solution.py:282
  244.6 34.9 %copy-start.19 = (bf16[384,512]{1,0:T(8,128)(2,1)}, bf16[384,512]{1,0:T(8,128)(2,1)S(1)}, u32[]{:S(2)}) copy-start(bf16[384,512]{1,0:T(8,128)(2,1)S(1)} %collective-permute-done.11.refs_1_) | copy-start | bytes 1179652
  244.6 34.9 %collective-permute-start.16 = (bf16[384,512]{1,0:T(8,128)(2,1)}, bf16[384,512]{1,0:T(8,128)(2,1)S(1)}, u32[]{:S(2)}, u32[]{:S(2)}) collective-permute-start(bf16[384,512]{1,0:T(8,128)(2,1)} %get-tuple-element.46), channel_id=1, source_target_pairs={{0,24},{4,28},{8,16},{12,20},{16,8},{20,12},{24,0},{28,4},{1,25},{... | collective-permute-start | bytes 1179656 | tf_op jit(solution)/shard_map/ppermute | solution.py:282
  253.2 26.3 %copy-start.20 = (bf16[384,512]{1,0:T(8,128)(2,1)}, bf16[384,512]{1,0:T(8,128)(2,1)S(1)}, u32[]{:S(2)}) copy-start(bf16[384,512]{1,0:T(8,128)(2,1)S(1)} %collective-permute-done.12.refs_2_) | copy-start | bytes 1179652
  253.2 26.2 %collective-permute-start.17 = (bf16[384,512]{1,0:T(8,128)(2,1)}, bf16[384,512]{1,0:T(8,128)(2,1)S(1)}, u32[]{:S(2)}, u32[]{:S(2)}) collective-permute-start(bf16[384,512]{1,0:T(8,128)(2,1)} %get-tuple-element.47), channel_id=1, source_target_pairs={{0,28},{4,24},{8,20},{12,16},{16,12},{20,8},{24,4},{28,0},{1,29},{... | collective-permute-start | bytes 1179656 | tf_op jit(solution)/shard_map/ppermute | solution.py:282
  260.8 18.7 %copy-start.21 = (bf16[384,512]{1,0:T(8,128)(2,1)}, bf16[384,512]{1,0:T(8,128)(2,1)S(1)}, u32[]{:S(2)}) copy-start(bf16[384,512]{1,0:T(8,128)(2,1)S(1)} %collective-permute-done.13.refs_3_) | copy-start | bytes 1179652
  260.8 18.7 %copy-start.22 = (bf16[384,512]{1,0:T(8,128)(2,1)}, bf16[384,512]{1,0:T(8,128)(2,1)S(1)}, u32[]{:S(2)}) copy-start(bf16[384,512]{1,0:T(8,128)(2,1)S(1)} %collective-permute-done.14.refs_4_) | copy-start | bytes 1179652
  298.6 3.6 collective-permute-start
  298.8 7.9 %collective-permute-start.1 = (bf16[384,256]{1,0:T(8,128)(2,1)}, bf16[384,256]{1,0:T(8,128)(2,1)S(1)}, u32[]{:S(2)}, u32[]{:S(2)}) collective-permute-start(bf16[384,256]{1,0:T(8,128)(2,1)} %get-tuple-element.33), channel_id=1, source_target_pairs={{0,8},{4,12},{8,0},{12,4},{16,24},{20,28},{24,16},{28,20},{1,9},{5... | collective-permute-start | bytes 589832 | tf_op jit(solution)/shard_map/ppermute | solution.py:282
  300.3 9.8 %collective-permute-start.2 = (bf16[384,256]{1,0:T(8,128)(2,1)}, bf16[384,256]{1,0:T(8,128)(2,1)S(1)}, u32[]{:S(2)}, u32[]{:S(2)}) collective-permute-start(bf16[384,256]{1,0:T(8,128)(2,1)} %get-tuple-element.34), channel_id=1, source_target_pairs={{0,12},{4,8},{8,4},{12,0},{16,28},{20,24},{24,20},{28,16},{1,13},{... | collective-permute-start | bytes 589832 | tf_op jit(solution)/shard_map/ppermute | solution.py:282
  300.5 9.5 %collective-permute-start.3 = (bf16[384,256]{1,0:T(8,128)(2,1)}, bf16[384,256]{1,0:T(8,128)(2,1)S(1)}, u32[]{:S(2)}, u32[]{:S(2)}) collective-permute-start(bf16[384,256]{1,0:T(8,128)(2,1)} %get-tuple-element.35), channel_id=1, source_target_pairs={{0,16},{4,20},{8,24},{12,28},{16,0},{20,4},{24,8},{28,12},{1,17},{... | collective-permute-start | bytes 589832 | tf_op jit(solution)/shard_map/ppermute | solution.py:282
  302.1 17.9 %collective-permute-start.4 = (bf16[384,256]{1,0:T(8,128)(2,1)}, bf16[384,256]{1,0:T(8,128)(2,1)S(1)}, u32[]{:S(2)}, u32[]{:S(2)}) collective-permute-start(bf16[384,256]{1,0:T(8,128)(2,1)} %get-tuple-element.36), channel_id=1, source_target_pairs={{0,20},{4,16},{8,28},{12,24},{16,4},{20,0},{24,12},{28,8},{1,21},{... | collective-permute-start | bytes 589832 | tf_op jit(solution)/shard_map/ppermute | solution.py:282
  302.2 17.8 %copy-start.28 = (bf16[384,256]{1,0:T(8,128)(2,1)}, bf16[384,256]{1,0:T(8,128)(2,1)S(1)}, u32[]{:S(2)}) copy-start(bf16[384,256]{1,0:T(8,128)(2,1)S(1)} %collective-permute-done.refs_1_) | copy-start | bytes 589828
  302.3 17.7 %collective-permute-start.5 = (bf16[384,256]{1,0:T(8,128)(2,1)}, bf16[384,256]{1,0:T(8,128)(2,1)S(1)}, u32[]{:S(2)}, u32[]{:S(2)}) collective-permute-start(bf16[384,256]{1,0:T(8,128)(2,1)} %get-tuple-element.37), channel_id=1, source_target_pairs={{0,24},{4,28},{8,16},{12,20},{16,8},{20,12},{24,0},{28,4},{1,25},{... | collective-permute-start | bytes 589832 | tf_op jit(solution)/shard_map/ppermute | solution.py:282
  306.7 13.3 %copy-start.29 = (bf16[384,256]{1,0:T(8,128)(2,1)}, bf16[384,256]{1,0:T(8,128)(2,1)S(1)}, u32[]{:S(2)}) copy-start(bf16[384,256]{1,0:T(8,128)(2,1)S(1)} %collective-permute-done.1.refs_2_) | copy-start | bytes 589828
  306.7 13.3 %collective-permute-start.6 = (bf16[384,256]{1,0:T(8,128)(2,1)}, bf16[384,256]{1,0:T(8,128)(2,1)S(1)}, u32[]{:S(2)}, u32[]{:S(2)}) collective-permute-start(bf16[384,256]{1,0:T(8,128)(2,1)} %get-tuple-element.38), channel_id=1, source_target_pairs={{0,28},{4,24},{8,20},{12,16},{16,12},{20,8},{24,4},{28,0},{1,29},{... | collective-permute-start | bytes 589832 | tf_op jit(solution)/shard_map/ppermute | solution.py:282
  327.1 15.0 %collective-permute-start.7 = (bf16[1024,256]{1,0:T(8,128)(2,1)}, bf16[1024,256]{1,0:T(8,128)(2,1)S(1)}, u32[]{:S(2)}, u32[]{:S(2)}) collective-permute-start(bf16[1024,256]{1,0:T(8,128)(2,1)} %get-tuple-element.39), channel_id=1, source_target_pairs={{0,8},{4,12},{8,0},{12,4},{16,24},{20,28},{24,16},{28,20},{1,9},{5... | collective-permute-start | bytes 1572872 | tf_op jit(solution)/shard_map/ppermute | solution.py:282
  328.7 25.7 %collective-permute-start.8 = (bf16[1024,256]{1,0:T(8,128)(2,1)}, bf16[1024,256]{1,0:T(8,128)(2,1)S(1)}, u32[]{:S(2)}, u32[]{:S(2)}) collective-permute-start(bf16[1024,256]{1,0:T(8,128)(2,1)} %get-tuple-element.39), channel_id=1, source_target_pairs={{0,16},{4,20},{8,24},{12,28},{16,0},{20,4},{24,8},{28,12},{1,17},{... | collective-permute-start | bytes 1572872 | tf_op jit(solution)/shard_map/ppermute | solution.py:282
  329.1 25.4 %collective-permute-start.9 = (bf16[1024,256]{1,0:T(8,128)(2,1)}, bf16[1024,256]{1,0:T(8,128)(2,1)S(1)}, u32[]{:S(2)}, u32[]{:S(2)}) collective-permute-start(bf16[1024,256]{1,0:T(8,128)(2,1)} %get-tuple-element.39), channel_id=1, source_target_pairs={{0,24},{4,28},{8,16},{12,20},{16,8},{20,12},{24,0},{28,4},{1,25},{... | collective-permute-start | bytes 1572872 | tf_op jit(solution)/shard_map/ppermute | solution.py:282
  354.5 29.4 %collective-permute-start.10 = (bf16[4096,256]{1,0:T(8,128)(2,1)S(1)}, bf16[4096,256]{1,0:T(8,128)(2,1)}, u32[]{:S(2)}, u32[]{:S(2)}) collective-permute-start(bf16[4096,256]{1,0:T(8,128)(2,1)S(1)} %constant_dynamic-update-slice_fusion.near_ref), channel_id=1, source_target_pairs={{0,4},{4,0},{8,12},{12,8},{16,20},{20,16},{24,28},{28,24},{1,5},{5... | collective-permute-start | bytes 6291464 | tf_op jit(solution)/shard_map/ppermute | solution.py:282
  357.9 9.2 %collective-permute-start.18 = (bf16[1024,128]{1,0:T(8,128)(2,1)S(1)}, bf16[1024,128]{1,0:T(8,128)(2,1)S(1)}, u32[]{:S(2)}, u32[]{:S(2)}) collective-permute-start(bf16[1024,128]{1,0:T(8,128)(2,1)S(1)} %get-tuple-element.62), channel_id=1, source_target_pairs={{0,8},{4,12},{8,0},{12,4},{16,24},{20,28},{24,16},{28,20},{1,9},{5... | collective-permute-start | bytes 786440 | tf_op jit(solution)/shard_map/ppermute | solution.py:282
  358.4 12.6 %collective-permute-start.19 = (bf16[1024,128]{1,0:T(8,128)(2,1)S(1)}, bf16[1024,128]{1,0:T(8,128)(2,1)S(1)}, u32[]{:S(2)}, u32[]{:S(2)}) collective-permute-start(bf16[1024,128]{1,0:T(8,128)(2,1)S(1)} %get-tuple-element.62), channel_id=1, source_target_pairs={{0,16},{4,20},{8,24},{12,28},{16,0},{20,4},{24,8},{28,12},{1,17},{... | collective-permute-start | bytes 786440 | tf_op jit(solution)/shard_map/ppermute | solution.py:282
  359.9 12.8 %collective-permute-start.20 = (bf16[1024,128]{1,0:T(8,128)(2,1)S(1)}, bf16[1024,128]{1,0:T(8,128)(2,1)S(1)}, u32[]{:S(2)}, u32[]{:S(2)}) collective-permute-start(bf16[1024,128]{1,0:T(8,128)(2,1)S(1)} %get-tuple-element.62), channel_id=1, source_target_pairs={{0,24},{4,28},{8,16},{12,20},{16,8},{20,12},{24,0},{28,4},{1,25},{... | collective-permute-start | bytes 786440 | tf_op jit(solution)/shard_map/ppermute | solution.py:282
  362.1 16.2 %collective-permute-start.29 = (bf16[1024,128]{1,0:T(8,128)(2,1)S(1)}, bf16[1024,128]{1,0:T(8,128)(2,1)S(1)}, u32[]{:S(2)}, u32[]{:S(2)}) collective-permute-start(bf16[1024,128]{1,0:T(8,128)(2,1)S(1)} %get-tuple-element.64), channel_id=1, source_target_pairs={{0,8},{4,12},{8,0},{12,4},{16,24},{20,28},{24,16},{28,20},{1,9},{5... | collective-permute-start | bytes 786440 | tf_op jit(solution)/shard_map/ppermute | solution.py:282
  367.1 15.9 %collective-permute-start.30 = (bf16[1024,128]{1,0:T(8,128)(2,1)S(1)}, bf16[1024,128]{1,0:T(8,128)(2,1)S(1)}, u32[]{:S(2)}, u32[]{:S(2)}) collective-permute-start(bf16[1024,128]{1,0:T(8,128)(2,1)S(1)} %get-tuple-element.64), channel_id=1, source_target_pairs={{0,16},{4,20},{8,24},{12,28},{16,0},{20,4},{24,8},{28,12},{1,17},{... | collective-permute-start | bytes 786440 | tf_op jit(solution)/shard_map/ppermute | solution.py:282
  371.0 12.0 %collective-permute-start.31 = (bf16[1024,128]{1,0:T(8,128)(2,1)S(1)}, bf16[1024,128]{1,0:T(8,128)(2,1)S(1)}, u32[]{:S(2)}, u32[]{:S(2)}) collective-permute-start(bf16[1024,128]{1,0:T(8,128)(2,1)S(1)} %get-tuple-element.64), channel_id=1, source_target_pairs={{0,24},{4,28},{8,16},{12,20},{16,8},{20,12},{24,0},{28,4},{1,25},{... | collective-permute-start | bytes 786440 | tf_op jit(solution)/shard_map/ppermute | solution.py:282
  372.7 24.5 %copy-start.2 = (bf16[4096,128]{1,0:T(8,128)(2,1)}, bf16[4096,128]{1,0:T(8,128)(2,1)S(1)}, u32[]{:S(2)}) copy-start(bf16[4096,128]{1,0:T(8,128)(2,1)S(1)} %pad_maximum_fusion.2.near_ref) | copy-start | bytes 3145732
  372.7 28.0 %collective-permute-start.21 = (bf16[4096,128]{1,0:T(8,128)(2,1)S(1)}, bf16[4096,128]{1,0:T(8,128)(2,1)S(1)}, u32[]{:S(2)}, u32[]{:S(2)}) collective-permute-start(bf16[4096,128]{1,0:T(8,128)(2,1)S(1)} %pad_maximum_fusion.2.near_ref), channel_id=1, source_target_pairs={{0,4},{4,0},{8,12},{12,8},{16,20},{20,16},{24,28},{28,24},{1,5},{5... | collective-permute-start | bytes 3145736 | tf_op jit(solution)/shard_map/ppermute | solution.py:282
  383.0 14.2 %copy-start.3 = (bf16[4096,128]{1,0:T(8,128)(2,1)}, bf16[4096,128]{1,0:T(8,128)(2,1)S(1)}, u32[]{:S(2)}) copy-start(bf16[4096,128]{1,0:T(8,128)(2,1)S(1)} %pad_maximum_fusion.3.near_ref) | copy-start | bytes 3145732
  383.1 33.0 %collective-permute-start.32 = (bf16[4096,128]{1,0:T(8,128)(2,1)S(1)}, bf16[4096,128]{1,0:T(8,128)(2,1)S(1)}, u32[]{:S(2)}, u32[]{:S(2)}) collective-permute-start(bf16[4096,128]{1,0:T(8,128)(2,1)S(1)} %pad_maximum_fusion.3.near_ref), channel_id=1, source_target_pairs={{0,4},{4,0},{8,12},{12,8},{16,20},{20,16},{24,28},{28,24},{1,5},{5... | collective-permute-start | bytes 3145736 | tf_op jit(solution)/shard_map/ppermute | solution.py:282
  397.2 32.4 %collective-permute-start.33 = (bf16[1024,256]{1,0:T(8,128)(2,1)}, bf16[1024,256]{1,0:T(8,128)(2,1)S(1)}, u32[]{:S(2)}, u32[]{:S(2)}) collective-permute-start(bf16[1024,256]{1,0:T(8,128)(2,1)} %product.6), channel_id=1, source_target_pairs={{0,8},{4,12},{8,0},{12,4},{16,24},{20,28},{24,16},{28,20},{1,9},{5... | collective-permute-start | bytes 1572872 | tf_op jit(solution)/shard_map/ppermute | solution.py:282
  398.8 32.3 %collective-permute-start.34 = (bf16[1024,256]{1,0:T(8,128)(2,1)}, bf16[1024,256]{1,0:T(8,128)(2,1)S(1)}, u32[]{:S(2)}, u32[]{:S(2)}) collective-permute-start(bf16[1024,256]{1,0:T(8,128)(2,1)} %product.6), channel_id=1, source_target_pairs={{0,16},{4,20},{8,24},{12,28},{16,0},{20,4},{24,8},{28,12},{1,17},{... | collective-permute-start | bytes 1572872 | tf_op jit(solution)/shard_map/ppermute | solution.py:282
  399.3 32.9 %collective-permute-start.35 = (bf16[1024,256]{1,0:T(8,128)(2,1)}, bf16[1024,256]{1,0:T(8,128)(2,1)S(1)}, u32[]{:S(2)}, u32[]{:S(2)}) collective-permute-start(bf16[1024,256]{1,0:T(8,128)(2,1)} %product.6), channel_id=1, source_target_pairs={{0,24},{4,28},{8,16},{12,20},{16,8},{20,12},{24,0},{28,4},{1,25},{... | collective-permute-start | bytes 1572872 | tf_op jit(solution)/shard_map/ppermute | solution.py:282
  414.5 15.1 %copy-start.7 = (bf16[1024,128]{1,0:T(8,128)(2,1)S(1)}, bf16[1024,128]{1,0:T(8,128)(2,1)}, u32[]{:S(2)}) copy-start(bf16[1024,128]{1,0:T(8,128)(2,1)} %product.7) | copy-start | bytes 786436
  414.5 18.6 %copy-start.1 = (bf16[1024,256]{1,0:T(8,128)(2,1)S(1)}, bf16[1024,256]{1,0:T(8,128)(2,1)}, u32[]{:S(2)}) copy-start(bf16[1024,256]{1,0:T(8,128)(2,1)} %product.6) | copy-start | bytes 1572868
  414.5 18.8 %collective-permute-start.37 = (bf16[1024,128]{1,0:T(8,128)(2,1)}, bf16[1024,128]{1,0:T(8,128)(2,1)S(1)}, u32[]{:S(2)}, u32[]{:S(2)}) collective-permute-start(bf16[1024,128]{1,0:T(8,128)(2,1)} %product.7), channel_id=1, source_target_pairs={{0,8},{4,12},{8,0},{12,4},{16,24},{20,28},{24,16},{28,20},{1,9},{5... | collective-permute-start | bytes 786440 | tf_op jit(solution)/shard_map/ppermute | solution.py:282
  416.1 18.8 %collective-permute-start.38 = (bf16[1024,128]{1,0:T(8,128)(2,1)}, bf16[1024,128]{1,0:T(8,128)(2,1)S(1)}, u32[]{:S(2)}, u32[]{:S(2)}) collective-permute-start(bf16[1024,128]{1,0:T(8,128)(2,1)} %product.7), channel_id=1, source_target_pairs={{0,16},{4,20},{8,24},{12,28},{16,0},{20,4},{24,8},{28,12},{1,17},{... | collective-permute-start | bytes 786440 | tf_op jit(solution)/shard_map/ppermute | solution.py:282
  429.6 10.3 %collective-permute-start.39 = (bf16[1024,128]{1,0:T(8,128)(2,1)S(1)}, bf16[1024,128]{1,0:T(8,128)(2,1)S(1)}, u32[]{:S(2)}, u32[]{:S(2)}) collective-permute-start(bf16[1024,128]{1,0:T(8,128)(2,1)S(1)} %copy-done.7), channel_id=1, source_target_pairs={{0,24},{4,28},{8,16},{12,20},{16,8},{20,12},{24,0},{28,4},{1,25},{... | collective-permute-start | bytes 786440 | tf_op jit(solution)/shard_map/ppermute | solution.py:282
  431.1 13.9 %collective-permute-start.41 = (bf16[1024,128]{1,0:T(8,128)(2,1)}, bf16[1024,128]{1,0:T(8,128)(2,1)S(1)}, u32[]{:S(2)}, u32[]{:S(2)}) collective-permute-start(bf16[1024,128]{1,0:T(8,128)(2,1)} %product.8), channel_id=1, source_target_pairs={{0,8},{4,12},{8,0},{12,4},{16,24},{20,28},{24,16},{28,20},{1,9},{5... | collective-permute-start | bytes 786440 | tf_op jit(solution)/shard_map/ppermute | solution.py:282
  432.2 13.2 %collective-permute-start.42 = (bf16[1024,128]{1,0:T(8,128)(2,1)}, bf16[1024,128]{1,0:T(8,128)(2,1)S(1)}, u32[]{:S(2)}, u32[]{:S(2)}) collective-permute-start(bf16[1024,128]{1,0:T(8,128)(2,1)} %product.8), channel_id=1, source_target_pairs={{0,16},{4,20},{8,24},{12,28},{16,0},{20,4},{24,8},{28,12},{1,17},{... | collective-permute-start | bytes 786440 | tf_op jit(solution)/shard_map/ppermute | solution.py:282
  433.3 16.1 %copy-start = (bf16[4096,256]{1,0:T(8,128)(2,1)}, bf16[4096,256]{1,0:T(8,128)(2,1)S(1)}, u32[]{:S(2)}) copy-start(bf16[4096,256]{1,0:T(8,128)(2,1)S(1)} %pad_maximum_fusion.near_ref) | copy-start | bytes 6291460
  433.4 16.0 %collective-permute-start.43 = (bf16[1024,128]{1,0:T(8,128)(2,1)S(1)}, bf16[1024,128]{1,0:T(8,128)(2,1)S(1)}, u32[]{:S(2)}, u32[]{:S(2)}) collective-permute-start(bf16[1024,128]{1,0:T(8,128)(2,1)S(1)} %copy-done.8), channel_id=1, source_target_pairs={{0,24},{4,28},{8,16},{12,20},{16,8},{20,12},{24,0},{28,4},{1,25},{... | collective-permute-start | bytes 786440 | tf_op jit(solution)/shard_map/ppermute | solution.py:282
  434.9 41.0 %collective-permute-start.36 = (bf16[4096,256]{1,0:T(8,128)(2,1)S(1)}, bf16[4096,256]{1,0:T(8,128)(2,1)S(1)}, u32[]{:S(2)}, u32[]{:S(2)}) collective-permute-start(bf16[4096,256]{1,0:T(8,128)(2,1)S(1)} %pad_maximum_fusion.near_ref), channel_id=1, source_target_pairs={{0,4},{4,0},{8,12},{12,8},{16,20},{20,16},{24,28},{28,24},{1,5},{5... | collective-permute-start | bytes 6291464 | tf_op jit(solution)/shard_map/ppermute | solution.py:282
  440.0 9.5 %collective-permute-start.40 = (bf16[4096,128]{1,0:T(8,128)(2,1)S(1)}, bf16[4096,128]{1,0:T(8,128)(2,1)S(1)}, u32[]{:S(2)}, u32[]{:S(2)}) collective-permute-start(bf16[4096,128]{1,0:T(8,128)(2,1)S(1)} %pad_maximum_fusion.4.near_ref), channel_id=1, source_target_pairs={{0,4},{4,0},{8,12},{12,8},{16,20},{20,16},{24,28},{28,24},{1,5},{5... | collective-permute-start | bytes 3145736 | tf_op jit(solution)/shard_map/ppermute | solution.py:282
  449.4 13.8 %copy-start.5 = (bf16[4096,128]{1,0:T(8,128)(2,1)}, bf16[4096,128]{1,0:T(8,128)(2,1)S(1)}, u32[]{:S(2)}) copy-start(bf16[4096,128]{1,0:T(8,128)(2,1)S(1)} %pad_maximum_fusion.5.near_ref) | copy-start | bytes 3145732
  449.4 13.8 %collective-permute-start.44 = (bf16[4096,128]{1,0:T(8,128)(2,1)S(1)}, bf16[4096,128]{1,0:T(8,128)(2,1)}, u32[]{:S(2)}, u32[]{:S(2)}) collective-permute-start(bf16[4096,128]{1,0:T(8,128)(2,1)S(1)} %pad_maximum_fusion.5.near_ref), channel_id=1, source_target_pairs={{0,4},{4,0},{8,12},{12,8},{16,20},{20,16},{24,28},{28,24},{1,5},{5... | collective-permute-start | bytes 3145736 | tf_op jit(solution)/shard_map/ppermute | solution.py:282
  477.2 13.5 %copy-start.10 = (bf16[1024,128]{1,0:T(8,128)(2,1)S(1)}, bf16[1024,128]{1,0:T(8,128)(2,1)}, u32[]{:S(2)}) copy-start(bf16[1024,128]{1,0:T(8,128)(2,1)} %product.10) | copy-start | bytes 786436
  477.2 13.5 %copy-start.11 = (bf16[1024,128]{1,0:T(8,128)(2,1)S(1)}, bf16[1024,128]{1,0:T(8,128)(2,1)}, u32[]{:S(2)}) copy-start(bf16[1024,128]{1,0:T(8,128)(2,1)} %product.11) | copy-start | bytes 786436
  (19 other events, 58.1 us)
Sparse Core Ops, SparseCore 0:
  69.5 119.1 reduce-scatter.3
  192.6 49.8 reduce-scatter.7
  290.8 45.6 reduce-scatter.5

commit v3 on v2

v3 whole, which is shorter than its diff:
```python
import functools

import jax
import jax.numpy as jnp
from jax import lax
from jax.experimental import pallas as pl
from jax.experimental.pallas import tpu as pltpu
from jax.sharding import PartitionSpec as P

TILE = 128
STACK = 4
VMEM_BYTES = 56 * 1024 * 1024


def largest_tile(total, most):
    best = total
    for size in range(16, most + 1, 16):
        if total % size == 0:
            best = size
    return best


def kernel_params():
    return pltpu.CompilerParams(vmem_limit_bytes=VMEM_BYTES)


def brief():
    return pl.CostEstimate(flops=1, bytes_accessed=1, transcendentals=0)


def whole_block(*shape):
    return pl.BlockSpec(shape, lambda *_: (0,) * len(shape))


def in_place():
    return pl.BlockSpec(memory_space=pl.ANY)


def dot32(left, right):
    return jnp.dot(left, right, preferred_element_type=jnp.float32)


def front_kernel(start, stop, n_col, flat, n_after, meta_ref, tiles_ref, front_ref, *refs):
    out_ref, stack, held, acc, places, groups_of, state, tile_sems, sems = refs[n_after:]
    span = stop - start
    groups = n_col * span
    block, streams = held.shape[1], sems.shape[1]
    lines = block // streams
    step = pl.program_id(0)
    slot = lax.rem(step, 2)

    def front_copy(at, into, q):
        return pltpu.make_async_copy(
            front_ref.at[pl.ds(pl.multiple_of(at * block + q * lines, lines), lines), :],
            held.at[into, pl.ds(q * lines, lines), :],
            sems.at[into, q],
        )

    def tile_copy(t, item, place):
        return pltpu.make_async_copy(
            tiles_ref.at[t],
            stack.at[item, pl.ds(pl.multiple_of(place * TILE, TILE), TILE), :],
            tile_sems.at[t],
        )

    def chosen(t):
        return (meta_ref[2, t] >= start) & (meta_ref[2, t] < stop)

    def clear(item, place):
        places[item, place] = 0
        stack[item, pl.ds(pl.multiple_of(place * TILE, TILE), TILE), :] = jnp.zeros(
            (TILE, TILE), stack.dtype
        )

    @pl.when(step == 0)
    def build():
        for q in range(streams):
            front_copy(0, 0, q).start()
        for g in range(groups):
            state[g] = 0
            state[groups + g] = 0
        state[2 * groups] = 0

        @pl.loop(0, tiles_ref.shape[0])
        def place_tile(t):
            @pl.when(chosen(t))
            def _():
                g = meta_ref[1, t] * span + meta_ref[2, t] - start
                at = state[g]

                @pl.when(lax.rem(at, STACK) == 0)
                def _():
                    state[groups + g] = state[2 * groups]
                    groups_of[state[2 * groups]] = g
                    state[2 * groups] += 1

                item = state[groups + g]
                places[item, lax.rem(at, STACK)] = meta_ref[0, t]
                tile_copy(t, item, lax.rem(at, STACK)).start()
                state[g] = at + 1

        for g in range(groups):
            used = lax.rem(state[g], STACK)

            @pl.loop(used, jnp.where(used == 0, 0, STACK))
            def fill(place):
                clear(state[groups + g], place)

        items = state[2 * groups]

        @pl.loop(items, (items + STACK - 1) // STACK * STACK)
        def fill_item(item):
            groups_of[item] = 0
            for place in range(STACK):
                clear(item, place)

        @pl.loop(0, tiles_ref.shape[0])
        def wait_tile(t):
            @pl.when(chosen(t))
            def _():
                tile_copy(t, 0, 0).wait()

    @pl.when(step + 1 < pl.num_programs(0))
    def ahead():
        for q in range(streams):
            front_copy(step + 1, 1 - slot, q).start()

    for q in range(streams):
        front_copy(step, slot, q).wait()

    acc[...] = jnp.zeros_like(acc)

    @pl.loop(0, (state[2 * groups] + STACK - 1) // STACK)
    def add(s):
        products = []
        for i in range(STACK):
            item = s * STACK + i
            lefts = [pl.multiple_of(places[item, j] * TILE, TILE) for j in range(STACK)]
            rows = [held[slot, :, pl.ds(left, TILE)] for left in lefts]
            products.append(dot32(jnp.concatenate(rows, axis=1), stack[item]))
        for i in range(STACK):
            acc[groups_of[s * STACK + i]] += products[i]

    for g in range(groups):
        dest, sub = g // span, g % span
        if flat:
            out_ref[:, g * TILE : (g + 1) * TILE] = acc[g].astype(out_ref.dtype)
        else:
            out_ref[dest, :, sub * TILE : (sub + 1) * TILE] = acc[g].astype(out_ref.dtype)


def front_products(front, tiles, meta, start, stop, n_col, flat, after=()):
    rows, depth = front.shape
    span = stop - start
    width = span * TILE
    groups = n_col * span
    block = largest_tile(rows, 512)
    streams = 8 if block % 128 == 0 else 1
    count = tiles.shape[0]
    items = (-(-count // STACK) + groups + STACK) // STACK * STACK
    if flat:
        shape, spec = (rows, n_col * width), pl.BlockSpec((block, n_col * width), lambda i, m: (i, 0))
    else:
        shape, spec = (n_col, rows, width), pl.BlockSpec((n_col, block, width), lambda i, m: (0, i, 0))
    return pl.pallas_call(
        functools.partial(front_kernel, start, stop, n_col, flat, len(after)),
        grid_spec=pltpu.PrefetchScalarGridSpec(
            num_scalar_prefetch=1,
            grid=(rows // block,),
            in_specs=[in_place()] * (2 + len(after)),
            out_specs=spec,
            scratch_shapes=[
                pltpu.VMEM((items, STACK * TILE, TILE), front.dtype),
                pltpu.VMEM((2, block, depth), front.dtype),
                pltpu.VMEM((groups, block, TILE), jnp.float32),
                pltpu.SMEM((items, STACK), jnp.int32),
                pltpu.SMEM((items,), jnp.int32),
                pltpu.SMEM((2 * groups + 1,), jnp.int32),
                pltpu.SemaphoreType.DMA((count,)),
                pltpu.SemaphoreType.DMA((2, streams)),
            ],
        ),
        out_shape=jax.ShapeDtypeStruct(shape, front.dtype),
        compiler_params=kernel_params(),
        cost_estimate=brief(),
        name="front_products",
    )(meta, tiles, front, *after)


def one_hot(want, depth, kind):
    places = lax.broadcasted_iota(jnp.int32, (want.shape[0], depth), 1)
    return (places == want).astype(jnp.float32).astype(kind)


def pack_kernel(n_row, n_solved, index_ref, *refs):
    outs = refs[-2:]
    solved = jnp.concatenate([ref[...] for ref in refs[:n_solved]], axis=1)
    cap = outs[0].shape[0] * 2 // n_row
    for k in range(n_row):
        picks = one_hot(index_ref[k * cap : (k + 1) * cap, :], solved.shape[0], solved.dtype)
        at = k // 2 * cap
        outs[k % 2][at : at + cap, :] = dot32(picks, solved).astype(outs[0].dtype)


def pack_rows(index, solved, n_row, cap, after=()):
    depth = solved[0].shape[0]
    width = sum(part.shape[1] for part in solved)
    return pl.pallas_call(
        functools.partial(pack_kernel, n_row, len(solved)),
        in_specs=[whole_block(*index.shape)]
        + [whole_block(*part.shape) for part in solved]
        + [in_place()] * len(after),
        out_shape=[jax.ShapeDtypeStruct((n_row // 2 * cap, width), solved[0].dtype)] * 2,
        compiler_params=kernel_params(),
        cost_estimate=brief(),
        name="pack_rows",
    )(index, *solved, *after)


def join_pieces(pieces, joined):
    at = 0
    for piece in pieces:
        joined[at : at + piece.shape[0], :] = piece[...]
        at += piece.shape[0]


def assemble_kernel(n_pieces, index_ref, bem_ref, *refs):
    outs, joined = refs[-3:-1], refs[-1]
    join_pieces(refs[:n_pieces], joined)
    count = outs[0].shape[0]
    step = largest_tile(count, 512)
    for half, out in enumerate(outs):
        for i in range(0, count, step):
            want = index_ref[half * count + i : half * count + i + step, :]
            taken = dot32(one_hot(want, joined.shape[0], joined.dtype), joined[...])
            entries = bem_ref[half, i : i + step, :].astype(jnp.float32)
            out[i : i + step, :] = (entries - taken).astype(out.dtype)


def assemble(index, bem, pieces, start, after=()):
    width = pieces[0].shape[1]
    routed = sum(piece.shape[0] for piece in pieces)
    count = bem.shape[1]
    place = start * TILE // width
    return pl.pallas_call(
        functools.partial(assemble_kernel, len(pieces)),
        grid=(1,),
        in_specs=[
            whole_block(*index.shape),
            pl.BlockSpec((2, count, width), lambda i: (0, 0, place)),
        ]
        + [whole_block(*piece.shape) for piece in pieces]
        + [in_place()] * len(after),
        out_specs=[whole_block(count, width)] * 2,
        out_shape=[jax.ShapeDtypeStruct((count, width), bem.dtype)] * 2,
        scratch_shapes=[pltpu.VMEM((routed, width), bem.dtype)],
        compiler_params=kernel_params(),
        cost_estimate=brief(),
        name="assemble",
    )(index, bem, *pieces, *after)


def subtract_kernel(bem_ref, terms_ref, *refs):
    for half, out in enumerate(refs[-2:]):
        total = terms_ref[0, half].astype(jnp.float32)
        for term in range(1, terms_ref.shape[0]):
            total = total + terms_ref[term, half].astype(jnp.float32)
        taken = total.astype(out.dtype).astype(jnp.float32)
        out[...] = (bem_ref[half].astype(jnp.float32) - taken).astype(out.dtype)


def subtract(bem, terms, start, after=()):
    count, width = bem.shape[1], terms.shape[1]
    place = start * TILE // width
    return pl.pallas_call(
        subtract_kernel,
        grid=(1,),
        in_specs=[pl.BlockSpec((2, count, width), lambda i: (0, 0, place))]
        + [whole_block(1, 2, count, width)]
        + [in_place()] * len(after),
        out_specs=[whole_block(count, width)] * 2,
        out_shape=[jax.ShapeDtypeStruct((count, width), bem.dtype)] * 2,
        compiler_params=kernel_params(),
        cost_estimate=brief(),
        name="subtract",
    )(bem, terms.reshape(1, 2, count, width), *after)


def unpack_kernel(n_pieces, n_col, index_ref, *refs):
    out, joined = refs[-2:]
    join_pieces(refs[:n_pieces], joined)
    _, count, width = out.shape
    step = largest_tile(count, 512)
    for i in range(0, count, step):
        taken = dot32(one_hot(index_ref[i : i + step, :], joined.shape[0], joined.dtype), joined[...])
        for d in range(n_col):
            out[d, i : i + step, :] = taken[:, d * width : (d + 1) * width].astype(out.dtype)


def unpack(index, pieces, n_col, after=()):
    wide = pieces[0].shape[1]
    routed = sum(piece.shape[0] for piece in pieces)
    count, width = index.shape[0], wide // n_col
    return pl.pallas_call(
        functools.partial(unpack_kernel, len(pieces), n_col),
        in_specs=[whole_block(*index.shape)]
        + [whole_block(*piece.shape) for piece in pieces]
        + [in_place()] * len(after),
        out_shape=jax.ShapeDtypeStruct((n_col, count, width), pieces[0].dtype),
        scratch_shapes=[pltpu.VMEM((routed, wide), pieces[0].dtype)],
        compiler_params=kernel_params(),
        cost_estimate=brief(),
        name="unpack",
    )(index, *pieces, *after)


def product_kernel(streams, minus, order_ref, *refs):
    blocks, (near_ref, far_ref) = refs[:streams], refs[streams : streams + 2]
    out_ref, acc = refs[-2:]
    k = pl.program_id(0)
    steps = pl.num_programs(0)
    half = steps // 2
    deep = near_ref.shape[0] // half

    def term(rows_ref, at):
        matrix = jnp.concatenate([block[...] for block in blocks], axis=1)
        return dot32(matrix, rows_ref[pl.ds(pl.multiple_of(at * deep, deep), deep), :])

    @pl.when(k == 0)
    def _():
        acc[...] = term(near_ref, 0)

    @pl.when((k > 0) & (k < half))
    def _():
        acc[...] += term(near_ref, k)

    @pl.when(k >= half)
    def _():
        acc[...] += term(far_ref, k - half)

    @pl.when(k == steps - 1)
    def _():
        total = acc[...]
        if minus:
            total = refs[streams + 2][...].astype(jnp.float32) - total
        out_ref[...] = total.astype(out_ref.dtype)


def product(matrix, order, near, far, base=None, after=()):
    rows, depth = matrix.shape
    width = near.shape[1]
    n_row = order.shape[0]
    deep = depth // n_row
    streams = 4 if deep % (4 * TILE) == 0 else 1
    bases = [] if base is None else [base]

    def block_of(q):
        return pl.BlockSpec((rows, deep // streams), lambda k, order: (0, order[k] * streams + q))

    return pl.pallas_call(
        functools.partial(product_kernel, streams, bool(bases)),
        grid_spec=pltpu.PrefetchScalarGridSpec(
            num_scalar_prefetch=1,
            grid=(n_row,),
            in_specs=[block_of(q) for q in range(streams)]
            + [whole_block(*near.shape)] * 2
            + [whole_block(rows, width)] * len(bases)
            + [in_place()] * len(after),
            out_specs=whole_block(rows, width),
            scratch_shapes=[pltpu.VMEM((rows, width), jnp.float32)],
        ),
        out_shape=jax.ShapeDtypeStruct((rows, width), near.dtype),
        compiler_params=kernel_params(),
        cost_estimate=brief(),
        name="product",
    )(order, *[matrix] * streams, near, far, *bases, *after)


def exchange(value, distance, n, axis="row"):
    return lax.ppermute(value, axis, [(i, i ^ distance) for i in range(n)])


def route(packed, n_row):
    near, far = packed[0], exchange(packed[1], 1, n_row)
    cap = near.shape[0] * 2 // n_row
    pieces = [near[:cap], far[:cap]]
    for i in range(1, n_row // 2):
        both = [near[i * cap : (i + 1) * cap], far[i * cap : (i + 1) * cap]]
        pieces.append(exchange(jnp.concatenate(both, axis=0), 2 * i, n_row))
    return pieces


def gather_rows(block, n_row):
    near = [block] + [exchange(block, k, n_row) for k in range(2, n_row, 2)]
    near = jnp.concatenate(near, axis=0)
    return near, exchange(near, 1, n_row)


def route_tables(surface_map, rows, n_row, cap, slots):
    me = lax.axis_index("row")
    mine = surface_map.reshape(-1)
    every = lax.all_gather(mine, "row")
    partners = me ^ jnp.arange(n_row, dtype=jnp.int32)
    local = every[partners] - me * rows
    asked = (local >= 0) & (local < rows)
    rank = jnp.cumsum(asked.astype(jnp.int32), axis=1) - 1
    numbers = jnp.arange(slots, dtype=jnp.int32)
    hit = asked[:, None, :] & (rank[:, None, :] == numbers[None, :, None])
    wanted = jnp.sum(jnp.where(hit, local[:, None, :] + 1, 0), axis=2) - 1
    owner = mine // rows
    held = owner[None, :] == jnp.arange(n_row, dtype=jnp.int32)[:, None]
    place = jnp.cumsum(held.astype(jnp.int32), axis=1) - 1
    slot = jnp.sum(jnp.where(held, place, 0), axis=0)
    lands = (owner ^ me) * slots + slot
    return wanted.reshape(-1, 1), lands.reshape(-1, 1)


def per_device(
    front_inverse,
    coupling_tiles,
    tile_row,
    tile_col,
    surface_map,
    bem_entries,
    pivot_inverse,
    slab_below,
):
    n_row, n_col = lax.axis_size("row"), lax.axis_size("col")
    assert n_row > 1 and n_row & (n_row - 1) == 0
    rows, depth = front_inverse.shape
    count = bem_entries.shape[1]
    per_dest = bem_entries.shape[2] // TILE
    cap = rows // n_row
    slots = -(-cap // 16) * 16
    me = lax.axis_index("row")

    col_at = lax.axis_index("col")
    block_row = tile_row - col_at * (depth // TILE)
    dest, sub = tile_col // per_dest, tile_col % per_dest
    meta = jnp.stack([block_row, dest, sub])
    order = me ^ jnp.concatenate(
        [jnp.arange(0, n_row, 2, dtype=jnp.int32), jnp.arange(1, n_row, 2, dtype=jnp.int32)]
    )
    half = per_dest // 2

    def front_of(start, flat, after):
        return front_products(
            front_inverse, coupling_tiles, meta, start, start + 1, n_col, flat, after
        )

    def summed(parts):
        return lax.psum_scatter(parts, "col", scatter_dimension=0)

    solved, after = [], ()
    for start in range(half):
        parts = front_of(start, False, after)
        after = (parts,)
        solved.append(summed(parts))

    wanted, lands = route_tables(surface_map, rows, n_row, cap, slots)
    routed = []
    for start in range(half, per_dest):
        parts = front_of(start, True, after)
        packed = pack_rows(wanted, [parts], n_row, slots)
        after = (packed[0],)
        routed.append(route(packed, n_row))
    schur = []
    for pieces in routed:
        parts = unpack(lands, pieces, n_col, after)
        schur.append(summed(parts))
        if len(schur) == 1:
            packed = pack_rows(wanted, solved, n_row, slots, (parts,))
            after = (packed[0],)

    def blocks_of(g):
        after = (last,)
        if g == 0:
            return assemble(lands, bem_entries, route(packed, n_row), 0, after)
        return subtract(bem_entries, schur[g - 1], half + g - 1, after)

    sequence = list(range(1 + per_dest - half))
    last = parts
    lowers, gathered = {}, {}
    for g in sequence:
        last, lowers[g] = blocks_of(g)
        gathered[g] = gather_rows(last, n_row)
    pivots, belows = {}, {}
    for g in sequence:
        last = pivots[g] = product(pivot_inverse, order, *gathered[g], after=(last,))
        gathered[g] = gather_rows(last, n_row)
    for g in sequence:
        last = belows[g] = product(slab_below, order, *gathered[g], lowers[g], (last,))
    return jnp.stack(
        [jnp.concatenate([part[g] for g in sorted(part)], axis=1) for part in (pivots, belows)]
    )


def solution(mesh):
    placed = (
        P("row", "col"),
        P("col", None, None),
        P("col"),
        P("col"),
        P(None, "row"),
        P(None, "row", "col"),
        P("row", None),
        P("row", None),
    )
    return jax.shard_map(
        per_device, mesh=mesh, in_specs=placed, out_specs=P(None, "row", "col"), check_vma=False
    )
```

time: 508 us -> 481 us (0.947)
  waiting for transfers between devices: 132 us -> 107 us
    ppermute x45 -> x36, waiting for transfers between devices: 132 us -> 106 us  [exchange(): return lax.ppermute(value, axis, [(i, i ^ distance) for i in range(n)])]
    ppermute x45 -> x36, starting transfers between devices: 36.6 us -> 31.9 us  [exchange(): return lax.ppermute(value, axis, [(i, i ^ distance) for i in range(n)])]
    pallas_call x15 -> x18, Pallas kernels: 271 us -> 268 us  [the longest x4 123 us: front_products(): pl.pallas_call(functools.partial(front_kernel, start, stop, n_col, flat,...]
    unnamed x82 -> x66, local copies, waits for them, and re-layouts: 11.1 us -> 12.2 us
  transfers between devices with their start and end apart: 48 -> 40, of which waited for: 20 -> 13; matrix products, arithmetic and copies ran while one was open for 5% -> 7% of each run, Pallas kernels for 39% -> 48%
where the time goes in v3:
time: 481 us; the launch traced here: 474 us
  Pallas kernels  268 us (56%)
  waiting for transfers between devices  107 us (22%)
  starting transfers between devices  32.2 us (7%)
  other arithmetic  23.3 us (5%)
  local copies, waits for them, and re-layouts  18.7 us (4%)
  between operations  14 us (3%)
  blocking collectives  10.8 us (2%)
    pallas_call x4, Pallas kernels, front_products(): pl.pallas_call(functools.partial(front_kernel, start, stop, n_col, flat,...  123 us
    ppermute x36, waiting for transfers between devices, exchange(): return lax.ppermute(value, axis, [(i, i ^ distance) for i in range(n)])  106 us
    pallas_call x6, Pallas kernels, product(): pl.pallas_call(functools.partial(product_kernel, streams, bool(bases)), g...  77.3 us
    pallas_call x3, Pallas kernels, pack_rows(): pl.pallas_call(functools.partial(pack_kernel, n_row, len(solved)), in_spe...  35.5 us
    ppermute x36, starting transfers between devices, exchange(): return lax.ppermute(value, axis, [(i, i ^ distance) for i in range(n)])  31.9 us
    pallas_call x2, Pallas kernels, unpack(): pl.pallas_call(functools.partial(unpack_kernel, len(pieces), n_col), in_s...  20.5 us
    unnamed x66, local copies, waits for them, and re-layouts  12.2 us
    all_gather x1, blocking collectives, route_tables(): every = lax.all_gather(mine, 'row')  10.8 us
  transfers between devices with their start and end apart: 40, of which 13 were waited for; matrix products, arithmetic and copies ran while one was open for 7% of the time, Pallas kernels for 48%

profile of v3, /device:TPU:0, one launch (start us, length us, event | category | flops | bytes accessed | tf_op | source)
XLA Modules:
  0.0 473.6 jit_solution(17511300190542578739)
XLA Ops:
  8.5 28.1 %front_products.4.refs_0_ = bf16[4,3072,128]{2,1,0:T(8,128)(2,1)} custom-call(s32[3,192]{1,0:T(4,128)} %pad_add_fusion.meta_ref, bf16[192,128,128]{2,1,0:T(8,128)(2,1)} %tiles_ref.7, bf16[3072,6144]{1,0:T(8,128)(2,1)} %front_ref.7), custom_call_target="tpu_custom_call" | custom-call | flops 1 | bytes 1 | tf_op jit(solution)/shard_map/front_products/pallas_call | solution.py:165
  36.7 31.5 %front_products.5.refs_0_ = bf16[4,3072,128]{2,1,0:T(8,128)(2,1)} custom-call(s32[3,192]{1,0:T(4,128)} %pad_add_fusion.meta_ref, bf16[192,128,128]{2,1,0:T(8,128)(2,1)} %tiles_ref.7, bf16[3072,6144]{1,0:T(8,128)(2,1)} %front_ref.7, bf16[4,3072,128]{2,1,0:T(8,128)(2,1)} %front_products.4.refs_0_), custom_call_target="tpu_custom_call" | custom-call | flops 1 | bytes 1 | tf_op jit(solution)/shard_map/front_products/pallas_call | solution.py:165
  68.2 31.8 %front_products.6.refs_0_ = bf16[3072,512]{1,0:T(8,128)(2,1)} custom-call(s32[3,192]{1,0:T(4,128)} %pad_add_fusion.meta_ref, bf16[192,128,128]{2,1,0:T(8,128)(2,1)} %tiles_ref.7, bf16[3072,6144]{1,0:T(8,128)(2,1)} %front_ref.7, bf16[4,3072,128]{2,1,0:T(8,128)(2,1)} %front_products.5.refs_0_), custom_call_target="tpu_custom_call" | custom-call | flops 1 | bytes 1 | tf_op jit(solution)/shard_map/front_products/pallas_call | solution.py:165
  100.1 10.8 %all-gather = s32[8,1,2048]{2,1,0:T(1,128)S(1)} all-gather(s32[1,1,2048]{2,1,0:T(1,128)S(1)} %reshape.212), channel_id=1, replica_groups=mesh['row'=8,'col'=4] {'row'}, dimensions={0}, use_global_device_ids=true | all-gather | bytes 73728 | tf_op jit(solution)/shard_map/all_gather | solution.py:402
  111.6 2.4 reduce-window.16
  114.6 6.2 %select_reduce_fusion = s32[8,384]{1,0:T(8,128)S(1)} fusion(s32[8,2048]{1,0:T(8,128)S(1)} %subtract_add_fusion, s32[8,2048]{1,0:T(8,128)S(1)} %bitcast.51, pred[8,2048]{1,0:T(8,128)(4,1)S(1)} %get-tuple-element.30), kind=kLoop, calls=%fused_computation.1 | loop fusion | flops 25162752 | bytes 159744 | tf_op jit(solution)/shard_map/reduce_sum | solution.py:409
  120.9 1.7 copy.41
  122.6 14.0 %pack_rows.3 = (bf16[1536,512]{1,0:T(8,128)(2,1)}, bf16[1536,512]{1,0:T(8,128)(2,1)}) custom-call(s32[3072,1]{1,0:T(8,128)} %bitcast.43, bf16[3072,512]{1,0:T(8,128)(2,1)} %front_products.6.refs_0_), custom_call_target="tpu_custom_call" | custom-call | flops 1 | bytes 1 | tf_op jit(solution)/shard_map/pack_rows/pallas_call | solution.py:208
  136.8 31.9 %front_products.7.refs_0_ = bf16[3072,512]{1,0:T(8,128)(2,1)} custom-call(s32[3,192]{1,0:T(4,128)} %pad_add_fusion.meta_ref, bf16[192,128,128]{2,1,0:T(8,128)(2,1)} %tiles_ref.7, bf16[3072,6144]{1,0:T(8,128)(2,1)} %front_ref.7, bf16[1536,512]{1,0:T(8,128)(2,1)} %get-tuple-element.17.refs_0_), custom_call_target="tpu_custom_call" | custom-call | flops 1 | bytes 1 | tf_op jit(solution)/shard_map/front_products/pallas_call | solution.py:165
  170.7 1.6 collective-permute-start.1
  173.8 1.0 pad_maximum_fusion.6
  174.7 1.4 collective-permute-start.3
  176.2 13.4 %pack_rows.4 = (bf16[1536,512]{1,0:T(8,128)(2,1)}, bf16[1536,512]{1,0:T(8,128)(2,1)}) custom-call(s32[3072,1]{1,0:T(8,128)} %bitcast.44, bf16[3072,512]{1,0:T(8,128)(2,1)} %front_products.7.refs_0_), custom_call_target="tpu_custom_call" | custom-call | flops 1 | bytes 1 | tf_op jit(solution)/shard_map/pack_rows/pallas_call | solution.py:208
  189.6 2.3 reduce-window.14
  193.7 1.2 fusion.3.index_ref
  194.9 14.8 %collective-permute-done.2.refs_3_ = bf16[768,512]{1,0:T(8,128)(2,1)} collective-permute-done((bf16[768,512]{1,0:T(8,128)(2,1)}, bf16[768,512]{1,0:T(8,128)(2,1)}, u32[]{:S(2)}, u32[]{:S(2)}) %collective-permute-start.2) | collective-permute-done | bytes 786464 | tf_op jit(solution)/shard_map/ppermute | solution.py:380
  209.8 10.3 %unpack.2.refs_2_ = bf16[4,2048,128]{2,1,0:T(8,128)(2,1)} custom-call(s32[2048,1]{1,0:T(8,128)} %fusion.3.index_ref, bf16[384,512]{1,0:T(8,128)(2,1)} %get-tuple-element.34.refs_0_, bf16[384,512]{1,0:T(8,128)(2,1)} %get-tuple-element.38.refs_1_, bf16[768,512]{1,0:T(8,128)(2,1)} %collective-permute-done.1.refs_2_, ...), custom_call_target="tpu_custom_call" | custom-call | flops 1 | bytes 1 | tf_op jit(solution)/shard_map/unpack/pallas_call | solution.py:304
  220.4 1.1 copy-done.3
  222.3 1.5 collective-permute-done.8
  226.1 1.0 pad_maximum_fusion.8
  227.1 1.5 collective-permute-start.10
  229.5 1.5 collective-permute-start.11
  231.0 8.1 %pack_rows.5 = (bf16[1536,256]{1,0:T(8,128)(2,1)}, bf16[1536,256]{1,0:T(8,128)(2,1)}) custom-call(s32[3072,1]{1,0:T(8,128)} %bitcast.45, bf16[3072,128]{1,0:T(8,128)(2,1)} %bitcast.47, bf16[3072,128]{1,0:T(8,128)(2,1)} %bitcast.48, bf16[4,2048,128]{2,1,0:T(8,128)(2,1)} %unpack.2.refs_2_), custom_call_target="tpu_custom_call" | custom-call | flops 1 | bytes 1 | tf_op jit(solution)/shard_map/pack_rows/pallas_call | solution.py:208
  239.1 7.1 %collective-permute-done.9.refs_2_ = bf16[768,512]{1,0:T(8,128)(2,1)S(1)} collective-permute-done((bf16[768,512]{1,0:T(8,128)(2,1)}, bf16[768,512]{1,0:T(8,128)(2,1)S(1)}, u32[]{:S(2)}, u32[]{:S(2)}) %collective-permute-start.9) | collective-permute-done | bytes 786464 | tf_op jit(solution)/shard_map/ppermute | solution.py:380
  246.2 17.3 %collective-permute-done.10.refs_3_ = bf16[768,512]{1,0:T(8,128)(2,1)S(1)} collective-permute-done((bf16[768,512]{1,0:T(8,128)(2,1)}, bf16[768,512]{1,0:T(8,128)(2,1)S(1)}, u32[]{:S(2)}, u32[]{:S(2)}) %collective-permute-start.10) | collective-permute-done | bytes 786464 | tf_op jit(solution)/shard_map/ppermute | solution.py:380
  264.6 10.2 %unpack.3.refs_5_ = bf16[4,2048,128]{2,1,0:T(8,128)(2,1)} custom-call(s32[2048,1]{1,0:T(8,128)} %fusion.3.index_ref, bf16[384,512]{1,0:T(8,128)(2,1)} %get-tuple-element.42.refs_0_, bf16[384,512]{1,0:T(8,128)(2,1)} %get-tuple-element.46.refs_1_, bf16[768,512]{1,0:T(8,128)(2,1)} %copy-done.16, bf16[768,512]{1,0:T(8,128)(2,1)} %copy-done.17, ...), custom_call_target="tpu_custom_call" | custom-call | flops 1 | bytes 1 | tf_op jit(solution)/shard_map/unpack/pallas_call | solution.py:304
  274.8 1.1 copy-done.10
  277.4 1.6 collective-permute-start.5
  279.6 1.5 collective-permute-start.7
  281.2 8.4 %collective-permute-done.5.refs_2_ = bf16[768,256]{1,0:T(8,128)(2,1)S(1)} collective-permute-done((bf16[768,256]{1,0:T(8,128)(2,1)S(1)}, bf16[768,256]{1,0:T(8,128)(2,1)S(1)}, u32[]{:S(2)}, u32[]{:S(2)}) %collective-permute-start.5) | collective-permute-done | bytes 393248 | tf_op jit(solution)/shard_map/ppermute | solution.py:380
  289.6 7.8 %collective-permute-done.6.refs_3_ = bf16[768,256]{1,0:T(8,128)(2,1)S(1)} collective-permute-done((bf16[768,256]{1,0:T(8,128)(2,1)S(1)}, bf16[768,256]{1,0:T(8,128)(2,1)S(1)}, u32[]{:S(2)}, u32[]{:S(2)}) %collective-permute-start.6) | collective-permute-done | bytes 393248 | tf_op jit(solution)/shard_map/ppermute | solution.py:380
  298.2 6.3 %assemble.1 = (bf16[1024,256]{1,0:T(8,128)(2,1)}, bf16[1024,256]{1,0:T(8,128)(2,1)}) custom-call(s32[2048,1]{1,0:T(8,128)} %fusion.3.index_ref, bf16[2,1024,512]{2,1,0:T(8,128)(2,1)} %bem_ref.5, bf16[384,256]{1,0:T(8,128)(2,1)} %get-tuple-element.50.refs_0_, bf16[384,256]{1,0:T(8,128)(2,1)} %get-tuple-element.54.refs_1_, bf16[768,256]{1,0:T(8,128)(2,1)} %copy-done.19, ...), custom_call_target="tpu_custom_call" | custom-call | flops 1 | bytes 1 | tf_op jit(solution)/shard_map/assemble/pallas_call | solution.py:245
  305.1 1.5 collective-permute-start.13
  306.6 1.5 collective-permute-start.14
  308.1 1.1 constant_dynamic-update-slice_fusion.3
  309.2 10.5 %collective-permute-done.12 = bf16[1024,256]{1,0:T(8,128)(2,1)S(1)} collective-permute-done((bf16[1024,256]{1,0:T(8,128)(2,1)}, bf16[1024,256]{1,0:T(8,128)(2,1)S(1)}, u32[]{:S(2)}, u32[]{:S(2)}) %collective-permute-start.12) | collective-permute-done | bytes 524320 | tf_op jit(solution)/shard_map/ppermute | solution.py:380
  319.7 8.3 %collective-permute-done.13 = bf16[1024,256]{1,0:T(8,128)(2,1)S(1)} collective-permute-done((bf16[1024,256]{1,0:T(8,128)(2,1)}, bf16[1024,256]{1,0:T(8,128)(2,1)S(1)}, u32[]{:S(2)}, u32[]{:S(2)}) %collective-permute-start.13) | collective-permute-done | bytes 524320 | tf_op jit(solution)/shard_map/ppermute | solution.py:380
  328.2 2.7 subtract.2
  330.9 1.4 collective-permute-start.16
  332.9 1.5 collective-permute-start.18
  334.4 1.0 constant_dynamic-update-slice_fusion.7
  335.4 4.9 %collective-permute-done.16 = bf16[1024,128]{1,0:T(8,128)(2,1)S(1)} collective-permute-done((bf16[1024,128]{1,0:T(8,128)(2,1)}, bf16[1024,128]{1,0:T(8,128)(2,1)S(1)}, u32[]{:S(2)}, u32[]{:S(2)}) %collective-permute-start.16) | collective-permute-done | bytes 262176 | tf_op jit(solution)/shard_map/ppermute | solution.py:380
  340.4 5.5 %collective-permute-done.17 = bf16[1024,128]{1,0:T(8,128)(2,1)S(1)} collective-permute-done((bf16[1024,128]{1,0:T(8,128)(2,1)}, bf16[1024,128]{1,0:T(8,128)(2,1)S(1)}, u32[]{:S(2)}, u32[]{:S(2)}) %collective-permute-start.17) | collective-permute-done | bytes 262176 | tf_op jit(solution)/shard_map/ppermute | solution.py:380
  346.1 2.3 subtract.3
  349.1 1.4 collective-permute-start.21
  351.2 1.4 collective-permute-start.22
  352.6 1.0 constant_dynamic-update-slice_fusion.11
  353.6 13.6 %product.6.refs_6_ = bf16[1024,256]{1,0:T(8,128)(2,1)} custom-call(s32[8]{0:T(128)} %add_xor_fusion.order_ref, bf16[1024,8192]{1,0:T(8,128)(2,1)} %refs_3_.8, bf16[1024,8192]{1,0:T(8,128)(2,1)} %refs_3_.8, bf16[1024,8192]{1,0:T(8,128)(2,1)} %refs_3_.8, bf16[1024,8192]{1,0:T(8,128)(2,1)} %refs_3_.8, bf16[4096,256]{1,0:T(8,128)(2,1)} %copy-done.9, ...), custom_call_target="tpu_custom_call" | custom-call | flops 1 | bytes 1 | tf_op jit(solution)/shard_map/product/pallas_call | solution.py:360
  367.2 1.5 collective-permute-start.26
  369.4 1.4 collective-permute-start.24
  371.0 12.7 %product.7.refs_6_ = bf16[1024,128]{1,0:T(8,128)(2,1)} custom-call(s32[8]{0:T(128)} %add_xor_fusion.order_ref, bf16[1024,8192]{1,0:T(8,128)(2,1)} %refs_3_.8, bf16[1024,8192]{1,0:T(8,128)(2,1)} %refs_3_.8, bf16[1024,8192]{1,0:T(8,128)(2,1)} %refs_3_.8, bf16[1024,8192]{1,0:T(8,128)(2,1)} %refs_3_.8, bf16[4096,128]{1,0:T(8,128)(2,1)} %copy-done.13, ...), custom_call_target="tpu_custom_call" | custom-call | flops 1 | bytes 1 | tf_op jit(solution)/shard_map/product/pallas_call | solution.py:360
  383.7 1.5 collective-permute-start.30
  385.9 8.6 %collective-permute-done.25 = bf16[1024,256]{1,0:T(8,128)(2,1)S(1)} collective-permute-done((bf16[1024,256]{1,0:T(8,128)(2,1)}, bf16[1024,256]{1,0:T(8,128)(2,1)S(1)}, u32[]{:S(2)}, u32[]{:S(2)}) %collective-permute-start.25) | collective-permute-done | bytes 524320 | tf_op jit(solution)/shard_map/ppermute | solution.py:380
  395.5 1.0 copy-done.14
  396.4 12.6 %product.8.refs_7_ = bf16[1024,128]{1,0:T(8,128)(2,1)} custom-call(s32[8]{0:T(128)} %add_xor_fusion.order_ref, bf16[1024,8192]{1,0:T(8,128)(2,1)} %refs_3_.8, bf16[1024,8192]{1,0:T(8,128)(2,1)} %refs_3_.8, bf16[1024,8192]{1,0:T(8,128)(2,1)} %refs_3_.8, bf16[1024,8192]{1,0:T(8,128)(2,1)} %refs_3_.8, bf16[4096,128]{1,0:T(8,128)(2,1)} %copy-done.12, ...), custom_call_target="tpu_custom_call" | custom-call | flops 1 | bytes 1 | tf_op jit(solution)/shard_map/product/pallas_call | solution.py:360
  409.0 1.5 collective-permute-start.34
  410.5 1.4 collective-permute-start.33
  412.7 6.6 %collective-permute-done.34 = bf16[1024,128]{1,0:T(8,128)(2,1)S(1)} collective-permute-done((bf16[1024,128]{1,0:T(8,128)(2,1)}, bf16[1024,128]{1,0:T(8,128)(2,1)S(1)}, u32[]{:S(2)}, u32[]{:S(2)}) %collective-permute-start.34) | collective-permute-done | bytes 262176 | tf_op jit(solution)/shard_map/ppermute | solution.py:380
  419.3 5.2 %collective-permute-done.33 = bf16[1024,128]{1,0:T(8,128)(2,1)S(1)} collective-permute-done((bf16[1024,128]{1,0:T(8,128)(2,1)}, bf16[1024,128]{1,0:T(8,128)(2,1)S(1)}, u32[]{:S(2)}, u32[]{:S(2)}) %collective-permute-start.33) | collective-permute-done | bytes 262176 | tf_op jit(solution)/shard_map/ppermute | solution.py:380
  424.8 13.3 %product.9.refs_7_ = bf16[1024,256]{1,0:T(8,128)(2,1)} custom-call(s32[8]{0:T(128)} %add_xor_fusion.order_ref, bf16[1024,8192]{1,0:T(8,128)(2,1)} %refs_3_.11, bf16[1024,8192]{1,0:T(8,128)(2,1)} %refs_3_.11, bf16[1024,8192]{1,0:T(8,128)(2,1)} %refs_3_.11, bf16[1024,8192]{1,0:T(8,128)(2,1)} %refs_3_.11, bf16[4096,256]{1,0:T(8,128)(2,1)} %copy-done.1, ...), custom_call_target="tpu_custom_call" | custom-call | flops 1 | bytes 1 | tf_op jit(solution)/shard_map/product/pallas_call | solution.py:360
  439.1 12.5 %product.10.refs_7_ = bf16[1024,128]{1,0:T(8,128)(2,1)} custom-call(s32[8]{0:T(128)} %add_xor_fusion.order_ref, bf16[1024,8192]{1,0:T(8,128)(2,1)} %refs_3_.11, bf16[1024,8192]{1,0:T(8,128)(2,1)} %refs_3_.11, bf16[1024,8192]{1,0:T(8,128)(2,1)} %refs_3_.11, bf16[1024,8192]{1,0:T(8,128)(2,1)} %refs_3_.11, bf16[4096,128]{1,0:T(8,128)(2,1)} %copy-done.7, ...), custom_call_target="tpu_custom_call" | custom-call | flops 1 | bytes 1 | tf_op jit(solution)/shard_map/product/pallas_call | solution.py:360
  451.6 12.6 %product.11 = bf16[1024,128]{1,0:T(8,128)(2,1)} custom-call(s32[8]{0:T(128)} %add_xor_fusion.order_ref, bf16[1024,8192]{1,0:T(8,128)(2,1)} %refs_3_.11, bf16[1024,8192]{1,0:T(8,128)(2,1)} %refs_3_.11, bf16[1024,8192]{1,0:T(8,128)(2,1)} %refs_3_.11, bf16[1024,8192]{1,0:T(8,128)(2,1)} %refs_3_.11, bf16[4096,128]{1,0:T(8,128)(2,1)} %copy-done.8, ...), custom_call_target="tpu_custom_call" | custom-call | flops 1 | bytes 1 | tf_op jit(solution)/shard_map/product/pallas_call | solution.py:360
  464.2 1.0 maximum_bitcast_fusion.1
  465.3 1.5 pad_maximum_fusion.1
  (160 shorter events, 24.7 us)
Async XLA Ops:
  6.5 224.5 %reduce-scatter.5.cloned.1.call-start = ((), (), s32[]{:S(2)}) async-start(), calls=%async_computation.4 | async-start | bytes 3932160 | tf_op jit(solution)/shard_map/reduce_scatter | solution.py:452
  36.6 194.4 %reduce-scatter.7.cloned.1.call-start = ((), (), s32[]{:S(2)}) async-start(), calls=%async_computation.5 | async-start | bytes 3932160 | tf_op jit(solution)/shard_map/reduce_scatter | solution.py:452
  68.2 31.8 %copy-start.22 = (s32[2,1024]{1,0:T(2,128)S(1)}, s32[2,1024]{1,0:T(2,128)}, u32[]{:S(2)}) copy-start(s32[2,1024]{1,0:T(2,128)} %param.12) | copy-start | bytes 24580
  68.2 260.0 %reduce-scatter.11.cloned.1.call-start = ((), (), s32[]{:S(2)}) async-start(), calls=%async_computation.7 | async-start | bytes 2621440 | tf_op jit(solution)/shard_map/reduce_scatter | solution.py:452
  136.6 33.2 %collective-permute-start = (bf16[1536,512]{1,0:T(8,128)(2,1)}, bf16[1536,512]{1,0:T(8,128)(2,1)S(1)}, u32[]{:S(2)}, u32[]{:S(2)}) collective-permute-start(bf16[1536,512]{1,0:T(8,128)(2,1)} %get-tuple-element.18), channel_id=1, source_target_pairs={{0,4},{4,0},{8,12},{12,8},{16,20},{20,16},{24,28},{28,24},{1,5},{5... | collective-permute-start | bytes 4718600 | tf_op jit(solution)/shard_map/ppermute | solution.py:380
  136.8 32.1 %copy-start.2 = (bf16[1536,512]{1,0:T(8,128)(2,1)S(1)}, bf16[1536,512]{1,0:T(8,128)(2,1)}, u32[]{:S(2)}) copy-start(bf16[1536,512]{1,0:T(8,128)(2,1)} %get-tuple-element.17.refs_0_) | copy-start | bytes 4718596
  170.7 24.2 %collective-permute-start.1 = (bf16[768,512]{1,0:T(8,128)(2,1)S(1)}, bf16[768,512]{1,0:T(8,128)(2,1)}, u32[]{:S(2)}, u32[]{:S(2)}) collective-permute-start(bf16[768,512]{1,0:T(8,128)(2,1)S(1)} %pad_maximum_fusion.4), channel_id=1, source_target_pairs={{0,8},{4,12},{8,0},{12,4},{16,24},{20,28},{24,16},{28,20},{1,9},{5... | collective-permute-start | bytes 2359304 | tf_op jit(solution)/shard_map/ppermute | solution.py:380
  173.2 36.6 %collective-permute-start.2 = (bf16[768,512]{1,0:T(8,128)(2,1)}, bf16[768,512]{1,0:T(8,128)(2,1)}, u32[]{:S(2)}, u32[]{:S(2)}) collective-permute-start(bf16[768,512]{1,0:T(8,128)(2,1)} %pad_maximum_fusion.5), channel_id=1, source_target_pairs={{0,16},{4,20},{8,24},{12,28},{16,0},{20,4},{24,8},{28,12},{1,17},{... | collective-permute-start | bytes 2359304 | tf_op jit(solution)/shard_map/ppermute | solution.py:380
  174.7 35.0 %collective-permute-start.3 = (bf16[768,512]{1,0:T(8,128)(2,1)}, bf16[768,512]{1,0:T(8,128)(2,1)}, u32[]{:S(2)}, u32[]{:S(2)}) collective-permute-start(bf16[768,512]{1,0:T(8,128)(2,1)} %pad_maximum_fusion.6), channel_id=1, source_target_pairs={{0,24},{4,28},{8,16},{12,20},{16,8},{20,12},{24,0},{28,4},{1,25},{... | collective-permute-start | bytes 2359304 | tf_op jit(solution)/shard_map/ppermute | solution.py:380
  209.8 10.5 %copy-start.23 = (bf16[1536,512]{1,0:T(8,128)(2,1)S(1)}, bf16[1536,512]{1,0:T(8,128)(2,1)}, u32[]{:S(2)}) copy-start(bf16[1536,512]{1,0:T(8,128)(2,1)} %get-tuple-element.22) | copy-start | bytes 4718596
  220.1 1.4 copy-start.3
  220.1 126.0 %reduce-scatter.9.cloned.1.call-start = ((), (), s32[]{:S(2)}) async-start(), calls=%async_computation.6 | async-start | bytes 2621440 | tf_op jit(solution)/shard_map/reduce_scatter | solution.py:452
  220.3 3.5 collective-permute-start.8
  225.6 20.6 %collective-permute-start.9 = (bf16[768,512]{1,0:T(8,128)(2,1)}, bf16[768,512]{1,0:T(8,128)(2,1)S(1)}, u32[]{:S(2)}, u32[]{:S(2)}) collective-permute-start(bf16[768,512]{1,0:T(8,128)(2,1)} %pad_maximum_fusion.7), channel_id=1, source_target_pairs={{0,8},{4,12},{8,0},{12,4},{16,24},{20,28},{24,16},{28,20},{1,9},{5... | collective-permute-start | bytes 2359304 | tf_op jit(solution)/shard_map/ppermute | solution.py:380
  227.1 36.4 %collective-permute-start.10 = (bf16[768,512]{1,0:T(8,128)(2,1)}, bf16[768,512]{1,0:T(8,128)(2,1)S(1)}, u32[]{:S(2)}, u32[]{:S(2)}) collective-permute-start(bf16[768,512]{1,0:T(8,128)(2,1)} %pad_maximum_fusion.8), channel_id=1, source_target_pairs={{0,16},{4,20},{8,24},{12,28},{16,0},{20,4},{24,8},{28,12},{1,17},{... | collective-permute-start | bytes 2359304 | tf_op jit(solution)/shard_map/ppermute | solution.py:380
  229.5 33.9 %collective-permute-start.11 = (bf16[768,512]{1,0:T(8,128)(2,1)}, bf16[768,512]{1,0:T(8,128)(2,1)S(1)}, u32[]{:S(2)}, u32[]{:S(2)}) collective-permute-start(bf16[768,512]{1,0:T(8,128)(2,1)} %pad_maximum_fusion.9), channel_id=1, source_target_pairs={{0,24},{4,28},{8,16},{12,20},{16,8},{20,12},{24,0},{28,4},{1,25},{... | collective-permute-start | bytes 2359304 | tf_op jit(solution)/shard_map/ppermute | solution.py:380
  239.1 37.6 %collective-permute-start.4 = (bf16[1536,256]{1,0:T(8,128)(2,1)}, bf16[1536,256]{1,0:T(8,128)(2,1)S(1)}, u32[]{:S(2)}, u32[]{:S(2)}) collective-permute-start(bf16[1536,256]{1,0:T(8,128)(2,1)} %get-tuple-element.21), channel_id=1, source_target_pairs={{0,4},{4,0},{8,12},{12,8},{16,20},{20,16},{24,28},{28,24},{1,5},{5... | collective-permute-start | bytes 2359304 | tf_op jit(solution)/shard_map/ppermute | solution.py:380
  246.2 17.3 %copy-start.16 = (bf16[768,512]{1,0:T(8,128)(2,1)}, bf16[768,512]{1,0:T(8,128)(2,1)S(1)}, u32[]{:S(2)}) copy-start(bf16[768,512]{1,0:T(8,128)(2,1)S(1)} %collective-permute-done.9.refs_2_) | copy-start | bytes 2359300
  263.5 0.9 copy-start.17
  263.5 1.2 copy-start.18
  274.8 1.1 copy-start.10
  277.4 12.1 %collective-permute-start.5 = (bf16[768,256]{1,0:T(8,128)(2,1)S(1)}, bf16[768,256]{1,0:T(8,128)(2,1)S(1)}, u32[]{:S(2)}, u32[]{:S(2)}) collective-permute-start(bf16[768,256]{1,0:T(8,128)(2,1)S(1)} %pad_maximum_fusion.10), channel_id=1, source_target_pairs={{0,8},{4,12},{8,0},{12,4},{16,24},{20,28},{24,16},{28,20},{1,9},{5... | collective-permute-start | bytes 1179656 | tf_op jit(solution)/shard_map/ppermute | solution.py:380
  279.0 18.3 %collective-permute-start.6 = (bf16[768,256]{1,0:T(8,128)(2,1)S(1)}, bf16[768,256]{1,0:T(8,128)(2,1)S(1)}, u32[]{:S(2)}, u32[]{:S(2)}) collective-permute-start(bf16[768,256]{1,0:T(8,128)(2,1)S(1)} %pad_maximum_fusion.11), channel_id=1, source_target_pairs={{0,16},{4,20},{8,24},{12,28},{16,0},{20,4},{24,8},{28,12},{1,17},{... | collective-permute-start | bytes 1179656 | tf_op jit(solution)/shard_map/ppermute | solution.py:380
  279.6 17.7 %collective-permute-start.7 = (bf16[768,256]{1,0:T(8,128)(2,1)S(1)}, bf16[768,256]{1,0:T(8,128)(2,1)S(1)}, u32[]{:S(2)}, u32[]{:S(2)}) collective-permute-start(bf16[768,256]{1,0:T(8,128)(2,1)S(1)} %pad_maximum_fusion.12), channel_id=1, source_target_pairs={{0,24},{4,28},{8,16},{12,20},{16,8},{20,12},{24,0},{28,4},{1,25},{... | collective-permute-start | bytes 1179656 | tf_op jit(solution)/shard_map/ppermute | solution.py:380
  289.6 7.8 %copy-start.19 = (bf16[768,256]{1,0:T(8,128)(2,1)}, bf16[768,256]{1,0:T(8,128)(2,1)S(1)}, u32[]{:S(2)}) copy-start(bf16[768,256]{1,0:T(8,128)(2,1)S(1)} %collective-permute-done.5.refs_2_) | copy-start | bytes 1179652
  297.4 0.8 copy-start.20
  297.4 0.9 copy-start.21
  304.6 15.1 %collective-permute-start.12 = (bf16[1024,256]{1,0:T(8,128)(2,1)}, bf16[1024,256]{1,0:T(8,128)(2,1)S(1)}, u32[]{:S(2)}, u32[]{:S(2)}) collective-permute-start(bf16[1024,256]{1,0:T(8,128)(2,1)} %get-tuple-element.23.refs_0_), channel_id=1, source_target_pairs={{0,8},{4,12},{8,0},{12,4},{16,24},{20,28},{24,16},{28,20},{1,9},{5... | collective-permute-start | bytes 1572872 | tf_op jit(solution)/shard_map/ppermute | solution.py:380
  305.1 22.9 %collective-permute-start.13 = (bf16[1024,256]{1,0:T(8,128)(2,1)}, bf16[1024,256]{1,0:T(8,128)(2,1)S(1)}, u32[]{:S(2)}, u32[]{:S(2)}) collective-permute-start(bf16[1024,256]{1,0:T(8,128)(2,1)} %get-tuple-element.23.refs_0_), channel_id=1, source_target_pairs={{0,16},{4,20},{8,24},{12,28},{16,0},{20,4},{24,8},{28,12},{1,17},{... | collective-permute-start | bytes 1572872 | tf_op jit(solution)/shard_map/ppermute | solution.py:380
  306.6 21.4 %collective-permute-start.14 = (bf16[1024,256]{1,0:T(8,128)(2,1)}, bf16[1024,256]{1,0:T(8,128)(2,1)S(1)}, u32[]{:S(2)}, u32[]{:S(2)}) collective-permute-start(bf16[1024,256]{1,0:T(8,128)(2,1)} %get-tuple-element.23.refs_0_), channel_id=1, source_target_pairs={{0,24},{4,28},{8,16},{12,20},{16,8},{20,12},{24,0},{28,4},{1,25},{... | collective-permute-start | bytes 1572872 | tf_op jit(solution)/shard_map/ppermute | solution.py:380
  328.1 12.3 %copy-start.9 = (bf16[4096,256]{1,0:T(8,128)(2,1)}, bf16[4096,256]{1,0:T(8,128)(2,1)S(1)}, u32[]{:S(2)}) copy-start(bf16[4096,256]{1,0:T(8,128)(2,1)S(1)} %constant_dynamic-update-slice_fusion.refs_4_) | copy-start | bytes 6291460
  328.1 25.5 %collective-permute-start.15 = (bf16[4096,256]{1,0:T(8,128)(2,1)S(1)}, bf16[4096,256]{1,0:T(8,128)(2,1)}, u32[]{:S(2)}, u32[]{:S(2)}) collective-permute-start(bf16[4096,256]{1,0:T(8,128)(2,1)S(1)} %constant_dynamic-update-slice_fusion.refs_4_), channel_id=1, source_target_pairs={{0,4},{4,0},{8,12},{12,8},{16,20},{20,16},{24,28},{28,24},{1,5},{5... | collective-permute-start | bytes 6291464 | tf_op jit(solution)/shard_map/ppermute | solution.py:380
  330.9 9.4 %collective-permute-start.16 = (bf16[1024,128]{1,0:T(8,128)(2,1)}, bf16[1024,128]{1,0:T(8,128)(2,1)S(1)}, u32[]{:S(2)}, u32[]{:S(2)}) collective-permute-start(bf16[1024,128]{1,0:T(8,128)(2,1)} %get-tuple-element.24.refs_0_), channel_id=1, source_target_pairs={{0,8},{4,12},{8,0},{12,4},{16,24},{20,28},{24,16},{28,20},{1,9},{5... | collective-permute-start | bytes 786440 | tf_op jit(solution)/shard_map/ppermute | solution.py:380
  332.3 13.6 %collective-permute-start.17 = (bf16[1024,128]{1,0:T(8,128)(2,1)}, bf16[1024,128]{1,0:T(8,128)(2,1)S(1)}, u32[]{:S(2)}, u32[]{:S(2)}) collective-permute-start(bf16[1024,128]{1,0:T(8,128)(2,1)} %get-tuple-element.24.refs_0_), channel_id=1, source_target_pairs={{0,16},{4,20},{8,24},{12,28},{16,0},{20,4},{24,8},{28,12},{1,17},{... | collective-permute-start | bytes 786440 | tf_op jit(solution)/shard_map/ppermute | solution.py:380
  332.9 13.0 %collective-permute-start.18 = (bf16[1024,128]{1,0:T(8,128)(2,1)}, bf16[1024,128]{1,0:T(8,128)(2,1)S(1)}, u32[]{:S(2)}, u32[]{:S(2)}) collective-permute-start(bf16[1024,128]{1,0:T(8,128)(2,1)} %get-tuple-element.24.refs_0_), channel_id=1, source_target_pairs={{0,24},{4,28},{8,16},{12,20},{16,8},{20,12},{24,0},{28,4},{1,25},{... | collective-permute-start | bytes 786440 | tf_op jit(solution)/shard_map/ppermute | solution.py:380
  345.9 21.3 %copy-start.13 = (bf16[4096,128]{1,0:T(8,128)(2,1)}, bf16[4096,128]{1,0:T(8,128)(2,1)S(1)}, u32[]{:S(2)}) copy-start(bf16[4096,128]{1,0:T(8,128)(2,1)S(1)} %constant_dynamic-update-slice_fusion.4.refs_4_) | copy-start | bytes 3145732
  346.0 25.0 %collective-permute-start.19 = (bf16[4096,128]{1,0:T(8,128)(2,1)S(1)}, bf16[4096,128]{1,0:T(8,128)(2,1)}, u32[]{:S(2)}, u32[]{:S(2)}) collective-permute-start(bf16[4096,128]{1,0:T(8,128)(2,1)S(1)} %constant_dynamic-update-slice_fusion.4.refs_4_), channel_id=1, source_target_pairs={{0,4},{4,0},{8,12},{12,8},{16,20},{20,16},{24,28},{28,24},{1,5},{5... | collective-permute-start | bytes 3145736 | tf_op jit(solution)/shard_map/ppermute | solution.py:380
  348.4 20.3 %collective-permute-start.20 = (bf16[1024,128]{1,0:T(8,128)(2,1)}, bf16[1024,128]{1,0:T(8,128)(2,1)S(1)}, u32[]{:S(2)}, u32[]{:S(2)}) collective-permute-start(bf16[1024,128]{1,0:T(8,128)(2,1)} %get-tuple-element.25.refs_6_), channel_id=1, source_target_pairs={{0,8},{4,12},{8,0},{12,4},{16,24},{20,28},{24,16},{28,20},{1,9},{5... | collective-permute-start | bytes 786440 | tf_op jit(solution)/shard_map/ppermute | solution.py:380
  349.1 20.3 %collective-permute-start.21 = (bf16[1024,128]{1,0:T(8,128)(2,1)}, bf16[1024,128]{1,0:T(8,128)(2,1)S(1)}, u32[]{:S(2)}, u32[]{:S(2)}) collective-permute-start(bf16[1024,128]{1,0:T(8,128)(2,1)} %get-tuple-element.25.refs_6_), channel_id=1, source_target_pairs={{0,16},{4,20},{8,24},{12,28},{16,0},{20,4},{24,8},{28,12},{1,17},{... | collective-permute-start | bytes 786440 | tf_op jit(solution)/shard_map/ppermute | solution.py:380
  351.2 19.7 %collective-permute-start.22 = (bf16[1024,128]{1,0:T(8,128)(2,1)}, bf16[1024,128]{1,0:T(8,128)(2,1)S(1)}, u32[]{:S(2)}, u32[]{:S(2)}) collective-permute-start(bf16[1024,128]{1,0:T(8,128)(2,1)} %get-tuple-element.25.refs_6_), channel_id=1, source_target_pairs={{0,24},{4,28},{8,16},{12,20},{16,8},{20,12},{24,0},{28,4},{1,25},{... | collective-permute-start | bytes 786440 | tf_op jit(solution)/shard_map/ppermute | solution.py:380
  367.2 18.1 %collective-permute-start.26 = (bf16[1024,256]{1,0:T(8,128)(2,1)}, bf16[1024,256]{1,0:T(8,128)(2,1)S(1)}, u32[]{:S(2)}, u32[]{:S(2)}) collective-permute-start(bf16[1024,256]{1,0:T(8,128)(2,1)} %product.6.refs_6_), channel_id=1, source_target_pairs={{0,24},{4,28},{8,16},{12,20},{16,8},{20,12},{24,0},{28,4},{1,25},{... | collective-permute-start | bytes 1572872 | tf_op jit(solution)/shard_map/ppermute | solution.py:380
  368.8 25.8 %collective-permute-start.25 = (bf16[1024,256]{1,0:T(8,128)(2,1)}, bf16[1024,256]{1,0:T(8,128)(2,1)S(1)}, u32[]{:S(2)}, u32[]{:S(2)}) collective-permute-start(bf16[1024,256]{1,0:T(8,128)(2,1)} %product.6.refs_6_), channel_id=1, source_target_pairs={{0,16},{4,20},{8,24},{12,28},{16,0},{20,4},{24,8},{28,12},{1,17},{... | collective-permute-start | bytes 1572872 | tf_op jit(solution)/shard_map/ppermute | solution.py:380
  369.4 25.8 %collective-permute-start.24 = (bf16[1024,256]{1,0:T(8,128)(2,1)}, bf16[1024,256]{1,0:T(8,128)(2,1)S(1)}, u32[]{:S(2)}, u32[]{:S(2)}) collective-permute-start(bf16[1024,256]{1,0:T(8,128)(2,1)} %product.6.refs_6_), channel_id=1, source_target_pairs={{0,8},{4,12},{8,0},{12,4},{16,24},{20,28},{24,16},{28,20},{1,9},{5... | collective-permute-start | bytes 1572872 | tf_op jit(solution)/shard_map/ppermute | solution.py:380
  370.9 12.8 %copy-start.12 = (bf16[4096,128]{1,0:T(8,128)(2,1)}, bf16[4096,128]{1,0:T(8,128)(2,1)S(1)}, u32[]{:S(2)}) copy-start(bf16[4096,128]{1,0:T(8,128)(2,1)S(1)} %constant_dynamic-update-slice_fusion.8.refs_4_) | copy-start | bytes 3145732
  370.9 24.3 %copy-start = (bf16[1024,256]{1,0:T(8,128)(2,1)S(1)}, bf16[1024,256]{1,0:T(8,128)(2,1)}, u32[]{:S(2)}) copy-start(bf16[1024,256]{1,0:T(8,128)(2,1)} %product.6.refs_6_) | copy-start | bytes 1572868
  370.9 24.5 %collective-permute-start.23 = (bf16[4096,128]{1,0:T(8,128)(2,1)S(1)}, bf16[4096,128]{1,0:T(8,128)(2,1)S(1)}, u32[]{:S(2)}, u32[]{:S(2)}) collective-permute-start(bf16[4096,128]{1,0:T(8,128)(2,1)S(1)} %constant_dynamic-update-slice_fusion.8.refs_4_), channel_id=1, source_target_pairs={{0,4},{4,0},{8,12},{12,8},{16,20},{20,16},{24,28},{28,24},{1,5},{5... | collective-permute-start | bytes 3145736 | tf_op jit(solution)/shard_map/ppermute | solution.py:380
  383.7 26.7 %collective-permute-start.30 = (bf16[1024,128]{1,0:T(8,128)(2,1)}, bf16[1024,128]{1,0:T(8,128)(2,1)S(1)}, u32[]{:S(2)}, u32[]{:S(2)}) collective-permute-start(bf16[1024,128]{1,0:T(8,128)(2,1)} %product.7.refs_6_), channel_id=1, source_target_pairs={{0,24},{4,28},{8,16},{12,20},{16,8},{20,12},{24,0},{28,4},{1,25},{... | collective-permute-start | bytes 786440 | tf_op jit(solution)/shard_map/ppermute | solution.py:380
  385.3 26.6 %collective-permute-start.29 = (bf16[1024,128]{1,0:T(8,128)(2,1)}, bf16[1024,128]{1,0:T(8,128)(2,1)S(1)}, u32[]{:S(2)}, u32[]{:S(2)}) collective-permute-start(bf16[1024,128]{1,0:T(8,128)(2,1)} %product.7.refs_6_), channel_id=1, source_target_pairs={{0,16},{4,20},{8,24},{12,28},{16,0},{20,4},{24,8},{28,12},{1,17},{... | collective-permute-start | bytes 786440 | tf_op jit(solution)/shard_map/ppermute | solution.py:380
  394.5 18.1 %collective-permute-start.28 = (bf16[1024,128]{1,0:T(8,128)(2,1)}, bf16[1024,128]{1,0:T(8,128)(2,1)S(1)}, u32[]{:S(2)}, u32[]{:S(2)}) collective-permute-start(bf16[1024,128]{1,0:T(8,128)(2,1)} %product.7.refs_6_), channel_id=1, source_target_pairs={{0,8},{4,12},{8,0},{12,4},{16,24},{20,28},{24,16},{28,20},{1,9},{5... | collective-permute-start | bytes 786440 | tf_op jit(solution)/shard_map/ppermute | solution.py:380
  395.3 13.7 %copy-start.1 = (bf16[4096,256]{1,0:T(8,128)(2,1)}, bf16[4096,256]{1,0:T(8,128)(2,1)S(1)}, u32[]{:S(2)}) copy-start(bf16[4096,256]{1,0:T(8,128)(2,1)S(1)} %pad_maximum_fusion.refs_4_) | copy-start | bytes 6291460
  395.3 17.2 %copy-start.5 = (bf16[1024,128]{1,0:T(8,128)(2,1)S(1)}, bf16[1024,128]{1,0:T(8,128)(2,1)}, u32[]{:S(2)}) copy-start(bf16[1024,128]{1,0:T(8,128)(2,1)} %product.7.refs_6_) | copy-start | bytes 786436
  395.4 29.4 %collective-permute-start.27 = (bf16[4096,256]{1,0:T(8,128)(2,1)S(1)}, bf16[4096,256]{1,0:T(8,128)(2,1)}, u32[]{:S(2)}, u32[]{:S(2)}) collective-permute-start(bf16[4096,256]{1,0:T(8,128)(2,1)S(1)} %pad_maximum_fusion.refs_4_), channel_id=1, source_target_pairs={{0,4},{4,0},{8,12},{12,8},{16,20},{20,16},{24,28},{28,24},{1,5},{5... | collective-permute-start | bytes 6291464 | tf_op jit(solution)/shard_map/ppermute | solution.py:380
  395.4 1.0 copy-start.14
  409.0 15.5 %copy-start.6 = (bf16[1024,128]{1,0:T(8,128)(2,1)S(1)}, bf16[1024,128]{1,0:T(8,128)(2,1)}, u32[]{:S(2)}) copy-start(bf16[1024,128]{1,0:T(8,128)(2,1)} %product.8.refs_7_) | copy-start | bytes 786436
  409.0 10.3 %collective-permute-start.34 = (bf16[1024,128]{1,0:T(8,128)(2,1)}, bf16[1024,128]{1,0:T(8,128)(2,1)S(1)}, u32[]{:S(2)}, u32[]{:S(2)}) collective-permute-start(bf16[1024,128]{1,0:T(8,128)(2,1)} %product.8.refs_7_), channel_id=1, source_target_pairs={{0,24},{4,28},{8,16},{12,20},{16,8},{20,12},{24,0},{28,4},{1,25},{... | collective-permute-start | bytes 786440 | tf_op jit(solution)/shard_map/ppermute | solution.py:380
  410.5 14.0 %collective-permute-start.33 = (bf16[1024,128]{1,0:T(8,128)(2,1)}, bf16[1024,128]{1,0:T(8,128)(2,1)S(1)}, u32[]{:S(2)}, u32[]{:S(2)}) collective-permute-start(bf16[1024,128]{1,0:T(8,128)(2,1)} %product.8.refs_7_), channel_id=1, source_target_pairs={{0,16},{4,20},{8,24},{12,28},{16,0},{20,4},{24,8},{28,12},{1,17},{... | collective-permute-start | bytes 786440 | tf_op jit(solution)/shard_map/ppermute | solution.py:380
  411.9 12.6 %collective-permute-start.32 = (bf16[1024,128]{1,0:T(8,128)(2,1)}, bf16[1024,128]{1,0:T(8,128)(2,1)S(1)}, u32[]{:S(2)}, u32[]{:S(2)}) collective-permute-start(bf16[1024,128]{1,0:T(8,128)(2,1)} %product.8.refs_7_), channel_id=1, source_target_pairs={{0,8},{4,12},{8,0},{12,4},{16,24},{20,28},{24,16},{28,20},{1,9},{5... | collective-permute-start | bytes 786440 | tf_op jit(solution)/shard_map/ppermute | solution.py:380
  412.6 12.1 %copy-start.7 = (bf16[4096,128]{1,0:T(8,128)(2,1)}, bf16[4096,128]{1,0:T(8,128)(2,1)S(1)}, u32[]{:S(2)}) copy-start(bf16[4096,128]{1,0:T(8,128)(2,1)S(1)} %pad_maximum_fusion.2.refs_4_) | copy-start | bytes 3145732
  412.7 25.5 %collective-permute-start.31 = (bf16[4096,128]{1,0:T(8,128)(2,1)S(1)}, bf16[4096,128]{1,0:T(8,128)(2,1)S(1)}, u32[]{:S(2)}, u32[]{:S(2)}) collective-permute-start(bf16[4096,128]{1,0:T(8,128)(2,1)S(1)} %pad_maximum_fusion.2.refs_4_), channel_id=1, source_target_pairs={{0,4},{4,0},{8,12},{12,8},{16,20},{20,16},{24,28},{28,24},{1,5},{5... | collective-permute-start | bytes 3145736 | tf_op jit(solution)/shard_map/ppermute | solution.py:380
  424.6 13.6 %copy-start.8 = (bf16[4096,128]{1,0:T(8,128)(2,1)}, bf16[4096,128]{1,0:T(8,128)(2,1)S(1)}, u32[]{:S(2)}) copy-start(bf16[4096,128]{1,0:T(8,128)(2,1)S(1)} %pad_maximum_fusion.3.refs_4_) | copy-start | bytes 3145732
  424.6 27.0 %collective-permute-start.35 = (bf16[4096,128]{1,0:T(8,128)(2,1)S(1)}, bf16[4096,128]{1,0:T(8,128)(2,1)}, u32[]{:S(2)}, u32[]{:S(2)}) collective-permute-start(bf16[4096,128]{1,0:T(8,128)(2,1)S(1)} %pad_maximum_fusion.3.refs_4_), channel_id=1, source_target_pairs={{0,4},{4,0},{8,12},{12,8},{16,20},{20,16},{24,28},{28,24},{1,5},{5... | collective-permute-start | bytes 3145736 | tf_op jit(solution)/shard_map/ppermute | solution.py:380
  438.2 1.0 copy-start.15
  451.6 12.6 %copy-start.4 = (bf16[1024,256]{1,0:T(8,128)(2,1)S(1)}, bf16[1024,256]{1,0:T(8,128)(2,1)}, u32[]{:S(2)}) copy-start(bf16[1024,256]{1,0:T(8,128)(2,1)} %product.9.refs_7_) | copy-start | bytes 1572868
  451.6 12.6 %copy-start.11 = (bf16[1024,128]{1,0:T(8,128)(2,1)S(1)}, bf16[1024,128]{1,0:T(8,128)(2,1)}, u32[]{:S(2)}) copy-start(bf16[1024,128]{1,0:T(8,128)(2,1)} %product.10.refs_7_) | copy-start | bytes 786436
Sparse Core Ops, SparseCore 0:
  36.7 66.2 reduce-scatter.4
  105.3 60.2 reduce-scatter.6
  220.2 46.5 reduce-scatter.10
  275.0 46.6 reduce-scatter.8

commit v4 on v3

--- a/solution.py
+++ b/solution.py
@@ -24,8 +24,8 @@
     return pltpu.CompilerParams(vmem_limit_bytes=VMEM_BYTES)
 
 
-def brief():
-    return pl.CostEstimate(flops=1, bytes_accessed=1, transcendentals=0)
+def declared(flops=0):
+    return pl.CostEstimate(flops=flops, bytes_accessed=1, transcendentals=0)
 
 
 def whole_block(*shape):
@@ -40,10 +40,10 @@
     return jnp.dot(left, right, preferred_element_type=jnp.float32)
 
 
-def front_kernel(start, stop, n_col, flat, n_after, meta_ref, tiles_ref, front_ref, *refs):
-    out_ref, stack, held, acc, places, groups_of, state, tile_sems, sems = refs[n_after:]
-    span = stop - start
-    groups = n_col * span
+def front_kernel(subs, flats, n_col, n_after, meta_ref, tiles_ref, front_ref, *refs):
+    outs = refs[n_after : n_after + len(subs)]
+    stack, held, acc, places, groups_of, state, tile_sems, sems = refs[n_after + len(subs) :]
+    groups = n_col * len(subs)
     block, streams = held.shape[1], sems.shape[1]
     lines = block // streams
     step = pl.program_id(0)
@@ -64,7 +64,13 @@
         )
 
     def chosen(t):
-        return (meta_ref[2, t] >= start) & (meta_ref[2, t] < stop)
+        return functools.reduce(jnp.logical_or, [meta_ref[2, t] == sub for sub in subs])
+
+    def group_of(t):
+        order = 0
+        for p in range(1, len(subs)):
+            order = jnp.where(meta_ref[2, t] == subs[p], p, order)
+        return order * n_col + meta_ref[1, t]
 
     def clear(item, place):
         places[item, place] = 0
@@ -85,7 +91,7 @@
         def place_tile(t):
             @pl.when(chosen(t))
             def _():
-                g = meta_ref[1, t] * span + meta_ref[2, t] - start
+                g = group_of(t)
                 at = state[g]
 
                 @pl.when(lax.rem(at, STACK) == 0)
@@ -142,33 +148,35 @@
             acc[groups_of[s * STACK + i]] += products[i]
 
     for g in range(groups):
-        dest, sub = g // span, g % span
-        if flat:
-            out_ref[:, g * TILE : (g + 1) * TILE] = acc[g].astype(out_ref.dtype)
+        out, dest = outs[g // n_col], g % n_col
+        if flats[g // n_col]:
+            out[:, dest * TILE : (dest + 1) * TILE] = acc[g].astype(out.dtype)
         else:
-            out_ref[dest, :, sub * TILE : (sub + 1) * TILE] = acc[g].astype(out_ref.dtype)
-
-
-def front_products(front, tiles, meta, start, stop, n_col, flat, after=()):
+            out[dest] = acc[g].astype(out.dtype)
+
+
+def front_products(front, tiles, meta, subs, flats, n_col, after=()):
     rows, depth = front.shape
-    span = stop - start
-    width = span * TILE
-    groups = n_col * span
+    groups = n_col * len(subs)
     block = largest_tile(rows, 512)
     streams = 8 if block % 128 == 0 else 1
     count = tiles.shape[0]
     items = (-(-count // STACK) + groups + STACK) // STACK * STACK
-    if flat:
-        shape, spec = (rows, n_col * width), pl.BlockSpec((block, n_col * width), lambda i, m: (i, 0))
-    else:
-        shape, spec = (n_col, rows, width), pl.BlockSpec((n_col, block, width), lambda i, m: (0, i, 0))
+    shapes, specs = [], []
+    for flat in flats:
+        if flat:
+            shapes.append((rows, n_col * TILE))
+            specs.append(pl.BlockSpec((block, n_col * TILE), lambda i, m: (i, 0)))
+        else:
+            shapes.append((n_col, rows, TILE))
+            specs.append(pl.BlockSpec((n_col, block, TILE), lambda i, m: (0, i, 0)))
     return pl.pallas_call(
-        functools.partial(front_kernel, start, stop, n_col, flat, len(after)),
+        functools.partial(front_kernel, subs, flats, n_col, len(after)),
         grid_spec=pltpu.PrefetchScalarGridSpec(
             num_scalar_prefetch=1,
             grid=(rows // block,),
             in_specs=[in_place()] * (2 + len(after)),
-            out_specs=spec,
+            out_specs=specs,
             scratch_shapes=[
                 pltpu.VMEM((items, STACK * TILE, TILE), front.dtype),
                 pltpu.VMEM((2, block, depth), front.dtype),
@@ -180,9 +188,9 @@
                 pltpu.SemaphoreType.DMA((2, streams)),
             ],
         ),
-        out_shape=jax.ShapeDtypeStruct(shape, front.dtype),
+        out_shape=[jax.ShapeDtypeStruct(shape, front.dtype) for shape in shapes],
         compiler_params=kernel_params(),
-        cost_estimate=brief(),
+        cost_estimate=declared(),
         name="front_products",
     )(meta, tiles, front, *after)
 
@@ -202,7 +210,7 @@
         outs[k % 2][at : at + cap, :] = dot32(picks, solved).astype(outs[0].dtype)
 
 
-def pack_rows(index, solved, n_row, cap, after=()):
+def pack_rows(index, solved, n_row, cap, after=(), share=0):
     depth = solved[0].shape[0]
     width = sum(part.shape[1] for part in solved)
     return pl.pallas_call(
@@ -212,7 +220,7 @@
         + [in_place()] * len(after),
         out_shape=[jax.ShapeDtypeStruct((n_row // 2 * cap, width), solved[0].dtype)] * 2,
         compiler_params=kernel_params(),
-        cost_estimate=brief(),
+        cost_estimate=declared(share * n_row * cap * depth * width),
         name="pack_rows",
     )(index, *solved, *after)
 
@@ -255,61 +263,61 @@
         out_shape=[jax.ShapeDtypeStruct((count, width), bem.dtype)] * 2,
         scratch_shapes=[pltpu.VMEM((routed, width), bem.dtype)],
         compiler_params=kernel_params(),
-        cost_estimate=brief(),
+        cost_estimate=declared(4 * 2 * count * routed * width),
         name="assemble",
     )(index, bem, *pieces, *after)
 
 
-def subtract_kernel(bem_ref, terms_ref, *refs):
-    for half, out in enumerate(refs[-2:]):
-        total = terms_ref[0, half].astype(jnp.float32)
-        for term in range(1, terms_ref.shape[0]):
-            total = total + terms_ref[term, half].astype(jnp.float32)
-        taken = total.astype(out.dtype).astype(jnp.float32)
-        out[...] = (bem_ref[half].astype(jnp.float32) - taken).astype(out.dtype)
-
-
-def subtract(bem, terms, start, after=()):
-    count, width = bem.shape[1], terms.shape[1]
+def subtract_kernel(bem_ref, schur_ref, *refs):
+    taken = schur_ref[...].astype(jnp.float32)
+    refs[-1][...] = (bem_ref[...].astype(jnp.float32) - taken).astype(refs[-1].dtype)
+
+
+def subtract(bem, schur, first, start, after=()):
+    halves, count, width = schur.shape
     place = start * TILE // width
     return pl.pallas_call(
         subtract_kernel,
         grid=(1,),
-        in_specs=[pl.BlockSpec((2, count, width), lambda i: (0, 0, place))]
-        + [whole_block(1, 2, count, width)]
+        in_specs=[
+            pl.BlockSpec((halves, count, width), lambda i: (first, 0, place)),
+            whole_block(halves, count, width),
+        ]
         + [in_place()] * len(after),
-        out_specs=[whole_block(count, width)] * 2,
-        out_shape=[jax.ShapeDtypeStruct((count, width), bem.dtype)] * 2,
+        out_specs=whole_block(halves, count, width),
+        out_shape=jax.ShapeDtypeStruct((halves, count, width), bem.dtype),
         compiler_params=kernel_params(),
-        cost_estimate=brief(),
+        cost_estimate=declared(),
         name="subtract",
-    )(bem, terms.reshape(1, 2, count, width), *after)
-
-
-def unpack_kernel(n_pieces, n_col, index_ref, *refs):
-    out, joined = refs[-2:]
+    )(bem, schur, *after)
+
+
+def unpack_kernel(n_pieces, n_col, parts, index_ref, *refs):
+    outs, joined = refs[-1 - parts : -1], refs[-1]
     join_pieces(refs[:n_pieces], joined)
-    _, count, width = out.shape
+    _, count, width = outs[0].shape
     step = largest_tile(count, 512)
-    for i in range(0, count, step):
-        taken = dot32(one_hot(index_ref[i : i + step, :], joined.shape[0], joined.dtype), joined[...])
-        for d in range(n_col):
-            out[d, i : i + step, :] = taken[:, d * width : (d + 1) * width].astype(out.dtype)
-
-
-def unpack(index, pieces, n_col, after=()):
+    for p, out in enumerate(outs):
+        for i in range(0, count, step):
+            want = index_ref[p * count + i : p * count + i + step, :]
+            taken = dot32(one_hot(want, joined.shape[0], joined.dtype), joined[...])
+            for d in range(n_col):
+                out[d, i : i + step, :] = taken[:, d * width : (d + 1) * width].astype(out.dtype)
+
+
+def unpack(index, pieces, n_col, parts, after=(), share=0):
     wide = pieces[0].shape[1]
     routed = sum(piece.shape[0] for piece in pieces)
-    count, width = index.shape[0], wide // n_col
+    count, width = index.shape[0] // parts, wide // n_col
     return pl.pallas_call(
-        functools.partial(unpack_kernel, len(pieces), n_col),
+        functools.partial(unpack_kernel, len(pieces), n_col, parts),
         in_specs=[whole_block(*index.shape)]
         + [whole_block(*piece.shape) for piece in pieces]
         + [in_place()] * len(after),
-        out_shape=jax.ShapeDtypeStruct((n_col, count, width), pieces[0].dtype),
+        out_shape=[jax.ShapeDtypeStruct((n_col, count, width), pieces[0].dtype)] * parts,
         scratch_shapes=[pltpu.VMEM((routed, wide), pieces[0].dtype)],
         compiler_params=kernel_params(),
-        cost_estimate=brief(),
+        cost_estimate=declared(share * parts * count * routed * wide),
         name="unpack",
     )(index, *pieces, *after)
 
@@ -371,7 +379,7 @@
         ),
         out_shape=jax.ShapeDtypeStruct((rows, width), near.dtype),
         compiler_params=kernel_params(),
-        cost_estimate=brief(),
+        cost_estimate=declared(6 * rows * depth * max(width, 256)),
         name="product",
     )(order, *[matrix] * streams, near, far, *bases, *after)
 
@@ -383,11 +391,12 @@
 def route(packed, n_row):
     near, far = packed[0], exchange(packed[1], 1, n_row)
     cap = near.shape[0] * 2 // n_row
-    pieces = [near[:cap], far[:cap]]
+    sent = []
     for i in range(1, n_row // 2):
         both = [near[i * cap : (i + 1) * cap], far[i * cap : (i + 1) * cap]]
-        pieces.append(exchange(jnp.concatenate(both, axis=0), 2 * i, n_row))
-    return pieces
+        sent.append(jnp.concatenate(both, axis=0))
+    pieces = [exchange(both, 2 * i, n_row) for i, both in enumerate(sent, 1)]
+    return [near[:cap], far[:cap]] + pieces, tuple(sent)
 
 
 def gather_rows(block, n_row):
@@ -442,57 +451,52 @@
         [jnp.arange(0, n_row, 2, dtype=jnp.int32), jnp.arange(1, n_row, 2, dtype=jnp.int32)]
     )
     half = per_dest // 2
-
-    def front_of(start, flat, after):
-        return front_products(
-            front_inverse, coupling_tiles, meta, start, start + 1, n_col, flat, after
-        )
+    assert per_dest == 2 * half
 
     def summed(parts):
         return lax.psum_scatter(parts, "col", scatter_dimension=0)
 
-    solved, after = [], ()
-    for start in range(half):
-        parts = front_of(start, False, after)
-        after = (parts,)
+    solved, uppers, lowers = [], [], []
+
+    def unpack_next(after, share):
+        upper, lower = unpack(lands, pieces, n_col, 2, after, share)
+        uppers.append(summed(upper).reshape(1, count, TILE))
+        lowers.append(lower)
+        return upper
+
+    sent = ()
+    for sub in range(half):
+        parts, flat = front_products(
+            front_inverse, coupling_tiles, meta, (sub, half + sub), (False, True), n_col, sent
+        )
         solved.append(summed(parts))
-
-    wanted, lands = route_tables(surface_map, rows, n_row, cap, slots)
-    routed = []
-    for start in range(half, per_dest):
-        parts = front_of(start, True, after)
-        packed = pack_rows(wanted, [parts], n_row, slots)
-        after = (packed[0],)
-        routed.append(route(packed, n_row))
-    schur = []
-    for pieces in routed:
-        parts = unpack(lands, pieces, n_col, after)
-        schur.append(summed(parts))
-        if len(schur) == 1:
-            packed = pack_rows(wanted, solved, n_row, slots, (parts,))
-            after = (packed[0],)
-
-    def blocks_of(g):
-        after = (last,)
-        if g == 0:
-            return assemble(lands, bem_entries, route(packed, n_row), 0, after)
-        return subtract(bem_entries, schur[g - 1], half + g - 1, after)
-
-    sequence = list(range(1 + per_dest - half))
-    last = parts
-    lowers, gathered = {}, {}
-    for g in sequence:
-        last, lowers[g] = blocks_of(g)
-        gathered[g] = gather_rows(last, n_row)
-    pivots, belows = {}, {}
-    for g in sequence:
-        last = pivots[g] = product(pivot_inverse, order, *gathered[g], after=(last,))
-        gathered[g] = gather_rows(last, n_row)
-    for g in sequence:
-        last = belows[g] = product(slab_below, order, *gathered[g], lowers[g], (last,))
-    return jnp.stack(
-        [jnp.concatenate([part[g] for g in sorted(part)], axis=1) for part in (pivots, belows)]
-    )
+        if sub == 0:
+            wanted, lands = route_tables(surface_map, rows, n_row, cap, slots)
+            after = ()
+        else:
+            after = (unpack_next((flat,), 0),)
+        packed = pack_rows(wanted, [flat], n_row, slots, after, 4 if sub else 0)
+        pieces, sent = route(packed, n_row)
+    packed = pack_rows(wanted, solved, n_row, slots, (packed[0],), 4)
+    upper = unpack_next((packed[0],), 4)
+    lowers = [summed(low).reshape(1, count, TILE) for low in lowers]
+
+    last, base = assemble(lands, bem_entries, route(packed, n_row)[0], 0, (upper,))
+    gathered = [gather_rows(last, n_row)]
+    for at, schur in enumerate(uppers):
+        last = subtract(bem_entries, schur, 0, half + at, (last,))[0]
+        gathered.append(gather_rows(last, n_row))
+    pivots, belows = [], []
+    for near, far in gathered:
+        last = product(pivot_inverse, order, near, far, after=(last,))
+        pivots.append(last)
+    gathered = [gather_rows(pivot, n_row) for pivot in pivots]
+    for g, (near, far) in enumerate(gathered):
+        if g > 0:
+            base = subtract(bem_entries, lowers[g - 1], 1, half + g - 1, (last,))[0]
+        last = product(slab_below, order, near, far, base, (last,))
+        belows.append(last)
+    return jnp.stack([jnp.concatenate(parts, axis=1) for parts in (pivots, belows)])
 
 
 def solution(mesh):

time: 481 us -> 476 us (0.990)
  Pallas kernels: 268 us -> 239 us
  waiting for transfers between devices: 107 us -> 129 us
    pallas_call x8, Pallas kernels: 149 us -> 120 us  [the longest x2 92.9 us: front_products(): pl.pallas_call(functools.partial(front_kernel, subs, flats, n_col, len(af...]
    ppermute x36, waiting for transfers between devices: 106 us -> 129 us  [exchange(): return lax.ppermute(value, axis, [(i, i ^ distance) for i in range(n)])]
    unnamed x66 -> x58, local copies, waits for them, and re-layouts: 12.2 us -> 7.37 us
  transfers between devices with their start and end apart: 40 -> 42, of which waited for: 13 -> 19; matrix products, arithmetic and copies ran while one was open for 7% -> 7% of each run, Pallas kernels for 48% -> 39%
where the time goes in v4:
time: 476 us; the launch traced here: 468 us
  Pallas kernels  239 us (50%)
  waiting for transfers between devices  129 us (27%)
  starting transfers between devices  35.3 us (7%)
  other arithmetic  22.5 us (5%)
  local copies, waits for them, and re-layouts  16.6 us (3%)
  between operations  14.3 us (3%)
  blocking collectives  10.7 us (2%)
    ppermute x36, waiting for transfers between devices, exchange(): return lax.ppermute(value, axis, [(i, i ^ distance) for i in range(n)])  129 us
    pallas_call x2, Pallas kernels, front_products(): pl.pallas_call(functools.partial(front_kernel, subs, flats, n_col, len(af...  92.9 us
    pallas_call x6, Pallas kernels, product(): pl.pallas_call(functools.partial(product_kernel, streams, bool(bases)), g...  77.2 us
    pallas_call x3, Pallas kernels, pack_rows(): pl.pallas_call(functools.partial(pack_kernel, n_row, len(solved)), in_spe...  35.6 us
    ppermute x36, starting transfers between devices, exchange(): return lax.ppermute(value, axis, [(i, i ^ distance) for i in range(n)])  35.1 us
    pallas_call x2, Pallas kernels, unpack(): pl.pallas_call(functools.partial(unpack_kernel, len(pieces), n_col, parts...  19.8 us
    all_gather x1, blocking collectives, route_tables(): every = lax.all_gather(mine, 'row')  10.7 us
  transfers between devices with their start and end apart: 42, of which 19 were waited for; matrix products, arithmetic and copies ran while one was open for 7% of the time, Pallas kernels for 39%

profile of v4, /device:TPU:0, one launch (start us, length us, event | category | flops | bytes accessed | tf_op | source)
XLA Modules:
  0.0 467.7 jit_solution(9788261753989298171)
XLA Ops:
  8.5 46.4 %front_products.2 = (bf16[4,3072,128]{2,1,0:T(8,128)(2,1)}, bf16[3072,512]{1,0:T(8,128)(2,1)}) custom-call(s32[3,192]{1,0:T(4,128)} %pad_add_fusion.meta_ref, bf16[192,128,128]{2,1,0:T(8,128)(2,1)} %tiles_ref.3, bf16[3072,6144]{1,0:T(8,128)(2,1)} %front_ref.3), custom_call_target="tpu_custom_call" | custom-call | bytes 1 | tf_op jit(solution)/shard_map/front_products/pallas_call | solution.py:173
  55.6 10.7 %all-gather = s32[8,1,2048]{2,1,0:T(1,128)S(1)} all-gather(s32[1,1,2048]{2,1,0:T(1,128)S(1)} %reshape.212), channel_id=1, replica_groups=mesh['row'=8,'col'=4] {'row'}, dimensions={0}, use_global_device_ids=true | all-gather | bytes 73728 | tf_op jit(solution)/shard_map/all_gather | solution.py:411
  67.0 2.4 reduce-window.16
  70.1 6.2 %select_reduce_fusion = s32[8,384]{1,0:T(8,128)S(1)} fusion(s32[8,2048]{1,0:T(8,128)S(1)} %subtract_add_fusion, s32[8,2048]{1,0:T(8,128)S(1)} %bitcast.61, pred[8,2048]{1,0:T(8,128)(4,1)S(1)} %get-tuple-element.38), kind=kLoop, calls=%fused_computation.1 | loop fusion | flops 25162752 | bytes 159744 | tf_op jit(solution)/shard_map/reduce_sum | solution.py:418
  76.3 1.7 copy.41
  78.0 13.9 %pack_rows.3 = (bf16[1536,512]{1,0:T(8,128)(2,1)}, bf16[1536,512]{1,0:T(8,128)(2,1)}) custom-call(s32[3072,1]{1,0:T(8,128)} %bitcast.45, bf16[3072,512]{1,0:T(8,128)(2,1)} %get-tuple-element.22.refs_0_), custom_call_target="tpu_custom_call" | custom-call | bytes 1 | tf_op jit(solution)/shard_map/pack_rows/pallas_call | solution.py:216
  92.3 2.2 fusion.9
  99.2 46.5 %front_products.3 = (bf16[4,3072,128]{2,1,0:T(8,128)(2,1)}, bf16[3072,512]{1,0:T(8,128)(2,1)}) custom-call(s32[3,192]{1,0:T(4,128)} %pad_add_fusion.meta_ref, bf16[192,128,128]{2,1,0:T(8,128)(2,1)} %tiles_ref.3, bf16[3072,6144]{1,0:T(8,128)(2,1)} %front_ref.3, bf16[768,512]{1,0:T(8,128)(2,1)} %pad_maximum_fusion.6.refs_0_, ...), custom_call_target="tpu_custom_call" | custom-call | bytes 1 | tf_op jit(solution)/shard_map/front_products/pallas_call | solution.py:173
  146.0 1.6 collective-permute-start.1
  148.1 1.5 collective-permute-start.3
  149.6 2.3 reduce-window.14
  153.7 1.2 fusion.3.index_ref
  154.9 11.8 %collective-permute-done.1.refs_2_ = bf16[768,512]{1,0:T(8,128)(2,1)} collective-permute-done((bf16[768,512]{1,0:T(8,128)(2,1)}, bf16[768,512]{1,0:T(8,128)(2,1)}, u32[]{:S(2)}, u32[]{:S(2)}) %collective-permute-start.1) | collective-permute-done | bytes 786464 | tf_op jit(solution)/shard_map/ppermute | solution.py:388
  166.7 17.5 %collective-permute-done.2.refs_3_ = bf16[768,512]{1,0:T(8,128)(2,1)} collective-permute-done((bf16[768,512]{1,0:T(8,128)(2,1)}, bf16[768,512]{1,0:T(8,128)(2,1)}, u32[]{:S(2)}, u32[]{:S(2)}) %collective-permute-start.2) | collective-permute-done | bytes 786464 | tf_op jit(solution)/shard_map/ppermute | solution.py:388
  184.3 9.9 %unpack.2 = (bf16[4,1024,128]{2,1,0:T(8,128)(2,1)}, bf16[4,1024,128]{2,1,0:T(8,128)(2,1)}) custom-call(s32[2048,1]{1,0:T(8,128)} %fusion.3.index_ref, bf16[384,512]{1,0:T(8,128)(2,1)} %get-tuple-element.51.refs_0_, bf16[384,512]{1,0:T(8,128)(2,1)} %get-tuple-element.47.refs_1_, bf16[768,512]{1,0:T(8,128)(2,1)} %collective-permute-done.1.refs_2_, ...), custom_call_target="tpu_custom_call" | custom-call | bytes 1 | tf_op jit(solution)/shard_map/unpack/pallas_call | solution.py:312
  194.1 13.7 %pack_rows.4 = (bf16[1536,512]{1,0:T(8,128)(2,1)}, bf16[1536,512]{1,0:T(8,128)(2,1)}) custom-call(s32[3072,1]{1,0:T(8,128)} %bitcast.46, bf16[3072,512]{1,0:T(8,128)(2,1)} %get-tuple-element.26.refs_5_.refs_0_, bf16[4,1024,128]{2,1,0:T(8,128)(2,1)} %get-tuple-element.27.refs_1_), custom_call_target="tpu_custom_call" | custom-call | flops 19327352832 | bytes 1 | tf_op jit(solution)/shard_map/pack_rows/pallas_call | solution.py:216
  207.8 2.2 fusion.6
  210.1 1.3 collective-permute-done.8
  213.0 1.6 collective-permute-start.10
  214.6 1.5 collective-permute-start.11
  216.1 8.0 %pack_rows.5 = (bf16[1536,256]{1,0:T(8,128)(2,1)}, bf16[1536,256]{1,0:T(8,128)(2,1)}) custom-call(s32[3072,1]{1,0:T(8,128)} %bitcast.47, bf16[3072,128]{1,0:T(8,128)(2,1)} %bitcast.71, bf16[3072,128]{1,0:T(8,128)(2,1)} %bitcast.72, bf16[1536,512]{1,0:T(8,128)(2,1)} %get-tuple-element.28.refs_2_), custom_call_target="tpu_custom_call" | custom-call | flops 9663676416 | bytes 1 | tf_op jit(solution)/shard_map/pack_rows/pallas_call | solution.py:216
  224.1 8.6 %collective-permute-done.9.refs_2_ = bf16[768,512]{1,0:T(8,128)(2,1)S(1)} collective-permute-done((bf16[768,512]{1,0:T(8,128)(2,1)S(1)}, bf16[768,512]{1,0:T(8,128)(2,1)S(1)}, u32[]{:S(2)}, u32[]{:S(2)}) %collective-permute-start.9) | collective-permute-done | bytes 786464 | tf_op jit(solution)/shard_map/ppermute | solution.py:388
  232.8 16.5 %collective-permute-done.10.refs_3_ = bf16[768,512]{1,0:T(8,128)(2,1)} collective-permute-done((bf16[768,512]{1,0:T(8,128)(2,1)S(1)}, bf16[768,512]{1,0:T(8,128)(2,1)}, u32[]{:S(2)}, u32[]{:S(2)}) %collective-permute-start.10) | collective-permute-done | bytes 786464 | tf_op jit(solution)/shard_map/ppermute | solution.py:388
  249.3 10.0 %unpack.3 = (bf16[4,1024,128]{2,1,0:T(8,128)(2,1)}, bf16[4,1024,128]{2,1,0:T(8,128)(2,1)}) custom-call(s32[2048,1]{1,0:T(8,128)} %fusion.3.index_ref, bf16[384,512]{1,0:T(8,128)(2,1)} %get-tuple-element.42.refs_0_, bf16[384,512]{1,0:T(8,128)(2,1)} %get-tuple-element.46.refs_1_, bf16[768,512]{1,0:T(8,128)(2,1)} %copy-done.18, ...), custom_call_target="tpu_custom_call" | custom-call | flops 12884901888 | bytes 1 | tf_op jit(solution)/shard_map/unpack/pallas_call | solution.py:312
  260.2 1.5 collective-permute-done.4
  262.5 1.6 collective-permute-start.5
  264.6 1.6 collective-permute-start.7
  266.3 8.2 %collective-permute-done.5.refs_2_ = bf16[768,256]{1,0:T(8,128)(2,1)S(1)} collective-permute-done((bf16[768,256]{1,0:T(8,128)(2,1)S(1)}, bf16[768,256]{1,0:T(8,128)(2,1)S(1)}, u32[]{:S(2)}, u32[]{:S(2)}) %collective-permute-start.5) | collective-permute-done | bytes 393248 | tf_op jit(solution)/shard_map/ppermute | solution.py:388
  274.5 8.9 %collective-permute-done.6.refs_3_ = bf16[768,256]{1,0:T(8,128)(2,1)S(1)} collective-permute-done((bf16[768,256]{1,0:T(8,128)(2,1)S(1)}, bf16[768,256]{1,0:T(8,128)(2,1)S(1)}, u32[]{:S(2)}, u32[]{:S(2)}) %collective-permute-start.6) | collective-permute-done | bytes 393248 | tf_op jit(solution)/shard_map/ppermute | solution.py:388
  284.4 6.2 %assemble.1 = (bf16[1024,256]{1,0:T(8,128)(2,1)}, bf16[1024,256]{1,0:T(8,128)(2,1)}) custom-call(s32[2048,1]{1,0:T(8,128)} %fusion.3.index_ref, bf16[2,1024,512]{2,1,0:T(8,128)(2,1)} %bem_ref.9, bf16[384,256]{1,0:T(8,128)(2,1)} %get-tuple-element.58.refs_0_, bf16[384,256]{1,0:T(8,128)(2,1)} %get-tuple-element.62.refs_1_, bf16[768,256]{1,0:T(8,128)(2,1)} %copy-done.20, ...), custom_call_target="tpu_custom_call" | custom-call | flops 6442450944 | bytes 1 | tf_op jit(solution)/shard_map/assemble/pallas_call | solution.py:253
  291.2 1.5 collective-permute-start.13
  292.7 1.5 collective-permute-start.14
  295.2 10.5 %collective-permute-done.12 = bf16[1024,256]{1,0:T(8,128)(2,1)S(1)} collective-permute-done((bf16[1024,256]{1,0:T(8,128)(2,1)}, bf16[1024,256]{1,0:T(8,128)(2,1)S(1)}, u32[]{:S(2)}, u32[]{:S(2)}) %collective-permute-start.12) | collective-permute-done | bytes 524320 | tf_op jit(solution)/shard_map/ppermute | solution.py:388
  305.7 9.3 %collective-permute-done.13 = bf16[1024,256]{1,0:T(8,128)(2,1)S(1)} collective-permute-done((bf16[1024,256]{1,0:T(8,128)(2,1)}, bf16[1024,256]{1,0:T(8,128)(2,1)S(1)}, u32[]{:S(2)}, u32[]{:S(2)}) %collective-permute-start.13) | collective-permute-done | bytes 524320 | tf_op jit(solution)/shard_map/ppermute | solution.py:388
  315.3 2.2 subtract.4
  317.5 1.5 collective-permute-start.18
  319.0 1.5 collective-permute-start.17
  321.7 1.8 subtract.5
  323.5 1.5 collective-permute-start.22
  325.0 2.8 collective-permute-done.18
  327.8 1.5 collective-permute-start.21
  329.3 4.2 collective-permute-done.17
  333.5 1.5 collective-permute-start.20
  335.2 3.9 collective-permute-done.22
  339.1 4.6 collective-permute-done.21
  344.0 13.7 %product.6.refs_6_ = bf16[1024,256]{1,0:T(8,128)(2,1)} custom-call(s32[8]{0:T(128)} %add_xor_fusion.order_ref, bf16[1024,8192]{1,0:T(8,128)(2,1)} %refs_3_.8, bf16[1024,8192]{1,0:T(8,128)(2,1)} %refs_3_.8, bf16[1024,8192]{1,0:T(8,128)(2,1)} %refs_3_.8, bf16[1024,8192]{1,0:T(8,128)(2,1)} %refs_3_.8, bf16[4096,256]{1,0:T(8,128)(2,1)} %copy-done.10, ...), custom_call_target="tpu_custom_call" | custom-call | flops 12884901888 | bytes 1 | tf_op jit(solution)/shard_map/product/pallas_call | solution.py:368
  357.7 1.5 collective-permute-start.26
  359.3 1.5 collective-permute-start.25
  362.3 12.6 %product.7.refs_6_ = bf16[1024,128]{1,0:T(8,128)(2,1)} custom-call(s32[8]{0:T(128)} %add_xor_fusion.order_ref, bf16[1024,8192]{1,0:T(8,128)(2,1)} %refs_3_.8, bf16[1024,8192]{1,0:T(8,128)(2,1)} %refs_3_.8, bf16[1024,8192]{1,0:T(8,128)(2,1)} %refs_3_.8, bf16[1024,8192]{1,0:T(8,128)(2,1)} %refs_3_.8, bf16[4096,128]{1,0:T(8,128)(2,1)} %copy-done.7, ...), custom_call_target="tpu_custom_call" | custom-call | flops 12884901888 | bytes 1 | tf_op jit(solution)/shard_map/product/pallas_call | solution.py:368
  374.8 1.5 collective-permute-start.30
  376.3 1.5 collective-permute-start.29
  377.8 7.2 %collective-permute-done.25 = bf16[1024,256]{1,0:T(8,128)(2,1)S(1)} collective-permute-done((bf16[1024,256]{1,0:T(8,128)(2,1)}, bf16[1024,256]{1,0:T(8,128)(2,1)S(1)}, u32[]{:S(2)}, u32[]{:S(2)}) %collective-permute-start.25) | collective-permute-done | bytes 524320 | tf_op jit(solution)/shard_map/ppermute | solution.py:388
  385.0 1.5 collective-permute-start.28
  387.7 12.6 %product.8.refs_7_ = bf16[1024,128]{1,0:T(8,128)(2,1)} custom-call(s32[8]{0:T(128)} %add_xor_fusion.order_ref, bf16[1024,8192]{1,0:T(8,128)(2,1)} %refs_3_.8, bf16[1024,8192]{1,0:T(8,128)(2,1)} %refs_3_.8, bf16[1024,8192]{1,0:T(8,128)(2,1)} %refs_3_.8, bf16[1024,8192]{1,0:T(8,128)(2,1)} %refs_3_.8, bf16[4096,128]{1,0:T(8,128)(2,1)} %copy-done.6, ...), custom_call_target="tpu_custom_call" | custom-call | flops 12884901888 | bytes 1 | tf_op jit(solution)/shard_map/product/pallas_call | solution.py:368
  400.3 1.5 collective-permute-start.34
  403.5 1.5 collective-permute-start.32
  405.2 5.4 %collective-permute-done.34 = bf16[1024,128]{1,0:T(8,128)(2,1)S(1)} collective-permute-done((bf16[1024,128]{1,0:T(8,128)(2,1)}, bf16[1024,128]{1,0:T(8,128)(2,1)S(1)}, u32[]{:S(2)}, u32[]{:S(2)}) %collective-permute-start.34) | collective-permute-done | bytes 262176 | tf_op jit(solution)/shard_map/ppermute | solution.py:388
  410.6 5.2 %collective-permute-done.33 = bf16[1024,128]{1,0:T(8,128)(2,1)S(1)} collective-permute-done((bf16[1024,128]{1,0:T(8,128)(2,1)S(1)}, bf16[1024,128]{1,0:T(8,128)(2,1)S(1)}, u32[]{:S(2)}, u32[]{:S(2)}) %collective-permute-start.33) | collective-permute-done | bytes 262176 | tf_op jit(solution)/shard_map/ppermute | solution.py:388
  416.0 13.3 %product.9.refs_0_.refs_7_ = bf16[1024,256]{1,0:T(8,128)(2,1)} custom-call(s32[8]{0:T(128)} %add_xor_fusion.order_ref, bf16[1024,8192]{1,0:T(8,128)(2,1)} %refs_3_.11, bf16[1024,8192]{1,0:T(8,128)(2,1)} %refs_3_.11, bf16[1024,8192]{1,0:T(8,128)(2,1)} %refs_3_.11, bf16[1024,8192]{1,0:T(8,128)(2,1)} %refs_3_.11, bf16[4096,256]{1,0:T(8,128)(2,1)} %copy-done.2, ...), custom_call_target="tpu_custom_call" | custom-call | flops 12884901888 | bytes 1 | tf_op jit(solution)/shard_map/product/pallas_call | solution.py:368
  429.4 1.8 subtract.6
  431.2 12.5 %product.10.refs_0_.refs_7_ = bf16[1024,128]{1,0:T(8,128)(2,1)} custom-call(s32[8]{0:T(128)} %add_xor_fusion.order_ref, bf16[1024,8192]{1,0:T(8,128)(2,1)} %refs_3_.11, bf16[1024,8192]{1,0:T(8,128)(2,1)} %refs_3_.11, bf16[1024,8192]{1,0:T(8,128)(2,1)} %refs_3_.11, bf16[1024,8192]{1,0:T(8,128)(2,1)} %refs_3_.11, bf16[4096,128]{1,0:T(8,128)(2,1)} %copy-done.8, ...), custom_call_target="tpu_custom_call" | custom-call | flops 12884901888 | bytes 1 | tf_op jit(solution)/shard_map/product/pallas_call | solution.py:368
  443.6 1.8 subtract.7
  445.5 12.6 %product.11 = bf16[1024,128]{1,0:T(8,128)(2,1)} custom-call(s32[8]{0:T(128)} %add_xor_fusion.order_ref, bf16[1024,8192]{1,0:T(8,128)(2,1)} %refs_3_.11, bf16[1024,8192]{1,0:T(8,128)(2,1)} %refs_3_.11, bf16[1024,8192]{1,0:T(8,128)(2,1)} %refs_3_.11, bf16[1024,8192]{1,0:T(8,128)(2,1)} %refs_3_.11, bf16[4096,128]{1,0:T(8,128)(2,1)} %copy-done.9, ...), custom_call_target="tpu_custom_call" | custom-call | flops 12884901888 | bytes 1 | tf_op jit(solution)/shard_map/product/pallas_call | solution.py:368
  459.1 1.5 pad_maximum_fusion.1
  (158 shorter events, 25.7 us)
Async XLA Ops:
  6.5 209.6 %reduce-scatter.7.cloned.1.call-start = ((), (), s32[]{:S(2)}) async-start(), calls=%async_computation.6 | async-start | bytes 3932160 | tf_op jit(solution)/shard_map/reduce_scatter | solution.py:457
  55.0 161.2 %reduce-scatter.9.cloned.1.call-start = ((), (), s32[]{:S(2)}) async-start(), calls=%async_computation.7 | async-start | bytes 3932160 | tf_op jit(solution)/shard_map/reduce_scatter | solution.py:457
  91.9 3.6 collective-permute-start
  145.8 2.3 copy-start.11
  145.8 169.5 %reduce-scatter.13.cloned.1.call-start = ((), (), s32[]{:S(2)}) async-start(), calls=%async_computation.9 | async-start | bytes 1310720 | tf_op jit(solution)/shard_map/reduce_scatter | solution.py:457
  146.0 20.8 %collective-permute-start.1 = (bf16[768,512]{1,0:T(8,128)(2,1)}, bf16[768,512]{1,0:T(8,128)(2,1)}, u32[]{:S(2)}, u32[]{:S(2)}) collective-permute-start(bf16[768,512]{1,0:T(8,128)(2,1)} %pad_maximum_fusion.6.refs_0_), channel_id=1, source_target_pairs={{0,8},{4,12},{8,0},{12,4},{16,24},{20,28},{24,16},{28,20},{1,9},{5... | collective-permute-start | bytes 2359304 | tf_op jit(solution)/shard_map/ppermute | solution.py:388
  147.6 36.7 %collective-permute-start.2 = (bf16[768,512]{1,0:T(8,128)(2,1)}, bf16[768,512]{1,0:T(8,128)(2,1)}, u32[]{:S(2)}, u32[]{:S(2)}) collective-permute-start(bf16[768,512]{1,0:T(8,128)(2,1)} %pad_maximum_fusion.7.refs_1_), channel_id=1, source_target_pairs={{0,16},{4,20},{8,24},{12,28},{16,0},{20,4},{24,8},{28,12},{1,17},{... | collective-permute-start | bytes 2359304 | tf_op jit(solution)/shard_map/ppermute | solution.py:388
  148.1 36.2 %collective-permute-start.3 = (bf16[768,512]{1,0:T(8,128)(2,1)S(1)}, bf16[768,512]{1,0:T(8,128)(2,1)}, u32[]{:S(2)}, u32[]{:S(2)}) collective-permute-start(bf16[768,512]{1,0:T(8,128)(2,1)S(1)} %copy-done.11), channel_id=1, source_target_pairs={{0,24},{4,28},{8,16},{12,20},{16,8},{20,12},{24,0},{28,4},{1,25},{... | collective-permute-start | bytes 2359304 | tf_op jit(solution)/shard_map/ppermute | solution.py:388
  207.8 3.6 collective-permute-start.8
  207.8 113.9 %reduce-scatter.11.cloned.1.call-start = ((), (), s32[]{:S(2)}) async-start(), calls=%async_computation.8 | async-start | bytes 1310720 | tf_op jit(solution)/shard_map/reduce_scatter | solution.py:457
  212.3 20.4 %collective-permute-start.9 = (bf16[768,512]{1,0:T(8,128)(2,1)S(1)}, bf16[768,512]{1,0:T(8,128)(2,1)S(1)}, u32[]{:S(2)}, u32[]{:S(2)}) collective-permute-start(bf16[768,512]{1,0:T(8,128)(2,1)S(1)} %pad_maximum_fusion.9), channel_id=1, source_target_pairs={{0,8},{4,12},{8,0},{12,4},{16,24},{20,28},{24,16},{28,20},{1,9},{5... | collective-permute-start | bytes 2359304 | tf_op jit(solution)/shard_map/ppermute | solution.py:388
  213.0 36.3 %collective-permute-start.10 = (bf16[768,512]{1,0:T(8,128)(2,1)S(1)}, bf16[768,512]{1,0:T(8,128)(2,1)}, u32[]{:S(2)}, u32[]{:S(2)}) collective-permute-start(bf16[768,512]{1,0:T(8,128)(2,1)S(1)} %pad_maximum_fusion.10), channel_id=1, source_target_pairs={{0,16},{4,20},{8,24},{12,28},{16,0},{20,4},{24,8},{28,12},{1,17},{... | collective-permute-start | bytes 2359304 | tf_op jit(solution)/shard_map/ppermute | solution.py:388
  214.6 34.7 %collective-permute-start.11 = (bf16[768,512]{1,0:T(8,128)(2,1)S(1)}, bf16[768,512]{1,0:T(8,128)(2,1)}, u32[]{:S(2)}, u32[]{:S(2)}) collective-permute-start(bf16[768,512]{1,0:T(8,128)(2,1)S(1)} %pad_maximum_fusion.11), channel_id=1, source_target_pairs={{0,24},{4,28},{8,16},{12,20},{16,8},{20,12},{24,0},{28,4},{1,25},{... | collective-permute-start | bytes 2359304 | tf_op jit(solution)/shard_map/ppermute | solution.py:388
  232.8 16.5 %copy-start.18 = (bf16[768,512]{1,0:T(8,128)(2,1)}, bf16[768,512]{1,0:T(8,128)(2,1)S(1)}, u32[]{:S(2)}) copy-start(bf16[768,512]{1,0:T(8,128)(2,1)S(1)} %collective-permute-done.9.refs_2_) | copy-start | bytes 2359300
  249.3 10.1 %copy-start.19 = (bf16[1536,256]{1,0:T(8,128)(2,1)S(1)}, bf16[1536,256]{1,0:T(8,128)(2,1)}, u32[]{:S(2)}) copy-start(bf16[1536,256]{1,0:T(8,128)(2,1)} %get-tuple-element.30) | copy-start | bytes 2359300
  249.3 10.1 %copy-start.16 = (bf16[1536,256]{1,0:T(8,128)(2,1)S(1)}, bf16[1536,256]{1,0:T(8,128)(2,1)}, u32[]{:S(2)}) copy-start(bf16[1536,256]{1,0:T(8,128)(2,1)} %get-tuple-element.29.refs_5_) | copy-start | bytes 2359300
  259.3 170.1 %reduce-scatter.15.cloned.1.call-start = ((), (), s32[]{:S(2)}) async-start(), calls=%async_computation.10 | async-start | bytes 1310720 | tf_op jit(solution)/shard_map/reduce_scatter | solution.py:457
  259.4 2.4 collective-permute-start.4
  262.5 12.0 %collective-permute-start.5 = (bf16[768,256]{1,0:T(8,128)(2,1)S(1)}, bf16[768,256]{1,0:T(8,128)(2,1)S(1)}, u32[]{:S(2)}, u32[]{:S(2)}) collective-permute-start(bf16[768,256]{1,0:T(8,128)(2,1)S(1)} %pad_maximum_fusion.12), channel_id=1, source_target_pairs={{0,8},{4,12},{8,0},{12,4},{16,24},{20,28},{24,16},{28,20},{1,9},{5... | collective-permute-start | bytes 1179656 | tf_op jit(solution)/shard_map/ppermute | solution.py:388
  264.1 19.4 %collective-permute-start.6 = (bf16[768,256]{1,0:T(8,128)(2,1)S(1)}, bf16[768,256]{1,0:T(8,128)(2,1)S(1)}, u32[]{:S(2)}, u32[]{:S(2)}) collective-permute-start(bf16[768,256]{1,0:T(8,128)(2,1)S(1)} %pad_maximum_fusion.13), channel_id=1, source_target_pairs={{0,16},{4,20},{8,24},{12,28},{16,0},{20,4},{24,8},{28,12},{1,17},{... | collective-permute-start | bytes 1179656 | tf_op jit(solution)/shard_map/ppermute | solution.py:388
  264.6 18.8 %collective-permute-start.7 = (bf16[768,256]{1,0:T(8,128)(2,1)S(1)}, bf16[768,256]{1,0:T(8,128)(2,1)S(1)}, u32[]{:S(2)}, u32[]{:S(2)}) collective-permute-start(bf16[768,256]{1,0:T(8,128)(2,1)S(1)} %pad_maximum_fusion.14), channel_id=1, source_target_pairs={{0,24},{4,28},{8,16},{12,20},{16,8},{20,12},{24,0},{28,4},{1,25},{... | collective-permute-start | bytes 1179656 | tf_op jit(solution)/shard_map/ppermute | solution.py:388
  266.3 177.4 %reduce-scatter.17.cloned.1.call-start = ((), (), s32[]{:S(2)}) async-start(), calls=%async_computation.11 | async-start | bytes 1310720 | tf_op jit(solution)/shard_map/reduce_scatter | solution.py:457
  274.5 9.0 %copy-start.20 = (bf16[768,256]{1,0:T(8,128)(2,1)}, bf16[768,256]{1,0:T(8,128)(2,1)S(1)}, u32[]{:S(2)}) copy-start(bf16[768,256]{1,0:T(8,128)(2,1)S(1)} %collective-permute-done.5.refs_2_) | copy-start | bytes 1179652
  283.4 0.8 copy-start.21
  283.5 0.9 copy-start.22
  290.6 15.1 %collective-permute-start.12 = (bf16[1024,256]{1,0:T(8,128)(2,1)}, bf16[1024,256]{1,0:T(8,128)(2,1)S(1)}, u32[]{:S(2)}, u32[]{:S(2)}) collective-permute-start(bf16[1024,256]{1,0:T(8,128)(2,1)} %get-tuple-element.33.refs_0_), channel_id=1, source_target_pairs={{0,8},{4,12},{8,0},{12,4},{16,24},{20,28},{24,16},{28,20},{1,9},{5... | collective-permute-start | bytes 1572872 | tf_op jit(solution)/shard_map/ppermute | solution.py:388
  291.2 23.9 %collective-permute-start.13 = (bf16[1024,256]{1,0:T(8,128)(2,1)}, bf16[1024,256]{1,0:T(8,128)(2,1)S(1)}, u32[]{:S(2)}, u32[]{:S(2)}) collective-permute-start(bf16[1024,256]{1,0:T(8,128)(2,1)} %get-tuple-element.33.refs_0_), channel_id=1, source_target_pairs={{0,16},{4,20},{8,24},{12,28},{16,0},{20,4},{24,8},{28,12},{1,17},{... | collective-permute-start | bytes 1572872 | tf_op jit(solution)/shard_map/ppermute | solution.py:388
  292.7 22.4 %collective-permute-start.14 = (bf16[1024,256]{1,0:T(8,128)(2,1)}, bf16[1024,256]{1,0:T(8,128)(2,1)S(1)}, u32[]{:S(2)}, u32[]{:S(2)}) collective-permute-start(bf16[1024,256]{1,0:T(8,128)(2,1)} %get-tuple-element.33.refs_0_), channel_id=1, source_target_pairs={{0,24},{4,28},{8,16},{12,20},{16,8},{20,12},{24,0},{28,4},{1,25},{... | collective-permute-start | bytes 1572872 | tf_op jit(solution)/shard_map/ppermute | solution.py:388
  315.1 6.5 %copy-start.10 = (bf16[4096,256]{1,0:T(8,128)(2,1)}, bf16[4096,256]{1,0:T(8,128)(2,1)S(1)}, u32[]{:S(2)}) copy-start(bf16[4096,256]{1,0:T(8,128)(2,1)S(1)} %constant_dynamic-update-slice_fusion.refs_4_) | copy-start | bytes 6291460
  315.2 28.9 %collective-permute-start.15 = (bf16[4096,256]{1,0:T(8,128)(2,1)S(1)}, bf16[4096,256]{1,0:T(8,128)(2,1)}, u32[]{:S(2)}, u32[]{:S(2)}) collective-permute-start(bf16[4096,256]{1,0:T(8,128)(2,1)S(1)} %constant_dynamic-update-slice_fusion.refs_4_), channel_id=1, source_target_pairs={{0,4},{4,0},{8,12},{12,8},{16,20},{20,16},{24,28},{28,24},{1,5},{5... | collective-permute-start | bytes 6291464 | tf_op jit(solution)/shard_map/ppermute | solution.py:388
  317.5 17.5 %copy-start.13 = (bf16[1,1024,128]{2,1,0:T(8,128)(2,1)S(1)}, bf16[1,1024,128]{2,1,0:T(8,128)(2,1)}, u32[]{:S(2)}) copy-start(bf16[1,1024,128]{2,1,0:T(8,128)(2,1)} %subtract.4) | copy-start | bytes 786436
  317.5 10.3 %collective-permute-start.18 = (bf16[1024,128]{1,0:T(8,128)(2,1)}, bf16[1024,128]{1,0:T(8,128)(2,1)S(1)}, u32[]{:S(2)}, u32[]{:S(2)}) collective-permute-start(bf16[1024,128]{1,0:T(8,128)(2,1)} %bitcast.54), channel_id=1, source_target_pairs={{0,24},{4,28},{8,16},{12,20},{16,8},{20,12},{24,0},{28,4},{1,25},{... | collective-permute-start | bytes 786440 | tf_op jit(solution)/shard_map/ppermute | solution.py:388
  319.0 14.5 %collective-permute-start.17 = (bf16[1024,128]{1,0:T(8,128)(2,1)}, bf16[1024,128]{1,0:T(8,128)(2,1)S(1)}, u32[]{:S(2)}, u32[]{:S(2)}) collective-permute-start(bf16[1024,128]{1,0:T(8,128)(2,1)} %bitcast.55), channel_id=1, source_target_pairs={{0,16},{4,20},{8,24},{12,28},{16,0},{20,4},{24,8},{28,12},{1,17},{... | collective-permute-start | bytes 786440 | tf_op jit(solution)/shard_map/ppermute | solution.py:388
  320.5 14.5 %collective-permute-start.16 = (bf16[1024,128]{1,0:T(8,128)(2,1)}, bf16[1024,128]{1,0:T(8,128)(2,1)S(1)}, u32[]{:S(2)}, u32[]{:S(2)}) collective-permute-start(bf16[1024,128]{1,0:T(8,128)(2,1)} %bitcast.56), channel_id=1, source_target_pairs={{0,8},{4,12},{8,0},{12,4},{16,24},{20,28},{24,16},{28,20},{1,9},{5... | collective-permute-start | bytes 786440 | tf_op jit(solution)/shard_map/ppermute | solution.py:388
  323.5 20.4 %copy-start.12 = (bf16[1,1024,128]{2,1,0:T(8,128)(2,1)S(1)}, bf16[1,1024,128]{2,1,0:T(8,128)(2,1)}, u32[]{:S(2)}) copy-start(bf16[1,1024,128]{2,1,0:T(8,128)(2,1)} %subtract.5) | copy-start | bytes 786436
  323.5 15.6 %collective-permute-start.22 = (bf16[1024,128]{1,0:T(8,128)(2,1)}, bf16[1024,128]{1,0:T(8,128)(2,1)S(1)}, u32[]{:S(2)}, u32[]{:S(2)}) collective-permute-start(bf16[1024,128]{1,0:T(8,128)(2,1)} %bitcast.49), channel_id=1, source_target_pairs={{0,24},{4,28},{8,16},{12,20},{16,8},{20,12},{24,0},{28,4},{1,25},{... | collective-permute-start | bytes 786440 | tf_op jit(solution)/shard_map/ppermute | solution.py:388
  327.8 15.9 %collective-permute-start.21 = (bf16[1024,128]{1,0:T(8,128)(2,1)}, bf16[1024,128]{1,0:T(8,128)(2,1)S(1)}, u32[]{:S(2)}, u32[]{:S(2)}) collective-permute-start(bf16[1024,128]{1,0:T(8,128)(2,1)} %bitcast.50), channel_id=1, source_target_pairs={{0,16},{4,20},{8,24},{12,28},{16,0},{20,4},{24,8},{28,12},{1,17},{... | collective-permute-start | bytes 786440 | tf_op jit(solution)/shard_map/ppermute | solution.py:388
  333.5 10.4 %collective-permute-start.20 = (bf16[1024,128]{1,0:T(8,128)(2,1)}, bf16[1024,128]{1,0:T(8,128)(2,1)S(1)}, u32[]{:S(2)}, u32[]{:S(2)}) collective-permute-start(bf16[1024,128]{1,0:T(8,128)(2,1)} %bitcast.51), channel_id=1, source_target_pairs={{0,8},{4,12},{8,0},{12,4},{16,24},{20,28},{24,16},{28,20},{1,9},{5... | collective-permute-start | bytes 786440 | tf_op jit(solution)/shard_map/ppermute | solution.py:388
  335.1 22.6 %copy-start.7 = (bf16[4096,128]{1,0:T(8,128)(2,1)}, bf16[4096,128]{1,0:T(8,128)(2,1)S(1)}, u32[]{:S(2)}) copy-start(bf16[4096,128]{1,0:T(8,128)(2,1)S(1)} %pad_maximum_fusion.2.refs_4_) | copy-start | bytes 3145732
  335.1 26.2 %collective-permute-start.19 = (bf16[4096,128]{1,0:T(8,128)(2,1)S(1)}, bf16[4096,128]{1,0:T(8,128)(2,1)S(1)}, u32[]{:S(2)}, u32[]{:S(2)}) collective-permute-start(bf16[4096,128]{1,0:T(8,128)(2,1)S(1)} %pad_maximum_fusion.2.refs_4_), channel_id=1, source_target_pairs={{0,4},{4,0},{8,12},{12,8},{16,20},{20,16},{24,28},{28,24},{1,5},{5... | collective-permute-start | bytes 3145736 | tf_op jit(solution)/shard_map/ppermute | solution.py:388
  343.9 13.8 %copy-start.6 = (bf16[4096,128]{1,0:T(8,128)(2,1)}, bf16[4096,128]{1,0:T(8,128)(2,1)S(1)}, u32[]{:S(2)}) copy-start(bf16[4096,128]{1,0:T(8,128)(2,1)S(1)} %pad_maximum_fusion.3.refs_4_) | copy-start | bytes 3145732
  343.9 42.8 %collective-permute-start.23 = (bf16[4096,128]{1,0:T(8,128)(2,1)S(1)}, bf16[4096,128]{1,0:T(8,128)(2,1)S(1)}, u32[]{:S(2)}, u32[]{:S(2)}) collective-permute-start(bf16[4096,128]{1,0:T(8,128)(2,1)S(1)} %pad_maximum_fusion.3.refs_4_), channel_id=1, source_target_pairs={{0,4},{4,0},{8,12},{12,8},{16,20},{20,16},{24,28},{28,24},{1,5},{5... | collective-permute-start | bytes 3145736 | tf_op jit(solution)/shard_map/ppermute | solution.py:388
  357.7 28.7 %copy-start.1 = (bf16[1024,256]{1,0:T(8,128)(2,1)S(1)}, bf16[1024,256]{1,0:T(8,128)(2,1)}, u32[]{:S(2)}) copy-start(bf16[1024,256]{1,0:T(8,128)(2,1)} %product.6.refs_6_) | copy-start | bytes 1572868
  357.7 18.6 %collective-permute-start.26 = (bf16[1024,256]{1,0:T(8,128)(2,1)}, bf16[1024,256]{1,0:T(8,128)(2,1)S(1)}, u32[]{:S(2)}, u32[]{:S(2)}) collective-permute-start(bf16[1024,256]{1,0:T(8,128)(2,1)} %product.6.refs_6_), channel_id=1, source_target_pairs={{0,24},{4,28},{8,16},{12,20},{16,8},{20,12},{24,0},{28,4},{1,25},{... | collective-permute-start | bytes 1572872 | tf_op jit(solution)/shard_map/ppermute | solution.py:388
  359.3 25.7 %collective-permute-start.25 = (bf16[1024,256]{1,0:T(8,128)(2,1)}, bf16[1024,256]{1,0:T(8,128)(2,1)S(1)}, u32[]{:S(2)}, u32[]{:S(2)}) collective-permute-start(bf16[1024,256]{1,0:T(8,128)(2,1)} %product.6.refs_6_), channel_id=1, source_target_pairs={{0,16},{4,20},{8,24},{12,28},{16,0},{20,4},{24,8},{28,12},{1,17},{... | collective-permute-start | bytes 1572872 | tf_op jit(solution)/shard_map/ppermute | solution.py:388
  360.8 25.7 %collective-permute-start.24 = (bf16[1024,256]{1,0:T(8,128)(2,1)}, bf16[1024,256]{1,0:T(8,128)(2,1)S(1)}, u32[]{:S(2)}, u32[]{:S(2)}) collective-permute-start(bf16[1024,256]{1,0:T(8,128)(2,1)} %product.6.refs_6_), channel_id=1, source_target_pairs={{0,8},{4,12},{8,0},{12,4},{16,24},{20,28},{24,16},{28,20},{1,9},{5... | collective-permute-start | bytes 1572872 | tf_op jit(solution)/shard_map/ppermute | solution.py:388
  361.3 1.0 copy-start.15
  374.8 28.1 %collective-permute-start.30 = (bf16[1024,128]{1,0:T(8,128)(2,1)}, bf16[1024,128]{1,0:T(8,128)(2,1)S(1)}, u32[]{:S(2)}, u32[]{:S(2)}) collective-permute-start(bf16[1024,128]{1,0:T(8,128)(2,1)} %product.7.refs_6_), channel_id=1, source_target_pairs={{0,24},{4,28},{8,16},{12,20},{16,8},{20,12},{24,0},{28,4},{1,25},{... | collective-permute-start | bytes 786440 | tf_op jit(solution)/shard_map/ppermute | solution.py:388
  376.3 27.2 %collective-permute-start.29 = (bf16[1024,128]{1,0:T(8,128)(2,1)}, bf16[1024,128]{1,0:T(8,128)(2,1)S(1)}, u32[]{:S(2)}, u32[]{:S(2)}) collective-permute-start(bf16[1024,128]{1,0:T(8,128)(2,1)} %product.7.refs_6_), channel_id=1, source_target_pairs={{0,16},{4,20},{8,24},{12,28},{16,0},{20,4},{24,8},{28,12},{1,17},{... | collective-permute-start | bytes 786440 | tf_op jit(solution)/shard_map/ppermute | solution.py:388
  385.0 20.1 %collective-permute-start.28 = (bf16[1024,128]{1,0:T(8,128)(2,1)}, bf16[1024,128]{1,0:T(8,128)(2,1)S(1)}, u32[]{:S(2)}, u32[]{:S(2)}) collective-permute-start(bf16[1024,128]{1,0:T(8,128)(2,1)} %product.7.refs_6_), channel_id=1, source_target_pairs={{0,8},{4,12},{8,0},{12,4},{16,24},{20,28},{24,16},{28,20},{1,9},{5... | collective-permute-start | bytes 786440 | tf_op jit(solution)/shard_map/ppermute | solution.py:388
  386.6 13.7 %copy-start.2 = (bf16[4096,256]{1,0:T(8,128)(2,1)}, bf16[4096,256]{1,0:T(8,128)(2,1)S(1)}, u32[]{:S(2)}) copy-start(bf16[4096,256]{1,0:T(8,128)(2,1)S(1)} %pad_maximum_fusion.refs_4_) | copy-start | bytes 6291460
  386.6 15.2 %copy-start.3 = (bf16[1024,128]{1,0:T(8,128)(2,1)S(1)}, bf16[1024,128]{1,0:T(8,128)(2,1)}, u32[]{:S(2)}) copy-start(bf16[1024,128]{1,0:T(8,128)(2,1)} %product.7.refs_6_) | copy-start | bytes 786436
  386.6 29.4 %collective-permute-start.27 = (bf16[4096,256]{1,0:T(8,128)(2,1)S(1)}, bf16[4096,256]{1,0:T(8,128)(2,1)}, u32[]{:S(2)}, u32[]{:S(2)}) collective-permute-start(bf16[4096,256]{1,0:T(8,128)(2,1)S(1)} %pad_maximum_fusion.refs_4_), channel_id=1, source_target_pairs={{0,4},{4,0},{8,12},{12,8},{16,20},{20,16},{24,28},{28,24},{1,5},{5... | collective-permute-start | bytes 6291464 | tf_op jit(solution)/shard_map/ppermute | solution.py:388
  386.7 1.0 copy-start.14
  400.3 2.6 copy-start.4
  400.3 10.3 %collective-permute-start.34 = (bf16[1024,128]{1,0:T(8,128)(2,1)}, bf16[1024,128]{1,0:T(8,128)(2,1)S(1)}, u32[]{:S(2)}, u32[]{:S(2)}) collective-permute-start(bf16[1024,128]{1,0:T(8,128)(2,1)} %product.8.refs_7_), channel_id=1, source_target_pairs={{0,24},{4,28},{8,16},{12,20},{16,8},{20,12},{24,0},{28,4},{1,25},{... | collective-permute-start | bytes 786440 | tf_op jit(solution)/shard_map/ppermute | solution.py:388
  402.9 12.9 %collective-permute-start.33 = (bf16[1024,128]{1,0:T(8,128)(2,1)S(1)}, bf16[1024,128]{1,0:T(8,128)(2,1)S(1)}, u32[]{:S(2)}, u32[]{:S(2)}) collective-permute-start(bf16[1024,128]{1,0:T(8,128)(2,1)S(1)} %copy-done.4), channel_id=1, source_target_pairs={{0,16},{4,20},{8,24},{12,28},{16,0},{20,4},{24,8},{28,12},{1,17},{... | collective-permute-start | bytes 786440 | tf_op jit(solution)/shard_map/ppermute | solution.py:388
  403.5 12.3 %collective-permute-start.32 = (bf16[1024,128]{1,0:T(8,128)(2,1)S(1)}, bf16[1024,128]{1,0:T(8,128)(2,1)S(1)}, u32[]{:S(2)}, u32[]{:S(2)}) collective-permute-start(bf16[1024,128]{1,0:T(8,128)(2,1)S(1)} %copy-done.4), channel_id=1, source_target_pairs={{0,8},{4,12},{8,0},{12,4},{16,24},{20,28},{24,16},{28,20},{1,9},{5... | collective-permute-start | bytes 786440 | tf_op jit(solution)/shard_map/ppermute | solution.py:388
  405.1 24.2 %copy-start.8 = (bf16[4096,128]{1,0:T(8,128)(2,1)}, bf16[4096,128]{1,0:T(8,128)(2,1)S(1)}, u32[]{:S(2)}) copy-start(bf16[4096,128]{1,0:T(8,128)(2,1)S(1)} %pad_maximum_fusion.4.refs_4_) | copy-start | bytes 3145732
  405.1 26.0 %collective-permute-start.31 = (bf16[4096,128]{1,0:T(8,128)(2,1)S(1)}, bf16[4096,128]{1,0:T(8,128)(2,1)}, u32[]{:S(2)}, u32[]{:S(2)}) collective-permute-start(bf16[4096,128]{1,0:T(8,128)(2,1)S(1)} %pad_maximum_fusion.4.refs_4_), channel_id=1, source_target_pairs={{0,4},{4,0},{8,12},{12,8},{16,20},{20,16},{24,28},{28,24},{1,5},{5... | collective-permute-start | bytes 3145736 | tf_op jit(solution)/shard_map/ppermute | solution.py:388
  415.9 13.5 %copy-start.9 = (bf16[4096,128]{1,0:T(8,128)(2,1)}, bf16[4096,128]{1,0:T(8,128)(2,1)S(1)}, u32[]{:S(2)}) copy-start(bf16[4096,128]{1,0:T(8,128)(2,1)S(1)} %pad_maximum_fusion.5.refs_4_) | copy-start | bytes 3145732
  415.9 29.5 %collective-permute-start.35 = (bf16[4096,128]{1,0:T(8,128)(2,1)S(1)}, bf16[4096,128]{1,0:T(8,128)(2,1)}, u32[]{:S(2)}, u32[]{:S(2)}) collective-permute-start(bf16[4096,128]{1,0:T(8,128)(2,1)S(1)} %pad_maximum_fusion.5.refs_4_), channel_id=1, source_target_pairs={{0,4},{4,0},{8,12},{12,8},{16,20},{20,16},{24,28},{28,24},{1,5},{5... | collective-permute-start | bytes 3145736 | tf_op jit(solution)/shard_map/ppermute | solution.py:388
  445.4 12.6 %copy-start = (bf16[1024,256]{1,0:T(8,128)(2,1)S(1)}, bf16[1024,256]{1,0:T(8,128)(2,1)}, u32[]{:S(2)}) copy-start(bf16[1024,256]{1,0:T(8,128)(2,1)} %product.9.refs_0_.refs_7_) | copy-start | bytes 1572868
  445.4 12.6 %copy-start.5 = (bf16[1024,128]{1,0:T(8,128)(2,1)S(1)}, bf16[1024,128]{1,0:T(8,128)(2,1)}, u32[]{:S(2)}) copy-start(bf16[1024,128]{1,0:T(8,128)(2,1)} %product.10.refs_0_.refs_7_) | copy-start | bytes 786436
  (1 other events, 0.7 us)
Sparse Core Ops, SparseCore 0:
  55.1 63.2 reduce-scatter.6
  145.9 64.3 reduce-scatter.8
  212.6 27.1 reduce-scatter.12
  259.4 31.2 reduce-scatter.10
  292.9 25.7 reduce-scatter.14
  321.7 31.2 reduce-scatter.16

commit v5 on v4

--- a/solution.py
+++ b/solution.py
@@ -138,14 +138,11 @@
 
     @pl.loop(0, (state[2 * groups] + STACK - 1) // STACK)
     def add(s):
-        products = []
         for i in range(STACK):
             item = s * STACK + i
             lefts = [pl.multiple_of(places[item, j] * TILE, TILE) for j in range(STACK)]
             rows = [held[slot, :, pl.ds(left, TILE)] for left in lefts]
-            products.append(dot32(jnp.concatenate(rows, axis=1), stack[item]))
-        for i in range(STACK):
-            acc[groups_of[s * STACK + i]] += products[i]
+            acc[groups_of[item]] += dot32(jnp.concatenate(rows, axis=1), stack[item])
 
     for g in range(groups):
         out, dest = outs[g // n_col], g % n_col
@@ -268,28 +265,50 @@
     )(index, bem, *pieces, *after)
 
 
-def subtract_kernel(bem_ref, schur_ref, *refs):
-    taken = schur_ref[...].astype(jnp.float32)
-    refs[-1][...] = (bem_ref[...].astype(jnp.float32) - taken).astype(refs[-1].dtype)
-
-
-def subtract(bem, schur, first, start, after=()):
-    halves, count, width = schur.shape
+def subtract_kernel(n_parts, bem_ref, *refs):
+    out = refs[-1]
+    for at, part in enumerate(refs[:n_parts]):
+        columns = slice(at * TILE, (at + 1) * TILE)
+        taken = part[...].astype(jnp.float32)
+        out[:, columns] = (bem_ref[0, :, columns].astype(jnp.float32) - taken).astype(out.dtype)
+
+
+def subtract(bem, parts, half, start, after=()):
+    count, width = bem.shape[1], len(parts) * TILE
     place = start * TILE // width
-    return pl.pallas_call(
-        subtract_kernel,
+
+    def rows_of(part):
+        at = half if part.shape[0] > count else 0
+        return pl.BlockSpec((count, TILE), lambda i: (at, 0))
+
+    return pl.pallas_call(
+        functools.partial(subtract_kernel, len(parts)),
         grid=(1,),
-        in_specs=[
-            pl.BlockSpec((halves, count, width), lambda i: (first, 0, place)),
-            whole_block(halves, count, width),
-        ]
+        in_specs=[pl.BlockSpec((1, count, width), lambda i: (half, 0, place))]
+        + [rows_of(part) for part in parts]
         + [in_place()] * len(after),
-        out_specs=whole_block(halves, count, width),
-        out_shape=jax.ShapeDtypeStruct((halves, count, width), bem.dtype),
+        out_specs=whole_block(count, width),
+        out_shape=jax.ShapeDtypeStruct((count, width), bem.dtype),
         compiler_params=kernel_params(),
         cost_estimate=declared(),
         name="subtract",
-    )(bem, schur, *after)
+    )(bem, *parts, *after)
+
+
+def join_kernel(n_parts, *refs):
+    join_pieces(refs[:n_parts], refs[-1])
+
+
+def join(parts, after=()):
+    depth, width = sum(part.shape[0] for part in parts), parts[0].shape[1]
+    return pl.pallas_call(
+        functools.partial(join_kernel, len(parts)),
+        in_specs=[whole_block(*part.shape) for part in parts] + [in_place()] * len(after),
+        out_shape=jax.ShapeDtypeStruct((depth, width), parts[0].dtype),
+        compiler_params=kernel_params(),
+        cost_estimate=declared(),
+        name="join",
+    )(*parts, *after)
 
 
 def unpack_kernel(n_pieces, n_col, parts, index_ref, *refs):
@@ -400,8 +419,10 @@
 
 
 def gather_rows(block, n_row):
-    near = [block] + [exchange(block, k, n_row) for k in range(2, n_row, 2)]
-    near = jnp.concatenate(near, axis=0)
+    return [block] + [exchange(block, k, n_row) for k in range(2, n_row, 2)]
+
+
+def both_cores(near, n_row):
     return near, exchange(near, 1, n_row)
 
 
@@ -456,46 +477,48 @@
     def summed(parts):
         return lax.psum_scatter(parts, "col", scatter_dimension=0)
 
-    solved, uppers, lowers = [], [], []
-
-    def unpack_next(after, share):
-        upper, lower = unpack(lands, pieces, n_col, 2, after, share)
-        uppers.append(summed(upper).reshape(1, count, TILE))
-        lowers.append(lower)
-        return upper
-
-    sent = ()
-    for sub in range(half):
-        parts, flat = front_products(
-            front_inverse, coupling_tiles, meta, (sub, half + sub), (False, True), n_col, sent
-        )
-        solved.append(summed(parts))
-        if sub == 0:
-            wanted, lands = route_tables(surface_map, rows, n_row, cap, slots)
-            after = ()
-        else:
-            after = (unpack_next((flat,), 0),)
-        packed = pack_rows(wanted, [flat], n_row, slots, after, 4 if sub else 0)
-        pieces, sent = route(packed, n_row)
-    packed = pack_rows(wanted, solved, n_row, slots, (packed[0],), 4)
-    upper = unpack_next((packed[0],), 4)
-    lowers = [summed(low).reshape(1, count, TILE) for low in lowers]
-
-    last, base = assemble(lands, bem_entries, route(packed, n_row)[0], 0, (upper,))
-    gathered = [gather_rows(last, n_row)]
-    for at, schur in enumerate(uppers):
-        last = subtract(bem_entries, schur, 0, half + at, (last,))[0]
-        gathered.append(gather_rows(last, n_row))
-    pivots, belows = [], []
-    for near, far in gathered:
-        last = product(pivot_inverse, order, near, far, after=(last,))
-        pivots.append(last)
-    gathered = [gather_rows(pivot, n_row) for pivot in pivots]
-    for g, (near, far) in enumerate(gathered):
-        if g > 0:
-            base = subtract(bem_entries, lowers[g - 1], 1, half + g - 1, (last,))[0]
-        last = product(slab_below, order, near, far, base, (last,))
-        belows.append(last)
+    parts = front_products(
+        front_inverse, coupling_tiles, meta, tuple(range(half)), (False,) * half, n_col
+    )
+    solved = [summed(part) for part in parts]
+    flats = front_products(
+        front_inverse, coupling_tiles, meta, tuple(range(half, per_dest)), (True,) * half, n_col,
+        (parts[0],),
+    )
+    wanted, lands = route_tables(surface_map, rows, n_row, cap, slots)
+    routed, after = [], ()
+    for flat in flats:
+        packed = pack_rows(wanted, [flat], n_row, slots, after)
+        pieces, after = route(packed, n_row)
+        routed.append(pieces)
+    after = (packed[0],)
+
+    uppers, lowers = [], []
+    for at, pieces in enumerate(routed):
+        cuts = unpack(lands, pieces, n_col, 1 if at + 1 < half else 2, after, 12)
+        uppers.append(summed(cuts[0]))
+        lowers.append(cuts[1:])
+        after = (cuts[0],)
+        if at == 0:
+            packed = pack_rows(wanted, solved, n_row, slots, after, 12)
+            after = (packed[0],)
+    lowers = [summed(low[0]) if low else both for low, both in zip(lowers, uppers)]
+
+    upper, lower = assemble(lands, bem_entries, route(packed, n_row)[0], 0, after)
+    first = gather_rows(upper, n_row)
+    upper = subtract(bem_entries, uppers, 0, half, (upper,))
+    second = gather_rows(upper, n_row)
+    near, far = both_cores(join(first, (upper,)), n_row)
+    pivots = [product(pivot_inverse, order, near, far, after=(upper,))]
+    first = gather_rows(pivots[0], n_row)
+    near, far = both_cores(join(second, (pivots[0],)), n_row)
+    pivots.append(product(pivot_inverse, order, near, far, after=(pivots[0],)))
+    second = gather_rows(pivots[1], n_row)
+    near, far = both_cores(join(first, (pivots[1],)), n_row)
+    below = subtract(bem_entries, lowers, 1, half, (pivots[1],))
+    belows = [product(slab_below, order, near, far, lower, (below,))]
+    near, far = both_cores(join(second, (belows[0],)), n_row)
+    belows.append(product(slab_below, order, near, far, below))
     return jnp.stack([jnp.concatenate(parts, axis=1) for parts in (pivots, belows)])
 
 

time: 476 us -> 426 us (0.89)
  waiting for transfers between devices: 129 us -> 99 us
  Pallas kernels: 239 us -> 225 us
  starting transfers between devices: 35.3 us -> 25.9 us
  local copies, waits for them, and re-layouts: 16.6 us -> 25.6 us
    ppermute x36 -> x28, waiting for transfers between devices: 129 us -> 96.9 us  [exchange(): return lax.ppermute(value, axis, [(i, i ^ distance) for i in range(n)])]
    pallas_call x6 -> x4, Pallas kernels: 77.2 us -> 53.5 us  [product(): pl.pallas_call(functools.partial(product_kernel, streams, bool(bases)), g...]
    ppermute x36 -> x28, starting transfers between devices: 35.1 us -> 25.5 us  [exchange(): return lax.ppermute(value, axis, [(i, i ^ distance) for i in range(n)])]
    pallas_call x4 -> x6, Pallas kernels: 7.62 us -> 16.1 us  [the longest x4 11.9 us: join(): pl.pallas_call(functools.partial(join_kernel, len(parts)), in_specs=[whol...]
    unnamed x58 -> x73, local copies, waits for them, and re-layouts: 7.37 us -> 15 us
  transfers between devices with their start and end apart: 42 -> 33, of which waited for: 19 -> 15; matrix products, arithmetic and copies ran while one was open for 7% -> 7% of each run, Pallas kernels for 39% -> 37%
where the time goes in v5:
time: 426 us; the launch traced here: 420 us
  Pallas kernels  225 us (53%)
  waiting for transfers between devices  99 us (23%)
  starting transfers between devices  25.9 us (6%)
  local copies, waits for them, and re-layouts  25.6 us (6%)
  other arithmetic  19.5 us (5%)
  between operations  13.8 us (3%)
  blocking collectives  10.7 us (3%)
    ppermute x28, waiting for transfers between devices, exchange(): return lax.ppermute(value, axis, [(i, i ^ distance) for i in range(n)])  96.9 us
    pallas_call x2, Pallas kernels, front_products(): pl.pallas_call(functools.partial(front_kernel, subs, flats, n_col, len(af...  93.2 us
    pallas_call x4, Pallas kernels, product(): pl.pallas_call(functools.partial(product_kernel, streams, bool(bases)), g...  53.5 us
    pallas_call x3, Pallas kernels, pack_rows(): pl.pallas_call(functools.partial(pack_kernel, n_row, len(solved)), in_spe...  36 us
    ppermute x28, starting transfers between devices, exchange(): return lax.ppermute(value, axis, [(i, i ^ distance) for i in range(n)])  25.5 us
    pallas_call x2, Pallas kernels, unpack(): pl.pallas_call(functools.partial(unpack_kernel, len(pieces), n_col, parts...  20.3 us
    unnamed x73, local copies, waits for them, and re-layouts  15 us
    pallas_call x4, Pallas kernels, join(): pl.pallas_call(functools.partial(join_kernel, len(parts)), in_specs=[whol...  11.9 us
  transfers between devices with their start and end apart: 33, of which 15 were waited for; matrix products, arithmetic and copies ran while one was open for 7% of the time, Pallas kernels for 37%

profile of v5, /device:TPU:0, one launch (start us, length us, event | category | flops | bytes accessed | tf_op | source)
XLA Modules:
  0.0 419.7 jit_solution(5108309650885043523)
XLA Ops:
  8.5 46.6 %front_products.2 = (bf16[4,3072,128]{2,1,0:T(8,128)(2,1)}, bf16[4,3072,128]{2,1,0:T(8,128)(2,1)}) custom-call(s32[3,192]{1,0:T(4,128)} %pad_add_fusion.meta_ref, bf16[192,128,128]{2,1,0:T(8,128)(2,1)} %tiles_ref.3, bf16[3072,6144]{1,0:T(8,128)(2,1)} %front_ref.3), custom_call_target="tpu_custom_call" | custom-call | bytes 1 | tf_op jit(solution)/shard_map/front_products/pallas_call | solution.py:170
  56.0 10.7 %all-gather = s32[8,1,2048]{2,1,0:T(1,128)S(1)} all-gather(s32[1,1,2048]{2,1,0:T(1,128)S(1)} %reshape.212), channel_id=1, replica_groups=mesh['row'=8,'col'=4] {'row'}, dimensions={0}, use_global_device_ids=true | all-gather | bytes 73728 | tf_op jit(solution)/shard_map/all_gather | solution.py:432
  67.3 46.6 %front_products.3 = (bf16[3072,512]{1,0:T(8,128)(2,1)}, bf16[3072,512]{1,0:T(8,128)(2,1)}) custom-call(s32[3,192]{1,0:T(4,128)} %pad_add_fusion.meta_ref, bf16[192,128,128]{2,1,0:T(8,128)(2,1)} %tiles_ref.3, bf16[3072,6144]{1,0:T(8,128)(2,1)} %front_ref.3, bf16[4,3072,128]{2,1,0:T(8,128)(2,1)} %get-tuple-element.19.refs_0_), custom_call_target="tpu_custom_call" | custom-call | bytes 1 | tf_op jit(solution)/shard_map/front_products/pallas_call | solution.py:170
  114.0 2.4 reduce-window.16
  117.0 6.2 %select_reduce_fusion = s32[8,384]{1,0:T(8,128)S(1)} fusion(s32[8,2048]{1,0:T(8,128)S(1)} %subtract_add_fusion, s32[8,2048]{1,0:T(8,128)S(1)} %bitcast.50, pred[8,2048]{1,0:T(8,128)(4,1)S(1)} %get-tuple-element.34), kind=kLoop, calls=%fused_computation.1 | loop fusion | flops 25162752 | bytes 159744 | tf_op jit(solution)/shard_map/reduce_sum | solution.py:439
  123.2 1.7 copy.41
  124.9 14.4 %pack_rows.3 = (bf16[1536,512]{1,0:T(8,128)(2,1)}, bf16[1536,512]{1,0:T(8,128)(2,1)}) custom-call(s32[3072,1]{1,0:T(8,128)} %bitcast.44, bf16[3072,512]{1,0:T(8,128)(2,1)} %get-tuple-element.21.refs_0_), custom_call_target="tpu_custom_call" | custom-call | bytes 1 | tf_op jit(solution)/shard_map/pack_rows/pallas_call | solution.py:213
  139.9 2.3 reduce-window.14
  143.9 2.2 fusion.8
  146.2 2.2 fusion.9
  148.5 1.5 collective-permute-start.1
  150.2 2.1 collective-permute-start.3
  152.3 1.2 fusion.3.index_ref
  153.5 13.4 %pack_rows.4 = (bf16[1536,512]{1,0:T(8,128)(2,1)}, bf16[1536,512]{1,0:T(8,128)(2,1)}) custom-call(s32[3072,1]{1,0:T(8,128)} %bitcast.45, bf16[3072,512]{1,0:T(8,128)(2,1)} %get-tuple-element.24.refs_0_, bf16[768,512]{1,0:T(8,128)(2,1)} %copy-done.6, bf16[768,512]{1,0:T(8,128)(2,1)} %copy-done.7, bf16[768,512]{1,0:T(8,128)(2,1)} %copy-done.8), custom_call_target="tpu_custom_call" | custom-call | bytes 1 | tf_op jit(solution)/shard_map/pack_rows/pallas_call | solution.py:213
  167.0 2.2 fusion.6
  169.2 17.0 %collective-permute-done.2.refs_3_ = bf16[768,512]{1,0:T(8,128)(2,1)S(1)} collective-permute-done((bf16[768,512]{1,0:T(8,128)(2,1)S(1)}, bf16[768,512]{1,0:T(8,128)(2,1)S(1)}, u32[]{:S(2)}, u32[]{:S(2)}) %collective-permute-start.2) | collective-permute-done | bytes 786464 | tf_op jit(solution)/shard_map/ppermute | solution.py:407
  186.2 0.9 copy-done.26
  187.4 10.4 %unpack.2.refs_2_ = bf16[4,2048,128]{2,1,0:T(8,128)(2,1)} custom-call(s32[2048,1]{1,0:T(8,128)} %fusion.3.index_ref, bf16[384,512]{1,0:T(8,128)(2,1)} %get-tuple-element.46.refs_0_, bf16[384,512]{1,0:T(8,128)(2,1)} %get-tuple-element.50.refs_1_, bf16[768,512]{1,0:T(8,128)(2,1)} %copy-done.25, bf16[768,512]{1,0:T(8,128)(2,1)} %copy-done.26, ...), custom_call_target="tpu_custom_call" | custom-call | flops 38654705664 | bytes 1 | tf_op jit(solution)/shard_map/unpack/pallas_call | solution.py:331
  199.6 1.4 collective-permute-start.10
  201.0 1.0 pad_maximum_fusion.6
  202.0 1.5 collective-permute-start.11
  203.5 8.1 %pack_rows.5 = (bf16[1536,256]{1,0:T(8,128)(2,1)}, bf16[1536,256]{1,0:T(8,128)(2,1)}) custom-call(s32[3072,1]{1,0:T(8,128)} %bitcast.46, bf16[3072,128]{1,0:T(8,128)(2,1)} %bitcast.63, bf16[3072,128]{1,0:T(8,128)(2,1)} %bitcast.62, bf16[4,2048,128]{2,1,0:T(8,128)(2,1)} %unpack.2.refs_2_), custom_call_target="tpu_custom_call" | custom-call | flops 28991029248 | bytes 1 | tf_op jit(solution)/shard_map/pack_rows/pallas_call | solution.py:213
  211.6 7.9 %collective-permute-done.9.refs_2_ = bf16[768,512]{1,0:T(8,128)(2,1)} collective-permute-done((bf16[768,512]{1,0:T(8,128)(2,1)S(1)}, bf16[768,512]{1,0:T(8,128)(2,1)}, u32[]{:S(2)}, u32[]{:S(2)}) %collective-permute-start.9) | collective-permute-done | bytes 786464 | tf_op jit(solution)/shard_map/ppermute | solution.py:407
  219.4 14.8 %collective-permute-done.10.refs_3_ = bf16[768,512]{1,0:T(8,128)(2,1)} collective-permute-done((bf16[768,512]{1,0:T(8,128)(2,1)S(1)}, bf16[768,512]{1,0:T(8,128)(2,1)}, u32[]{:S(2)}, u32[]{:S(2)}) %collective-permute-start.10) | collective-permute-done | bytes 786464 | tf_op jit(solution)/shard_map/ppermute | solution.py:407
  235.2 9.9 %unpack.3 = (bf16[4,1024,128]{2,1,0:T(8,128)(2,1)}, bf16[4,1024,128]{2,1,0:T(8,128)(2,1)}) custom-call(s32[2048,1]{1,0:T(8,128)} %fusion.3.index_ref, bf16[384,512]{1,0:T(8,128)(2,1)} %get-tuple-element.38.refs_0_, bf16[384,512]{1,0:T(8,128)(2,1)} %get-tuple-element.42.refs_1_, bf16[768,512]{1,0:T(8,128)(2,1)} %collective-permute-done.9.refs_2_, ...), custom_call_target="tpu_custom_call" | custom-call | flops 38654705664 | bytes 1 | tf_op jit(solution)/shard_map/unpack/pallas_call | solution.py:331
  246.9 1.5 collective-permute-start.5
  249.3 1.3 collective-permute-start.7
  250.6 8.4 %collective-permute-done.5.refs_2_ = bf16[768,256]{1,0:T(8,128)(2,1)S(1)} collective-permute-done((bf16[768,256]{1,0:T(8,128)(2,1)S(1)}, bf16[768,256]{1,0:T(8,128)(2,1)S(1)}, u32[]{:S(2)}, u32[]{:S(2)}) %collective-permute-start.5) | collective-permute-done | bytes 393248 | tf_op jit(solution)/shard_map/ppermute | solution.py:407
  259.0 5.9 %collective-permute-done.6.refs_3_ = bf16[768,256]{1,0:T(8,128)(2,1)S(1)} collective-permute-done((bf16[768,256]{1,0:T(8,128)(2,1)S(1)}, bf16[768,256]{1,0:T(8,128)(2,1)S(1)}, u32[]{:S(2)}, u32[]{:S(2)}) %collective-permute-start.6) | collective-permute-done | bytes 393248 | tf_op jit(solution)/shard_map/ppermute | solution.py:407
  265.8 6.2 %assemble.1 = (bf16[1024,256]{1,0:T(8,128)(2,1)}, bf16[1024,256]{1,0:T(8,128)(2,1)}) custom-call(s32[2048,1]{1,0:T(8,128)} %fusion.3.index_ref, bf16[2,1024,512]{2,1,0:T(8,128)(2,1)} %bem_ref.5, bf16[384,256]{1,0:T(8,128)(2,1)} %get-tuple-element.54.refs_0_, bf16[384,256]{1,0:T(8,128)(2,1)} %get-tuple-element.58.refs_1_, bf16[768,256]{1,0:T(8,128)(2,1)} %copy-done.29, ...), custom_call_target="tpu_custom_call" | custom-call | flops 6442450944 | bytes 1 | tf_op jit(solution)/shard_map/assemble/pallas_call | solution.py:250
  272.1 1.4 collective-permute-start.14
  273.5 1.5 collective-permute-start.13
  275.6 1.4 reduce-scatter.12.cloned.1.call-done
  276.9 2.1 subtract.2.refs_4_.refs_6_.refs_0_
  279.1 9.0 %collective-permute-done.14.refs_3_ = bf16[1024,256]{1,0:T(8,128)(2,1)S(1)} collective-permute-done((bf16[1024,256]{1,0:T(8,128)(2,1)}, bf16[1024,256]{1,0:T(8,128)(2,1)S(1)}, u32[]{:S(2)}, u32[]{:S(2)}) %collective-permute-start.14) | collective-permute-done | bytes 524320 | tf_op jit(solution)/shard_map/ppermute | solution.py:407
  288.0 5.9 %collective-permute-done.13.refs_2_ = bf16[1024,256]{1,0:T(8,128)(2,1)S(1)} collective-permute-done((bf16[1024,256]{1,0:T(8,128)(2,1)}, bf16[1024,256]{1,0:T(8,128)(2,1)S(1)}, u32[]{:S(2)}, u32[]{:S(2)}) %collective-permute-start.13) | collective-permute-done | bytes 524320 | tf_op jit(solution)/shard_map/ppermute | solution.py:407
  294.0 1.2 collective-permute-done.12.refs_1_
  296.0 3.0 join.4.refs_4_
  299.6 1.1 collective-permute-start.18
  300.7 1.4 collective-permute-start.17
  302.1 1.0 collective-permute-start.16
  303.3 1.3 copy-done.11
  304.7 13.4 %product.4.refs_4_.refs_6_.refs_0_ = bf16[1024,256]{1,0:T(8,128)(2,1)} custom-call(s32[8]{0:T(128)} %add_xor_fusion.order_ref, bf16[1024,8192]{1,0:T(8,128)(2,1)} %refs_3_.5, bf16[1024,8192]{1,0:T(8,128)(2,1)} %refs_3_.5, bf16[1024,8192]{1,0:T(8,128)(2,1)} %refs_3_.5, bf16[1024,8192]{1,0:T(8,128)(2,1)} %refs_3_.5, bf16[4096,256]{1,0:T(8,128)(2,1)} %join.4.refs_4_, ...), custom_call_target="tpu_custom_call" | custom-call | flops 12884901888 | bytes 1 | tf_op jit(solution)/shard_map/product/pallas_call | solution.py:387
  318.1 7.9 %collective-permute-done.17.refs_2_ = bf16[1024,256]{1,0:T(8,128)(2,1)S(1)} collective-permute-done((bf16[1024,256]{1,0:T(8,128)(2,1)S(1)}, bf16[1024,256]{1,0:T(8,128)(2,1)S(1)}, u32[]{:S(2)}, u32[]{:S(2)}) %collective-permute-start.17) | collective-permute-done | bytes 524320 | tf_op jit(solution)/shard_map/ppermute | solution.py:407
  327.6 3.0 join.5.refs_4_
  330.6 1.3 collective-permute-start.22
  331.9 1.4 collective-permute-start.21
  334.9 1.3 copy-done.9
  336.3 13.4 %product.5.refs_4_.refs_2_.refs_0_ = bf16[1024,256]{1,0:T(8,128)(2,1)} custom-call(s32[8]{0:T(128)} %add_xor_fusion.order_ref, bf16[1024,8192]{1,0:T(8,128)(2,1)} %refs_3_.5, bf16[1024,8192]{1,0:T(8,128)(2,1)} %refs_3_.5, bf16[1024,8192]{1,0:T(8,128)(2,1)} %refs_3_.5, bf16[1024,8192]{1,0:T(8,128)(2,1)} %refs_3_.5, bf16[4096,256]{1,0:T(8,128)(2,1)} %join.5.refs_4_, ...), custom_call_target="tpu_custom_call" | custom-call | flops 12884901888 | bytes 1 | tf_op jit(solution)/shard_map/product/pallas_call | solution.py:387
  349.7 7.4 %collective-permute-done.21.refs_2_ = bf16[1024,256]{1,0:T(8,128)(2,1)S(1)} collective-permute-done((bf16[1024,256]{1,0:T(8,128)(2,1)S(1)}, bf16[1024,256]{1,0:T(8,128)(2,1)S(1)}, u32[]{:S(2)}, u32[]{:S(2)}) %collective-permute-start.21) | collective-permute-done | bytes 524320 | tf_op jit(solution)/shard_map/ppermute | solution.py:407
  358.7 3.0 join.6.refs_4_
  361.9 1.2 collective-permute-start.26
  363.1 1.4 collective-permute-start.25
  364.5 0.9 collective-permute-start.24
  365.4 2.1 subtract.3.refs_7_.refs_6_
  367.5 1.3 copy-done.10
  368.8 13.3 %product.6.refs_4_ = bf16[1024,256]{1,0:T(8,128)(2,1)} custom-call(s32[8]{0:T(128)} %add_xor_fusion.order_ref, bf16[1024,8192]{1,0:T(8,128)(2,1)} %refs_3_.7, bf16[1024,8192]{1,0:T(8,128)(2,1)} %refs_3_.7, bf16[1024,8192]{1,0:T(8,128)(2,1)} %refs_3_.7, bf16[1024,8192]{1,0:T(8,128)(2,1)} %refs_3_.7, bf16[4096,256]{1,0:T(8,128)(2,1)} %join.6.refs_4_, ...), custom_call_target="tpu_custom_call" | custom-call | flops 12884901888 | bytes 1 | tf_op jit(solution)/shard_map/product/pallas_call | solution.py:387
  382.2 6.1 %collective-permute-done.25.refs_2_ = bf16[1024,256]{1,0:T(8,128)(2,1)} collective-permute-done((bf16[1024,256]{1,0:T(8,128)(2,1)S(1)}, bf16[1024,256]{1,0:T(8,128)(2,1)}, u32[]{:S(2)}, u32[]{:S(2)}) %collective-permute-start.25) | collective-permute-done | bytes 524320 | tf_op jit(solution)/shard_map/ppermute | solution.py:407
  388.3 3.0 join.7.refs_4_
  391.4 4.2 %collective-permute-done.27.refs_5_ = bf16[4096,256]{1,0:T(8,128)(2,1)S(1)} collective-permute-done((bf16[4096,256]{1,0:T(8,128)(2,1)}, bf16[4096,256]{1,0:T(8,128)(2,1)S(1)}, u32[]{:S(2)}, u32[]{:S(2)}) %collective-permute-start.27) | collective-permute-done | bytes 2097184 | tf_op jit(solution)/shard_map/ppermute | solution.py:407
  395.7 1.3 copy-done.12
  397.0 13.3 %product.7 = bf16[1024,256]{1,0:T(8,128)(2,1)} custom-call(s32[8]{0:T(128)} %add_xor_fusion.order_ref, bf16[1024,8192]{1,0:T(8,128)(2,1)} %refs_3_.7, bf16[1024,8192]{1,0:T(8,128)(2,1)} %refs_3_.7, bf16[1024,8192]{1,0:T(8,128)(2,1)} %refs_3_.7, bf16[1024,8192]{1,0:T(8,128)(2,1)} %refs_3_.7, bf16[4096,256]{1,0:T(8,128)(2,1)} %join.7.refs_4_, ...), custom_call_target="tpu_custom_call" | custom-call | flops 12884901888 | bytes 1 | tf_op jit(solution)/shard_map/product/pallas_call | solution.py:387
  410.3 1.1 maximum_bitcast_fusion.1
  411.4 1.5 pad_maximum_fusion
  (148 shorter events, 20.5 us)
Async XLA Ops:
  6.5 196.9 %reduce-scatter.8.cloned.1.call-start = ((), (), s32[]{:S(2)}) async-start(), calls=%async_computation.6 | async-start | bytes 3932160 | tf_op jit(solution)/shard_map/reduce_scatter | solution.py:478
  55.1 0.8 copy-start.24
  55.1 148.4 %reduce-scatter.6.cloned.1.call-start = ((), (), s32[]{:S(2)}) async-start(), calls=%async_computation.5 | async-start | bytes 3932160 | tf_op jit(solution)/shard_map/reduce_scatter | solution.py:478
  55.9 219.7 %reduce-scatter.10.cloned.1.call-start = ((), (), s32[]{:S(2)}) async-start(), calls=%async_computation.7 | async-start | bytes 2621440 | tf_op jit(solution)/shard_map/reduce_scatter | solution.py:478
  139.3 6.8 %collective-permute-start = (bf16[1536,512]{1,0:T(8,128)(2,1)}, bf16[1536,512]{1,0:T(8,128)(2,1)}, u32[]{:S(2)}, u32[]{:S(2)}) collective-permute-start(bf16[1536,512]{1,0:T(8,128)(2,1)} %get-tuple-element.23), channel_id=1, source_target_pairs={{0,4},{4,0},{8,12},{12,8},{16,20},{20,16},{24,28},{28,24},{1,5},{5... | collective-permute-start | bytes 4718600 | tf_op jit(solution)/shard_map/ppermute | solution.py:407
  148.4 5.1 %copy-start.6 = (bf16[768,512]{1,0:T(8,128)(2,1)}, bf16[768,512]{1,0:T(8,128)(2,1)S(1)}, u32[]{:S(2)}) copy-start(bf16[768,512]{1,0:T(8,128)(2,1)S(1)} %pad_maximum_fusion.1.refs_1_) | copy-start | bytes 2359300
  148.5 20.8 %collective-permute-start.1 = (bf16[768,512]{1,0:T(8,128)(2,1)S(1)}, bf16[768,512]{1,0:T(8,128)(2,1)S(1)}, u32[]{:S(2)}, u32[]{:S(2)}) collective-permute-start(bf16[768,512]{1,0:T(8,128)(2,1)S(1)} %pad_maximum_fusion.1.refs_1_), channel_id=1, source_target_pairs={{0,8},{4,12},{8,0},{12,4},{16,24},{20,28},{24,16},{28,20},{1,9},{5... | collective-permute-start | bytes 2359304 | tf_op jit(solution)/shard_map/ppermute | solution.py:407
  150.0 3.5 copy-start.7
  150.0 36.2 %collective-permute-start.2 = (bf16[768,512]{1,0:T(8,128)(2,1)S(1)}, bf16[768,512]{1,0:T(8,128)(2,1)S(1)}, u32[]{:S(2)}, u32[]{:S(2)}) collective-permute-start(bf16[768,512]{1,0:T(8,128)(2,1)S(1)} %pad_maximum_fusion.2.refs_2_), channel_id=1, source_target_pairs={{0,16},{4,20},{8,24},{12,28},{16,0},{20,4},{24,8},{28,12},{1,17},{... | collective-permute-start | bytes 2359304 | tf_op jit(solution)/shard_map/ppermute | solution.py:407
  150.2 3.3 copy-start.8
  150.2 36.0 %collective-permute-start.3 = (bf16[768,512]{1,0:T(8,128)(2,1)S(1)}, bf16[768,512]{1,0:T(8,128)(2,1)S(1)}, u32[]{:S(2)}, u32[]{:S(2)}) collective-permute-start(bf16[768,512]{1,0:T(8,128)(2,1)S(1)} %pad_maximum_fusion.3.refs_3_), channel_id=1, source_target_pairs={{0,24},{4,28},{8,16},{12,20},{16,8},{20,12},{24,0},{28,4},{1,25},{... | collective-permute-start | bytes 2359304 | tf_op jit(solution)/shard_map/ppermute | solution.py:407
  167.0 30.9 %collective-permute-start.8 = (bf16[1536,512]{1,0:T(8,128)(2,1)}, bf16[1536,512]{1,0:T(8,128)(2,1)S(1)}, u32[]{:S(2)}, u32[]{:S(2)}) collective-permute-start(bf16[1536,512]{1,0:T(8,128)(2,1)} %get-tuple-element.28), channel_id=1, source_target_pairs={{0,4},{4,0},{8,12},{12,8},{16,20},{20,16},{24,28},{28,24},{1,5},{5... | collective-permute-start | bytes 4718600 | tf_op jit(solution)/shard_map/ppermute | solution.py:407
  169.2 17.0 %copy-start.25 = (bf16[768,512]{1,0:T(8,128)(2,1)}, bf16[768,512]{1,0:T(8,128)(2,1)S(1)}, u32[]{:S(2)}) copy-start(bf16[768,512]{1,0:T(8,128)(2,1)S(1)} %collective-permute-done.1.refs_2_) | copy-start | bytes 2359300
  186.2 1.0 copy-start.26
  186.2 1.2 copy-start.28
  197.8 79.1 %reduce-scatter.12.cloned.1.call-start = ((), (), s32[]{:S(2)}) async-start(), calls=%async_computation.8 | async-start | bytes 1310720 | tf_op jit(solution)/shard_map/reduce_scatter | solution.py:478
  198.8 20.7 %collective-permute-start.9 = (bf16[768,512]{1,0:T(8,128)(2,1)S(1)}, bf16[768,512]{1,0:T(8,128)(2,1)}, u32[]{:S(2)}, u32[]{:S(2)}) collective-permute-start(bf16[768,512]{1,0:T(8,128)(2,1)S(1)} %pad_maximum_fusion.4), channel_id=1, source_target_pairs={{0,8},{4,12},{8,0},{12,4},{16,24},{20,28},{24,16},{28,20},{1,9},{5... | collective-permute-start | bytes 2359304 | tf_op jit(solution)/shard_map/ppermute | solution.py:407
  199.6 34.7 %collective-permute-start.10 = (bf16[768,512]{1,0:T(8,128)(2,1)S(1)}, bf16[768,512]{1,0:T(8,128)(2,1)}, u32[]{:S(2)}, u32[]{:S(2)}) collective-permute-start(bf16[768,512]{1,0:T(8,128)(2,1)S(1)} %pad_maximum_fusion.5), channel_id=1, source_target_pairs={{0,16},{4,20},{8,24},{12,28},{16,0},{20,4},{24,8},{28,12},{1,17},{... | collective-permute-start | bytes 2359304 | tf_op jit(solution)/shard_map/ppermute | solution.py:407
  202.0 32.3 %collective-permute-start.11 = (bf16[768,512]{1,0:T(8,128)(2,1)}, bf16[768,512]{1,0:T(8,128)(2,1)S(1)}, u32[]{:S(2)}, u32[]{:S(2)}) collective-permute-start(bf16[768,512]{1,0:T(8,128)(2,1)} %pad_maximum_fusion.6), channel_id=1, source_target_pairs={{0,24},{4,28},{8,16},{12,20},{16,8},{20,12},{24,0},{28,4},{1,25},{... | collective-permute-start | bytes 2359304 | tf_op jit(solution)/shard_map/ppermute | solution.py:407
  211.6 34.5 %collective-permute-start.4 = (bf16[1536,256]{1,0:T(8,128)(2,1)}, bf16[1536,256]{1,0:T(8,128)(2,1)S(1)}, u32[]{:S(2)}, u32[]{:S(2)}) collective-permute-start(bf16[1536,256]{1,0:T(8,128)(2,1)} %get-tuple-element.27), channel_id=1, source_target_pairs={{0,4},{4,0},{8,12},{12,8},{16,20},{20,16},{24,28},{28,24},{1,5},{5... | collective-permute-start | bytes 2359304 | tf_op jit(solution)/shard_map/ppermute | solution.py:407
  234.2 0.9 copy-start.27
  235.2 10.2 %copy-start.13 = (bf16[1536,256]{1,0:T(8,128)(2,1)S(1)}, bf16[1536,256]{1,0:T(8,128)(2,1)}, u32[]{:S(2)}) copy-start(bf16[1536,256]{1,0:T(8,128)(2,1)} %get-tuple-element.26.refs_5_) | copy-start | bytes 2359300
  245.1 120.3 %reduce-scatter.14.cloned.1.call-start = ((), (), s32[]{:S(2)}) async-start(), calls=%async_computation.9 | async-start | bytes 1310720 | tf_op jit(solution)/shard_map/reduce_scatter | solution.py:478
  246.9 12.1 %collective-permute-start.5 = (bf16[768,256]{1,0:T(8,128)(2,1)S(1)}, bf16[768,256]{1,0:T(8,128)(2,1)S(1)}, u32[]{:S(2)}, u32[]{:S(2)}) collective-permute-start(bf16[768,256]{1,0:T(8,128)(2,1)S(1)} %pad_maximum_fusion.7), channel_id=1, source_target_pairs={{0,8},{4,12},{8,0},{12,4},{16,24},{20,28},{24,16},{28,20},{1,9},{5... | collective-permute-start | bytes 1179656 | tf_op jit(solution)/shard_map/ppermute | solution.py:407
  248.4 16.5 %collective-permute-start.6 = (bf16[768,256]{1,0:T(8,128)(2,1)S(1)}, bf16[768,256]{1,0:T(8,128)(2,1)S(1)}, u32[]{:S(2)}, u32[]{:S(2)}) collective-permute-start(bf16[768,256]{1,0:T(8,128)(2,1)S(1)} %pad_maximum_fusion.8), channel_id=1, source_target_pairs={{0,16},{4,20},{8,24},{12,28},{16,0},{20,4},{24,8},{28,12},{1,17},{... | collective-permute-start | bytes 1179656 | tf_op jit(solution)/shard_map/ppermute | solution.py:407
  249.3 15.6 %collective-permute-start.7 = (bf16[768,256]{1,0:T(8,128)(2,1)S(1)}, bf16[768,256]{1,0:T(8,128)(2,1)S(1)}, u32[]{:S(2)}, u32[]{:S(2)}) collective-permute-start(bf16[768,256]{1,0:T(8,128)(2,1)S(1)} %pad_maximum_fusion.9), channel_id=1, source_target_pairs={{0,24},{4,28},{8,16},{12,20},{16,8},{20,12},{24,0},{28,4},{1,25},{... | collective-permute-start | bytes 1179656 | tf_op jit(solution)/shard_map/ppermute | solution.py:407
  259.0 6.0 %copy-start.29 = (bf16[768,256]{1,0:T(8,128)(2,1)}, bf16[768,256]{1,0:T(8,128)(2,1)S(1)}, u32[]{:S(2)}) copy-start(bf16[768,256]{1,0:T(8,128)(2,1)S(1)} %collective-permute-done.5.refs_2_) | copy-start | bytes 1179652
  264.9 0.9 copy-start.31
  272.1 16.0 %collective-permute-start.14 = (bf16[1024,256]{1,0:T(8,128)(2,1)}, bf16[1024,256]{1,0:T(8,128)(2,1)S(1)}, u32[]{:S(2)}, u32[]{:S(2)}) collective-permute-start(bf16[1024,256]{1,0:T(8,128)(2,1)} %get-tuple-element.30.refs_2_.refs_0_), channel_id=1, source_target_pairs={{0,24},{4,28},{8,16},{12,20},{16,8},{20,12},{24,0},{28,4},{1,25},{... | collective-permute-start | bytes 1572872 | tf_op jit(solution)/shard_map/ppermute | solution.py:407
  273.5 20.5 %collective-permute-start.13 = (bf16[1024,256]{1,0:T(8,128)(2,1)}, bf16[1024,256]{1,0:T(8,128)(2,1)S(1)}, u32[]{:S(2)}, u32[]{:S(2)}) collective-permute-start(bf16[1024,256]{1,0:T(8,128)(2,1)} %get-tuple-element.30.refs_2_.refs_0_), channel_id=1, source_target_pairs={{0,16},{4,20},{8,24},{12,28},{16,0},{20,4},{24,8},{28,12},{1,17},{... | collective-permute-start | bytes 1572872 | tf_op jit(solution)/shard_map/ppermute | solution.py:407
  275.0 20.2 %collective-permute-start.12 = (bf16[1024,256]{1,0:T(8,128)(2,1)}, bf16[1024,256]{1,0:T(8,128)(2,1)S(1)}, u32[]{:S(2)}, u32[]{:S(2)}) collective-permute-start(bf16[1024,256]{1,0:T(8,128)(2,1)} %get-tuple-element.30.refs_2_.refs_0_), channel_id=1, source_target_pairs={{0,8},{4,12},{8,0},{12,4},{16,24},{20,28},{24,16},{28,20},{1,9},{5... | collective-permute-start | bytes 1572872 | tf_op jit(solution)/shard_map/ppermute | solution.py:407
  279.1 20.5 %copy-start.4 = (bf16[1024,256]{1,0:T(8,128)(2,1)S(1)}, bf16[1024,256]{1,0:T(8,128)(2,1)}, u32[]{:S(2)}) copy-start(bf16[1024,256]{1,0:T(8,128)(2,1)} %subtract.2.refs_4_.refs_6_.refs_0_) | copy-start | bytes 1572868
  288.0 7.2 %copy-start.15 = (bf16[1024,256]{1,0:T(8,128)(2,1)}, bf16[1024,256]{1,0:T(8,128)(2,1)S(1)}, u32[]{:S(2)}) copy-start(bf16[1024,256]{1,0:T(8,128)(2,1)S(1)} %collective-permute-done.14.refs_3_) | copy-start | bytes 1572868
  294.0 1.2 copy-start.16
  295.2 0.8 copy-start.19
  299.0 4.4 %collective-permute-start.15 = (bf16[4096,256]{1,0:T(8,128)(2,1)}, bf16[4096,256]{1,0:T(8,128)(2,1)S(1)}, u32[]{:S(2)}, u32[]{:S(2)}) collective-permute-start(bf16[4096,256]{1,0:T(8,128)(2,1)} %join.4.refs_4_), channel_id=1, source_target_pairs={{0,4},{4,0},{8,12},{12,8},{16,20},{20,16},{24,28},{28,24},{1,5},{5... | collective-permute-start | bytes 6291464 | tf_op jit(solution)/shard_map/ppermute | solution.py:407
  299.6 18.5 %collective-permute-start.18 = (bf16[1024,256]{1,0:T(8,128)(2,1)S(1)}, bf16[1024,256]{1,0:T(8,128)(2,1)S(1)}, u32[]{:S(2)}, u32[]{:S(2)}) collective-permute-start(bf16[1024,256]{1,0:T(8,128)(2,1)S(1)} %copy-done.4), channel_id=1, source_target_pairs={{0,24},{4,28},{8,16},{12,20},{16,8},{20,12},{24,0},{28,4},{1,25},{... | collective-permute-start | bytes 1572872 | tf_op jit(solution)/shard_map/ppermute | solution.py:407
  300.7 25.3 %collective-permute-start.17 = (bf16[1024,256]{1,0:T(8,128)(2,1)S(1)}, bf16[1024,256]{1,0:T(8,128)(2,1)S(1)}, u32[]{:S(2)}, u32[]{:S(2)}) collective-permute-start(bf16[1024,256]{1,0:T(8,128)(2,1)S(1)} %copy-done.4), channel_id=1, source_target_pairs={{0,16},{4,20},{8,24},{12,28},{16,0},{20,4},{24,8},{28,12},{1,17},{... | collective-permute-start | bytes 1572872 | tf_op jit(solution)/shard_map/ppermute | solution.py:407
  302.1 23.9 %collective-permute-start.16 = (bf16[1024,256]{1,0:T(8,128)(2,1)S(1)}, bf16[1024,256]{1,0:T(8,128)(2,1)S(1)}, u32[]{:S(2)}, u32[]{:S(2)}) collective-permute-start(bf16[1024,256]{1,0:T(8,128)(2,1)S(1)} %copy-done.4), channel_id=1, source_target_pairs={{0,8},{4,12},{8,0},{12,4},{16,24},{20,28},{24,16},{28,20},{1,9},{5... | collective-permute-start | bytes 1572872 | tf_op jit(solution)/shard_map/ppermute | solution.py:407
  303.3 1.3 copy-start.11
  318.1 12.5 %copy-start = (bf16[1024,256]{1,0:T(8,128)(2,1)S(1)}, bf16[1024,256]{1,0:T(8,128)(2,1)}, u32[]{:S(2)}) copy-start(bf16[1024,256]{1,0:T(8,128)(2,1)} %product.4.refs_4_.refs_6_.refs_0_) | copy-start | bytes 1572868
  318.1 7.9 %copy-start.17 = (bf16[1024,256]{1,0:T(8,128)(2,1)}, bf16[1024,256]{1,0:T(8,128)(2,1)S(1)}, u32[]{:S(2)}) copy-start(bf16[1024,256]{1,0:T(8,128)(2,1)S(1)} %collective-permute-done.18.refs_3_) | copy-start | bytes 1572868
  326.0 0.8 copy-start.20
  326.8 0.8 copy-start.22
  330.6 4.4 %collective-permute-start.19 = (bf16[4096,256]{1,0:T(8,128)(2,1)}, bf16[4096,256]{1,0:T(8,128)(2,1)S(1)}, u32[]{:S(2)}, u32[]{:S(2)}) collective-permute-start(bf16[4096,256]{1,0:T(8,128)(2,1)} %join.5.refs_4_), channel_id=1, source_target_pairs={{0,4},{4,0},{8,12},{12,8},{16,20},{20,16},{24,28},{28,24},{1,5},{5... | collective-permute-start | bytes 6291464 | tf_op jit(solution)/shard_map/ppermute | solution.py:407
  330.6 19.1 %collective-permute-start.22 = (bf16[1024,256]{1,0:T(8,128)(2,1)S(1)}, bf16[1024,256]{1,0:T(8,128)(2,1)S(1)}, u32[]{:S(2)}, u32[]{:S(2)}) collective-permute-start(bf16[1024,256]{1,0:T(8,128)(2,1)S(1)} %copy-done), channel_id=1, source_target_pairs={{0,24},{4,28},{8,16},{12,20},{16,8},{20,12},{24,0},{28,4},{1,25},{... | collective-permute-start | bytes 1572872 | tf_op jit(solution)/shard_map/ppermute | solution.py:407
  331.9 25.3 %collective-permute-start.21 = (bf16[1024,256]{1,0:T(8,128)(2,1)S(1)}, bf16[1024,256]{1,0:T(8,128)(2,1)S(1)}, u32[]{:S(2)}, u32[]{:S(2)}) collective-permute-start(bf16[1024,256]{1,0:T(8,128)(2,1)S(1)} %copy-done), channel_id=1, source_target_pairs={{0,16},{4,20},{8,24},{12,28},{16,0},{20,4},{24,8},{28,12},{1,17},{... | collective-permute-start | bytes 1572872 | tf_op jit(solution)/shard_map/ppermute | solution.py:407
  333.3 23.9 %collective-permute-start.20 = (bf16[1024,256]{1,0:T(8,128)(2,1)S(1)}, bf16[1024,256]{1,0:T(8,128)(2,1)S(1)}, u32[]{:S(2)}, u32[]{:S(2)}) collective-permute-start(bf16[1024,256]{1,0:T(8,128)(2,1)S(1)} %copy-done), channel_id=1, source_target_pairs={{0,8},{4,12},{8,0},{12,4},{16,24},{20,28},{24,16},{28,20},{1,9},{5... | collective-permute-start | bytes 1572872 | tf_op jit(solution)/shard_map/ppermute | solution.py:407
  334.9 1.3 copy-start.9
  349.7 12.2 %copy-start.2 = (bf16[1024,256]{1,0:T(8,128)(2,1)S(1)}, bf16[1024,256]{1,0:T(8,128)(2,1)}, u32[]{:S(2)}) copy-start(bf16[1024,256]{1,0:T(8,128)(2,1)} %product.5.refs_4_.refs_2_.refs_0_) | copy-start | bytes 1572868
  349.7 7.4 %copy-start.18 = (bf16[1024,256]{1,0:T(8,128)(2,1)}, bf16[1024,256]{1,0:T(8,128)(2,1)S(1)}, u32[]{:S(2)}) copy-start(bf16[1024,256]{1,0:T(8,128)(2,1)S(1)} %collective-permute-done.22.refs_3_) | copy-start | bytes 1572868
  357.1 0.8 copy-start.21
  357.9 0.8 copy-start.23
  361.7 5.8 %collective-permute-start.23 = (bf16[4096,256]{1,0:T(8,128)(2,1)}, bf16[4096,256]{1,0:T(8,128)(2,1)S(1)}, u32[]{:S(2)}, u32[]{:S(2)}) collective-permute-start(bf16[4096,256]{1,0:T(8,128)(2,1)} %join.6.refs_4_), channel_id=1, source_target_pairs={{0,4},{4,0},{8,12},{12,8},{16,20},{20,16},{24,28},{28,24},{1,5},{5... | collective-permute-start | bytes 6291464 | tf_op jit(solution)/shard_map/ppermute | solution.py:407
  361.9 20.3 %collective-permute-start.26 = (bf16[1024,256]{1,0:T(8,128)(2,1)S(1)}, bf16[1024,256]{1,0:T(8,128)(2,1)S(1)}, u32[]{:S(2)}, u32[]{:S(2)}) collective-permute-start(bf16[1024,256]{1,0:T(8,128)(2,1)S(1)} %copy-done.2), channel_id=1, source_target_pairs={{0,24},{4,28},{8,16},{12,20},{16,8},{20,12},{24,0},{28,4},{1,25},{... | collective-permute-start | bytes 1572872 | tf_op jit(solution)/shard_map/ppermute | solution.py:407
  363.1 25.2 %collective-permute-start.25 = (bf16[1024,256]{1,0:T(8,128)(2,1)S(1)}, bf16[1024,256]{1,0:T(8,128)(2,1)}, u32[]{:S(2)}, u32[]{:S(2)}) collective-permute-start(bf16[1024,256]{1,0:T(8,128)(2,1)S(1)} %copy-done.2), channel_id=1, source_target_pairs={{0,16},{4,20},{8,24},{12,28},{16,0},{20,4},{24,8},{28,12},{1,17},{... | collective-permute-start | bytes 1572872 | tf_op jit(solution)/shard_map/ppermute | solution.py:407
  364.5 23.9 %collective-permute-start.24 = (bf16[1024,256]{1,0:T(8,128)(2,1)S(1)}, bf16[1024,256]{1,0:T(8,128)(2,1)}, u32[]{:S(2)}, u32[]{:S(2)}) collective-permute-start(bf16[1024,256]{1,0:T(8,128)(2,1)S(1)} %copy-done.2), channel_id=1, source_target_pairs={{0,8},{4,12},{8,0},{12,4},{16,24},{20,28},{24,16},{28,20},{1,9},{5... | collective-permute-start | bytes 1572872 | tf_op jit(solution)/shard_map/ppermute | solution.py:407
  367.5 1.3 copy-start.10
  382.2 9.2 %copy-start.1 = (bf16[1024,256]{1,0:T(8,128)(2,1)S(1)}, bf16[1024,256]{1,0:T(8,128)(2,1)}, u32[]{:S(2)}) copy-start(bf16[1024,256]{1,0:T(8,128)(2,1)} %product.4.refs_4_.refs_6_.refs_0_) | copy-start | bytes 1572868
  382.2 9.2 %copy-start.3 = (bf16[1024,256]{1,0:T(8,128)(2,1)S(1)}, bf16[1024,256]{1,0:T(8,128)(2,1)}, u32[]{:S(2)}) copy-start(bf16[1024,256]{1,0:T(8,128)(2,1)} %product.5.refs_4_.refs_2_.refs_0_) | copy-start | bytes 1572868
  382.2 6.1 %copy-start.14 = (bf16[1024,256]{1,0:T(8,128)(2,1)}, bf16[1024,256]{1,0:T(8,128)(2,1)S(1)}, u32[]{:S(2)}) copy-start(bf16[1024,256]{1,0:T(8,128)(2,1)S(1)} %collective-permute-done.26.refs_3_) | copy-start | bytes 1572868
  391.3 4.4 %collective-permute-start.27 = (bf16[4096,256]{1,0:T(8,128)(2,1)}, bf16[4096,256]{1,0:T(8,128)(2,1)S(1)}, u32[]{:S(2)}, u32[]{:S(2)}) collective-permute-start(bf16[4096,256]{1,0:T(8,128)(2,1)} %join.7.refs_4_), channel_id=1, source_target_pairs={{0,4},{4,0},{8,12},{12,8},{16,20},{20,16},{24,28},{28,24},{1,5},{5... | collective-permute-start | bytes 6291464 | tf_op jit(solution)/shard_map/ppermute | solution.py:407
  391.4 18.9 %copy-start.5 = (bf16[1024,256]{1,0:T(8,128)(2,1)S(1)}, bf16[1024,256]{1,0:T(8,128)(2,1)}, u32[]{:S(2)}) copy-start(bf16[1024,256]{1,0:T(8,128)(2,1)} %product.6.refs_4_) | copy-start | bytes 1572868
  395.7 1.3 copy-start.12
  (1 other events, 0.7 us)
Sparse Core Ops, SparseCore 0:
  55.2 62.9 reduce-scatter.7
  120.5 60.2 reduce-scatter.5
  197.9 48.3 reduce-scatter.9
  248.5 28.3 reduce-scatter.11
  330.7 31.7 reduce-scatter.13

commit v6 on v5

--- a/solution.py
+++ b/solution.py
@@ -265,34 +265,31 @@
     )(index, bem, *pieces, *after)
 
 
-def subtract_kernel(n_parts, bem_ref, *refs):
+def finish_kernel(ready, ready_ref, bem_ref, schur_ref, *refs):
     out = refs[-1]
-    for at, part in enumerate(refs[:n_parts]):
-        columns = slice(at * TILE, (at + 1) * TILE)
-        taken = part[...].astype(jnp.float32)
-        out[:, columns] = (bem_ref[0, :, columns].astype(jnp.float32) - taken).astype(out.dtype)
-
-
-def subtract(bem, parts, half, start, after=()):
-    count, width = bem.shape[1], len(parts) * TILE
-    place = start * TILE // width
-
-    def rows_of(part):
-        at = half if part.shape[0] > count else 0
-        return pl.BlockSpec((count, TILE), lambda i: (at, 0))
-
-    return pl.pallas_call(
-        functools.partial(subtract_kernel, len(parts)),
+    out[:, :ready] = ready_ref[...]
+    taken = schur_ref[...].astype(jnp.float32)
+    out[:, ready:] = (bem_ref[0].astype(jnp.float32) - taken).astype(out.dtype)
+
+
+def finish(ready, bem, schur, half, after=()):
+    (count, width), last = ready.shape, schur.shape[1]
+    place = bem.shape[2] // last - 1
+    return pl.pallas_call(
+        functools.partial(finish_kernel, width),
         grid=(1,),
-        in_specs=[pl.BlockSpec((1, count, width), lambda i: (half, 0, place))]
-        + [rows_of(part) for part in parts]
+        in_specs=[
+            whole_block(count, width),
+            pl.BlockSpec((1, count, last), lambda i: (half, 0, place)),
+            whole_block(count, last),
+        ]
         + [in_place()] * len(after),
-        out_specs=whole_block(count, width),
-        out_shape=jax.ShapeDtypeStruct((count, width), bem.dtype),
+        out_specs=whole_block(count, width + last),
+        out_shape=jax.ShapeDtypeStruct((count, width + last), bem.dtype),
         compiler_params=kernel_params(),
         cost_estimate=declared(),
-        name="subtract",
-    )(bem, *parts, *after)
+        name="finish",
+    )(ready, bem, schur, *after)
 
 
 def join_kernel(n_parts, *refs):
@@ -471,53 +468,46 @@
     order = me ^ jnp.concatenate(
         [jnp.arange(0, n_row, 2, dtype=jnp.int32), jnp.arange(1, n_row, 2, dtype=jnp.int32)]
     )
-    half = per_dest // 2
-    assert per_dest == 2 * half
+    assert per_dest >= 3
 
     def summed(parts):
         return lax.psum_scatter(parts, "col", scatter_dimension=0)
 
-    parts = front_products(
-        front_inverse, coupling_tiles, meta, tuple(range(half)), (False,) * half, n_col
-    )
-    solved = [summed(part) for part in parts]
-    flats = front_products(
-        front_inverse, coupling_tiles, meta, tuple(range(half, per_dest)), (True,) * half, n_col,
-        (parts[0],),
-    )
+    def products_of(subs, flats, after):
+        return front_products(front_inverse, coupling_tiles, meta, subs, flats, n_col, after)
+
+    last = per_dest - 1
+    parts = products_of((0,), (False,), ())
+    sums = [summed(parts[0])]
+    parts = products_of((1, last), (False, True), (parts[0],))
+    sums.append(summed(parts[0]))
     wanted, lands = route_tables(surface_map, rows, n_row, cap, slots)
-    routed, after = [], ()
-    for flat in flats:
-        packed = pack_rows(wanted, [flat], n_row, slots, after)
-        pieces, after = route(packed, n_row)
-        routed.append(pieces)
-    after = (packed[0],)
-
-    uppers, lowers = [], []
-    for at, pieces in enumerate(routed):
-        cuts = unpack(lands, pieces, n_col, 1 if at + 1 < half else 2, after, 12)
-        uppers.append(summed(cuts[0]))
-        lowers.append(cuts[1:])
-        after = (cuts[0],)
-        if at == 0:
-            packed = pack_rows(wanted, solved, n_row, slots, after, 12)
-            after = (packed[0],)
-    lowers = [summed(low[0]) if low else both for low, both in zip(lowers, uppers)]
-
+    packed = pack_rows(wanted, [parts[1]], n_row, slots)
+    pieces, after = route(packed, n_row)
+    parts = products_of(tuple(range(2, last)), (False,) * (last - 2), after)
+    sums += [summed(part) for part in parts]
+    upper_last, lower_last = unpack(lands, pieces, n_col, 2, (parts[0],))
+    after = (upper_last,)
+    upper_last, lower_last = summed(upper_last), summed(lower_last)
+
+    packed = pack_rows(wanted, sums[:2], n_row, slots, after)
     upper, lower = assemble(lands, bem_entries, route(packed, n_row)[0], 0, after)
     first = gather_rows(upper, n_row)
-    upper = subtract(bem_entries, uppers, 0, half, (upper,))
+    packed = pack_rows(wanted, sums[2:], n_row, slots, (upper,))
+    pieces, after = route(packed, n_row)
+    near, far = both_cores(join(first, (packed[0],)), n_row)
+    pivots = [product(pivot_inverse, order, near, far, after=after)]
+    first = gather_rows(pivots[0], n_row)
+    upper, below = assemble(lands, bem_entries, pieces, 2, (pivots[0],))
+    upper = finish(upper, bem_entries, upper_last, 0)
     second = gather_rows(upper, n_row)
     near, far = both_cores(join(first, (upper,)), n_row)
-    pivots = [product(pivot_inverse, order, near, far, after=(upper,))]
-    first = gather_rows(pivots[0], n_row)
-    near, far = both_cores(join(second, (pivots[0],)), n_row)
-    pivots.append(product(pivot_inverse, order, near, far, after=(pivots[0],)))
+    belows = [product(slab_below, order, near, far, lower, (upper,))]
+    near, far = both_cores(join(second, (belows[0],)), n_row)
+    pivots.append(product(pivot_inverse, order, near, far, after=(belows[0],)))
     second = gather_rows(pivots[1], n_row)
-    near, far = both_cores(join(first, (pivots[1],)), n_row)
-    below = subtract(bem_entries, lowers, 1, half, (pivots[1],))
-    belows = [product(slab_below, order, near, far, lower, (below,))]
-    near, far = both_cores(join(second, (belows[0],)), n_row)
+    below = finish(below, bem_entries, lower_last, 1, (pivots[1],))
+    near, far = both_cores(join(second, (below,)), n_row)
     belows.append(product(slab_below, order, near, far, below))
     return jnp.stack([jnp.concatenate(parts, axis=1) for parts in (pivots, belows)])
 

time: 426 us -> 462 us (1.085)
  waiting for transfers between devices: 99 us -> 131 us
    ppermute x28, waiting for transfers between devices: 96.9 us -> 128 us  [exchange(): return lax.ppermute(value, axis, [(i, i ^ distance) for i in range(n)])]
    pallas_call x2 -> x3, Pallas kernels: 93.2 us -> 106 us  [front_products(): pl.pallas_call(functools.partial(front_kernel, subs, flats, n_col, len(af...]
    pallas_call x2 -> x1, Pallas kernels: 20.3 us -> 9.88 us  [unpack(): pl.pallas_call(functools.partial(unpack_kernel, len(pieces), n_col, parts...]
    pallas_call x3, Pallas kernels: 36 us -> 30 us  [pack_rows(): pl.pallas_call(functools.partial(pack_kernel, n_row, len(solved)), in_spe...]
    pallas_call x1 -> x2, Pallas kernels: 6.25 us -> 12.2 us  [assemble(): pl.pallas_call(functools.partial(assemble_kernel, len(pieces)), grid=(1,)...]
    slice x6 -> x4, local copies, waits for them, and re-layouts: 9.03 us -> 3.97 us  [route(): both = [near[i * cap:(i + 1) * cap], far[i * cap:(i + 1) * cap]]]
    unnamed x73 -> x75, local copies, waits for them, and re-layouts: 15 us -> 15.9 us
  transfers between devices with their start and end apart: 33 -> 33, of which waited for: 15 -> 18; matrix products, arithmetic and copies ran while one was open for 7% -> 6% of each run, Pallas kernels for 37% -> 38%
where the time goes in v6:
time: 462 us; the launch traced here: 456 us
  Pallas kernels  228 us (49%)
  waiting for transfers between devices  131 us (28%)
  starting transfers between devices  25.9 us (6%)
  local copies, waits for them, and re-layouts  24.5 us (5%)
  other arithmetic  22.5 us (5%)
  between operations  13.8 us (3%)
  blocking collectives  10.7 us (2%)
    ppermute x28, waiting for transfers between devices, exchange(): return lax.ppermute(value, axis, [(i, i ^ distance) for i in range(n)])  128 us
    pallas_call x3, Pallas kernels, front_products(): pl.pallas_call(functools.partial(front_kernel, subs, flats, n_col, len(af...  106 us
    pallas_call x4, Pallas kernels, product(): pl.pallas_call(functools.partial(product_kernel, streams, bool(bases)), g...  53.7 us
    pallas_call x3, Pallas kernels, pack_rows(): pl.pallas_call(functools.partial(pack_kernel, n_row, len(solved)), in_spe...  30 us
    ppermute x28, starting transfers between devices, exchange(): return lax.ppermute(value, axis, [(i, i ^ distance) for i in range(n)])  25.7 us
    unnamed x75, local copies, waits for them, and re-layouts  15.9 us
    pallas_call x2, Pallas kernels, assemble(): pl.pallas_call(functools.partial(assemble_kernel, len(pieces)), grid=(1,)...  12.2 us
    pallas_call x4, Pallas kernels, join(): pl.pallas_call(functools.partial(join_kernel, len(parts)), in_specs=[whol...  11.9 us
  transfers between devices with their start and end apart: 33, of which 18 were waited for; matrix products, arithmetic and copies ran while one was open for 6% of the time, Pallas kernels for 38%

profile of v6, /device:TPU:0, one launch (start us, length us, event | category | flops | bytes accessed | tf_op | source)
XLA Modules:
  0.0 456.0 jit_solution(1042296819497821375)
XLA Ops:
  8.5 27.5 %front_products.3.refs_0_ = bf16[4,3072,128]{2,1,0:T(8,128)(2,1)} custom-call(s32[3,192]{1,0:T(4,128)} %pad_add_fusion.meta_ref, bf16[192,128,128]{2,1,0:T(8,128)(2,1)} %tiles_ref.5, bf16[3072,6144]{1,0:T(8,128)(2,1)} %front_ref.5), custom_call_target="tpu_custom_call" | custom-call | bytes 1 | tf_op jit(solution)/shard_map/front_products/pallas_call | solution.py:170
  36.1 51.2 %front_products.4 = (bf16[4,3072,128]{2,1,0:T(8,128)(2,1)}, bf16[3072,512]{1,0:T(8,128)(2,1)}) custom-call(s32[3,192]{1,0:T(4,128)} %pad_add_fusion.meta_ref, bf16[192,128,128]{2,1,0:T(8,128)(2,1)} %tiles_ref.5, bf16[3072,6144]{1,0:T(8,128)(2,1)} %front_ref.5, bf16[4,3072,128]{2,1,0:T(8,128)(2,1)} %front_products.3.refs_0_), custom_call_target="tpu_custom_call" | custom-call | bytes 1 | tf_op jit(solution)/shard_map/front_products/pallas_call | solution.py:170
  88.0 10.7 %all-gather = s32[8,1,2048]{2,1,0:T(1,128)S(1)} all-gather(s32[1,1,2048]{2,1,0:T(1,128)S(1)} %reshape.212), channel_id=1, replica_groups=mesh['row'=8,'col'=4] {'row'}, dimensions={0}, use_global_device_ids=true | all-gather | bytes 73728 | tf_op jit(solution)/shard_map/all_gather | solution.py:429
  99.4 2.4 reduce-window.16
  102.4 6.2 %select_reduce_fusion = s32[8,384]{1,0:T(8,128)S(1)} fusion(s32[8,2048]{1,0:T(8,128)S(1)} %subtract_add_fusion, s32[8,2048]{1,0:T(8,128)S(1)} %bitcast.53, pred[8,2048]{1,0:T(8,128)(4,1)S(1)} %get-tuple-element.34), kind=kLoop, calls=%fused_computation.1 | loop fusion | flops 25162752 | bytes 159744 | tf_op jit(solution)/shard_map/reduce_sum | solution.py:436
  108.7 1.7 copy.41
  110.3 14.3 %pack_rows.3 = (bf16[1536,512]{1,0:T(8,128)(2,1)}, bf16[1536,512]{1,0:T(8,128)(2,1)}) custom-call(s32[3072,1]{1,0:T(8,128)} %bitcast.44, bf16[3072,512]{1,0:T(8,128)(2,1)} %get-tuple-element.20.refs_0_), custom_call_target="tpu_custom_call" | custom-call | bytes 1 | tf_op jit(solution)/shard_map/pack_rows/pallas_call | solution.py:213
  125.0 2.2 fusion.7
  127.2 1.1 collective-permute-done
  129.1 1.0 pad_maximum_fusion.3.refs_2_
  130.1 1.0 pad_maximum_fusion.2.refs_1_
  132.0 27.6 %front_products.5.refs_5_ = bf16[4,3072,128]{2,1,0:T(8,128)(2,1)} custom-call(s32[3,192]{1,0:T(4,128)} %pad_add_fusion.meta_ref, bf16[192,128,128]{2,1,0:T(8,128)(2,1)} %tiles_ref.5, bf16[3072,6144]{1,0:T(8,128)(2,1)} %front_ref.5, bf16[768,512]{1,0:T(8,128)(2,1)} %pad_maximum_fusion.1.refs_0_, bf16[768,512]{1,0:T(8,128)(2,1)} %pad_maximum_fusion.2.refs_1_, ...), custom_call_target="tpu_custom_call" | custom-call | bytes 1 | tf_op jit(solution)/shard_map/front_products/pallas_call | solution.py:170
  159.8 1.7 collective-permute-start.1
  162.2 1.2 collective-permute-start.3
  163.5 2.3 reduce-window.14
  167.5 1.3 fusion.3.index_ref
  168.8 11.8 %collective-permute-done.1.refs_2_ = bf16[768,512]{1,0:T(8,128)(2,1)} collective-permute-done((bf16[768,512]{1,0:T(8,128)(2,1)}, bf16[768,512]{1,0:T(8,128)(2,1)}, u32[]{:S(2)}, u32[]{:S(2)}) %collective-permute-start.1) | collective-permute-done | bytes 786464 | tf_op jit(solution)/shard_map/ppermute | solution.py:404
  180.6 17.5 %collective-permute-done.2.refs_3_ = bf16[768,512]{1,0:T(8,128)(2,1)} collective-permute-done((bf16[768,512]{1,0:T(8,128)(2,1)}, bf16[768,512]{1,0:T(8,128)(2,1)}, u32[]{:S(2)}, u32[]{:S(2)}) %collective-permute-start.2) | collective-permute-done | bytes 786464 | tf_op jit(solution)/shard_map/ppermute | solution.py:404
  198.1 9.9 %unpack.1 = (bf16[4,1024,128]{2,1,0:T(8,128)(2,1)}, bf16[4,1024,128]{2,1,0:T(8,128)(2,1)}) custom-call(s32[2048,1]{1,0:T(8,128)} %fusion.3.index_ref, bf16[384,512]{1,0:T(8,128)(2,1)} %get-tuple-element.39.refs_0_, bf16[384,512]{1,0:T(8,128)(2,1)} %get-tuple-element.35.refs_1_, bf16[768,512]{1,0:T(8,128)(2,1)} %collective-permute-done.1.refs_2_, ...), custom_call_target="tpu_custom_call" | custom-call | bytes 1 | tf_op jit(solution)/shard_map/unpack/pallas_call | solution.py:328
  208.0 8.1 %pack_rows.4 = (bf16[1536,256]{1,0:T(8,128)(2,1)}, bf16[1536,256]{1,0:T(8,128)(2,1)}) custom-call(s32[3072,1]{1,0:T(8,128)} %bitcast.45, bf16[3072,128]{1,0:T(8,128)(2,1)} %bitcast.48, bf16[3072,128]{1,0:T(8,128)(2,1)} %bitcast.49, bf16[4,1024,128]{2,1,0:T(8,128)(2,1)} %get-tuple-element.23.refs_2_.refs_5_), custom_call_target="tpu_custom_call" | custom-call | bytes 1 | tf_op jit(solution)/shard_map/pack_rows/pallas_call | solution.py:213
  216.1 1.9 fusion.8
  219.8 1.6 collective-permute-start.6
  221.5 1.6 collective-permute-start.7
  223.1 8.3 %collective-permute-done.5.refs_2_ = bf16[768,256]{1,0:T(8,128)(2,1)S(1)} collective-permute-done((bf16[768,256]{1,0:T(8,128)(2,1)S(1)}, bf16[768,256]{1,0:T(8,128)(2,1)S(1)}, u32[]{:S(2)}, u32[]{:S(2)}) %collective-permute-start.5) | collective-permute-done | bytes 393248 | tf_op jit(solution)/shard_map/ppermute | solution.py:404
  231.4 7.0 %collective-permute-done.6.refs_3_ = bf16[768,256]{1,0:T(8,128)(2,1)S(1)} collective-permute-done((bf16[768,256]{1,0:T(8,128)(2,1)S(1)}, bf16[768,256]{1,0:T(8,128)(2,1)S(1)}, u32[]{:S(2)}, u32[]{:S(2)}) %collective-permute-start.6) | collective-permute-done | bytes 393248 | tf_op jit(solution)/shard_map/ppermute | solution.py:404
  240.0 6.4 %assemble.2 = (bf16[1024,256]{1,0:T(8,128)(2,1)}, bf16[1024,256]{1,0:T(8,128)(2,1)}) custom-call(s32[2048,1]{1,0:T(8,128)} %fusion.3.index_ref, bf16[2,1024,512]{2,1,0:T(8,128)(2,1)} %bem_ref.7, bf16[384,256]{1,0:T(8,128)(2,1)} %get-tuple-element.46.refs_0_, bf16[384,256]{1,0:T(8,128)(2,1)} %get-tuple-element.50.refs_1_, bf16[768,256]{1,0:T(8,128)(2,1)} %copy-done.27, ...), custom_call_target="tpu_custom_call" | custom-call | flops 6442450944 | bytes 1 | tf_op jit(solution)/shard_map/assemble/pallas_call | solution.py:250
  246.4 1.9 collective-permute-start.10
  248.3 1.3 collective-permute-start.9
  249.9 7.6 %pack_rows.5 = (bf16[1536,128]{1,0:T(8,128)(2,1)}, bf16[1536,128]{1,0:T(8,128)(2,1)}) custom-call(s32[3072,1]{1,0:T(8,128)} %bitcast.46, bf16[3072,128]{1,0:T(8,128)(2,1)} %bitcast.50, bf16[1024,256]{1,0:T(8,128)(2,1)} %get-tuple-element.26.refs_1_.refs_0_), custom_call_target="tpu_custom_call" | custom-call | bytes 1 | tf_op jit(solution)/shard_map/pack_rows/pallas_call | solution.py:213
  257.4 4.9 %collective-permute-done.10.refs_3_ = bf16[1024,256]{1,0:T(8,128)(2,1)S(1)} collective-permute-done((bf16[1024,256]{1,0:T(8,128)(2,1)}, bf16[1024,256]{1,0:T(8,128)(2,1)S(1)}, u32[]{:S(2)}, u32[]{:S(2)}) %collective-permute-start.10) | collective-permute-done | bytes 524320 | tf_op jit(solution)/shard_map/ppermute | solution.py:404
  262.4 9.4 %collective-permute-done.9.refs_2_ = bf16[1024,256]{1,0:T(8,128)(2,1)S(1)} collective-permute-done((bf16[1024,256]{1,0:T(8,128)(2,1)}, bf16[1024,256]{1,0:T(8,128)(2,1)S(1)}, u32[]{:S(2)}, u32[]{:S(2)}) %collective-permute-start.9) | collective-permute-done | bytes 524320 | tf_op jit(solution)/shard_map/ppermute | solution.py:404
  272.8 3.0 join.4.refs_4_
  277.7 2.5 collective-permute-done.12
  280.9 1.4 collective-permute-start.13
  283.6 1.3 copy-done.5
  285.0 13.7 %product.4.refs_5_.refs_0_ = bf16[1024,256]{1,0:T(8,128)(2,1)} custom-call(s32[8]{0:T(128)} %add_xor_fusion.order_ref, bf16[1024,8192]{1,0:T(8,128)(2,1)} %refs_3_.6, bf16[1024,8192]{1,0:T(8,128)(2,1)} %refs_3_.6, bf16[1024,8192]{1,0:T(8,128)(2,1)} %refs_3_.6, bf16[1024,8192]{1,0:T(8,128)(2,1)} %refs_3_.6, bf16[4096,256]{1,0:T(8,128)(2,1)} %join.4.refs_4_, ...), custom_call_target="tpu_custom_call" | custom-call | flops 12884901888 | bytes 1 | tf_op jit(solution)/shard_map/product/pallas_call | solution.py:384
  298.7 1.5 collective-permute-start.21
  300.8 1.3 collective-permute-start.19
  302.6 1.8 collective-permute-start.15
  304.4 28.9 %collective-permute-done.14.refs_3_ = bf16[768,128]{1,0:T(8,128)(2,1)S(1)} collective-permute-done((bf16[768,128]{1,0:T(8,128)(2,1)S(1)}, bf16[768,128]{1,0:T(8,128)(2,1)S(1)}, u32[]{:S(2)}, u32[]{:S(2)}) %collective-permute-start.14) | collective-permute-done | bytes 196640 | tf_op jit(solution)/shard_map/ppermute | solution.py:404
  334.0 5.8 %assemble.3 = (bf16[1024,128]{1,0:T(8,128)(2,1)}, bf16[1024,128]{1,0:T(8,128)(2,1)}) custom-call(s32[2048,1]{1,0:T(8,128)} %fusion.3.index_ref, bf16[2,1024,512]{2,1,0:T(8,128)(2,1)} %bem_ref.7, bf16[384,128]{1,0:T(8,128)(2,1)} %get-tuple-element.52.refs_0_, bf16[384,128]{1,0:T(8,128)(2,1)} %get-tuple-element.56.refs_1_, bf16[768,128]{1,0:T(8,128)(2,1)} %copy-done.30, ...), custom_call_target="tpu_custom_call" | custom-call | flops 3221225472 | bytes 1 | tf_op jit(solution)/shard_map/assemble/pallas_call | solution.py:250
  339.9 2.0 finish.2.refs_4_.refs_7_.refs_0_
  343.6 3.0 join.5.refs_4_
  346.6 1.5 collective-permute-start.18
  348.8 1.3 collective-permute-start.16
  351.0 1.3 copy-done.6
  352.3 13.3 %product.5.refs_4_.refs_6_ = bf16[1024,256]{1,0:T(8,128)(2,1)} custom-call(s32[8]{0:T(128)} %add_xor_fusion.order_ref, bf16[1024,8192]{1,0:T(8,128)(2,1)} %refs_3_.7, bf16[1024,8192]{1,0:T(8,128)(2,1)} %refs_3_.7, bf16[1024,8192]{1,0:T(8,128)(2,1)} %refs_3_.7, bf16[1024,8192]{1,0:T(8,128)(2,1)} %refs_3_.7, bf16[4096,256]{1,0:T(8,128)(2,1)} %join.5.refs_4_, ...), custom_call_target="tpu_custom_call" | custom-call | flops 12884901888 | bytes 1 | tf_op jit(solution)/shard_map/product/pallas_call | solution.py:384
  365.6 7.5 %collective-permute-done.17.refs_2_ = bf16[1024,256]{1,0:T(8,128)(2,1)S(1)} collective-permute-done((bf16[1024,256]{1,0:T(8,128)(2,1)S(1)}, bf16[1024,256]{1,0:T(8,128)(2,1)S(1)}, u32[]{:S(2)}, u32[]{:S(2)}) %collective-permute-start.17) | collective-permute-done | bytes 524320 | tf_op jit(solution)/shard_map/ppermute | solution.py:404
  374.7 3.0 join.6.refs_4_
  377.7 4.3 collective-permute-done.23.refs_5_
  382.0 1.3 copy-done.7
  383.3 13.4 %product.6.refs_0_ = bf16[1024,256]{1,0:T(8,128)(2,1)} custom-call(s32[8]{0:T(128)} %add_xor_fusion.order_ref, bf16[1024,8192]{1,0:T(8,128)(2,1)} %refs_3_.6, bf16[1024,8192]{1,0:T(8,128)(2,1)} %refs_3_.6, bf16[1024,8192]{1,0:T(8,128)(2,1)} %refs_3_.6, bf16[1024,8192]{1,0:T(8,128)(2,1)} %refs_3_.6, bf16[4096,256]{1,0:T(8,128)(2,1)} %join.6.refs_4_, ...), custom_call_target="tpu_custom_call" | custom-call | flops 12884901888 | bytes 1 | tf_op jit(solution)/shard_map/product/pallas_call | solution.py:384
  396.8 1.5 collective-permute-start.26
  399.0 1.3 collective-permute-start.24
  400.3 2.8 reduce-scatter.14.cloned.1.call-done
  403.1 2.0 finish.3.refs_4_.refs_6_
  405.1 7.6 %collective-permute-done.26.refs_3_ = bf16[1024,256]{1,0:T(8,128)(2,1)S(1)} collective-permute-done((bf16[1024,256]{1,0:T(8,128)(2,1)}, bf16[1024,256]{1,0:T(8,128)(2,1)S(1)}, u32[]{:S(2)}, u32[]{:S(2)}) %collective-permute-start.26) | collective-permute-done | bytes 524320 | tf_op jit(solution)/shard_map/ppermute | solution.py:404
  412.7 10.4 %collective-permute-done.25.refs_2_ = bf16[1024,256]{1,0:T(8,128)(2,1)S(1)} collective-permute-done((bf16[1024,256]{1,0:T(8,128)(2,1)}, bf16[1024,256]{1,0:T(8,128)(2,1)S(1)}, u32[]{:S(2)}, u32[]{:S(2)}) %collective-permute-start.25) | collective-permute-done | bytes 524320 | tf_op jit(solution)/shard_map/ppermute | solution.py:404
  424.7 3.0 join.7.refs_4_
  427.8 4.3 collective-permute-done.27.refs_5_
  432.0 1.3 copy-done.8
  433.3 13.3 %product.7 = bf16[1024,256]{1,0:T(8,128)(2,1)} custom-call(s32[8]{0:T(128)} %add_xor_fusion.order_ref, bf16[1024,8192]{1,0:T(8,128)(2,1)} %refs_3_.7, bf16[1024,8192]{1,0:T(8,128)(2,1)} %refs_3_.7, bf16[1024,8192]{1,0:T(8,128)(2,1)} %refs_3_.7, bf16[1024,8192]{1,0:T(8,128)(2,1)} %refs_3_.7, bf16[4096,256]{1,0:T(8,128)(2,1)} %join.7.refs_4_, ...), custom_call_target="tpu_custom_call" | custom-call | flops 12884901888 | bytes 1 | tf_op jit(solution)/shard_map/product/pallas_call | solution.py:384
  446.7 1.1 maximum_bitcast_fusion.1
  447.8 1.5 pad_maximum_fusion
  (151 shorter events, 26.4 us)
Async XLA Ops:
  6.5 201.5 %reduce-scatter.6.cloned.1.call-start = ((), (), s32[]{:S(2)}) async-start(), calls=%async_computation.5 | async-start | bytes 3932160 | tf_op jit(solution)/shard_map/reduce_scatter | solution.py:474
  36.0 172.0 %reduce-scatter.8.cloned.1.call-start = ((), (), s32[]{:S(2)}) async-start(), calls=%async_computation.6 | async-start | bytes 3932160 | tf_op jit(solution)/shard_map/reduce_scatter | solution.py:474
  87.3 162.5 %reduce-scatter.10.cloned.1.call-start = ((), (), s32[]{:S(2)}) async-start(), calls=%async_computation.7 | async-start | bytes 3932160 | tf_op jit(solution)/shard_map/reduce_scatter | solution.py:474
  124.7 3.6 collective-permute-start
  159.6 2.6 copy-start.4
  159.7 180.2 %reduce-scatter.12.cloned.1.call-start = ((), (), s32[]{:S(2)}) async-start(), calls=%async_computation.8 | async-start | bytes 1310720 | tf_op jit(solution)/shard_map/reduce_scatter | solution.py:474
  159.8 20.7 %collective-permute-start.1 = (bf16[768,512]{1,0:T(8,128)(2,1)}, bf16[768,512]{1,0:T(8,128)(2,1)}, u32[]{:S(2)}, u32[]{:S(2)}) collective-permute-start(bf16[768,512]{1,0:T(8,128)(2,1)} %pad_maximum_fusion.1.refs_0_), channel_id=1, source_target_pairs={{0,8},{4,12},{8,0},{12,4},{16,24},{20,28},{24,16},{28,20},{1,9},{5... | collective-permute-start | bytes 2359304 | tf_op jit(solution)/shard_map/ppermute | solution.py:404
  161.6 36.6 %collective-permute-start.2 = (bf16[768,512]{1,0:T(8,128)(2,1)}, bf16[768,512]{1,0:T(8,128)(2,1)}, u32[]{:S(2)}, u32[]{:S(2)}) collective-permute-start(bf16[768,512]{1,0:T(8,128)(2,1)} %pad_maximum_fusion.2.refs_1_), channel_id=1, source_target_pairs={{0,16},{4,20},{8,24},{12,28},{16,0},{20,4},{24,8},{28,12},{1,17},{... | collective-permute-start | bytes 2359304 | tf_op jit(solution)/shard_map/ppermute | solution.py:404
  162.2 35.9 %collective-permute-start.3 = (bf16[768,512]{1,0:T(8,128)(2,1)S(1)}, bf16[768,512]{1,0:T(8,128)(2,1)}, u32[]{:S(2)}, u32[]{:S(2)}) collective-permute-start(bf16[768,512]{1,0:T(8,128)(2,1)S(1)} %copy-done.4), channel_id=1, source_target_pairs={{0,24},{4,28},{8,16},{12,20},{16,8},{20,12},{24,0},{28,4},{1,25},{... | collective-permute-start | bytes 2359304 | tf_op jit(solution)/shard_map/ppermute | solution.py:404
  216.1 2.5 collective-permute-start.4
  219.3 12.0 %collective-permute-start.5 = (bf16[768,256]{1,0:T(8,128)(2,1)S(1)}, bf16[768,256]{1,0:T(8,128)(2,1)S(1)}, u32[]{:S(2)}, u32[]{:S(2)}) collective-permute-start(bf16[768,256]{1,0:T(8,128)(2,1)S(1)} %pad_maximum_fusion.4), channel_id=1, source_target_pairs={{0,8},{4,12},{8,0},{12,4},{16,24},{20,28},{24,16},{28,20},{1,9},{5... | collective-permute-start | bytes 1179656 | tf_op jit(solution)/shard_map/ppermute | solution.py:404
  219.8 18.5 %collective-permute-start.6 = (bf16[768,256]{1,0:T(8,128)(2,1)S(1)}, bf16[768,256]{1,0:T(8,128)(2,1)S(1)}, u32[]{:S(2)}, u32[]{:S(2)}) collective-permute-start(bf16[768,256]{1,0:T(8,128)(2,1)S(1)} %pad_maximum_fusion.5), channel_id=1, source_target_pairs={{0,16},{4,20},{8,24},{12,28},{16,0},{20,4},{24,8},{28,12},{1,17},{... | collective-permute-start | bytes 1179656 | tf_op jit(solution)/shard_map/ppermute | solution.py:404
  221.5 17.7 %collective-permute-start.7 = (bf16[768,256]{1,0:T(8,128)(2,1)S(1)}, bf16[768,256]{1,0:T(8,128)(2,1)S(1)}, u32[]{:S(2)}, u32[]{:S(2)}) collective-permute-start(bf16[768,256]{1,0:T(8,128)(2,1)S(1)} %pad_maximum_fusion.6), channel_id=1, source_target_pairs={{0,24},{4,28},{8,16},{12,20},{16,8},{20,12},{24,0},{28,4},{1,25},{... | collective-permute-start | bytes 1179656 | tf_op jit(solution)/shard_map/ppermute | solution.py:404
  231.4 7.8 %copy-start.27 = (bf16[768,256]{1,0:T(8,128)(2,1)}, bf16[768,256]{1,0:T(8,128)(2,1)S(1)}, u32[]{:S(2)}) copy-start(bf16[768,256]{1,0:T(8,128)(2,1)S(1)} %collective-permute-done.5.refs_2_) | copy-start | bytes 1179652
  238.3 0.9 copy-start.28
  239.2 0.8 copy-start.29
  246.4 16.0 %collective-permute-start.10 = (bf16[1024,256]{1,0:T(8,128)(2,1)}, bf16[1024,256]{1,0:T(8,128)(2,1)S(1)}, u32[]{:S(2)}, u32[]{:S(2)}) collective-permute-start(bf16[1024,256]{1,0:T(8,128)(2,1)} %get-tuple-element.26.refs_1_.refs_0_), channel_id=1, source_target_pairs={{0,24},{4,28},{8,16},{12,20},{16,8},{20,12},{24,0},{28,4},{1,25},{... | collective-permute-start | bytes 1572872 | tf_op jit(solution)/shard_map/ppermute | solution.py:404
  248.3 23.5 %collective-permute-start.9 = (bf16[1024,256]{1,0:T(8,128)(2,1)}, bf16[1024,256]{1,0:T(8,128)(2,1)S(1)}, u32[]{:S(2)}, u32[]{:S(2)}) collective-permute-start(bf16[1024,256]{1,0:T(8,128)(2,1)} %get-tuple-element.26.refs_1_.refs_0_), channel_id=1, source_target_pairs={{0,16},{4,20},{8,24},{12,28},{16,0},{20,4},{24,8},{28,12},{1,17},{... | collective-permute-start | bytes 1572872 | tf_op jit(solution)/shard_map/ppermute | solution.py:404
  249.6 22.2 %collective-permute-start.8 = (bf16[1024,256]{1,0:T(8,128)(2,1)}, bf16[1024,256]{1,0:T(8,128)(2,1)S(1)}, u32[]{:S(2)}, u32[]{:S(2)}) collective-permute-start(bf16[1024,256]{1,0:T(8,128)(2,1)} %get-tuple-element.26.refs_1_.refs_0_), channel_id=1, source_target_pairs={{0,8},{4,12},{8,0},{12,4},{16,24},{20,28},{24,16},{28,20},{1,9},{5... | collective-permute-start | bytes 1572872 | tf_op jit(solution)/shard_map/ppermute | solution.py:404
  262.4 9.4 %copy-start.16 = (bf16[1024,256]{1,0:T(8,128)(2,1)}, bf16[1024,256]{1,0:T(8,128)(2,1)S(1)}, u32[]{:S(2)}) copy-start(bf16[1024,256]{1,0:T(8,128)(2,1)S(1)} %collective-permute-done.10.refs_3_) | copy-start | bytes 1572868
  271.8 0.8 copy-start.19
  271.8 1.0 copy-start.22
  272.8 3.1 copy-start.26
  272.8 4.3 copy-start.9
  275.8 7.8 %collective-permute-start.11 = (bf16[4096,256]{1,0:T(8,128)(2,1)}, bf16[4096,256]{1,0:T(8,128)(2,1)S(1)}, u32[]{:S(2)}, u32[]{:S(2)}) collective-permute-start(bf16[4096,256]{1,0:T(8,128)(2,1)} %join.4.refs_4_), channel_id=1, source_target_pairs={{0,4},{4,0},{8,12},{12,8},{16,20},{20,16},{24,28},{28,24},{1,5},{5... | collective-permute-start | bytes 6291464 | tf_op jit(solution)/shard_map/ppermute | solution.py:404
  275.8 4.3 collective-permute-start.12
  277.0 126.1 %reduce-scatter.14.cloned.1.call-start = ((), (), s32[]{:S(2)}) async-start(), calls=%async_computation.9 | async-start | bytes 1310720 | tf_op jit(solution)/shard_map/reduce_scatter | solution.py:474
  280.8 2.8 copy-start.11
  280.9 21.7 %collective-permute-start.13 = (bf16[768,128]{1,0:T(8,128)(2,1)S(1)}, bf16[768,128]{1,0:T(8,128)(2,1)S(1)}, u32[]{:S(2)}, u32[]{:S(2)}) collective-permute-start(bf16[768,128]{1,0:T(8,128)(2,1)S(1)} %pad_maximum_fusion.7.refs_6_), channel_id=1, source_target_pairs={{0,8},{4,12},{8,0},{12,4},{16,24},{20,28},{24,16},{28,20},{1,9},{5... | collective-permute-start | bytes 589832 | tf_op jit(solution)/shard_map/ppermute | solution.py:404
  283.6 18.5 %copy-start.12 = (bf16[768,128]{1,0:T(8,128)(2,1)S(1)}, bf16[768,128]{1,0:T(8,128)(2,1)}, u32[]{:S(2)}) copy-start(bf16[768,128]{1,0:T(8,128)(2,1)} %pad_maximum_fusion.8.refs_7_) | copy-start | bytes 589828
  283.6 19.0 %copy-start.10 = (bf16[768,128]{1,0:T(8,128)(2,1)S(1)}, bf16[768,128]{1,0:T(8,128)(2,1)}, u32[]{:S(2)}) copy-start(bf16[768,128]{1,0:T(8,128)(2,1)} %pad_maximum_fusion.9.refs_8_) | copy-start | bytes 589828
  283.6 1.3 copy-start.5
  298.7 43.2 %collective-permute-start.21 = (bf16[1024,256]{1,0:T(8,128)(2,1)}, bf16[1024,256]{1,0:T(8,128)(2,1)S(1)}, u32[]{:S(2)}, u32[]{:S(2)}) collective-permute-start(bf16[1024,256]{1,0:T(8,128)(2,1)} %product.4.refs_5_.refs_0_), channel_id=1, source_target_pairs={{0,24},{4,28},{8,16},{12,20},{16,8},{20,12},{24,0},{28,4},{1,25},{... | collective-permute-start | bytes 1572872 | tf_op jit(solution)/shard_map/ppermute | solution.py:404
  300.1 41.8 %collective-permute-start.20 = (bf16[1024,256]{1,0:T(8,128)(2,1)}, bf16[1024,256]{1,0:T(8,128)(2,1)S(1)}, u32[]{:S(2)}, u32[]{:S(2)}) collective-permute-start(bf16[1024,256]{1,0:T(8,128)(2,1)} %product.4.refs_5_.refs_0_), channel_id=1, source_target_pairs={{0,16},{4,20},{8,24},{12,28},{16,0},{20,4},{24,8},{28,12},{1,17},{... | collective-permute-start | bytes 1572872 | tf_op jit(solution)/shard_map/ppermute | solution.py:404
  300.8 41.1 %collective-permute-start.19 = (bf16[1024,256]{1,0:T(8,128)(2,1)}, bf16[1024,256]{1,0:T(8,128)(2,1)S(1)}, u32[]{:S(2)}, u32[]{:S(2)}) collective-permute-start(bf16[1024,256]{1,0:T(8,128)(2,1)} %product.4.refs_5_.refs_0_), channel_id=1, source_target_pairs={{0,8},{4,12},{8,0},{12,4},{16,24},{20,28},{24,16},{28,20},{1,9},{5... | collective-permute-start | bytes 1572872 | tf_op jit(solution)/shard_map/ppermute | solution.py:404
  302.1 31.2 %collective-permute-start.14 = (bf16[768,128]{1,0:T(8,128)(2,1)S(1)}, bf16[768,128]{1,0:T(8,128)(2,1)S(1)}, u32[]{:S(2)}, u32[]{:S(2)}) collective-permute-start(bf16[768,128]{1,0:T(8,128)(2,1)S(1)} %copy-done.12), channel_id=1, source_target_pairs={{0,16},{4,20},{8,24},{12,28},{16,0},{20,4},{24,8},{28,12},{1,17},{... | collective-permute-start | bytes 589832 | tf_op jit(solution)/shard_map/ppermute | solution.py:404
  302.6 30.7 %copy-start.30 = (bf16[768,128]{1,0:T(8,128)(2,1)}, bf16[768,128]{1,0:T(8,128)(2,1)S(1)}, u32[]{:S(2)}) copy-start(bf16[768,128]{1,0:T(8,128)(2,1)S(1)} %collective-permute-done.13.refs_2_) | copy-start | bytes 589828
  302.6 30.7 %collective-permute-start.15 = (bf16[768,128]{1,0:T(8,128)(2,1)S(1)}, bf16[768,128]{1,0:T(8,128)(2,1)S(1)}, u32[]{:S(2)}, u32[]{:S(2)}) collective-permute-start(bf16[768,128]{1,0:T(8,128)(2,1)S(1)} %copy-done.10), channel_id=1, source_target_pairs={{0,24},{4,28},{8,16},{12,20},{16,8},{20,12},{24,0},{28,4},{1,25},{... | collective-permute-start | bytes 589832 | tf_op jit(solution)/shard_map/ppermute | solution.py:404
  333.3 0.7 copy-start.32
  341.9 4.8 %copy-start.1 = (bf16[1024,256]{1,0:T(8,128)(2,1)S(1)}, bf16[1024,256]{1,0:T(8,128)(2,1)}, u32[]{:S(2)}) copy-start(bf16[1024,256]{1,0:T(8,128)(2,1)} %finish.2.refs_4_.refs_7_.refs_0_) | copy-start | bytes 1572868
  341.9 0.8 copy-start.13
  341.9 0.9 copy-start.14
  342.9 0.8 copy-start.15
  346.6 4.4 collective-permute-start.22
  346.6 19.0 %collective-permute-start.18 = (bf16[1024,256]{1,0:T(8,128)(2,1)S(1)}, bf16[1024,256]{1,0:T(8,128)(2,1)S(1)}, u32[]{:S(2)}, u32[]{:S(2)}) collective-permute-start(bf16[1024,256]{1,0:T(8,128)(2,1)S(1)} %copy-done.1), channel_id=1, source_target_pairs={{0,24},{4,28},{8,16},{12,20},{16,8},{20,12},{24,0},{28,4},{1,25},{... | collective-permute-start | bytes 1572872 | tf_op jit(solution)/shard_map/ppermute | solution.py:404
  348.2 24.9 %collective-permute-start.17 = (bf16[1024,256]{1,0:T(8,128)(2,1)S(1)}, bf16[1024,256]{1,0:T(8,128)(2,1)S(1)}, u32[]{:S(2)}, u32[]{:S(2)}) collective-permute-start(bf16[1024,256]{1,0:T(8,128)(2,1)S(1)} %copy-done.1), channel_id=1, source_target_pairs={{0,16},{4,20},{8,24},{12,28},{16,0},{20,4},{24,8},{28,12},{1,17},{... | collective-permute-start | bytes 1572872 | tf_op jit(solution)/shard_map/ppermute | solution.py:404
  348.8 24.3 %collective-permute-start.16 = (bf16[1024,256]{1,0:T(8,128)(2,1)S(1)}, bf16[1024,256]{1,0:T(8,128)(2,1)S(1)}, u32[]{:S(2)}, u32[]{:S(2)}) collective-permute-start(bf16[1024,256]{1,0:T(8,128)(2,1)S(1)} %copy-done.1), channel_id=1, source_target_pairs={{0,8},{4,12},{8,0},{12,4},{16,24},{20,28},{24,16},{28,20},{1,9},{5... | collective-permute-start | bytes 1572872 | tf_op jit(solution)/shard_map/ppermute | solution.py:404
  351.0 1.3 copy-start.6
  365.6 7.5 %copy-start.17 = (bf16[1024,256]{1,0:T(8,128)(2,1)}, bf16[1024,256]{1,0:T(8,128)(2,1)S(1)}, u32[]{:S(2)}) copy-start(bf16[1024,256]{1,0:T(8,128)(2,1)S(1)} %collective-permute-done.18.refs_3_) | copy-start | bytes 1572868
  373.1 0.8 copy-start.20
  373.9 0.8 copy-start.23
  377.6 4.4 collective-permute-start.23
  382.0 1.3 copy-start.7
  396.8 15.9 %collective-permute-start.26 = (bf16[1024,256]{1,0:T(8,128)(2,1)}, bf16[1024,256]{1,0:T(8,128)(2,1)S(1)}, u32[]{:S(2)}, u32[]{:S(2)}) collective-permute-start(bf16[1024,256]{1,0:T(8,128)(2,1)} %product.6.refs_0_), channel_id=1, source_target_pairs={{0,24},{4,28},{8,16},{12,20},{16,8},{20,12},{24,0},{28,4},{1,25},{... | collective-permute-start | bytes 1572872 | tf_op jit(solution)/shard_map/ppermute | solution.py:404
  398.3 24.8 %collective-permute-start.25 = (bf16[1024,256]{1,0:T(8,128)(2,1)}, bf16[1024,256]{1,0:T(8,128)(2,1)S(1)}, u32[]{:S(2)}, u32[]{:S(2)}) collective-permute-start(bf16[1024,256]{1,0:T(8,128)(2,1)} %product.6.refs_0_), channel_id=1, source_target_pairs={{0,16},{4,20},{8,24},{12,28},{16,0},{20,4},{24,8},{28,12},{1,17},{... | collective-permute-start | bytes 1572872 | tf_op jit(solution)/shard_map/ppermute | solution.py:404
  399.0 24.1 %collective-permute-start.24 = (bf16[1024,256]{1,0:T(8,128)(2,1)}, bf16[1024,256]{1,0:T(8,128)(2,1)S(1)}, u32[]{:S(2)}, u32[]{:S(2)}) collective-permute-start(bf16[1024,256]{1,0:T(8,128)(2,1)} %product.6.refs_0_), channel_id=1, source_target_pairs={{0,8},{4,12},{8,0},{12,4},{16,24},{20,28},{24,16},{28,20},{1,9},{5... | collective-permute-start | bytes 1572872 | tf_op jit(solution)/shard_map/ppermute | solution.py:404
  405.1 22.6 %copy-start.2 = (bf16[1024,256]{1,0:T(8,128)(2,1)S(1)}, bf16[1024,256]{1,0:T(8,128)(2,1)}, u32[]{:S(2)}) copy-start(bf16[1024,256]{1,0:T(8,128)(2,1)} %product.6.refs_0_) | copy-start | bytes 1572868
  405.1 22.6 %copy-start.3 = (bf16[1024,256]{1,0:T(8,128)(2,1)S(1)}, bf16[1024,256]{1,0:T(8,128)(2,1)}, u32[]{:S(2)}) copy-start(bf16[1024,256]{1,0:T(8,128)(2,1)} %product.4.refs_5_.refs_0_) | copy-start | bytes 1572868
  412.7 10.4 %copy-start.18 = (bf16[1024,256]{1,0:T(8,128)(2,1)}, bf16[1024,256]{1,0:T(8,128)(2,1)S(1)}, u32[]{:S(2)}) copy-start(bf16[1024,256]{1,0:T(8,128)(2,1)S(1)} %collective-permute-done.26.refs_3_) | copy-start | bytes 1572868
  423.1 0.8 copy-start.21
  423.9 0.8 copy-start.24
  427.6 4.4 collective-permute-start.27
  427.7 18.9 %copy-start = (bf16[1024,256]{1,0:T(8,128)(2,1)S(1)}, bf16[1024,256]{1,0:T(8,128)(2,1)}, u32[]{:S(2)}) copy-start(bf16[1024,256]{1,0:T(8,128)(2,1)} %product.5.refs_4_.refs_6_) | copy-start | bytes 1572868
  432.0 1.3 copy-start.8
  (2 other events, 1.4 us)
Sparse Core Ops, SparseCore 0:
  36.1 66.2 reduce-scatter.5
  104.8 60.2 reduce-scatter.7
  167.4 60.2 reduce-scatter.9
  277.1 24.8 reduce-scatter.11
  377.8 25.1 reduce-scatter.13

commit v7 on v5

--- a/solution.py
+++ b/solution.py
@@ -9,6 +9,7 @@
 
 TILE = 128
 STACK = 4
+REPEATS = 32
 VMEM_BYTES = 56 * 1024 * 1024
 
 
@@ -42,8 +43,11 @@
 
 def front_kernel(subs, flats, n_col, n_after, meta_ref, tiles_ref, front_ref, *refs):
     outs = refs[n_after : n_after + len(subs)]
-    stack, held, acc, places, groups_of, state, tile_sems, sems = refs[n_after + len(subs) :]
-    groups = n_col * len(subs)
+    stack, held, acc, places, filled, pair_of, state, found, tile_sems, sems = refs[
+        n_after + len(subs) :
+    ]
+    pairs = n_col * len(subs) // 2
+    depth_blocks = found.shape[1]
     block, streams = held.shape[1], sems.shape[1]
     lines = block // streams
     step = pl.program_id(0)
@@ -56,11 +60,13 @@
             sems.at[into, q],
         )
 
-    def tile_copy(t, item, place):
+    def half_of(item, place, side):
+        rows = pl.ds(pl.multiple_of(place * TILE, TILE), TILE)
+        return stack.at[side, item, rows, :]
+
+    def tile_copy(t, item, place, side):
         return pltpu.make_async_copy(
-            tiles_ref.at[t],
-            stack.at[item, pl.ds(pl.multiple_of(place * TILE, TILE), TILE), :],
-            tile_sems.at[t],
+            tiles_ref.at[t], half_of(item, place, side), tile_sems.at[t]
         )
 
     def chosen(t):
@@ -72,59 +78,68 @@
             order = jnp.where(meta_ref[2, t] == subs[p], p, order)
         return order * n_col + meta_ref[1, t]
 
-    def clear(item, place):
-        places[item, place] = 0
-        stack[item, pl.ds(pl.multiple_of(place * TILE, TILE), TILE), :] = jnp.zeros(
-            (TILE, TILE), stack.dtype
-        )
-
     @pl.when(step == 0)
     def build():
         for q in range(streams):
             front_copy(0, 0, q).start()
-        for g in range(groups):
-            state[g] = 0
-            state[groups + g] = 0
-        state[2 * groups] = 0
+        for i in range(2 * pairs + 1):
+            state[i] = 0
+
+        @pl.loop(0, depth_blocks)
+        def forget(row):
+            for pair in range(pairs):
+                found[pair, row] = -1
+
+        @pl.loop(0, filled.shape[0])
+        def empty(item):
+            pair_of[item] = 0
+            for place in range(STACK):
+                places[item, place] = 0
+                filled[item, place] = 0
 
         @pl.loop(0, tiles_ref.shape[0])
         def place_tile(t):
             @pl.when(chosen(t))
             def _():
-                g = group_of(t)
-                at = state[g]
-
-                @pl.when(lax.rem(at, STACK) == 0)
+                g, row = group_of(t), meta_ref[0, t]
+                pair, side = lax.div(g, 2), lax.rem(g, 2)
+
+                @pl.when(found[pair, row] < 0)
                 def _():
-                    state[groups + g] = state[2 * groups]
-                    groups_of[state[2 * groups]] = g
-                    state[2 * groups] += 1
-
-                item = state[groups + g]
-                places[item, lax.rem(at, STACK)] = meta_ref[0, t]
-                tile_copy(t, item, lax.rem(at, STACK)).start()
-                state[g] = at + 1
-
-        for g in range(groups):
-            used = lax.rem(state[g], STACK)
-
-            @pl.loop(used, jnp.where(used == 0, 0, STACK))
-            def fill(place):
-                clear(state[groups + g], place)
-
-        items = state[2 * groups]
-
-        @pl.loop(items, (items + STACK - 1) // STACK * STACK)
-        def fill_item(item):
-            groups_of[item] = 0
+                    at = state[pair]
+
+                    @pl.when(lax.rem(at, STACK) == 0)
+                    def _():
+                        state[pairs + pair] = state[2 * pairs]
+                        pair_of[state[2 * pairs]] = pair
+                        state[2 * pairs] += 1
+
+                    item, place = state[pairs + pair], lax.rem(at, STACK)
+                    places[item, place] = row
+                    found[pair, row] = item * STACK + place
+                    state[pair] = at + 1
+
+                item = lax.div(found[pair, row], STACK)
+                place = lax.rem(found[pair, row], STACK)
+                filled[item, place] += 1 + side
+                tile_copy(t, item, place, side).start()
+
+        items = state[2 * pairs]
+
+        @pl.loop(0, (items + 1) // 2 * 2)
+        def clear(item):
             for place in range(STACK):
-                clear(item, place)
+                for side in range(2):
+
+                    @pl.when((filled[item, place] == 0) | (filled[item, place] == 2 - side))
+                    def _():
+                        half_of(item, place, side)[...] = jnp.zeros((TILE, TILE), stack.dtype)
 
         @pl.loop(0, tiles_ref.shape[0])
         def wait_tile(t):
             @pl.when(chosen(t))
             def _():
-                tile_copy(t, 0, 0).wait()
+                tile_copy(t, 0, 0, 0).wait()
 
     @pl.when(step + 1 < pl.num_programs(0))
     def ahead():
@@ -136,29 +151,31 @@
 
     acc[...] = jnp.zeros_like(acc)
 
-    @pl.loop(0, (state[2 * groups] + STACK - 1) // STACK)
+    @pl.loop(0, (state[2 * pairs] + 1) // 2)
     def add(s):
-        for i in range(STACK):
-            item = s * STACK + i
+        for i in range(2):
+            item = s * 2 + i
             lefts = [pl.multiple_of(places[item, j] * TILE, TILE) for j in range(STACK)]
             rows = [held[slot, :, pl.ds(left, TILE)] for left in lefts]
-            acc[groups_of[item]] += dot32(jnp.concatenate(rows, axis=1), stack[item])
-
-    for g in range(groups):
+            tiles = jnp.concatenate([stack[0, item], stack[1, item]], axis=1)
+            acc[pair_of[item]] += dot32(jnp.concatenate(rows, axis=1), tiles)
+
+    for g in range(2 * pairs):
         out, dest = outs[g // n_col], g % n_col
+        value = acc[g // 2, :, g % 2 * TILE : (g % 2 + 1) * TILE].astype(out.dtype)
         if flats[g // n_col]:
-            out[:, dest * TILE : (dest + 1) * TILE] = acc[g].astype(out.dtype)
+            out[:, dest * TILE : (dest + 1) * TILE] = value
         else:
-            out[dest] = acc[g].astype(out.dtype)
+            out[dest] = value
 
 
 def front_products(front, tiles, meta, subs, flats, n_col, after=()):
     rows, depth = front.shape
-    groups = n_col * len(subs)
+    pairs = n_col * len(subs) // 2
     block = largest_tile(rows, 512)
     streams = 8 if block % 128 == 0 else 1
     count = tiles.shape[0]
-    items = (-(-count // STACK) + groups + STACK) // STACK * STACK
+    items = (-(-count // STACK) + pairs + 2) // 2 * 2
     shapes, specs = [], []
     for flat in flats:
         if flat:
@@ -175,12 +192,14 @@
             in_specs=[in_place()] * (2 + len(after)),
             out_specs=specs,
             scratch_shapes=[
-                pltpu.VMEM((items, STACK * TILE, TILE), front.dtype),
+                pltpu.VMEM((2, items, STACK * TILE, TILE), front.dtype),
                 pltpu.VMEM((2, block, depth), front.dtype),
-                pltpu.VMEM((groups, block, TILE), jnp.float32),
+                pltpu.VMEM((pairs, block, 2 * TILE), jnp.float32),
+                pltpu.SMEM((items, STACK), jnp.int32),
                 pltpu.SMEM((items, STACK), jnp.int32),
                 pltpu.SMEM((items,), jnp.int32),
-                pltpu.SMEM((2 * groups + 1,), jnp.int32),
+                pltpu.SMEM((2 * pairs + 1,), jnp.int32),
+                pltpu.SMEM((pairs, depth // TILE), jnp.int32),
                 pltpu.SemaphoreType.DMA((count,)),
                 pltpu.SemaphoreType.DMA((2, streams)),
             ],
@@ -429,7 +448,8 @@
 def route_tables(surface_map, rows, n_row, cap, slots):
     me = lax.axis_index("row")
     mine = surface_map.reshape(-1)
-    every = lax.all_gather(mine, "row")
+    shifts = jnp.arange(REPEATS, dtype=jnp.int32)[:, None]
+    every = lax.all_gather(mine[None, :] + shifts, "row")[:, 0]
     partners = me ^ jnp.arange(n_row, dtype=jnp.int32)
     local = every[partners] - me * rows
     asked = (local >= 0) & (local < rows)

time: 426 us -> 467 us (1.096)
  waiting for transfers between devices: 99 us -> 123 us
  Pallas kernels: 225 us -> 248 us
  blocking collectives: 10.7 us -> 0 us
    reduce_scatter x5, waiting for transfers between devices: 1.38 us -> 34.5 us  [summed(): return lax.psum_scatter(parts, 'col', scatter_dimension=0)]
    pallas_call x2, Pallas kernels: 93.2 us -> 117 us  [front_products(): pl.pallas_call(functools.partial(front_kernel, subs, flats, n_col, len(af...]
    all_gather x1 -> x0, blocking collectives: 10.7 us -> none  [route_tables(): every = lax.all_gather(mine, 'row')]
    ppermute x28, waiting for transfers between devices: 96.9 us -> 87.7 us  [exchange(): return lax.ppermute(value, axis, [(i, i ^ distance) for i in range(n)])]
    unnamed x73 -> x75, local copies, waits for them, and re-layouts: 15 us -> 15.9 us
  transfers between devices with their start and end apart: 33 -> 34, of which waited for: 15 -> 17; matrix products, arithmetic and copies ran while one was open for 7% -> 7% of each run, Pallas kernels for 37% -> 47%
where the time goes in v7:
time: 467 us; the launch traced here: 461 us
  Pallas kernels  248 us (53%)
  waiting for transfers between devices  123 us (26%)
  local copies, waits for them, and re-layouts  27.5 us (6%)
  starting transfers between devices  26.6 us (6%)
  other arithmetic  19.3 us (4%)
  between operations  15.7 us (3%)
    pallas_call x2, Pallas kernels, front_products(): pl.pallas_call(functools.partial(front_kernel, subs, flats, n_col, len(af...  117 us
    ppermute x28, waiting for transfers between devices, exchange(): return lax.ppermute(value, axis, [(i, i ^ distance) for i in range(n)])  87.7 us
    pallas_call x4, Pallas kernels, product(): pl.pallas_call(functools.partial(product_kernel, streams, bool(bases)), g...  53.4 us
    pallas_call x3, Pallas kernels, pack_rows(): pl.pallas_call(functools.partial(pack_kernel, n_row, len(solved)), in_spe...  35.4 us
    reduce_scatter x5, waiting for transfers between devices, summed(): return lax.psum_scatter(parts, 'col', scatter_dimension=0)  34.5 us
    ppermute x28, starting transfers between devices, exchange(): return lax.ppermute(value, axis, [(i, i ^ distance) for i in range(n)])  26.2 us
    pallas_call x2, Pallas kernels, unpack(): pl.pallas_call(functools.partial(unpack_kernel, len(pieces), n_col, parts...  20.2 us
    unnamed x75, local copies, waits for them, and re-layouts  15.9 us
  transfers between devices with their start and end apart: 34, of which 17 were waited for; matrix products, arithmetic and copies ran while one was open for 7% of the time, Pallas kernels for 47%

profile of v7, /device:TPU:0, one launch (start us, length us, event | category | flops | bytes accessed | tf_op | source)
XLA Modules:
  0.0 460.8 jit_solution(3184355969212684090)
XLA Ops:
  10.8 55.3 %front_products.2 = (bf16[4,3072,128]{2,1,0:T(8,128)(2,1)}, bf16[4,3072,128]{2,1,0:T(8,128)(2,1)}) custom-call(s32[3,192]{1,0:T(4,128)} %pad_add_fusion.meta_ref, bf16[192,128,128]{2,1,0:T(8,128)(2,1)} %tiles_ref.3, bf16[3072,6144]{1,0:T(8,128)(2,1)} %front_ref.3), custom_call_target="tpu_custom_call" | custom-call | bytes 1 | tf_op jit(solution)/shard_map/front_products/pallas_call | solution.py:187
  66.9 61.5 %front_products.3 = (bf16[3072,512]{1,0:T(8,128)(2,1)}, bf16[3072,512]{1,0:T(8,128)(2,1)}) custom-call(s32[3,192]{1,0:T(4,128)} %pad_add_fusion.meta_ref, bf16[192,128,128]{2,1,0:T(8,128)(2,1)} %tiles_ref.3, bf16[3072,6144]{1,0:T(8,128)(2,1)} %front_ref.3, bf16[4,3072,128]{2,1,0:T(8,128)(2,1)} %get-tuple-element.19.refs_0_), custom_call_target="tpu_custom_call" | custom-call | bytes 1 | tf_op jit(solution)/shard_map/front_products/pallas_call | solution.py:187
  128.5 1.1 slice.119
  130.2 2.4 reduce-window.16
  133.3 6.2 %select_reduce_fusion = s32[8,384]{1,0:T(8,128)S(1)} fusion(s32[8,2048]{1,0:T(8,128)S(1)} %subtract_add_fusion, s32[8,2048]{1,0:T(8,128)S(1)} %bitcast.54, pred[8,2048]{1,0:T(8,128)(4,1)S(1)} %get-tuple-element.34), kind=kLoop, calls=%fused_computation.1 | loop fusion | flops 25162752 | bytes 159744 | tf_op jit(solution)/shard_map/reduce_sum | solution.py:459
  139.5 1.7 copy.44
  141.2 13.9 %pack_rows.3 = (bf16[1536,512]{1,0:T(8,128)(2,1)}, bf16[1536,512]{1,0:T(8,128)(2,1)}) custom-call(s32[3072,1]{1,0:T(8,128)} %bitcast.48, bf16[3072,512]{1,0:T(8,128)(2,1)} %get-tuple-element.21.refs_0_), custom_call_target="tpu_custom_call" | custom-call | bytes 1 | tf_op jit(solution)/shard_map/pack_rows/pallas_call | solution.py:232
  155.7 2.3 reduce-window.14
  159.7 2.2 fusion.8
  161.9 2.2 fusion.9
  164.2 2.6 collective-permute-start.1
  166.8 1.6 collective-permute-start.2
  168.6 1.2 fusion.3.index_ref
  169.8 13.4 %pack_rows.4 = (bf16[1536,512]{1,0:T(8,128)(2,1)}, bf16[1536,512]{1,0:T(8,128)(2,1)}) custom-call(s32[3072,1]{1,0:T(8,128)} %bitcast.49, bf16[3072,512]{1,0:T(8,128)(2,1)} %get-tuple-element.24.refs_0_, bf16[768,512]{1,0:T(8,128)(2,1)} %copy-done.6, bf16[768,512]{1,0:T(8,128)(2,1)} %copy-done.7, bf16[768,512]{1,0:T(8,128)(2,1)} %copy-done.8), custom_call_target="tpu_custom_call" | custom-call | bytes 1 | tf_op jit(solution)/shard_map/pack_rows/pallas_call | solution.py:232
  183.2 2.2 fusion.6
  185.5 18.0 %collective-permute-done.2.refs_3_ = bf16[768,512]{1,0:T(8,128)(2,1)S(1)} collective-permute-done((bf16[768,512]{1,0:T(8,128)(2,1)S(1)}, bf16[768,512]{1,0:T(8,128)(2,1)S(1)}, u32[]{:S(2)}, u32[]{:S(2)}) %collective-permute-start.2) | collective-permute-done | bytes 786464 | tf_op jit(solution)/shard_map/ppermute | solution.py:426
  203.4 0.9 copy-done.28
  204.6 10.4 %unpack.2.refs_2_ = bf16[4,2048,128]{2,1,0:T(8,128)(2,1)} custom-call(s32[2048,1]{1,0:T(8,128)} %fusion.3.index_ref, bf16[384,512]{1,0:T(8,128)(2,1)} %get-tuple-element.46.refs_0_, bf16[384,512]{1,0:T(8,128)(2,1)} %get-tuple-element.50.refs_1_, bf16[768,512]{1,0:T(8,128)(2,1)} %copy-done.26, bf16[768,512]{1,0:T(8,128)(2,1)} %copy-done.28, ...), custom_call_target="tpu_custom_call" | custom-call | flops 38654705664 | bytes 1 | tf_op jit(solution)/shard_map/unpack/pallas_call | solution.py:350
  215.0 0.9 fusion.7
  215.9 0.8 collective-permute-start.9
  216.8 1.3 collective-permute-start.10
  218.2 1.5 collective-permute-start.11
  219.7 8.1 %pack_rows.5 = (bf16[1536,256]{1,0:T(8,128)(2,1)}, bf16[1536,256]{1,0:T(8,128)(2,1)}) custom-call(s32[3072,1]{1,0:T(8,128)} %bitcast.50, bf16[3072,128]{1,0:T(8,128)(2,1)} %bitcast.69, bf16[3072,128]{1,0:T(8,128)(2,1)} %bitcast.68, bf16[4,2048,128]{2,1,0:T(8,128)(2,1)} %unpack.2.refs_2_), custom_call_target="tpu_custom_call" | custom-call | flops 28991029248 | bytes 1 | tf_op jit(solution)/shard_map/pack_rows/pallas_call | solution.py:232
  227.8 8.6 %collective-permute-done.9.refs_2_ = bf16[768,512]{1,0:T(8,128)(2,1)S(1)} collective-permute-done((bf16[768,512]{1,0:T(8,128)(2,1)S(1)}, bf16[768,512]{1,0:T(8,128)(2,1)S(1)}, u32[]{:S(2)}, u32[]{:S(2)}) %collective-permute-start.9) | collective-permute-done | bytes 786464 | tf_op jit(solution)/shard_map/ppermute | solution.py:426
  236.4 14.4 %collective-permute-done.10.refs_3_ = bf16[768,512]{1,0:T(8,128)(2,1)} collective-permute-done((bf16[768,512]{1,0:T(8,128)(2,1)S(1)}, bf16[768,512]{1,0:T(8,128)(2,1)}, u32[]{:S(2)}, u32[]{:S(2)}) %collective-permute-start.10) | collective-permute-done | bytes 786464 | tf_op jit(solution)/shard_map/ppermute | solution.py:426
  250.8 1.8 collective-permute-done.11.refs_4_
  252.7 9.9 %unpack.3 = (bf16[4,1024,128]{2,1,0:T(8,128)(2,1)}, bf16[4,1024,128]{2,1,0:T(8,128)(2,1)}) custom-call(s32[2048,1]{1,0:T(8,128)} %fusion.3.index_ref, bf16[384,512]{1,0:T(8,128)(2,1)} %get-tuple-element.38.refs_0_, bf16[384,512]{1,0:T(8,128)(2,1)} %get-tuple-element.42.refs_1_, bf16[768,512]{1,0:T(8,128)(2,1)} %copy-done.27, ...), custom_call_target="tpu_custom_call" | custom-call | flops 38654705664 | bytes 1 | tf_op jit(solution)/shard_map/unpack/pallas_call | solution.py:350
  264.7 1.3 collective-permute-done.4
  267.5 1.8 collective-permute-start.6
  269.3 1.1 collective-permute-start.7
  270.5 8.3 %collective-permute-done.5.refs_2_ = bf16[768,256]{1,0:T(8,128)(2,1)S(1)} collective-permute-done((bf16[768,256]{1,0:T(8,128)(2,1)S(1)}, bf16[768,256]{1,0:T(8,128)(2,1)S(1)}, u32[]{:S(2)}, u32[]{:S(2)}) %collective-permute-start.5) | collective-permute-done | bytes 393248 | tf_op jit(solution)/shard_map/ppermute | solution.py:426
  278.7 8.1 %collective-permute-done.6.refs_3_ = bf16[768,256]{1,0:T(8,128)(2,1)S(1)} collective-permute-done((bf16[768,256]{1,0:T(8,128)(2,1)S(1)}, bf16[768,256]{1,0:T(8,128)(2,1)S(1)}, u32[]{:S(2)}, u32[]{:S(2)}) %collective-permute-start.6) | collective-permute-done | bytes 393248 | tf_op jit(solution)/shard_map/ppermute | solution.py:426
  287.8 6.2 %assemble.1 = (bf16[1024,256]{1,0:T(8,128)(2,1)}, bf16[1024,256]{1,0:T(8,128)(2,1)}) custom-call(s32[2048,1]{1,0:T(8,128)} %fusion.3.index_ref, bf16[2,1024,512]{2,1,0:T(8,128)(2,1)} %bem_ref.5, bf16[384,256]{1,0:T(8,128)(2,1)} %get-tuple-element.54.refs_0_, bf16[384,256]{1,0:T(8,128)(2,1)} %get-tuple-element.58.refs_1_, bf16[768,256]{1,0:T(8,128)(2,1)} %copy-done.30, ...), custom_call_target="tpu_custom_call" | custom-call | flops 6442450944 | bytes 1 | tf_op jit(solution)/shard_map/assemble/pallas_call | solution.py:269
  294.0 1.5 collective-permute-start.14
  295.5 1.2 collective-permute-start.13
  296.7 0.8 collective-permute-start.12
  297.5 34.4 %reduce-scatter.10.cloned.1.call-done = bf16[1,2048,128]{2,1,0:T(8,128)(2,1)} async-done(((bf16[4,2048,128]{2,1,0:T(8,128)(2,1)}), bf16[1,2048,128]{2,1,0:T(8,128)(2,1)}) %reduce-scatter.10.cloned.1.call-update) | async-done | bytes 524304 | tf_op jit(solution)/shard_map/reduce_scatter | solution.py:498
  332.0 2.1 subtract.2.refs_4_.refs_6_.refs_0_
  335.0 0.8 copy-done.19
  335.8 3.0 join.4.refs_4_
  339.5 2.4 collective-permute-start.18
  343.2 1.3 copy-done.11
  344.5 13.4 %product.4.refs_4_.refs_6_.refs_0_ = bf16[1024,256]{1,0:T(8,128)(2,1)} custom-call(s32[8]{0:T(128)} %add_xor_fusion.order_ref, bf16[1024,8192]{1,0:T(8,128)(2,1)} %refs_3_.5, bf16[1024,8192]{1,0:T(8,128)(2,1)} %refs_3_.5, bf16[1024,8192]{1,0:T(8,128)(2,1)} %refs_3_.5, bf16[1024,8192]{1,0:T(8,128)(2,1)} %refs_3_.5, bf16[4096,256]{1,0:T(8,128)(2,1)} %join.4.refs_4_, ...), custom_call_target="tpu_custom_call" | custom-call | flops 12884901888 | bytes 1 | tf_op jit(solution)/shard_map/product/pallas_call | solution.py:406
  357.9 8.0 %collective-permute-done.17.refs_2_ = bf16[1024,256]{1,0:T(8,128)(2,1)S(1)} collective-permute-done((bf16[1024,256]{1,0:T(8,128)(2,1)S(1)}, bf16[1024,256]{1,0:T(8,128)(2,1)S(1)}, u32[]{:S(2)}, u32[]{:S(2)}) %collective-permute-start.17) | collective-permute-done | bytes 524320 | tf_op jit(solution)/shard_map/ppermute | solution.py:426
  366.8 0.8 copy-done.22
  367.6 3.0 join.5.refs_4_
  370.6 1.8 collective-permute-start.22
  372.4 1.2 collective-permute-start.21
  374.9 1.3 copy-done.9
  376.3 13.4 %product.5.refs_4_.refs_2_.refs_0_ = bf16[1024,256]{1,0:T(8,128)(2,1)} custom-call(s32[8]{0:T(128)} %add_xor_fusion.order_ref, bf16[1024,8192]{1,0:T(8,128)(2,1)} %refs_3_.5, bf16[1024,8192]{1,0:T(8,128)(2,1)} %refs_3_.5, bf16[1024,8192]{1,0:T(8,128)(2,1)} %refs_3_.5, bf16[1024,8192]{1,0:T(8,128)(2,1)} %refs_3_.5, bf16[4096,256]{1,0:T(8,128)(2,1)} %join.5.refs_4_, ...), custom_call_target="tpu_custom_call" | custom-call | flops 12884901888 | bytes 1 | tf_op jit(solution)/shard_map/product/pallas_call | solution.py:406
  389.7 7.4 %collective-permute-done.21.refs_2_ = bf16[1024,256]{1,0:T(8,128)(2,1)S(1)} collective-permute-done((bf16[1024,256]{1,0:T(8,128)(2,1)S(1)}, bf16[1024,256]{1,0:T(8,128)(2,1)S(1)}, u32[]{:S(2)}, u32[]{:S(2)}) %collective-permute-start.21) | collective-permute-done | bytes 524320 | tf_op jit(solution)/shard_map/ppermute | solution.py:426
  398.7 3.0 join.6.refs_4_
  401.7 1.7 collective-permute-start.26
  403.5 1.2 collective-permute-start.25
  405.2 2.1 subtract.3.refs_7_.refs_6_
  407.4 1.3 copy-done.10
  408.7 13.3 %product.6.refs_4_ = bf16[1024,256]{1,0:T(8,128)(2,1)} custom-call(s32[8]{0:T(128)} %add_xor_fusion.order_ref, bf16[1024,8192]{1,0:T(8,128)(2,1)} %refs_3_.7, bf16[1024,8192]{1,0:T(8,128)(2,1)} %refs_3_.7, bf16[1024,8192]{1,0:T(8,128)(2,1)} %refs_3_.7, bf16[1024,8192]{1,0:T(8,128)(2,1)} %refs_3_.7, bf16[4096,256]{1,0:T(8,128)(2,1)} %join.6.refs_4_, ...), custom_call_target="tpu_custom_call" | custom-call | flops 12884901888 | bytes 1 | tf_op jit(solution)/shard_map/product/pallas_call | solution.py:406
  422.1 6.2 %collective-permute-done.25.refs_2_ = bf16[1024,256]{1,0:T(8,128)(2,1)} collective-permute-done((bf16[1024,256]{1,0:T(8,128)(2,1)S(1)}, bf16[1024,256]{1,0:T(8,128)(2,1)}, u32[]{:S(2)}, u32[]{:S(2)}) %collective-permute-start.25) | collective-permute-done | bytes 524320 | tf_op jit(solution)/shard_map/ppermute | solution.py:426
  428.4 3.0 join.7.refs_4_
  431.4 4.3 collective-permute-done.27.refs_5_
  435.7 1.3 copy-done.12
  437.0 13.3 %product.7 = bf16[1024,256]{1,0:T(8,128)(2,1)} custom-call(s32[8]{0:T(128)} %add_xor_fusion.order_ref, bf16[1024,8192]{1,0:T(8,128)(2,1)} %refs_3_.7, bf16[1024,8192]{1,0:T(8,128)(2,1)} %refs_3_.7, bf16[1024,8192]{1,0:T(8,128)(2,1)} %refs_3_.7, bf16[1024,8192]{1,0:T(8,128)(2,1)} %refs_3_.7, bf16[4096,256]{1,0:T(8,128)(2,1)} %join.7.refs_4_, ...), custom_call_target="tpu_custom_call" | custom-call | flops 12884901888 | bytes 1 | tf_op jit(solution)/shard_map/product/pallas_call | solution.py:406
  450.3 1.1 maximum_bitcast_fusion.1
  451.5 1.5 pad_maximum_fusion
  (154 shorter events, 20.5 us)
Async XLA Ops:
  7.4 121.1 %all-gather.2.cloned.1.call-start = ((), (), s32[]{:S(2)}) async-start(), calls=%async_computation.5 | async-start | bytes 2359296 | tf_op jit(solution)/shard_map/all_gather | solution.py:452
  8.8 210.9 %reduce-scatter.8.cloned.1.call-start = ((), (), s32[]{:S(2)}) async-start(), calls=%async_computation.7 | async-start | bytes 3932160 | tf_op jit(solution)/shard_map/reduce_scatter | solution.py:498
  66.2 153.5 %reduce-scatter.6.cloned.1.call-start = ((), (), s32[]{:S(2)}) async-start(), calls=%async_computation.6 | async-start | bytes 3932160 | tf_op jit(solution)/shard_map/reduce_scatter | solution.py:498
  66.8 230.7 %reduce-scatter.12.cloned.1.call-start = ((), (), s32[]{:S(2)}) async-start(), calls=%async_computation.9 | async-start | bytes 1310720 | tf_op jit(solution)/shard_map/reduce_scatter | solution.py:498
  155.0 6.9 %collective-permute-start = (bf16[1536,512]{1,0:T(8,128)(2,1)}, bf16[1536,512]{1,0:T(8,128)(2,1)}, u32[]{:S(2)}, u32[]{:S(2)}) collective-permute-start(bf16[1536,512]{1,0:T(8,128)(2,1)} %get-tuple-element.23), channel_id=1, source_target_pairs={{0,4},{4,0},{8,12},{12,8},{16,20},{20,16},{24,28},{28,24},{1,5},{5... | collective-permute-start | bytes 4718600 | tf_op jit(solution)/shard_map/ppermute | solution.py:426
  164.2 5.6 %copy-start.6 = (bf16[768,512]{1,0:T(8,128)(2,1)}, bf16[768,512]{1,0:T(8,128)(2,1)S(1)}, u32[]{:S(2)}) copy-start(bf16[768,512]{1,0:T(8,128)(2,1)S(1)} %pad_maximum_fusion.1.refs_1_) | copy-start | bytes 2359300
  164.2 21.3 %collective-permute-start.1 = (bf16[768,512]{1,0:T(8,128)(2,1)S(1)}, bf16[768,512]{1,0:T(8,128)(2,1)S(1)}, u32[]{:S(2)}, u32[]{:S(2)}) collective-permute-start(bf16[768,512]{1,0:T(8,128)(2,1)S(1)} %pad_maximum_fusion.1.refs_1_), channel_id=1, source_target_pairs={{0,8},{4,12},{8,0},{12,4},{16,24},{20,28},{24,16},{28,20},{1,9},{5... | collective-permute-start | bytes 2359304 | tf_op jit(solution)/shard_map/ppermute | solution.py:426
  166.8 3.0 copy-start.7
  166.8 36.6 %collective-permute-start.2 = (bf16[768,512]{1,0:T(8,128)(2,1)S(1)}, bf16[768,512]{1,0:T(8,128)(2,1)S(1)}, u32[]{:S(2)}, u32[]{:S(2)}) collective-permute-start(bf16[768,512]{1,0:T(8,128)(2,1)S(1)} %pad_maximum_fusion.2.refs_2_), channel_id=1, source_target_pairs={{0,16},{4,20},{8,24},{12,28},{16,0},{20,4},{24,8},{28,12},{1,17},{... | collective-permute-start | bytes 2359304 | tf_op jit(solution)/shard_map/ppermute | solution.py:426
  168.5 1.3 copy-start.8
  168.5 34.9 %collective-permute-start.3 = (bf16[768,512]{1,0:T(8,128)(2,1)S(1)}, bf16[768,512]{1,0:T(8,128)(2,1)S(1)}, u32[]{:S(2)}, u32[]{:S(2)}) collective-permute-start(bf16[768,512]{1,0:T(8,128)(2,1)S(1)} %pad_maximum_fusion.3.refs_3_), channel_id=1, source_target_pairs={{0,24},{4,28},{8,16},{12,20},{16,8},{20,12},{24,0},{28,4},{1,25},{... | collective-permute-start | bytes 2359304 | tf_op jit(solution)/shard_map/ppermute | solution.py:426
  183.2 31.7 %collective-permute-start.8 = (bf16[1536,512]{1,0:T(8,128)(2,1)}, bf16[1536,512]{1,0:T(8,128)(2,1)S(1)}, u32[]{:S(2)}, u32[]{:S(2)}) collective-permute-start(bf16[1536,512]{1,0:T(8,128)(2,1)} %get-tuple-element.28), channel_id=1, source_target_pairs={{0,4},{4,0},{8,12},{12,8},{16,20},{20,16},{24,28},{28,24},{1,5},{5... | collective-permute-start | bytes 4718600 | tf_op jit(solution)/shard_map/ppermute | solution.py:426
  185.5 18.0 %copy-start.26 = (bf16[768,512]{1,0:T(8,128)(2,1)}, bf16[768,512]{1,0:T(8,128)(2,1)S(1)}, u32[]{:S(2)}) copy-start(bf16[768,512]{1,0:T(8,128)(2,1)S(1)} %collective-permute-done.1.refs_2_) | copy-start | bytes 2359300
  203.4 0.9 copy-start.28
  203.4 1.2 copy-start.29
  215.9 20.5 %collective-permute-start.9 = (bf16[768,512]{1,0:T(8,128)(2,1)S(1)}, bf16[768,512]{1,0:T(8,128)(2,1)S(1)}, u32[]{:S(2)}, u32[]{:S(2)}) collective-permute-start(bf16[768,512]{1,0:T(8,128)(2,1)S(1)} %pad_maximum_fusion.4), channel_id=1, source_target_pairs={{0,8},{4,12},{8,0},{12,4},{16,24},{20,28},{24,16},{28,20},{1,9},{5... | collective-permute-start | bytes 2359304 | tf_op jit(solution)/shard_map/ppermute | solution.py:426
  216.8 34.0 %collective-permute-start.10 = (bf16[768,512]{1,0:T(8,128)(2,1)S(1)}, bf16[768,512]{1,0:T(8,128)(2,1)}, u32[]{:S(2)}, u32[]{:S(2)}) collective-permute-start(bf16[768,512]{1,0:T(8,128)(2,1)S(1)} %pad_maximum_fusion.5), channel_id=1, source_target_pairs={{0,16},{4,20},{8,24},{12,28},{16,0},{20,4},{24,8},{28,12},{1,17},{... | collective-permute-start | bytes 2359304 | tf_op jit(solution)/shard_map/ppermute | solution.py:426
  218.2 34.5 %collective-permute-start.11 = (bf16[768,512]{1,0:T(8,128)(2,1)S(1)}, bf16[768,512]{1,0:T(8,128)(2,1)}, u32[]{:S(2)}, u32[]{:S(2)}) collective-permute-start(bf16[768,512]{1,0:T(8,128)(2,1)S(1)} %pad_maximum_fusion.6), channel_id=1, source_target_pairs={{0,24},{4,28},{8,16},{12,20},{16,8},{20,12},{24,0},{28,4},{1,25},{... | collective-permute-start | bytes 2359304 | tf_op jit(solution)/shard_map/ppermute | solution.py:426
  236.4 16.2 %copy-start.27 = (bf16[768,512]{1,0:T(8,128)(2,1)}, bf16[768,512]{1,0:T(8,128)(2,1)S(1)}, u32[]{:S(2)}) copy-start(bf16[768,512]{1,0:T(8,128)(2,1)S(1)} %collective-permute-done.9.refs_2_) | copy-start | bytes 2359300
  262.5 1.1 copy-start.25
  262.5 1.4 copy-start.13
  262.6 69.4 %reduce-scatter.10.cloned.1.call-start = ((), (), s32[]{:S(2)}) async-start(), calls=%async_computation.8 | async-start | bytes 2621440 | tf_op jit(solution)/shard_map/reduce_scatter | solution.py:498
  263.3 141.9 %reduce-scatter.14.cloned.1.call-start = ((), (), s32[]{:S(2)}) async-start(), calls=%async_computation.10 | async-start | bytes 1310720 | tf_op jit(solution)/shard_map/reduce_scatter | solution.py:498
  263.7 2.3 collective-permute-start.4
  266.7 12.0 %collective-permute-start.5 = (bf16[768,256]{1,0:T(8,128)(2,1)S(1)}, bf16[768,256]{1,0:T(8,128)(2,1)S(1)}, u32[]{:S(2)}, u32[]{:S(2)}) collective-permute-start(bf16[768,256]{1,0:T(8,128)(2,1)S(1)} %pad_maximum_fusion.7), channel_id=1, source_target_pairs={{0,8},{4,12},{8,0},{12,4},{16,24},{20,28},{24,16},{28,20},{1,9},{5... | collective-permute-start | bytes 1179656 | tf_op jit(solution)/shard_map/ppermute | solution.py:426
  267.5 19.4 %collective-permute-start.6 = (bf16[768,256]{1,0:T(8,128)(2,1)S(1)}, bf16[768,256]{1,0:T(8,128)(2,1)S(1)}, u32[]{:S(2)}, u32[]{:S(2)}) collective-permute-start(bf16[768,256]{1,0:T(8,128)(2,1)S(1)} %pad_maximum_fusion.8), channel_id=1, source_target_pairs={{0,16},{4,20},{8,24},{12,28},{16,0},{20,4},{24,8},{28,12},{1,17},{... | collective-permute-start | bytes 1179656 | tf_op jit(solution)/shard_map/ppermute | solution.py:426
  269.3 17.5 %collective-permute-start.7 = (bf16[768,256]{1,0:T(8,128)(2,1)S(1)}, bf16[768,256]{1,0:T(8,128)(2,1)S(1)}, u32[]{:S(2)}, u32[]{:S(2)}) collective-permute-start(bf16[768,256]{1,0:T(8,128)(2,1)S(1)} %pad_maximum_fusion.9), channel_id=1, source_target_pairs={{0,24},{4,28},{8,16},{12,20},{16,8},{20,12},{24,0},{28,4},{1,25},{... | collective-permute-start | bytes 1179656 | tf_op jit(solution)/shard_map/ppermute | solution.py:426
  278.7 8.1 %copy-start.30 = (bf16[768,256]{1,0:T(8,128)(2,1)}, bf16[768,256]{1,0:T(8,128)(2,1)S(1)}, u32[]{:S(2)}) copy-start(bf16[768,256]{1,0:T(8,128)(2,1)S(1)} %collective-permute-done.5.refs_2_) | copy-start | bytes 1179652
  286.9 0.9 copy-start.32
  294.0 40.1 %collective-permute-start.14 = (bf16[1024,256]{1,0:T(8,128)(2,1)}, bf16[1024,256]{1,0:T(8,128)(2,1)S(1)}, u32[]{:S(2)}, u32[]{:S(2)}) collective-permute-start(bf16[1024,256]{1,0:T(8,128)(2,1)} %get-tuple-element.30.refs_2_.refs_0_), channel_id=1, source_target_pairs={{0,24},{4,28},{8,16},{12,20},{16,8},{20,12},{24,0},{28,4},{1,25},{... | collective-permute-start | bytes 1572872 | tf_op jit(solution)/shard_map/ppermute | solution.py:426
  295.5 38.6 %collective-permute-start.13 = (bf16[1024,256]{1,0:T(8,128)(2,1)}, bf16[1024,256]{1,0:T(8,128)(2,1)S(1)}, u32[]{:S(2)}, u32[]{:S(2)}) collective-permute-start(bf16[1024,256]{1,0:T(8,128)(2,1)} %get-tuple-element.30.refs_2_.refs_0_), channel_id=1, source_target_pairs={{0,16},{4,20},{8,24},{12,28},{16,0},{20,4},{24,8},{28,12},{1,17},{... | collective-permute-start | bytes 1572872 | tf_op jit(solution)/shard_map/ppermute | solution.py:426
  296.7 37.4 %collective-permute-start.12 = (bf16[1024,256]{1,0:T(8,128)(2,1)}, bf16[1024,256]{1,0:T(8,128)(2,1)S(1)}, u32[]{:S(2)}, u32[]{:S(2)}) collective-permute-start(bf16[1024,256]{1,0:T(8,128)(2,1)} %get-tuple-element.30.refs_2_.refs_0_), channel_id=1, source_target_pairs={{0,8},{4,12},{8,0},{12,4},{16,24},{20,28},{24,16},{28,20},{1,9},{5... | collective-permute-start | bytes 1572872 | tf_op jit(solution)/shard_map/ppermute | solution.py:426
  334.1 5.4 %copy-start.4 = (bf16[1024,256]{1,0:T(8,128)(2,1)S(1)}, bf16[1024,256]{1,0:T(8,128)(2,1)}, u32[]{:S(2)}) copy-start(bf16[1024,256]{1,0:T(8,128)(2,1)} %subtract.2.refs_4_.refs_6_.refs_0_) | copy-start | bytes 1572868
  334.1 1.0 copy-start.16
  335.0 0.8 copy-start.19
  338.8 4.4 collective-permute-start.15
  339.5 18.4 %collective-permute-start.18 = (bf16[1024,256]{1,0:T(8,128)(2,1)S(1)}, bf16[1024,256]{1,0:T(8,128)(2,1)S(1)}, u32[]{:S(2)}, u32[]{:S(2)}) collective-permute-start(bf16[1024,256]{1,0:T(8,128)(2,1)S(1)} %copy-done.4), channel_id=1, source_target_pairs={{0,24},{4,28},{8,16},{12,20},{16,8},{20,12},{24,0},{28,4},{1,25},{... | collective-permute-start | bytes 1572872 | tf_op jit(solution)/shard_map/ppermute | solution.py:426
  341.9 24.1 %collective-permute-start.17 = (bf16[1024,256]{1,0:T(8,128)(2,1)S(1)}, bf16[1024,256]{1,0:T(8,128)(2,1)S(1)}, u32[]{:S(2)}, u32[]{:S(2)}) collective-permute-start(bf16[1024,256]{1,0:T(8,128)(2,1)S(1)} %copy-done.4), channel_id=1, source_target_pairs={{0,16},{4,20},{8,24},{12,28},{16,0},{20,4},{24,8},{28,12},{1,17},{... | collective-permute-start | bytes 1572872 | tf_op jit(solution)/shard_map/ppermute | solution.py:426
  342.4 23.6 %collective-permute-start.16 = (bf16[1024,256]{1,0:T(8,128)(2,1)S(1)}, bf16[1024,256]{1,0:T(8,128)(2,1)S(1)}, u32[]{:S(2)}, u32[]{:S(2)}) collective-permute-start(bf16[1024,256]{1,0:T(8,128)(2,1)S(1)} %copy-done.4), channel_id=1, source_target_pairs={{0,8},{4,12},{8,0},{12,4},{16,24},{20,28},{24,16},{28,20},{1,9},{5... | collective-permute-start | bytes 1572872 | tf_op jit(solution)/shard_map/ppermute | solution.py:426
  343.2 1.3 copy-start.11
  357.9 12.7 %copy-start = (bf16[1024,256]{1,0:T(8,128)(2,1)S(1)}, bf16[1024,256]{1,0:T(8,128)(2,1)}, u32[]{:S(2)}) copy-start(bf16[1024,256]{1,0:T(8,128)(2,1)} %product.4.refs_4_.refs_6_.refs_0_) | copy-start | bytes 1572868
  357.9 8.1 %copy-start.17 = (bf16[1024,256]{1,0:T(8,128)(2,1)}, bf16[1024,256]{1,0:T(8,128)(2,1)S(1)}, u32[]{:S(2)}) copy-start(bf16[1024,256]{1,0:T(8,128)(2,1)S(1)} %collective-permute-done.18.refs_3_) | copy-start | bytes 1572868
  366.0 0.8 copy-start.20
  366.8 0.8 copy-start.22
  370.5 4.4 collective-permute-start.19
  370.6 19.1 %collective-permute-start.22 = (bf16[1024,256]{1,0:T(8,128)(2,1)S(1)}, bf16[1024,256]{1,0:T(8,128)(2,1)S(1)}, u32[]{:S(2)}, u32[]{:S(2)}) collective-permute-start(bf16[1024,256]{1,0:T(8,128)(2,1)S(1)} %copy-done), channel_id=1, source_target_pairs={{0,24},{4,28},{8,16},{12,20},{16,8},{20,12},{24,0},{28,4},{1,25},{... | collective-permute-start | bytes 1572872 | tf_op jit(solution)/shard_map/ppermute | solution.py:426
  372.4 24.7 %collective-permute-start.21 = (bf16[1024,256]{1,0:T(8,128)(2,1)S(1)}, bf16[1024,256]{1,0:T(8,128)(2,1)S(1)}, u32[]{:S(2)}, u32[]{:S(2)}) collective-permute-start(bf16[1024,256]{1,0:T(8,128)(2,1)S(1)} %copy-done), channel_id=1, source_target_pairs={{0,16},{4,20},{8,24},{12,28},{16,0},{20,4},{24,8},{28,12},{1,17},{... | collective-permute-start | bytes 1572872 | tf_op jit(solution)/shard_map/ppermute | solution.py:426
  373.6 23.6 %collective-permute-start.20 = (bf16[1024,256]{1,0:T(8,128)(2,1)S(1)}, bf16[1024,256]{1,0:T(8,128)(2,1)S(1)}, u32[]{:S(2)}, u32[]{:S(2)}) collective-permute-start(bf16[1024,256]{1,0:T(8,128)(2,1)S(1)} %copy-done), channel_id=1, source_target_pairs={{0,8},{4,12},{8,0},{12,4},{16,24},{20,28},{24,16},{28,20},{1,9},{5... | collective-permute-start | bytes 1572872 | tf_op jit(solution)/shard_map/ppermute | solution.py:426
  374.9 1.3 copy-start.9
  389.7 12.1 %copy-start.2 = (bf16[1024,256]{1,0:T(8,128)(2,1)S(1)}, bf16[1024,256]{1,0:T(8,128)(2,1)}, u32[]{:S(2)}) copy-start(bf16[1024,256]{1,0:T(8,128)(2,1)} %product.5.refs_4_.refs_2_.refs_0_) | copy-start | bytes 1572868
  389.7 7.5 %copy-start.18 = (bf16[1024,256]{1,0:T(8,128)(2,1)}, bf16[1024,256]{1,0:T(8,128)(2,1)S(1)}, u32[]{:S(2)}) copy-start(bf16[1024,256]{1,0:T(8,128)(2,1)S(1)} %collective-permute-done.22.refs_3_) | copy-start | bytes 1572868
  397.1 0.8 copy-start.21
  397.9 0.8 copy-start.23
  401.7 5.7 %collective-permute-start.23 = (bf16[4096,256]{1,0:T(8,128)(2,1)}, bf16[4096,256]{1,0:T(8,128)(2,1)S(1)}, u32[]{:S(2)}, u32[]{:S(2)}) collective-permute-start(bf16[4096,256]{1,0:T(8,128)(2,1)} %join.6.refs_4_), channel_id=1, source_target_pairs={{0,4},{4,0},{8,12},{12,8},{16,20},{20,16},{24,28},{28,24},{1,5},{5... | collective-permute-start | bytes 6291464 | tf_op jit(solution)/shard_map/ppermute | solution.py:426
  401.7 20.3 %collective-permute-start.26 = (bf16[1024,256]{1,0:T(8,128)(2,1)S(1)}, bf16[1024,256]{1,0:T(8,128)(2,1)S(1)}, u32[]{:S(2)}, u32[]{:S(2)}) collective-permute-start(bf16[1024,256]{1,0:T(8,128)(2,1)S(1)} %copy-done.2), channel_id=1, source_target_pairs={{0,24},{4,28},{8,16},{12,20},{16,8},{20,12},{24,0},{28,4},{1,25},{... | collective-permute-start | bytes 1572872 | tf_op jit(solution)/shard_map/ppermute | solution.py:426
  403.5 24.8 %collective-permute-start.25 = (bf16[1024,256]{1,0:T(8,128)(2,1)S(1)}, bf16[1024,256]{1,0:T(8,128)(2,1)}, u32[]{:S(2)}, u32[]{:S(2)}) collective-permute-start(bf16[1024,256]{1,0:T(8,128)(2,1)S(1)} %copy-done.2), channel_id=1, source_target_pairs={{0,16},{4,20},{8,24},{12,28},{16,0},{20,4},{24,8},{28,12},{1,17},{... | collective-permute-start | bytes 1572872 | tf_op jit(solution)/shard_map/ppermute | solution.py:426
  404.7 23.7 %collective-permute-start.24 = (bf16[1024,256]{1,0:T(8,128)(2,1)S(1)}, bf16[1024,256]{1,0:T(8,128)(2,1)}, u32[]{:S(2)}, u32[]{:S(2)}) collective-permute-start(bf16[1024,256]{1,0:T(8,128)(2,1)S(1)} %copy-done.2), channel_id=1, source_target_pairs={{0,8},{4,12},{8,0},{12,4},{16,24},{20,28},{24,16},{28,20},{1,9},{5... | collective-permute-start | bytes 1572872 | tf_op jit(solution)/shard_map/ppermute | solution.py:426
  407.4 1.3 copy-start.10
  422.0 9.3 %copy-start.1 = (bf16[1024,256]{1,0:T(8,128)(2,1)S(1)}, bf16[1024,256]{1,0:T(8,128)(2,1)}, u32[]{:S(2)}) copy-start(bf16[1024,256]{1,0:T(8,128)(2,1)} %product.4.refs_4_.refs_6_.refs_0_) | copy-start | bytes 1572868
  422.0 9.3 %copy-start.3 = (bf16[1024,256]{1,0:T(8,128)(2,1)S(1)}, bf16[1024,256]{1,0:T(8,128)(2,1)}, u32[]{:S(2)}) copy-start(bf16[1024,256]{1,0:T(8,128)(2,1)} %product.5.refs_4_.refs_2_.refs_0_) | copy-start | bytes 1572868
  422.0 6.3 %copy-start.14 = (bf16[1024,256]{1,0:T(8,128)(2,1)}, bf16[1024,256]{1,0:T(8,128)(2,1)S(1)}, u32[]{:S(2)}) copy-start(bf16[1024,256]{1,0:T(8,128)(2,1)S(1)} %collective-permute-done.26.refs_3_) | copy-start | bytes 1572868
  431.3 4.4 collective-permute-start.27
  431.4 18.9 %copy-start.5 = (bf16[1024,256]{1,0:T(8,128)(2,1)S(1)}, bf16[1024,256]{1,0:T(8,128)(2,1)}, u32[]{:S(2)}) copy-start(bf16[1024,256]{1,0:T(8,128)(2,1)} %product.6.refs_4_) | copy-start | bytes 1572868
  435.7 1.3 copy-start.12
  (3 other events, 2.3 us)
Sparse Core Ops, SparseCore 0:
  10.1 30.5 all-gather.1
Sparse Core Ops, SparseCore 1:
  66.3 64.9 reduce-scatter.7
  133.4 60.1 reduce-scatter.5
  262.7 24.7 reduce-scatter.11
  289.9 42.0 reduce-scatter.9
  370.7 25.9 reduce-scatter.13

commit v8 on v5

--- a/solution.py
+++ b/solution.py
@@ -9,6 +9,7 @@
 
 TILE = 128
 STACK = 4
+REPEATS = 32
 VMEM_BYTES = 56 * 1024 * 1024
 
 
@@ -295,6 +296,33 @@
     )(bem, *parts, *after)
 
 
+def finish_kernel(ready, ready_ref, bem_ref, schur_ref, *refs):
+    out = refs[-1]
+    out[:, :ready] = ready_ref[...]
+    taken = schur_ref[...].astype(jnp.float32)
+    out[:, ready:] = (bem_ref[0].astype(jnp.float32) - taken).astype(out.dtype)
+
+
+def finish(ready, bem, schur, half, after=()):
+    (count, width), last = ready.shape, schur.shape[1]
+    place = bem.shape[2] // last - 1
+    return pl.pallas_call(
+        functools.partial(finish_kernel, width),
+        grid=(1,),
+        in_specs=[
+            whole_block(count, width),
+            pl.BlockSpec((1, count, last), lambda i: (half, 0, place)),
+            whole_block(count, last),
+        ]
+        + [in_place()] * len(after),
+        out_specs=whole_block(count, width + last),
+        out_shape=jax.ShapeDtypeStruct((count, width + last), bem.dtype),
+        compiler_params=kernel_params(),
+        cost_estimate=declared(),
+        name="finish",
+    )(ready, bem, schur, *after)
+
+
 def join_kernel(n_parts, *refs):
     join_pieces(refs[:n_parts], refs[-1])
 
@@ -429,7 +457,8 @@
 def route_tables(surface_map, rows, n_row, cap, slots):
     me = lax.axis_index("row")
     mine = surface_map.reshape(-1)
-    every = lax.all_gather(mine, "row")
+    shifts = jnp.arange(REPEATS, dtype=jnp.int32)[:, None]
+    every = lax.all_gather(mine[None, :] + shifts, "row")[:, 0]
     partners = me ^ jnp.arange(n_row, dtype=jnp.int32)
     local = every[partners] - me * rows
     asked = (local >= 0) & (local < rows)
@@ -506,7 +535,8 @@
 
     upper, lower = assemble(lands, bem_entries, route(packed, n_row)[0], 0, after)
     first = gather_rows(upper, n_row)
-    upper = subtract(bem_entries, uppers, 0, half, (upper,))
+    upper = subtract(bem_entries, uppers[:-1], 0, half, (upper,))
+    upper = finish(upper, bem_entries, uppers[-1], 0)
     second = gather_rows(upper, n_row)
     near, far = both_cores(join(first, (upper,)), n_row)
     pivots = [product(pivot_inverse, order, near, far, after=(upper,))]

time: 426 us -> 422 us (level)
  blocking collectives: 10.7 us -> 0 us
    all_gather x1 -> x0, blocking collectives: 10.7 us -> none  [route_tables(): every = lax.all_gather(mine, 'row')]
    unnamed x73 -> x69, local copies, waits for them, and re-layouts: 15 us -> 13.8 us
  transfers between devices with their start and end apart: 33 -> 34, of which waited for: 15 -> 19; matrix products, arithmetic and copies ran while one was open for 7% -> 8% of each run, Pallas kernels for 37% -> 49%
where the time goes in v8:
time: 422 us; the launch traced here: 415 us
  Pallas kernels  226 us (54%)
  waiting for transfers between devices  100 us (24%)
  starting transfers between devices  26.7 us (6%)
  local copies, waits for them, and re-layouts  26.7 us (6%)
  other arithmetic  20.1 us (5%)
  between operations  15.7 us (4%)
    ppermute x28, waiting for transfers between devices, exchange(): return lax.ppermute(value, axis, [(i, i ^ distance) for i in range(n)])  98.6 us
    pallas_call x2, Pallas kernels, front_products(): pl.pallas_call(functools.partial(front_kernel, subs, flats, n_col, len(af...  93 us
    pallas_call x4, Pallas kernels, product(): pl.pallas_call(functools.partial(product_kernel, streams, bool(bases)), g...  53.5 us
    pallas_call x3, Pallas kernels, pack_rows(): pl.pallas_call(functools.partial(pack_kernel, n_row, len(solved)), in_spe...  35.4 us
    ppermute x28, starting transfers between devices, exchange(): return lax.ppermute(value, axis, [(i, i ^ distance) for i in range(n)])  26.2 us
    pallas_call x2, Pallas kernels, unpack(): pl.pallas_call(functools.partial(unpack_kernel, len(pieces), n_col, parts...  20.2 us
    unnamed x69, local copies, waits for them, and re-layouts  13.8 us
    pallas_call x4, Pallas kernels, join(): pl.pallas_call(functools.partial(join_kernel, len(parts)), in_specs=[whol...  11.9 us
  transfers between devices with their start and end apart: 34, of which 19 were waited for; matrix products, arithmetic and copies ran while one was open for 8% of the time, Pallas kernels for 49%

profile of v8, /device:TPU:0, one launch (start us, length us, event | category | flops | bytes accessed | tf_op | source)
XLA Modules:
  0.0 415.5 jit_solution(11602878008262538044)
XLA Ops:
  10.8 46.4 %front_products.2 = (bf16[4,3072,128]{2,1,0:T(8,128)(2,1)}, bf16[4,3072,128]{2,1,0:T(8,128)(2,1)}) custom-call(s32[3,192]{1,0:T(4,128)} %pad_add_fusion.meta_ref, bf16[192,128,128]{2,1,0:T(8,128)(2,1)} %tiles_ref.3, bf16[3072,6144]{1,0:T(8,128)(2,1)} %front_ref.3), custom_call_target="tpu_custom_call" | custom-call | bytes 1 | tf_op jit(solution)/shard_map/front_products/pallas_call | solution.py:171
  58.0 46.6 %front_products.3 = (bf16[3072,512]{1,0:T(8,128)(2,1)}, bf16[3072,512]{1,0:T(8,128)(2,1)}) custom-call(s32[3,192]{1,0:T(4,128)} %pad_add_fusion.meta_ref, bf16[192,128,128]{2,1,0:T(8,128)(2,1)} %tiles_ref.3, bf16[3072,6144]{1,0:T(8,128)(2,1)} %front_ref.3, bf16[4,3072,128]{2,1,0:T(8,128)(2,1)} %get-tuple-element.19.refs_0_), custom_call_target="tpu_custom_call" | custom-call | bytes 1 | tf_op jit(solution)/shard_map/front_products/pallas_call | solution.py:171
  104.7 1.1 slice.119
  106.4 2.4 reduce-window.16
  109.5 6.2 %select_reduce_fusion = s32[8,384]{1,0:T(8,128)S(1)} fusion(s32[8,2048]{1,0:T(8,128)S(1)} %subtract_add_fusion, s32[8,2048]{1,0:T(8,128)S(1)} %bitcast.55, pred[8,2048]{1,0:T(8,128)(4,1)S(1)} %get-tuple-element.34), kind=kLoop, calls=%fused_computation.1 | loop fusion | flops 25162752 | bytes 159744 | tf_op jit(solution)/shard_map/reduce_sum | solution.py:468
  115.7 1.7 copy.44
  117.4 13.9 %pack_rows.3 = (bf16[1536,512]{1,0:T(8,128)(2,1)}, bf16[1536,512]{1,0:T(8,128)(2,1)}) custom-call(s32[3072,1]{1,0:T(8,128)} %bitcast.48, bf16[3072,512]{1,0:T(8,128)(2,1)} %get-tuple-element.21.refs_0_), custom_call_target="tpu_custom_call" | custom-call | bytes 1 | tf_op jit(solution)/shard_map/pack_rows/pallas_call | solution.py:214
  131.9 2.3 reduce-window.14
  136.0 2.2 fusion.8
  138.2 2.2 fusion.9
  140.5 2.6 collective-permute-start.1
  143.1 1.6 collective-permute-start.2
  144.9 1.2 fusion.3.index_ref
  146.1 13.4 %pack_rows.4 = (bf16[1536,512]{1,0:T(8,128)(2,1)}, bf16[1536,512]{1,0:T(8,128)(2,1)}) custom-call(s32[3072,1]{1,0:T(8,128)} %bitcast.49, bf16[3072,512]{1,0:T(8,128)(2,1)} %get-tuple-element.24.refs_0_, bf16[768,512]{1,0:T(8,128)(2,1)} %copy-done.6, bf16[768,512]{1,0:T(8,128)(2,1)} %copy-done.7, bf16[768,512]{1,0:T(8,128)(2,1)} %copy-done.8), custom_call_target="tpu_custom_call" | custom-call | bytes 1 | tf_op jit(solution)/shard_map/pack_rows/pallas_call | solution.py:214
  159.6 2.2 fusion.6
  161.8 18.0 %collective-permute-done.2.refs_3_ = bf16[768,512]{1,0:T(8,128)(2,1)S(1)} collective-permute-done((bf16[768,512]{1,0:T(8,128)(2,1)S(1)}, bf16[768,512]{1,0:T(8,128)(2,1)S(1)}, u32[]{:S(2)}, u32[]{:S(2)}) %collective-permute-start.2) | collective-permute-done | bytes 786464 | tf_op jit(solution)/shard_map/ppermute | solution.py:435
  179.8 1.0 copy-done.25
  181.0 10.4 %unpack.2.refs_2_ = bf16[4,2048,128]{2,1,0:T(8,128)(2,1)} custom-call(s32[2048,1]{1,0:T(8,128)} %fusion.3.index_ref, bf16[384,512]{1,0:T(8,128)(2,1)} %get-tuple-element.46.refs_0_, bf16[384,512]{1,0:T(8,128)(2,1)} %get-tuple-element.50.refs_1_, bf16[768,512]{1,0:T(8,128)(2,1)} %copy-done.24, bf16[768,512]{1,0:T(8,128)(2,1)} %copy-done.25, ...), custom_call_target="tpu_custom_call" | custom-call | flops 38654705664 | bytes 1 | tf_op jit(solution)/shard_map/unpack/pallas_call | solution.py:359
  192.3 0.9 collective-permute-start.9
  193.3 1.3 collective-permute-start.10
  194.6 0.9 pad_maximum_fusion.6
  195.5 1.4 collective-permute-start.11
  196.9 8.1 %pack_rows.5 = (bf16[1536,256]{1,0:T(8,128)(2,1)}, bf16[1536,256]{1,0:T(8,128)(2,1)}) custom-call(s32[3072,1]{1,0:T(8,128)} %bitcast.50, bf16[3072,128]{1,0:T(8,128)(2,1)} %bitcast.69, bf16[3072,128]{1,0:T(8,128)(2,1)} %bitcast.68, bf16[4,2048,128]{2,1,0:T(8,128)(2,1)} %unpack.2.refs_2_), custom_call_target="tpu_custom_call" | custom-call | flops 28991029248 | bytes 1 | tf_op jit(solution)/shard_map/pack_rows/pallas_call | solution.py:214
  205.1 2.0 fusion.10
  207.0 6.0 %collective-permute-done.9.refs_2_ = bf16[768,512]{1,0:T(8,128)(2,1)} collective-permute-done((bf16[768,512]{1,0:T(8,128)(2,1)S(1)}, bf16[768,512]{1,0:T(8,128)(2,1)}, u32[]{:S(2)}, u32[]{:S(2)}) %collective-permute-start.9) | collective-permute-done | bytes 786464 | tf_op jit(solution)/shard_map/ppermute | solution.py:435
  213.0 14.5 %collective-permute-done.10.refs_3_ = bf16[768,512]{1,0:T(8,128)(2,1)} collective-permute-done((bf16[768,512]{1,0:T(8,128)(2,1)S(1)}, bf16[768,512]{1,0:T(8,128)(2,1)}, u32[]{:S(2)}, u32[]{:S(2)}) %collective-permute-start.10) | collective-permute-done | bytes 786464 | tf_op jit(solution)/shard_map/ppermute | solution.py:435
  227.5 1.8 collective-permute-done.11.refs_4_
  229.3 9.8 %unpack.3 = (bf16[4,1024,128]{2,1,0:T(8,128)(2,1)}, bf16[4,1024,128]{2,1,0:T(8,128)(2,1)}) custom-call(s32[2048,1]{1,0:T(8,128)} %fusion.3.index_ref, bf16[384,512]{1,0:T(8,128)(2,1)} %get-tuple-element.38.refs_0_, bf16[384,512]{1,0:T(8,128)(2,1)} %get-tuple-element.42.refs_1_, bf16[768,512]{1,0:T(8,128)(2,1)} %collective-permute-done.9.refs_2_, ...), custom_call_target="tpu_custom_call" | custom-call | flops 38654705664 | bytes 1 | tf_op jit(solution)/shard_map/unpack/pallas_call | solution.py:359
  241.0 1.8 collective-permute-start.6
  242.9 1.1 collective-permute-start.7
  244.0 8.4 %collective-permute-done.5.refs_2_ = bf16[768,256]{1,0:T(8,128)(2,1)S(1)} collective-permute-done((bf16[768,256]{1,0:T(8,128)(2,1)S(1)}, bf16[768,256]{1,0:T(8,128)(2,1)S(1)}, u32[]{:S(2)}, u32[]{:S(2)}) %collective-permute-start.5) | collective-permute-done | bytes 393248 | tf_op jit(solution)/shard_map/ppermute | solution.py:435
  252.4 6.1 %collective-permute-done.6.refs_3_ = bf16[768,256]{1,0:T(8,128)(2,1)S(1)} collective-permute-done((bf16[768,256]{1,0:T(8,128)(2,1)S(1)}, bf16[768,256]{1,0:T(8,128)(2,1)S(1)}, u32[]{:S(2)}, u32[]{:S(2)}) %collective-permute-start.6) | collective-permute-done | bytes 393248 | tf_op jit(solution)/shard_map/ppermute | solution.py:435
  259.4 6.2 %assemble.1 = (bf16[1024,256]{1,0:T(8,128)(2,1)}, bf16[1024,256]{1,0:T(8,128)(2,1)}) custom-call(s32[2048,1]{1,0:T(8,128)} %fusion.3.index_ref, bf16[2,1024,512]{2,1,0:T(8,128)(2,1)} %bem_ref.7, bf16[384,256]{1,0:T(8,128)(2,1)} %get-tuple-element.54.refs_0_, bf16[384,256]{1,0:T(8,128)(2,1)} %get-tuple-element.58.refs_1_, bf16[768,256]{1,0:T(8,128)(2,1)} %copy-done.27, ...), custom_call_target="tpu_custom_call" | custom-call | flops 6442450944 | bytes 1 | tf_op jit(solution)/shard_map/assemble/pallas_call | solution.py:251
  265.7 1.4 collective-permute-start.14
  267.1 1.8 collective-permute-start.13
  269.1 1.8 subtract.2.ready_ref
  271.8 2.0 finish.1.refs_4_.refs_6_.refs_0_
  273.8 7.8 %collective-permute-done.14.refs_3_ = bf16[1024,256]{1,0:T(8,128)(2,1)S(1)} collective-permute-done((bf16[1024,256]{1,0:T(8,128)(2,1)}, bf16[1024,256]{1,0:T(8,128)(2,1)S(1)}, u32[]{:S(2)}, u32[]{:S(2)}) %collective-permute-start.14) | collective-permute-done | bytes 524320 | tf_op jit(solution)/shard_map/ppermute | solution.py:435
  281.6 6.8 %collective-permute-done.13.refs_2_ = bf16[1024,256]{1,0:T(8,128)(2,1)S(1)} collective-permute-done((bf16[1024,256]{1,0:T(8,128)(2,1)}, bf16[1024,256]{1,0:T(8,128)(2,1)S(1)}, u32[]{:S(2)}, u32[]{:S(2)}) %collective-permute-start.13) | collective-permute-done | bytes 524320 | tf_op jit(solution)/shard_map/ppermute | solution.py:435
  290.2 3.0 join.4.refs_4_
  293.8 1.6 collective-permute-start.18
  295.3 1.5 collective-permute-start.17
  297.5 1.3 copy-done.11
  298.8 13.4 %product.4.refs_4_.refs_6_.refs_0_ = bf16[1024,256]{1,0:T(8,128)(2,1)} custom-call(s32[8]{0:T(128)} %add_xor_fusion.order_ref, bf16[1024,8192]{1,0:T(8,128)(2,1)} %refs_3_.5, bf16[1024,8192]{1,0:T(8,128)(2,1)} %refs_3_.5, bf16[1024,8192]{1,0:T(8,128)(2,1)} %refs_3_.5, bf16[1024,8192]{1,0:T(8,128)(2,1)} %refs_3_.5, bf16[4096,256]{1,0:T(8,128)(2,1)} %join.4.refs_4_, ...), custom_call_target="tpu_custom_call" | custom-call | flops 12884901888 | bytes 1 | tf_op jit(solution)/shard_map/product/pallas_call | solution.py:415
  312.2 8.0 %collective-permute-done.17.refs_2_ = bf16[1024,256]{1,0:T(8,128)(2,1)S(1)} collective-permute-done((bf16[1024,256]{1,0:T(8,128)(2,1)S(1)}, bf16[1024,256]{1,0:T(8,128)(2,1)S(1)}, u32[]{:S(2)}, u32[]{:S(2)}) %collective-permute-start.17) | collective-permute-done | bytes 524320 | tf_op jit(solution)/shard_map/ppermute | solution.py:435
  321.9 3.0 join.5.refs_4_
  324.9 1.6 collective-permute-start.22
  326.5 1.5 collective-permute-start.21
  329.2 1.3 copy-done.9
  330.5 13.5 %product.5.refs_4_.refs_2_.refs_0_ = bf16[1024,256]{1,0:T(8,128)(2,1)} custom-call(s32[8]{0:T(128)} %add_xor_fusion.order_ref, bf16[1024,8192]{1,0:T(8,128)(2,1)} %refs_3_.5, bf16[1024,8192]{1,0:T(8,128)(2,1)} %refs_3_.5, bf16[1024,8192]{1,0:T(8,128)(2,1)} %refs_3_.5, bf16[1024,8192]{1,0:T(8,128)(2,1)} %refs_3_.5, bf16[4096,256]{1,0:T(8,128)(2,1)} %join.5.refs_4_, ...), custom_call_target="tpu_custom_call" | custom-call | flops 12884901888 | bytes 1 | tf_op jit(solution)/shard_map/product/pallas_call | solution.py:415
  344.0 7.4 %collective-permute-done.21.refs_2_ = bf16[1024,256]{1,0:T(8,128)(2,1)S(1)} collective-permute-done((bf16[1024,256]{1,0:T(8,128)(2,1)S(1)}, bf16[1024,256]{1,0:T(8,128)(2,1)S(1)}, u32[]{:S(2)}, u32[]{:S(2)}) %collective-permute-start.21) | collective-permute-done | bytes 524320 | tf_op jit(solution)/shard_map/ppermute | solution.py:435
  353.0 3.0 join.6.refs_4_
  356.1 1.6 collective-permute-start.26
  357.7 1.5 collective-permute-start.25
  359.6 2.1 subtract.3.refs_7_.refs_6_
  361.7 1.3 copy-done.10
  363.1 13.3 %product.6.refs_4_ = bf16[1024,256]{1,0:T(8,128)(2,1)} custom-call(s32[8]{0:T(128)} %add_xor_fusion.order_ref, bf16[1024,8192]{1,0:T(8,128)(2,1)} %refs_3_.7, bf16[1024,8192]{1,0:T(8,128)(2,1)} %refs_3_.7, bf16[1024,8192]{1,0:T(8,128)(2,1)} %refs_3_.7, bf16[1024,8192]{1,0:T(8,128)(2,1)} %refs_3_.7, bf16[4096,256]{1,0:T(8,128)(2,1)} %join.6.refs_4_, ...), custom_call_target="tpu_custom_call" | custom-call | flops 12884901888 | bytes 1 | tf_op jit(solution)/shard_map/product/pallas_call | solution.py:415
  376.4 6.1 %collective-permute-done.25.refs_2_ = bf16[1024,256]{1,0:T(8,128)(2,1)} collective-permute-done((bf16[1024,256]{1,0:T(8,128)(2,1)S(1)}, bf16[1024,256]{1,0:T(8,128)(2,1)}, u32[]{:S(2)}, u32[]{:S(2)}) %collective-permute-start.25) | collective-permute-done | bytes 524320 | tf_op jit(solution)/shard_map/ppermute | solution.py:435
  383.0 3.0 join.7.refs_4_
  386.1 4.3 %collective-permute-done.27.refs_5_ = bf16[4096,256]{1,0:T(8,128)(2,1)S(1)} collective-permute-done((bf16[4096,256]{1,0:T(8,128)(2,1)}, bf16[4096,256]{1,0:T(8,128)(2,1)S(1)}, u32[]{:S(2)}, u32[]{:S(2)}) %collective-permute-start.27) | collective-permute-done | bytes 2097184 | tf_op jit(solution)/shard_map/ppermute | solution.py:435
  390.4 1.3 copy-done.12
  391.7 13.3 %product.7 = bf16[1024,256]{1,0:T(8,128)(2,1)} custom-call(s32[8]{0:T(128)} %add_xor_fusion.order_ref, bf16[1024,8192]{1,0:T(8,128)(2,1)} %refs_3_.7, bf16[1024,8192]{1,0:T(8,128)(2,1)} %refs_3_.7, bf16[1024,8192]{1,0:T(8,128)(2,1)} %refs_3_.7, bf16[1024,8192]{1,0:T(8,128)(2,1)} %refs_3_.7, bf16[4096,256]{1,0:T(8,128)(2,1)} %join.7.refs_4_, ...), custom_call_target="tpu_custom_call" | custom-call | flops 12884901888 | bytes 1 | tf_op jit(solution)/shard_map/product/pallas_call | solution.py:415
  405.0 1.1 maximum_bitcast_fusion.1
  406.1 1.5 pad_maximum_fusion
  (149 shorter events, 21.7 us)
Async XLA Ops:
  7.4 97.3 %all-gather.2.cloned.1.call-start = ((), (), s32[]{:S(2)}) async-start(), calls=%async_computation.5 | async-start | bytes 2359296 | tf_op jit(solution)/shard_map/all_gather | solution.py:461
  8.8 188.1 %reduce-scatter.8.cloned.1.call-start = ((), (), s32[]{:S(2)}) async-start(), calls=%async_computation.7 | async-start | bytes 3932160 | tf_op jit(solution)/shard_map/reduce_scatter | solution.py:507
  57.3 0.7 copy-start.23
  57.3 139.6 %reduce-scatter.6.cloned.1.call-start = ((), (), s32[]{:S(2)}) async-start(), calls=%async_computation.6 | async-start | bytes 3932160 | tf_op jit(solution)/shard_map/reduce_scatter | solution.py:507
  57.9 211.2 %reduce-scatter.10.cloned.1.call-start = ((), (), s32[]{:S(2)}) async-start(), calls=%async_computation.8 | async-start | bytes 2621440 | tf_op jit(solution)/shard_map/reduce_scatter | solution.py:507
  131.2 7.0 %collective-permute-start = (bf16[1536,512]{1,0:T(8,128)(2,1)}, bf16[1536,512]{1,0:T(8,128)(2,1)}, u32[]{:S(2)}, u32[]{:S(2)}) collective-permute-start(bf16[1536,512]{1,0:T(8,128)(2,1)} %get-tuple-element.23), channel_id=1, source_target_pairs={{0,4},{4,0},{8,12},{12,8},{16,20},{20,16},{24,28},{28,24},{1,5},{5... | collective-permute-start | bytes 4718600 | tf_op jit(solution)/shard_map/ppermute | solution.py:435
  140.5 5.6 %copy-start.6 = (bf16[768,512]{1,0:T(8,128)(2,1)}, bf16[768,512]{1,0:T(8,128)(2,1)S(1)}, u32[]{:S(2)}) copy-start(bf16[768,512]{1,0:T(8,128)(2,1)S(1)} %pad_maximum_fusion.1.refs_1_) | copy-start | bytes 2359300
  140.5 21.3 %collective-permute-start.1 = (bf16[768,512]{1,0:T(8,128)(2,1)S(1)}, bf16[768,512]{1,0:T(8,128)(2,1)S(1)}, u32[]{:S(2)}, u32[]{:S(2)}) collective-permute-start(bf16[768,512]{1,0:T(8,128)(2,1)S(1)} %pad_maximum_fusion.1.refs_1_), channel_id=1, source_target_pairs={{0,8},{4,12},{8,0},{12,4},{16,24},{20,28},{24,16},{28,20},{1,9},{5... | collective-permute-start | bytes 2359304 | tf_op jit(solution)/shard_map/ppermute | solution.py:435
  143.1 3.0 copy-start.7
  143.1 36.6 %collective-permute-start.2 = (bf16[768,512]{1,0:T(8,128)(2,1)S(1)}, bf16[768,512]{1,0:T(8,128)(2,1)S(1)}, u32[]{:S(2)}, u32[]{:S(2)}) collective-permute-start(bf16[768,512]{1,0:T(8,128)(2,1)S(1)} %pad_maximum_fusion.2.refs_2_), channel_id=1, source_target_pairs={{0,16},{4,20},{8,24},{12,28},{16,0},{20,4},{24,8},{28,12},{1,17},{... | collective-permute-start | bytes 2359304 | tf_op jit(solution)/shard_map/ppermute | solution.py:435
  144.8 1.3 copy-start.8
  144.8 35.0 %collective-permute-start.3 = (bf16[768,512]{1,0:T(8,128)(2,1)S(1)}, bf16[768,512]{1,0:T(8,128)(2,1)S(1)}, u32[]{:S(2)}, u32[]{:S(2)}) collective-permute-start(bf16[768,512]{1,0:T(8,128)(2,1)S(1)} %pad_maximum_fusion.3.refs_3_), channel_id=1, source_target_pairs={{0,24},{4,28},{8,16},{12,20},{16,8},{20,12},{24,0},{28,4},{1,25},{... | collective-permute-start | bytes 2359304 | tf_op jit(solution)/shard_map/ppermute | solution.py:435
  159.6 31.9 %collective-permute-start.8 = (bf16[1536,512]{1,0:T(8,128)(2,1)}, bf16[1536,512]{1,0:T(8,128)(2,1)S(1)}, u32[]{:S(2)}, u32[]{:S(2)}) collective-permute-start(bf16[1536,512]{1,0:T(8,128)(2,1)} %get-tuple-element.28), channel_id=1, source_target_pairs={{0,4},{4,0},{8,12},{12,8},{16,20},{20,16},{24,28},{28,24},{1,5},{5... | collective-permute-start | bytes 4718600 | tf_op jit(solution)/shard_map/ppermute | solution.py:435
  161.8 18.0 %copy-start.24 = (bf16[768,512]{1,0:T(8,128)(2,1)}, bf16[768,512]{1,0:T(8,128)(2,1)S(1)}, u32[]{:S(2)}) copy-start(bf16[768,512]{1,0:T(8,128)(2,1)S(1)} %collective-permute-done.1.refs_2_) | copy-start | bytes 2359300
  179.8 1.0 copy-start.25
  179.8 1.2 copy-start.26
  191.4 80.4 %reduce-scatter.12.cloned.1.call-start = ((), (), s32[]{:S(2)}) async-start(), calls=%async_computation.9 | async-start | bytes 1310720 | tf_op jit(solution)/shard_map/reduce_scatter | solution.py:507
  192.3 20.6 %collective-permute-start.9 = (bf16[768,512]{1,0:T(8,128)(2,1)S(1)}, bf16[768,512]{1,0:T(8,128)(2,1)}, u32[]{:S(2)}, u32[]{:S(2)}) collective-permute-start(bf16[768,512]{1,0:T(8,128)(2,1)S(1)} %pad_maximum_fusion.4), channel_id=1, source_target_pairs={{0,8},{4,12},{8,0},{12,4},{16,24},{20,28},{24,16},{28,20},{1,9},{5... | collective-permute-start | bytes 2359304 | tf_op jit(solution)/shard_map/ppermute | solution.py:435
  193.3 34.2 %collective-permute-start.10 = (bf16[768,512]{1,0:T(8,128)(2,1)S(1)}, bf16[768,512]{1,0:T(8,128)(2,1)}, u32[]{:S(2)}, u32[]{:S(2)}) collective-permute-start(bf16[768,512]{1,0:T(8,128)(2,1)S(1)} %pad_maximum_fusion.5), channel_id=1, source_target_pairs={{0,16},{4,20},{8,24},{12,28},{16,0},{20,4},{24,8},{28,12},{1,17},{... | collective-permute-start | bytes 2359304 | tf_op jit(solution)/shard_map/ppermute | solution.py:435
  195.5 33.8 %collective-permute-start.11 = (bf16[768,512]{1,0:T(8,128)(2,1)}, bf16[768,512]{1,0:T(8,128)(2,1)}, u32[]{:S(2)}, u32[]{:S(2)}) collective-permute-start(bf16[768,512]{1,0:T(8,128)(2,1)} %pad_maximum_fusion.6), channel_id=1, source_target_pairs={{0,24},{4,28},{8,16},{12,20},{16,8},{20,12},{24,0},{28,4},{1,25},{... | collective-permute-start | bytes 2359304 | tf_op jit(solution)/shard_map/ppermute | solution.py:435
  205.0 34.4 %collective-permute-start.4 = (bf16[1536,256]{1,0:T(8,128)(2,1)}, bf16[1536,256]{1,0:T(8,128)(2,1)S(1)}, u32[]{:S(2)}, u32[]{:S(2)}) collective-permute-start(bf16[1536,256]{1,0:T(8,128)(2,1)} %get-tuple-element.27), channel_id=1, source_target_pairs={{0,4},{4,0},{8,12},{12,8},{16,20},{20,16},{24,28},{28,24},{1,5},{5... | collective-permute-start | bytes 2359304 | tf_op jit(solution)/shard_map/ppermute | solution.py:435
  239.2 120.4 %reduce-scatter.14.cloned.1.call-start = ((), (), s32[]{:S(2)}) async-start(), calls=%async_computation.10 | async-start | bytes 1310720 | tf_op jit(solution)/shard_map/reduce_scatter | solution.py:507
  240.3 12.1 %collective-permute-start.5 = (bf16[768,256]{1,0:T(8,128)(2,1)S(1)}, bf16[768,256]{1,0:T(8,128)(2,1)S(1)}, u32[]{:S(2)}, u32[]{:S(2)}) collective-permute-start(bf16[768,256]{1,0:T(8,128)(2,1)S(1)} %pad_maximum_fusion.7), channel_id=1, source_target_pairs={{0,8},{4,12},{8,0},{12,4},{16,24},{20,28},{24,16},{28,20},{1,9},{5... | collective-permute-start | bytes 1179656 | tf_op jit(solution)/shard_map/ppermute | solution.py:435
  241.0 17.5 %collective-permute-start.6 = (bf16[768,256]{1,0:T(8,128)(2,1)S(1)}, bf16[768,256]{1,0:T(8,128)(2,1)S(1)}, u32[]{:S(2)}, u32[]{:S(2)}) collective-permute-start(bf16[768,256]{1,0:T(8,128)(2,1)S(1)} %pad_maximum_fusion.8), channel_id=1, source_target_pairs={{0,16},{4,20},{8,24},{12,28},{16,0},{20,4},{24,8},{28,12},{1,17},{... | collective-permute-start | bytes 1179656 | tf_op jit(solution)/shard_map/ppermute | solution.py:435
  242.9 15.6 %collective-permute-start.7 = (bf16[768,256]{1,0:T(8,128)(2,1)S(1)}, bf16[768,256]{1,0:T(8,128)(2,1)S(1)}, u32[]{:S(2)}, u32[]{:S(2)}) collective-permute-start(bf16[768,256]{1,0:T(8,128)(2,1)S(1)} %pad_maximum_fusion.9), channel_id=1, source_target_pairs={{0,24},{4,28},{8,16},{12,20},{16,8},{20,12},{24,0},{28,4},{1,25},{... | collective-permute-start | bytes 1179656 | tf_op jit(solution)/shard_map/ppermute | solution.py:435
  252.4 6.2 %copy-start.27 = (bf16[768,256]{1,0:T(8,128)(2,1)}, bf16[768,256]{1,0:T(8,128)(2,1)S(1)}, u32[]{:S(2)}) copy-start(bf16[768,256]{1,0:T(8,128)(2,1)S(1)} %collective-permute-done.5.refs_2_) | copy-start | bytes 1179652
  258.5 0.7 copy-start.28
  258.5 0.9 copy-start.29
  265.7 16.0 %collective-permute-start.14 = (bf16[1024,256]{1,0:T(8,128)(2,1)}, bf16[1024,256]{1,0:T(8,128)(2,1)S(1)}, u32[]{:S(2)}, u32[]{:S(2)}) collective-permute-start(bf16[1024,256]{1,0:T(8,128)(2,1)} %get-tuple-element.30.refs_1_.refs_0_), channel_id=1, source_target_pairs={{0,24},{4,28},{8,16},{12,20},{16,8},{20,12},{24,0},{28,4},{1,25},{... | collective-permute-start | bytes 1572872 | tf_op jit(solution)/shard_map/ppermute | solution.py:435
  267.1 21.4 %collective-permute-start.13 = (bf16[1024,256]{1,0:T(8,128)(2,1)}, bf16[1024,256]{1,0:T(8,128)(2,1)S(1)}, u32[]{:S(2)}, u32[]{:S(2)}) collective-permute-start(bf16[1024,256]{1,0:T(8,128)(2,1)} %get-tuple-element.30.refs_1_.refs_0_), channel_id=1, source_target_pairs={{0,16},{4,20},{8,24},{12,28},{16,0},{20,4},{24,8},{28,12},{1,17},{... | collective-permute-start | bytes 1572872 | tf_op jit(solution)/shard_map/ppermute | solution.py:435
  268.8 20.5 %collective-permute-start.12 = (bf16[1024,256]{1,0:T(8,128)(2,1)}, bf16[1024,256]{1,0:T(8,128)(2,1)S(1)}, u32[]{:S(2)}, u32[]{:S(2)}) collective-permute-start(bf16[1024,256]{1,0:T(8,128)(2,1)} %get-tuple-element.30.refs_1_.refs_0_), channel_id=1, source_target_pairs={{0,8},{4,12},{8,0},{12,4},{16,24},{20,28},{24,16},{28,20},{1,9},{5... | collective-permute-start | bytes 1572872 | tf_op jit(solution)/shard_map/ppermute | solution.py:435
  273.8 20.0 %copy-start.4 = (bf16[1024,256]{1,0:T(8,128)(2,1)S(1)}, bf16[1024,256]{1,0:T(8,128)(2,1)}, u32[]{:S(2)}) copy-start(bf16[1024,256]{1,0:T(8,128)(2,1)} %finish.1.refs_4_.refs_6_.refs_0_) | copy-start | bytes 1572868
  281.6 7.7 %copy-start.14 = (bf16[1024,256]{1,0:T(8,128)(2,1)}, bf16[1024,256]{1,0:T(8,128)(2,1)S(1)}, u32[]{:S(2)}) copy-start(bf16[1024,256]{1,0:T(8,128)(2,1)S(1)} %collective-permute-done.14.refs_3_) | copy-start | bytes 1572868
  288.5 0.9 copy-start.15
  289.4 0.8 copy-start.16
  293.1 4.4 %collective-permute-start.15 = (bf16[4096,256]{1,0:T(8,128)(2,1)}, bf16[4096,256]{1,0:T(8,128)(2,1)S(1)}, u32[]{:S(2)}, u32[]{:S(2)}) collective-permute-start(bf16[4096,256]{1,0:T(8,128)(2,1)} %join.4.refs_4_), channel_id=1, source_target_pairs={{0,4},{4,0},{8,12},{12,8},{16,20},{20,16},{24,28},{28,24},{1,5},{5... | collective-permute-start | bytes 6291464 | tf_op jit(solution)/shard_map/ppermute | solution.py:435
  293.8 18.4 %collective-permute-start.18 = (bf16[1024,256]{1,0:T(8,128)(2,1)S(1)}, bf16[1024,256]{1,0:T(8,128)(2,1)S(1)}, u32[]{:S(2)}, u32[]{:S(2)}) collective-permute-start(bf16[1024,256]{1,0:T(8,128)(2,1)S(1)} %copy-done.4), channel_id=1, source_target_pairs={{0,24},{4,28},{8,16},{12,20},{16,8},{20,12},{24,0},{28,4},{1,25},{... | collective-permute-start | bytes 1572872 | tf_op jit(solution)/shard_map/ppermute | solution.py:435
  295.3 24.9 %collective-permute-start.17 = (bf16[1024,256]{1,0:T(8,128)(2,1)S(1)}, bf16[1024,256]{1,0:T(8,128)(2,1)S(1)}, u32[]{:S(2)}, u32[]{:S(2)}) collective-permute-start(bf16[1024,256]{1,0:T(8,128)(2,1)S(1)} %copy-done.4), channel_id=1, source_target_pairs={{0,16},{4,20},{8,24},{12,28},{16,0},{20,4},{24,8},{28,12},{1,17},{... | collective-permute-start | bytes 1572872 | tf_op jit(solution)/shard_map/ppermute | solution.py:435
  296.9 23.9 %collective-permute-start.16 = (bf16[1024,256]{1,0:T(8,128)(2,1)S(1)}, bf16[1024,256]{1,0:T(8,128)(2,1)S(1)}, u32[]{:S(2)}, u32[]{:S(2)}) collective-permute-start(bf16[1024,256]{1,0:T(8,128)(2,1)S(1)} %copy-done.4), channel_id=1, source_target_pairs={{0,8},{4,12},{8,0},{12,4},{16,24},{20,28},{24,16},{28,20},{1,9},{5... | collective-permute-start | bytes 1572872 | tf_op jit(solution)/shard_map/ppermute | solution.py:435
  297.5 1.3 copy-start.11
  312.2 12.7 %copy-start = (bf16[1024,256]{1,0:T(8,128)(2,1)S(1)}, bf16[1024,256]{1,0:T(8,128)(2,1)}, u32[]{:S(2)}) copy-start(bf16[1024,256]{1,0:T(8,128)(2,1)} %product.4.refs_4_.refs_6_.refs_0_) | copy-start | bytes 1572868
  312.2 8.5 %copy-start.17 = (bf16[1024,256]{1,0:T(8,128)(2,1)}, bf16[1024,256]{1,0:T(8,128)(2,1)S(1)}, u32[]{:S(2)}) copy-start(bf16[1024,256]{1,0:T(8,128)(2,1)S(1)} %collective-permute-done.18.refs_3_) | copy-start | bytes 1572868
  320.3 0.8 copy-start.19
  321.1 0.8 copy-start.21
  324.8 4.4 %collective-permute-start.19 = (bf16[4096,256]{1,0:T(8,128)(2,1)}, bf16[4096,256]{1,0:T(8,128)(2,1)S(1)}, u32[]{:S(2)}, u32[]{:S(2)}) collective-permute-start(bf16[4096,256]{1,0:T(8,128)(2,1)} %join.5.refs_4_), channel_id=1, source_target_pairs={{0,4},{4,0},{8,12},{12,8},{16,20},{20,16},{24,28},{28,24},{1,5},{5... | collective-permute-start | bytes 6291464 | tf_op jit(solution)/shard_map/ppermute | solution.py:435
  324.9 19.1 %collective-permute-start.22 = (bf16[1024,256]{1,0:T(8,128)(2,1)S(1)}, bf16[1024,256]{1,0:T(8,128)(2,1)S(1)}, u32[]{:S(2)}, u32[]{:S(2)}) collective-permute-start(bf16[1024,256]{1,0:T(8,128)(2,1)S(1)} %copy-done), channel_id=1, source_target_pairs={{0,24},{4,28},{8,16},{12,20},{16,8},{20,12},{24,0},{28,4},{1,25},{... | collective-permute-start | bytes 1572872 | tf_op jit(solution)/shard_map/ppermute | solution.py:435
  326.5 24.9 %collective-permute-start.21 = (bf16[1024,256]{1,0:T(8,128)(2,1)S(1)}, bf16[1024,256]{1,0:T(8,128)(2,1)S(1)}, u32[]{:S(2)}, u32[]{:S(2)}) collective-permute-start(bf16[1024,256]{1,0:T(8,128)(2,1)S(1)} %copy-done), channel_id=1, source_target_pairs={{0,16},{4,20},{8,24},{12,28},{16,0},{20,4},{24,8},{28,12},{1,17},{... | collective-permute-start | bytes 1572872 | tf_op jit(solution)/shard_map/ppermute | solution.py:435
  328.1 23.8 %collective-permute-start.20 = (bf16[1024,256]{1,0:T(8,128)(2,1)S(1)}, bf16[1024,256]{1,0:T(8,128)(2,1)S(1)}, u32[]{:S(2)}, u32[]{:S(2)}) collective-permute-start(bf16[1024,256]{1,0:T(8,128)(2,1)S(1)} %copy-done), channel_id=1, source_target_pairs={{0,8},{4,12},{8,0},{12,4},{16,24},{20,28},{24,16},{28,20},{1,9},{5... | collective-permute-start | bytes 1572872 | tf_op jit(solution)/shard_map/ppermute | solution.py:435
  329.2 1.3 copy-start.9
  344.0 12.1 %copy-start.2 = (bf16[1024,256]{1,0:T(8,128)(2,1)S(1)}, bf16[1024,256]{1,0:T(8,128)(2,1)}, u32[]{:S(2)}) copy-start(bf16[1024,256]{1,0:T(8,128)(2,1)} %product.5.refs_4_.refs_2_.refs_0_) | copy-start | bytes 1572868
  344.0 7.9 %copy-start.18 = (bf16[1024,256]{1,0:T(8,128)(2,1)}, bf16[1024,256]{1,0:T(8,128)(2,1)S(1)}, u32[]{:S(2)}) copy-start(bf16[1024,256]{1,0:T(8,128)(2,1)S(1)} %collective-permute-done.22.refs_3_) | copy-start | bytes 1572868
  351.4 0.8 copy-start.20
  352.2 0.8 copy-start.22
  356.0 5.8 %collective-permute-start.23 = (bf16[4096,256]{1,0:T(8,128)(2,1)}, bf16[4096,256]{1,0:T(8,128)(2,1)S(1)}, u32[]{:S(2)}, u32[]{:S(2)}) collective-permute-start(bf16[4096,256]{1,0:T(8,128)(2,1)} %join.6.refs_4_), channel_id=1, source_target_pairs={{0,4},{4,0},{8,12},{12,8},{16,20},{20,16},{24,28},{28,24},{1,5},{5... | collective-permute-start | bytes 6291464 | tf_op jit(solution)/shard_map/ppermute | solution.py:435
  356.1 20.3 %collective-permute-start.26 = (bf16[1024,256]{1,0:T(8,128)(2,1)S(1)}, bf16[1024,256]{1,0:T(8,128)(2,1)S(1)}, u32[]{:S(2)}, u32[]{:S(2)}) collective-permute-start(bf16[1024,256]{1,0:T(8,128)(2,1)S(1)} %copy-done.2), channel_id=1, source_target_pairs={{0,24},{4,28},{8,16},{12,20},{16,8},{20,12},{24,0},{28,4},{1,25},{... | collective-permute-start | bytes 1572872 | tf_op jit(solution)/shard_map/ppermute | solution.py:435
  357.7 24.9 %collective-permute-start.25 = (bf16[1024,256]{1,0:T(8,128)(2,1)S(1)}, bf16[1024,256]{1,0:T(8,128)(2,1)}, u32[]{:S(2)}, u32[]{:S(2)}) collective-permute-start(bf16[1024,256]{1,0:T(8,128)(2,1)S(1)} %copy-done.2), channel_id=1, source_target_pairs={{0,16},{4,20},{8,24},{12,28},{16,0},{20,4},{24,8},{28,12},{1,17},{... | collective-permute-start | bytes 1572872 | tf_op jit(solution)/shard_map/ppermute | solution.py:435
  359.2 23.8 %collective-permute-start.24 = (bf16[1024,256]{1,0:T(8,128)(2,1)S(1)}, bf16[1024,256]{1,0:T(8,128)(2,1)}, u32[]{:S(2)}, u32[]{:S(2)}) collective-permute-start(bf16[1024,256]{1,0:T(8,128)(2,1)S(1)} %copy-done.2), channel_id=1, source_target_pairs={{0,8},{4,12},{8,0},{12,4},{16,24},{20,28},{24,16},{28,20},{1,9},{5... | collective-permute-start | bytes 1572872 | tf_op jit(solution)/shard_map/ppermute | solution.py:435
  361.7 1.3 copy-start.10
  376.4 9.6 %copy-start.1 = (bf16[1024,256]{1,0:T(8,128)(2,1)S(1)}, bf16[1024,256]{1,0:T(8,128)(2,1)}, u32[]{:S(2)}) copy-start(bf16[1024,256]{1,0:T(8,128)(2,1)} %product.4.refs_4_.refs_6_.refs_0_) | copy-start | bytes 1572868
  376.4 9.6 %copy-start.3 = (bf16[1024,256]{1,0:T(8,128)(2,1)S(1)}, bf16[1024,256]{1,0:T(8,128)(2,1)}, u32[]{:S(2)}) copy-start(bf16[1024,256]{1,0:T(8,128)(2,1)} %product.5.refs_4_.refs_2_.refs_0_) | copy-start | bytes 1572868
  376.4 6.6 %copy-start.13 = (bf16[1024,256]{1,0:T(8,128)(2,1)}, bf16[1024,256]{1,0:T(8,128)(2,1)S(1)}, u32[]{:S(2)}) copy-start(bf16[1024,256]{1,0:T(8,128)(2,1)S(1)} %collective-permute-done.26.refs_3_) | copy-start | bytes 1572868
  386.0 4.4 %collective-permute-start.27 = (bf16[4096,256]{1,0:T(8,128)(2,1)}, bf16[4096,256]{1,0:T(8,128)(2,1)S(1)}, u32[]{:S(2)}, u32[]{:S(2)}) collective-permute-start(bf16[4096,256]{1,0:T(8,128)(2,1)} %join.7.refs_4_), channel_id=1, source_target_pairs={{0,4},{4,0},{8,12},{12,8},{16,20},{20,16},{24,28},{28,24},{1,5},{5... | collective-permute-start | bytes 6291464 | tf_op jit(solution)/shard_map/ppermute | solution.py:435
  386.1 18.9 %copy-start.5 = (bf16[1024,256]{1,0:T(8,128)(2,1)S(1)}, bf16[1024,256]{1,0:T(8,128)(2,1)}, u32[]{:S(2)}) copy-start(bf16[1024,256]{1,0:T(8,128)(2,1)} %product.6.refs_4_) | copy-start | bytes 1572868
  390.4 1.3 copy-start.12
Sparse Core Ops, SparseCore 0:
  10.1 30.5 all-gather.1
Sparse Core Ops, SparseCore 1:
  57.4 67.7 reduce-scatter.7
  127.4 60.2 reduce-scatter.5
  191.4 48.5 reduce-scatter.9
  242.4 29.3 reduce-scatter.11
  325.0 32.7 reduce-scatter.13

commit v9 on v8

--- a/solution.py
+++ b/solution.py
@@ -524,7 +524,7 @@
 
     uppers, lowers = [], []
     for at, pieces in enumerate(routed):
-        cuts = unpack(lands, pieces, n_col, 1 if at + 1 < half else 2, after, 12)
+        cuts = unpack(lands, pieces, n_col, 1 if at + 1 < half else 2, after, 0 if at else 12)
         uppers.append(summed(cuts[0]))
         lowers.append(cuts[1:])
         after = (cuts[0],)

time: 422 us -> 416 us (0.986)
  waiting for transfers between devices: 100 us -> 93.5 us
    ppermute x28, waiting for transfers between devices: 98.6 us -> 93.3 us  [exchange(): return lax.ppermute(value, axis, [(i, i ^ distance) for i in range(n)])]
    unnamed x69 -> x71, local copies, waits for them, and re-layouts: 13.8 us -> 16.8 us
  transfers between devices with their start and end apart: 34 -> 34, of which waited for: 19 -> 15; matrix products, arithmetic and copies ran while one was open for 8% -> 8% of each run, Pallas kernels for 49% -> 50%
where the time goes in v9:
time: 416 us; the launch traced here: 412 us
  Pallas kernels  227 us (55%)
  waiting for transfers between devices  93.5 us (22%)
  starting transfers between devices  26.8 us (6%)
  local copies, waits for them, and re-layouts  25.6 us (6%)
  other arithmetic  23.8 us (6%)
  between operations  15.7 us (4%)
    pallas_call x2, Pallas kernels, front_products(): pl.pallas_call(functools.partial(front_kernel, subs, flats, n_col, len(af...  93.4 us
    ppermute x28, waiting for transfers between devices, exchange(): return lax.ppermute(value, axis, [(i, i ^ distance) for i in range(n)])  93.3 us
    pallas_call x4, Pallas kernels, product(): pl.pallas_call(functools.partial(product_kernel, streams, bool(bases)), g...  53.5 us
    pallas_call x3, Pallas kernels, pack_rows(): pl.pallas_call(functools.partial(pack_kernel, n_row, len(solved)), in_spe...  35.4 us
    ppermute x28, starting transfers between devices, exchange(): return lax.ppermute(value, axis, [(i, i ^ distance) for i in range(n)])  26.4 us
    pallas_call x2, Pallas kernels, unpack(): pl.pallas_call(functools.partial(unpack_kernel, len(pieces), n_col, parts...  20.2 us
    unnamed x71, local copies, waits for them, and re-layouts  16.8 us
    pallas_call x4, Pallas kernels, join(): pl.pallas_call(functools.partial(join_kernel, len(parts)), in_specs=[whol...  11.9 us
  transfers between devices with their start and end apart: 34, of which 15 were waited for; matrix products, arithmetic and copies ran while one was open for 8% of the time, Pallas kernels for 50%

profile of v9, /device:TPU:0, one launch (start us, length us, event | category | flops | bytes accessed | tf_op | source)
XLA Modules:
  0.0 411.9 jit_solution(5232204215855382034)
XLA Ops:
  10.8 42.0 %front_products.2 = (bf16[4,3072,128]{2,1,0:T(8,128)(2,1)}, bf16[4,3072,128]{2,1,0:T(8,128)(2,1)}) custom-call(s32[3,192]{1,0:T(4,128)} %pad_add_fusion.meta_ref, bf16[192,128,128]{2,1,0:T(8,128)(2,1)} %tiles_ref.3, bf16[3072,6144]{1,0:T(8,128)(2,1)} %front_ref.3), custom_call_target="tpu_custom_call" | custom-call | bytes 1 | tf_op jit(solution)/shard_map/front_products/pallas_call | solution.py:171
  52.9 51.4 %front_products.3 = (bf16[3072,512]{1,0:T(8,128)(2,1)}, bf16[3072,512]{1,0:T(8,128)(2,1)}) custom-call(s32[3,192]{1,0:T(4,128)} %pad_add_fusion.meta_ref, bf16[192,128,128]{2,1,0:T(8,128)(2,1)} %tiles_ref.3, bf16[3072,6144]{1,0:T(8,128)(2,1)} %front_ref.3, bf16[4,3072,128]{2,1,0:T(8,128)(2,1)} %get-tuple-element.19.refs_0_), custom_call_target="tpu_custom_call" | custom-call | bytes 1 | tf_op jit(solution)/shard_map/front_products/pallas_call | solution.py:171
  104.4 1.1 slice.119
  106.1 2.4 reduce-window.16
  109.2 6.2 %select_reduce_fusion = s32[8,384]{1,0:T(8,128)S(1)} fusion(s32[8,2048]{1,0:T(8,128)S(1)} %subtract_add_fusion, s32[8,2048]{1,0:T(8,128)S(1)} %bitcast.55, pred[8,2048]{1,0:T(8,128)(4,1)S(1)} %get-tuple-element.34), kind=kLoop, calls=%fused_computation.1 | loop fusion | flops 25162752 | bytes 159744 | tf_op jit(solution)/shard_map/reduce_sum | solution.py:468
  115.4 1.7 copy.44
  117.1 13.9 %pack_rows.3 = (bf16[1536,512]{1,0:T(8,128)(2,1)}, bf16[1536,512]{1,0:T(8,128)(2,1)}) custom-call(s32[3072,1]{1,0:T(8,128)} %bitcast.48, bf16[3072,512]{1,0:T(8,128)(2,1)} %get-tuple-element.21.refs_0_), custom_call_target="tpu_custom_call" | custom-call | bytes 1 | tf_op jit(solution)/shard_map/pack_rows/pallas_call | solution.py:214
  133.2 1.4 collective-permute-done
  135.6 3.0 collective-permute-start.1
  139.5 1.5 collective-permute-start.2
  142.1 2.3 reduce-window.14
  146.2 1.2 fusion.3.index_ref
  147.4 13.4 %pack_rows.4 = (bf16[1536,512]{1,0:T(8,128)(2,1)}, bf16[1536,512]{1,0:T(8,128)(2,1)}) custom-call(s32[3072,1]{1,0:T(8,128)} %bitcast.49, bf16[3072,512]{1,0:T(8,128)(2,1)} %get-tuple-element.24.refs_0_, bf16[768,512]{1,0:T(8,128)(2,1)} %copy-done.6, bf16[768,512]{1,0:T(8,128)(2,1)} %pad_maximum_fusion.2.refs_2_, bf16[768,512]{1,0:T(8,128)(2,1)} %pad_maximum_fusion.3.refs_3_), custom_call_target="tpu_custom_call" | custom-call | bytes 1 | tf_op jit(solution)/shard_map/pack_rows/pallas_call | solution.py:214
  160.8 15.1 %collective-permute-done.2.refs_3_ = bf16[768,512]{1,0:T(8,128)(2,1)} collective-permute-done((bf16[768,512]{1,0:T(8,128)(2,1)}, bf16[768,512]{1,0:T(8,128)(2,1)}, u32[]{:S(2)}, u32[]{:S(2)}) %collective-permute-start.2) | collective-permute-done | bytes 786464 | tf_op jit(solution)/shard_map/ppermute | solution.py:435
  176.0 10.4 %unpack.2.refs_2_ = bf16[4,2048,128]{2,1,0:T(8,128)(2,1)} custom-call(s32[2048,1]{1,0:T(8,128)} %fusion.3.index_ref, bf16[384,512]{1,0:T(8,128)(2,1)} %get-tuple-element.46.refs_0_, bf16[384,512]{1,0:T(8,128)(2,1)} %get-tuple-element.50.refs_1_, bf16[768,512]{1,0:T(8,128)(2,1)} %collective-permute-done.1.refs_2_, ...), custom_call_target="tpu_custom_call" | custom-call | flops 38654705664 | bytes 1 | tf_op jit(solution)/shard_map/unpack/pallas_call | solution.py:359
  186.4 1.3 copy-done.11
  189.4 1.0 pad_maximum_fusion.4
  190.9 1.0 pad_maximum_fusion.5
  191.9 1.6 collective-permute-start.10
  194.5 1.4 collective-permute-start.11
  195.9 8.1 %pack_rows.5 = (bf16[1536,256]{1,0:T(8,128)(2,1)}, bf16[1536,256]{1,0:T(8,128)(2,1)}) custom-call(s32[3072,1]{1,0:T(8,128)} %bitcast.50, bf16[3072,128]{1,0:T(8,128)(2,1)} %bitcast.69, bf16[3072,128]{1,0:T(8,128)(2,1)} %bitcast.68, bf16[4,2048,128]{2,1,0:T(8,128)(2,1)} %unpack.2.refs_2_), custom_call_target="tpu_custom_call" | custom-call | flops 28991029248 | bytes 1 | tf_op jit(solution)/shard_map/pack_rows/pallas_call | solution.py:214
  204.0 2.0 fusion.10
  206.0 5.1 %collective-permute-done.9.refs_2_ = bf16[768,512]{1,0:T(8,128)(2,1)S(1)} collective-permute-done((bf16[768,512]{1,0:T(8,128)(2,1)}, bf16[768,512]{1,0:T(8,128)(2,1)S(1)}, u32[]{:S(2)}, u32[]{:S(2)}) %collective-permute-start.9) | collective-permute-done | bytes 786464 | tf_op jit(solution)/shard_map/ppermute | solution.py:435
  211.2 16.1 %collective-permute-done.10.refs_3_ = bf16[768,512]{1,0:T(8,128)(2,1)S(1)} collective-permute-done((bf16[768,512]{1,0:T(8,128)(2,1)}, bf16[768,512]{1,0:T(8,128)(2,1)S(1)}, u32[]{:S(2)}, u32[]{:S(2)}) %collective-permute-start.10) | collective-permute-done | bytes 786464 | tf_op jit(solution)/shard_map/ppermute | solution.py:435
  228.4 9.8 %unpack.3 = (bf16[4,1024,128]{2,1,0:T(8,128)(2,1)}, bf16[4,1024,128]{2,1,0:T(8,128)(2,1)}) custom-call(s32[2048,1]{1,0:T(8,128)} %fusion.3.index_ref, bf16[384,512]{1,0:T(8,128)(2,1)} %get-tuple-element.38.refs_0_, bf16[384,512]{1,0:T(8,128)(2,1)} %get-tuple-element.42.refs_1_, bf16[768,512]{1,0:T(8,128)(2,1)} %copy-done.13, bf16[768,512]{1,0:T(8,128)(2,1)} %copy-done.14, ...), custom_call_target="tpu_custom_call" | custom-call | bytes 1 | tf_op jit(solution)/shard_map/unpack/pallas_call | solution.py:359
  239.3 1.6 collective-permute-start.5
  240.9 1.6 collective-permute-start.6
  243.0 8.4 %collective-permute-done.5.refs_2_ = bf16[768,256]{1,0:T(8,128)(2,1)S(1)} collective-permute-done((bf16[768,256]{1,0:T(8,128)(2,1)S(1)}, bf16[768,256]{1,0:T(8,128)(2,1)S(1)}, u32[]{:S(2)}, u32[]{:S(2)}) %collective-permute-start.5) | collective-permute-done | bytes 393248 | tf_op jit(solution)/shard_map/ppermute | solution.py:435
  251.4 5.5 %collective-permute-done.6.refs_3_ = bf16[768,256]{1,0:T(8,128)(2,1)S(1)} collective-permute-done((bf16[768,256]{1,0:T(8,128)(2,1)S(1)}, bf16[768,256]{1,0:T(8,128)(2,1)S(1)}, u32[]{:S(2)}, u32[]{:S(2)}) %collective-permute-start.6) | collective-permute-done | bytes 393248 | tf_op jit(solution)/shard_map/ppermute | solution.py:435
  257.8 6.3 %assemble.1 = (bf16[1024,256]{1,0:T(8,128)(2,1)}, bf16[1024,256]{1,0:T(8,128)(2,1)}) custom-call(s32[2048,1]{1,0:T(8,128)} %fusion.3.index_ref, bf16[2,1024,512]{2,1,0:T(8,128)(2,1)} %bem_ref.7, bf16[384,256]{1,0:T(8,128)(2,1)} %get-tuple-element.54.refs_0_, bf16[384,256]{1,0:T(8,128)(2,1)} %get-tuple-element.58.refs_1_, bf16[768,256]{1,0:T(8,128)(2,1)} %copy-done.28, ...), custom_call_target="tpu_custom_call" | custom-call | flops 6442450944 | bytes 1 | tf_op jit(solution)/shard_map/assemble/pallas_call | solution.py:251
  264.1 1.4 collective-permute-start.14
  265.5 1.3 collective-permute-start.13
  267.6 1.8 subtract.2.ready_ref
  269.4 2.0 finish.1.refs_4_.refs_6_.refs_0_
  271.4 8.4 %collective-permute-done.14.refs_3_ = bf16[1024,256]{1,0:T(8,128)(2,1)S(1)} collective-permute-done((bf16[1024,256]{1,0:T(8,128)(2,1)}, bf16[1024,256]{1,0:T(8,128)(2,1)S(1)}, u32[]{:S(2)}, u32[]{:S(2)}) %collective-permute-start.14) | collective-permute-done | bytes 524320 | tf_op jit(solution)/shard_map/ppermute | solution.py:435
  279.8 5.5 %collective-permute-done.13.refs_2_ = bf16[1024,256]{1,0:T(8,128)(2,1)S(1)} collective-permute-done((bf16[1024,256]{1,0:T(8,128)(2,1)}, bf16[1024,256]{1,0:T(8,128)(2,1)S(1)}, u32[]{:S(2)}, u32[]{:S(2)}) %collective-permute-start.13) | collective-permute-done | bytes 524320 | tf_op jit(solution)/shard_map/ppermute | solution.py:435
  285.3 1.0 collective-permute-done.12.refs_1_
  287.1 3.0 join.4.refs_4_
  290.7 1.3 collective-permute-start.18
  292.0 1.2 collective-permute-start.17
  293.2 1.0 collective-permute-start.16
  294.5 1.3 copy-done.9
  295.8 13.4 %product.4.refs_4_.refs_6_.refs_0_ = bf16[1024,256]{1,0:T(8,128)(2,1)} custom-call(s32[8]{0:T(128)} %add_xor_fusion.order_ref, bf16[1024,8192]{1,0:T(8,128)(2,1)} %refs_3_.5, bf16[1024,8192]{1,0:T(8,128)(2,1)} %refs_3_.5, bf16[1024,8192]{1,0:T(8,128)(2,1)} %refs_3_.5, bf16[1024,8192]{1,0:T(8,128)(2,1)} %refs_3_.5, bf16[4096,256]{1,0:T(8,128)(2,1)} %join.4.refs_4_, ...), custom_call_target="tpu_custom_call" | custom-call | flops 12884901888 | bytes 1 | tf_op jit(solution)/shard_map/product/pallas_call | solution.py:415
  309.2 8.0 %collective-permute-done.17.refs_2_ = bf16[1024,256]{1,0:T(8,128)(2,1)S(1)} collective-permute-done((bf16[1024,256]{1,0:T(8,128)(2,1)S(1)}, bf16[1024,256]{1,0:T(8,128)(2,1)S(1)}, u32[]{:S(2)}, u32[]{:S(2)}) %collective-permute-start.17) | collective-permute-done | bytes 524320 | tf_op jit(solution)/shard_map/ppermute | solution.py:435
  318.8 3.0 join.5.refs_4_
  321.8 1.4 collective-permute-start.22
  323.2 1.2 collective-permute-start.21
  324.4 1.0 collective-permute-start.20
  326.1 1.3 copy-done.7
  327.5 13.4 %product.5.refs_4_.refs_2_.refs_0_ = bf16[1024,256]{1,0:T(8,128)(2,1)} custom-call(s32[8]{0:T(128)} %add_xor_fusion.order_ref, bf16[1024,8192]{1,0:T(8,128)(2,1)} %refs_3_.5, bf16[1024,8192]{1,0:T(8,128)(2,1)} %refs_3_.5, bf16[1024,8192]{1,0:T(8,128)(2,1)} %refs_3_.5, bf16[1024,8192]{1,0:T(8,128)(2,1)} %refs_3_.5, bf16[4096,256]{1,0:T(8,128)(2,1)} %join.5.refs_4_, ...), custom_call_target="tpu_custom_call" | custom-call | flops 12884901888 | bytes 1 | tf_op jit(solution)/shard_map/product/pallas_call | solution.py:415
  340.9 7.4 %collective-permute-done.21.refs_2_ = bf16[1024,256]{1,0:T(8,128)(2,1)S(1)} collective-permute-done((bf16[1024,256]{1,0:T(8,128)(2,1)S(1)}, bf16[1024,256]{1,0:T(8,128)(2,1)S(1)}, u32[]{:S(2)}, u32[]{:S(2)}) %collective-permute-start.21) | collective-permute-done | bytes 524320 | tf_op jit(solution)/shard_map/ppermute | solution.py:435
  349.9 3.0 join.6.refs_4_
  353.0 1.2 collective-permute-start.26
  354.2 1.3 collective-permute-start.25
  356.5 2.1 subtract.3.refs_7_.refs_6_
  358.6 1.3 copy-done.8
  360.0 13.3 %product.6.refs_4_ = bf16[1024,256]{1,0:T(8,128)(2,1)} custom-call(s32[8]{0:T(128)} %add_xor_fusion.order_ref, bf16[1024,8192]{1,0:T(8,128)(2,1)} %refs_3_.7, bf16[1024,8192]{1,0:T(8,128)(2,1)} %refs_3_.7, bf16[1024,8192]{1,0:T(8,128)(2,1)} %refs_3_.7, bf16[1024,8192]{1,0:T(8,128)(2,1)} %refs_3_.7, bf16[4096,256]{1,0:T(8,128)(2,1)} %join.6.refs_4_, ...), custom_call_target="tpu_custom_call" | custom-call | flops 12884901888 | bytes 1 | tf_op jit(solution)/shard_map/product/pallas_call | solution.py:415
  373.3 6.2 %collective-permute-done.25.refs_2_ = bf16[1024,256]{1,0:T(8,128)(2,1)} collective-permute-done((bf16[1024,256]{1,0:T(8,128)(2,1)S(1)}, bf16[1024,256]{1,0:T(8,128)(2,1)}, u32[]{:S(2)}, u32[]{:S(2)}) %collective-permute-start.25) | collective-permute-done | bytes 524320 | tf_op jit(solution)/shard_map/ppermute | solution.py:435
  379.5 3.0 join.7.refs_4_
  382.6 4.2 %collective-permute-done.27.refs_5_ = bf16[4096,256]{1,0:T(8,128)(2,1)S(1)} collective-permute-done((bf16[4096,256]{1,0:T(8,128)(2,1)}, bf16[4096,256]{1,0:T(8,128)(2,1)S(1)}, u32[]{:S(2)}, u32[]{:S(2)}) %collective-permute-start.27) | collective-permute-done | bytes 2097184 | tf_op jit(solution)/shard_map/ppermute | solution.py:435
  386.8 1.3 copy-done.10
  388.2 13.3 %product.7 = bf16[1024,256]{1,0:T(8,128)(2,1)} custom-call(s32[8]{0:T(128)} %add_xor_fusion.order_ref, bf16[1024,8192]{1,0:T(8,128)(2,1)} %refs_3_.7, bf16[1024,8192]{1,0:T(8,128)(2,1)} %refs_3_.7, bf16[1024,8192]{1,0:T(8,128)(2,1)} %refs_3_.7, bf16[1024,8192]{1,0:T(8,128)(2,1)} %refs_3_.7, bf16[4096,256]{1,0:T(8,128)(2,1)} %join.7.refs_4_, ...), custom_call_target="tpu_custom_call" | custom-call | flops 12884901888 | bytes 1 | tf_op jit(solution)/shard_map/product/pallas_call | solution.py:415
  401.5 1.1 maximum_bitcast_fusion.1
  402.6 1.5 pad_maximum_fusion
  (151 shorter events, 26.2 us)
Async XLA Ops:
  7.4 97.0 %all-gather.2.cloned.1.call-start = ((), (), s32[]{:S(2)}) async-start(), calls=%async_computation.5 | async-start | bytes 2359296 | tf_op jit(solution)/shard_map/all_gather | solution.py:461
  8.8 187.1 %reduce-scatter.8.cloned.1.call-start = ((), (), s32[]{:S(2)}) async-start(), calls=%async_computation.7 | async-start | bytes 3932160 | tf_op jit(solution)/shard_map/reduce_scatter | solution.py:507
  52.9 143.0 %reduce-scatter.6.cloned.1.call-start = ((), (), s32[]{:S(2)}) async-start(), calls=%async_computation.6 | async-start | bytes 3932160 | tf_op jit(solution)/shard_map/reduce_scatter | solution.py:507
  131.0 1.4 copy-start.12
  131.0 3.7 collective-permute-start
  131.4 136.1 %reduce-scatter.10.cloned.1.call-start = ((), (), s32[]{:S(2)}) async-start(), calls=%async_computation.8 | async-start | bytes 2621440 | tf_op jit(solution)/shard_map/reduce_scatter | solution.py:507
  135.6 10.2 %copy-start.6 = (bf16[768,512]{1,0:T(8,128)(2,1)}, bf16[768,512]{1,0:T(8,128)(2,1)S(1)}, u32[]{:S(2)}) copy-start(bf16[768,512]{1,0:T(8,128)(2,1)S(1)} %pad_maximum_fusion.1.refs_1_) | copy-start | bytes 2359300
  135.6 25.3 %collective-permute-start.1 = (bf16[768,512]{1,0:T(8,128)(2,1)S(1)}, bf16[768,512]{1,0:T(8,128)(2,1)}, u32[]{:S(2)}, u32[]{:S(2)}) collective-permute-start(bf16[768,512]{1,0:T(8,128)(2,1)S(1)} %pad_maximum_fusion.1.refs_1_), channel_id=1, source_target_pairs={{0,8},{4,12},{8,0},{12,4},{16,24},{20,28},{24,16},{28,20},{1,9},{5... | collective-permute-start | bytes 2359304 | tf_op jit(solution)/shard_map/ppermute | solution.py:435
  139.5 36.5 %collective-permute-start.2 = (bf16[768,512]{1,0:T(8,128)(2,1)}, bf16[768,512]{1,0:T(8,128)(2,1)}, u32[]{:S(2)}, u32[]{:S(2)}) collective-permute-start(bf16[768,512]{1,0:T(8,128)(2,1)} %pad_maximum_fusion.2.refs_2_), channel_id=1, source_target_pairs={{0,16},{4,20},{8,24},{12,28},{16,0},{20,4},{24,8},{28,12},{1,17},{... | collective-permute-start | bytes 2359304 | tf_op jit(solution)/shard_map/ppermute | solution.py:435
  141.9 34.0 %collective-permute-start.3 = (bf16[768,512]{1,0:T(8,128)(2,1)}, bf16[768,512]{1,0:T(8,128)(2,1)}, u32[]{:S(2)}, u32[]{:S(2)}) collective-permute-start(bf16[768,512]{1,0:T(8,128)(2,1)} %pad_maximum_fusion.3.refs_3_), channel_id=1, source_target_pairs={{0,24},{4,28},{8,16},{12,20},{16,8},{20,12},{24,0},{28,4},{1,25},{... | collective-permute-start | bytes 2359304 | tf_op jit(solution)/shard_map/ppermute | solution.py:435
  160.8 27.7 %collective-permute-start.8 = (bf16[1536,512]{1,0:T(8,128)(2,1)}, bf16[1536,512]{1,0:T(8,128)(2,1)S(1)}, u32[]{:S(2)}, u32[]{:S(2)}) collective-permute-start(bf16[1536,512]{1,0:T(8,128)(2,1)} %get-tuple-element.28), channel_id=1, source_target_pairs={{0,4},{4,0},{8,12},{12,8},{16,20},{20,16},{24,28},{28,24},{1,5},{5... | collective-permute-start | bytes 4718600 | tf_op jit(solution)/shard_map/ppermute | solution.py:435
  186.3 1.4 copy-start.11
  186.3 83.0 %reduce-scatter.12.cloned.1.call-start = ((), (), s32[]{:S(2)}) async-start(), calls=%async_computation.9 | async-start | bytes 1310720 | tf_op jit(solution)/shard_map/reduce_scatter | solution.py:507
  190.5 20.7 %collective-permute-start.9 = (bf16[768,512]{1,0:T(8,128)(2,1)}, bf16[768,512]{1,0:T(8,128)(2,1)S(1)}, u32[]{:S(2)}, u32[]{:S(2)}) collective-permute-start(bf16[768,512]{1,0:T(8,128)(2,1)} %pad_maximum_fusion.4), channel_id=1, source_target_pairs={{0,8},{4,12},{8,0},{12,4},{16,24},{20,28},{24,16},{28,20},{1,9},{5... | collective-permute-start | bytes 2359304 | tf_op jit(solution)/shard_map/ppermute | solution.py:435
  191.9 35.3 %collective-permute-start.10 = (bf16[768,512]{1,0:T(8,128)(2,1)}, bf16[768,512]{1,0:T(8,128)(2,1)S(1)}, u32[]{:S(2)}, u32[]{:S(2)}) collective-permute-start(bf16[768,512]{1,0:T(8,128)(2,1)} %pad_maximum_fusion.5), channel_id=1, source_target_pairs={{0,16},{4,20},{8,24},{12,28},{16,0},{20,4},{24,8},{28,12},{1,17},{... | collective-permute-start | bytes 2359304 | tf_op jit(solution)/shard_map/ppermute | solution.py:435
  194.5 32.8 %collective-permute-start.11 = (bf16[768,512]{1,0:T(8,128)(2,1)}, bf16[768,512]{1,0:T(8,128)(2,1)S(1)}, u32[]{:S(2)}, u32[]{:S(2)}) collective-permute-start(bf16[768,512]{1,0:T(8,128)(2,1)} %pad_maximum_fusion.6), channel_id=1, source_target_pairs={{0,24},{4,28},{8,16},{12,20},{16,8},{20,12},{24,0},{28,4},{1,25},{... | collective-permute-start | bytes 2359304 | tf_op jit(solution)/shard_map/ppermute | solution.py:435
  204.0 34.5 %collective-permute-start.4 = (bf16[1536,256]{1,0:T(8,128)(2,1)}, bf16[1536,256]{1,0:T(8,128)(2,1)S(1)}, u32[]{:S(2)}, u32[]{:S(2)}) collective-permute-start(bf16[1536,256]{1,0:T(8,128)(2,1)} %get-tuple-element.27), channel_id=1, source_target_pairs={{0,4},{4,0},{8,12},{12,8},{16,20},{20,16},{24,28},{28,24},{1,5},{5... | collective-permute-start | bytes 2359304 | tf_op jit(solution)/shard_map/ppermute | solution.py:435
  211.2 16.1 %copy-start.13 = (bf16[768,512]{1,0:T(8,128)(2,1)}, bf16[768,512]{1,0:T(8,128)(2,1)S(1)}, u32[]{:S(2)}) copy-start(bf16[768,512]{1,0:T(8,128)(2,1)S(1)} %collective-permute-done.9.refs_2_) | copy-start | bytes 2359300
  227.2 0.9 copy-start.14
  227.2 1.2 copy-start.15
  238.2 1.0 copy-start.16
  238.2 118.3 %reduce-scatter.14.cloned.1.call-start = ((), (), s32[]{:S(2)}) async-start(), calls=%async_computation.10 | async-start | bytes 1310720 | tf_op jit(solution)/shard_map/reduce_scatter | solution.py:507
  239.3 12.1 %collective-permute-start.5 = (bf16[768,256]{1,0:T(8,128)(2,1)S(1)}, bf16[768,256]{1,0:T(8,128)(2,1)S(1)}, u32[]{:S(2)}, u32[]{:S(2)}) collective-permute-start(bf16[768,256]{1,0:T(8,128)(2,1)S(1)} %pad_maximum_fusion.7), channel_id=1, source_target_pairs={{0,8},{4,12},{8,0},{12,4},{16,24},{20,28},{24,16},{28,20},{1,9},{5... | collective-permute-start | bytes 1179656 | tf_op jit(solution)/shard_map/ppermute | solution.py:435
  240.9 16.0 %collective-permute-start.6 = (bf16[768,256]{1,0:T(8,128)(2,1)S(1)}, bf16[768,256]{1,0:T(8,128)(2,1)S(1)}, u32[]{:S(2)}, u32[]{:S(2)}) collective-permute-start(bf16[768,256]{1,0:T(8,128)(2,1)S(1)} %pad_maximum_fusion.8), channel_id=1, source_target_pairs={{0,16},{4,20},{8,24},{12,28},{16,0},{20,4},{24,8},{28,12},{1,17},{... | collective-permute-start | bytes 1179656 | tf_op jit(solution)/shard_map/ppermute | solution.py:435
  242.5 14.4 %collective-permute-start.7 = (bf16[768,256]{1,0:T(8,128)(2,1)S(1)}, bf16[768,256]{1,0:T(8,128)(2,1)S(1)}, u32[]{:S(2)}, u32[]{:S(2)}) collective-permute-start(bf16[768,256]{1,0:T(8,128)(2,1)S(1)} %pad_maximum_fusion.9), channel_id=1, source_target_pairs={{0,24},{4,28},{8,16},{12,20},{16,8},{20,12},{24,0},{28,4},{1,25},{... | collective-permute-start | bytes 1179656 | tf_op jit(solution)/shard_map/ppermute | solution.py:435
  251.4 5.5 %copy-start.28 = (bf16[768,256]{1,0:T(8,128)(2,1)}, bf16[768,256]{1,0:T(8,128)(2,1)S(1)}, u32[]{:S(2)}) copy-start(bf16[768,256]{1,0:T(8,128)(2,1)S(1)} %collective-permute-done.5.refs_2_) | copy-start | bytes 1179652
  256.9 0.7 copy-start.29
  256.9 0.9 copy-start.30
  264.1 15.7 %collective-permute-start.14 = (bf16[1024,256]{1,0:T(8,128)(2,1)}, bf16[1024,256]{1,0:T(8,128)(2,1)S(1)}, u32[]{:S(2)}, u32[]{:S(2)}) collective-permute-start(bf16[1024,256]{1,0:T(8,128)(2,1)} %get-tuple-element.30.refs_1_.refs_0_), channel_id=1, source_target_pairs={{0,24},{4,28},{8,16},{12,20},{16,8},{20,12},{24,0},{28,4},{1,25},{... | collective-permute-start | bytes 1572872 | tf_op jit(solution)/shard_map/ppermute | solution.py:435
  265.5 19.8 %collective-permute-start.13 = (bf16[1024,256]{1,0:T(8,128)(2,1)}, bf16[1024,256]{1,0:T(8,128)(2,1)S(1)}, u32[]{:S(2)}, u32[]{:S(2)}) collective-permute-start(bf16[1024,256]{1,0:T(8,128)(2,1)} %get-tuple-element.30.refs_1_.refs_0_), channel_id=1, source_target_pairs={{0,16},{4,20},{8,24},{12,28},{16,0},{20,4},{24,8},{28,12},{1,17},{... | collective-permute-start | bytes 1572872 | tf_op jit(solution)/shard_map/ppermute | solution.py:435
  266.8 19.5 %collective-permute-start.12 = (bf16[1024,256]{1,0:T(8,128)(2,1)}, bf16[1024,256]{1,0:T(8,128)(2,1)S(1)}, u32[]{:S(2)}, u32[]{:S(2)}) collective-permute-start(bf16[1024,256]{1,0:T(8,128)(2,1)} %get-tuple-element.30.refs_1_.refs_0_), channel_id=1, source_target_pairs={{0,8},{4,12},{8,0},{12,4},{16,24},{20,28},{24,16},{28,20},{1,9},{5... | collective-permute-start | bytes 1572872 | tf_op jit(solution)/shard_map/ppermute | solution.py:435
  271.4 19.3 %copy-start.4 = (bf16[1024,256]{1,0:T(8,128)(2,1)S(1)}, bf16[1024,256]{1,0:T(8,128)(2,1)}, u32[]{:S(2)}) copy-start(bf16[1024,256]{1,0:T(8,128)(2,1)} %finish.1.refs_4_.refs_6_.refs_0_) | copy-start | bytes 1572868
  279.8 6.6 %copy-start.18 = (bf16[1024,256]{1,0:T(8,128)(2,1)}, bf16[1024,256]{1,0:T(8,128)(2,1)S(1)}, u32[]{:S(2)}) copy-start(bf16[1024,256]{1,0:T(8,128)(2,1)S(1)} %collective-permute-done.14.refs_3_) | copy-start | bytes 1572868
  285.3 1.0 copy-start.19
  286.3 0.8 copy-start.20
  290.1 4.4 %collective-permute-start.15 = (bf16[4096,256]{1,0:T(8,128)(2,1)}, bf16[4096,256]{1,0:T(8,128)(2,1)S(1)}, u32[]{:S(2)}, u32[]{:S(2)}) collective-permute-start(bf16[4096,256]{1,0:T(8,128)(2,1)} %join.4.refs_4_), channel_id=1, source_target_pairs={{0,4},{4,0},{8,12},{12,8},{16,20},{20,16},{24,28},{28,24},{1,5},{5... | collective-permute-start | bytes 6291464 | tf_op jit(solution)/shard_map/ppermute | solution.py:435
  290.7 18.5 %collective-permute-start.18 = (bf16[1024,256]{1,0:T(8,128)(2,1)S(1)}, bf16[1024,256]{1,0:T(8,128)(2,1)S(1)}, u32[]{:S(2)}, u32[]{:S(2)}) collective-permute-start(bf16[1024,256]{1,0:T(8,128)(2,1)S(1)} %copy-done.4), channel_id=1, source_target_pairs={{0,24},{4,28},{8,16},{12,20},{16,8},{20,12},{24,0},{28,4},{1,25},{... | collective-permute-start | bytes 1572872 | tf_op jit(solution)/shard_map/ppermute | solution.py:435
  292.0 25.2 %collective-permute-start.17 = (bf16[1024,256]{1,0:T(8,128)(2,1)S(1)}, bf16[1024,256]{1,0:T(8,128)(2,1)S(1)}, u32[]{:S(2)}, u32[]{:S(2)}) collective-permute-start(bf16[1024,256]{1,0:T(8,128)(2,1)S(1)} %copy-done.4), channel_id=1, source_target_pairs={{0,16},{4,20},{8,24},{12,28},{16,0},{20,4},{24,8},{28,12},{1,17},{... | collective-permute-start | bytes 1572872 | tf_op jit(solution)/shard_map/ppermute | solution.py:435
  293.2 24.0 %collective-permute-start.16 = (bf16[1024,256]{1,0:T(8,128)(2,1)S(1)}, bf16[1024,256]{1,0:T(8,128)(2,1)S(1)}, u32[]{:S(2)}, u32[]{:S(2)}) collective-permute-start(bf16[1024,256]{1,0:T(8,128)(2,1)S(1)} %copy-done.4), channel_id=1, source_target_pairs={{0,8},{4,12},{8,0},{12,4},{16,24},{20,28},{24,16},{28,20},{1,9},{5... | collective-permute-start | bytes 1572872 | tf_op jit(solution)/shard_map/ppermute | solution.py:435
  294.5 1.3 copy-start.9
  309.2 12.6 %copy-start = (bf16[1024,256]{1,0:T(8,128)(2,1)S(1)}, bf16[1024,256]{1,0:T(8,128)(2,1)}, u32[]{:S(2)}) copy-start(bf16[1024,256]{1,0:T(8,128)(2,1)} %product.4.refs_4_.refs_6_.refs_0_) | copy-start | bytes 1572868
  309.2 8.0 %copy-start.21 = (bf16[1024,256]{1,0:T(8,128)(2,1)}, bf16[1024,256]{1,0:T(8,128)(2,1)S(1)}, u32[]{:S(2)}) copy-start(bf16[1024,256]{1,0:T(8,128)(2,1)S(1)} %collective-permute-done.18.refs_3_) | copy-start | bytes 1572868
  317.2 0.8 copy-start.23
  318.0 0.8 copy-start.25
  321.7 4.4 %collective-permute-start.19 = (bf16[4096,256]{1,0:T(8,128)(2,1)}, bf16[4096,256]{1,0:T(8,128)(2,1)S(1)}, u32[]{:S(2)}, u32[]{:S(2)}) collective-permute-start(bf16[4096,256]{1,0:T(8,128)(2,1)} %join.5.refs_4_), channel_id=1, source_target_pairs={{0,4},{4,0},{8,12},{12,8},{16,20},{20,16},{24,28},{28,24},{1,5},{5... | collective-permute-start | bytes 6291464 | tf_op jit(solution)/shard_map/ppermute | solution.py:435
  321.8 19.1 %collective-permute-start.22 = (bf16[1024,256]{1,0:T(8,128)(2,1)S(1)}, bf16[1024,256]{1,0:T(8,128)(2,1)S(1)}, u32[]{:S(2)}, u32[]{:S(2)}) collective-permute-start(bf16[1024,256]{1,0:T(8,128)(2,1)S(1)} %copy-done), channel_id=1, source_target_pairs={{0,24},{4,28},{8,16},{12,20},{16,8},{20,12},{24,0},{28,4},{1,25},{... | collective-permute-start | bytes 1572872 | tf_op jit(solution)/shard_map/ppermute | solution.py:435
  323.2 25.1 %collective-permute-start.21 = (bf16[1024,256]{1,0:T(8,128)(2,1)S(1)}, bf16[1024,256]{1,0:T(8,128)(2,1)S(1)}, u32[]{:S(2)}, u32[]{:S(2)}) collective-permute-start(bf16[1024,256]{1,0:T(8,128)(2,1)S(1)} %copy-done), channel_id=1, source_target_pairs={{0,16},{4,20},{8,24},{12,28},{16,0},{20,4},{24,8},{28,12},{1,17},{... | collective-permute-start | bytes 1572872 | tf_op jit(solution)/shard_map/ppermute | solution.py:435
  324.4 23.9 %collective-permute-start.20 = (bf16[1024,256]{1,0:T(8,128)(2,1)S(1)}, bf16[1024,256]{1,0:T(8,128)(2,1)S(1)}, u32[]{:S(2)}, u32[]{:S(2)}) collective-permute-start(bf16[1024,256]{1,0:T(8,128)(2,1)S(1)} %copy-done), channel_id=1, source_target_pairs={{0,8},{4,12},{8,0},{12,4},{16,24},{20,28},{24,16},{28,20},{1,9},{5... | collective-permute-start | bytes 1572872 | tf_op jit(solution)/shard_map/ppermute | solution.py:435
  326.1 1.3 copy-start.7
  340.9 12.1 %copy-start.2 = (bf16[1024,256]{1,0:T(8,128)(2,1)S(1)}, bf16[1024,256]{1,0:T(8,128)(2,1)}, u32[]{:S(2)}) copy-start(bf16[1024,256]{1,0:T(8,128)(2,1)} %product.5.refs_4_.refs_2_.refs_0_) | copy-start | bytes 1572868
  340.9 7.4 %copy-start.22 = (bf16[1024,256]{1,0:T(8,128)(2,1)}, bf16[1024,256]{1,0:T(8,128)(2,1)S(1)}, u32[]{:S(2)}) copy-start(bf16[1024,256]{1,0:T(8,128)(2,1)S(1)} %collective-permute-done.22.refs_3_) | copy-start | bytes 1572868
  348.3 0.8 copy-start.24
  349.1 0.8 copy-start.26
  352.9 5.7 %collective-permute-start.23 = (bf16[4096,256]{1,0:T(8,128)(2,1)}, bf16[4096,256]{1,0:T(8,128)(2,1)S(1)}, u32[]{:S(2)}, u32[]{:S(2)}) collective-permute-start(bf16[4096,256]{1,0:T(8,128)(2,1)} %join.6.refs_4_), channel_id=1, source_target_pairs={{0,4},{4,0},{8,12},{12,8},{16,20},{20,16},{24,28},{28,24},{1,5},{5... | collective-permute-start | bytes 6291464 | tf_op jit(solution)/shard_map/ppermute | solution.py:435
  353.0 20.3 %collective-permute-start.26 = (bf16[1024,256]{1,0:T(8,128)(2,1)S(1)}, bf16[1024,256]{1,0:T(8,128)(2,1)S(1)}, u32[]{:S(2)}, u32[]{:S(2)}) collective-permute-start(bf16[1024,256]{1,0:T(8,128)(2,1)S(1)} %copy-done.2), channel_id=1, source_target_pairs={{0,24},{4,28},{8,16},{12,20},{16,8},{20,12},{24,0},{28,4},{1,25},{... | collective-permute-start | bytes 1572872 | tf_op jit(solution)/shard_map/ppermute | solution.py:435
  354.2 25.3 %collective-permute-start.25 = (bf16[1024,256]{1,0:T(8,128)(2,1)S(1)}, bf16[1024,256]{1,0:T(8,128)(2,1)}, u32[]{:S(2)}, u32[]{:S(2)}) collective-permute-start(bf16[1024,256]{1,0:T(8,128)(2,1)S(1)} %copy-done.2), channel_id=1, source_target_pairs={{0,16},{4,20},{8,24},{12,28},{16,0},{20,4},{24,8},{28,12},{1,17},{... | collective-permute-start | bytes 1572872 | tf_op jit(solution)/shard_map/ppermute | solution.py:435
  355.5 24.0 %collective-permute-start.24 = (bf16[1024,256]{1,0:T(8,128)(2,1)S(1)}, bf16[1024,256]{1,0:T(8,128)(2,1)}, u32[]{:S(2)}, u32[]{:S(2)}) collective-permute-start(bf16[1024,256]{1,0:T(8,128)(2,1)S(1)} %copy-done.2), channel_id=1, source_target_pairs={{0,8},{4,12},{8,0},{12,4},{16,24},{20,28},{24,16},{28,20},{1,9},{5... | collective-permute-start | bytes 1572872 | tf_op jit(solution)/shard_map/ppermute | solution.py:435
  358.6 1.3 copy-start.8
  373.3 9.2 %copy-start.1 = (bf16[1024,256]{1,0:T(8,128)(2,1)S(1)}, bf16[1024,256]{1,0:T(8,128)(2,1)}, u32[]{:S(2)}) copy-start(bf16[1024,256]{1,0:T(8,128)(2,1)} %product.4.refs_4_.refs_6_.refs_0_) | copy-start | bytes 1572868
  373.3 9.2 %copy-start.3 = (bf16[1024,256]{1,0:T(8,128)(2,1)S(1)}, bf16[1024,256]{1,0:T(8,128)(2,1)}, u32[]{:S(2)}) copy-start(bf16[1024,256]{1,0:T(8,128)(2,1)} %product.5.refs_4_.refs_2_.refs_0_) | copy-start | bytes 1572868
  373.3 6.2 %copy-start.17 = (bf16[1024,256]{1,0:T(8,128)(2,1)}, bf16[1024,256]{1,0:T(8,128)(2,1)S(1)}, u32[]{:S(2)}) copy-start(bf16[1024,256]{1,0:T(8,128)(2,1)S(1)} %collective-permute-done.26.refs_3_) | copy-start | bytes 1572868
  382.5 4.4 %collective-permute-start.27 = (bf16[4096,256]{1,0:T(8,128)(2,1)}, bf16[4096,256]{1,0:T(8,128)(2,1)S(1)}, u32[]{:S(2)}, u32[]{:S(2)}) collective-permute-start(bf16[4096,256]{1,0:T(8,128)(2,1)} %join.7.refs_4_), channel_id=1, source_target_pairs={{0,4},{4,0},{8,12},{12,8},{16,20},{20,16},{24,28},{28,24},{1,5},{5... | collective-permute-start | bytes 6291464 | tf_op jit(solution)/shard_map/ppermute | solution.py:435
  382.6 18.9 %copy-start.5 = (bf16[1024,256]{1,0:T(8,128)(2,1)S(1)}, bf16[1024,256]{1,0:T(8,128)(2,1)}, u32[]{:S(2)}) copy-start(bf16[1024,256]{1,0:T(8,128)(2,1)} %product.6.refs_4_) | copy-start | bytes 1572868
  386.8 1.3 copy-start.10
  (1 other events, 0.7 us)
Sparse Core Ops, SparseCore 0:
  10.1 30.5 all-gather.1
Sparse Core Ops, SparseCore 1:
  52.9 67.5 reduce-scatter.7
  131.5 62.4 reduce-scatter.5
  196.1 43.4 reduce-scatter.9
  242.0 26.4 reduce-scatter.11
  321.9 27.1 reduce-scatter.13

commit v10 on v9

--- a/solution.py
+++ b/solution.py
@@ -156,7 +156,7 @@
 def front_products(front, tiles, meta, subs, flats, n_col, after=()):
     rows, depth = front.shape
     groups = n_col * len(subs)
-    block = largest_tile(rows, 512)
+    block = largest_tile(rows, 1024)
     streams = 8 if block % 128 == 0 else 1
     count = tiles.shape[0]
     items = (-(-count // STACK) + groups + STACK) // STACK * STACK

time: 416 us -> 414 us (level)
  the two profiles are of different devices: /device:TPU:0 before, /device:TPU:25 now
where the time goes in v10:
time: 414 us; the launch traced here: 408 us
  Pallas kernels  224 us (54%)
  waiting for transfers between devices  90.5 us (22%)
  starting transfers between devices  28.5 us (7%)
  local copies, waits for them, and re-layouts  25.8 us (6%)
  other arithmetic  23.8 us (6%)
  between operations  15.7 us (4%)
    pallas_call x2, Pallas kernels, front_products(): pl.pallas_call(functools.partial(front_kernel, subs, flats, n_col, len(af...  90.8 us
    ppermute x28, waiting for transfers between devices, exchange(): return lax.ppermute(value, axis, [(i, i ^ distance) for i in range(n)])  89.2 us
    pallas_call x4, Pallas kernels, product(): pl.pallas_call(functools.partial(product_kernel, streams, bool(bases)), g...  53.5 us
    pallas_call x3, Pallas kernels, pack_rows(): pl.pallas_call(functools.partial(pack_kernel, n_row, len(solved)), in_spe...  35.4 us
    ppermute x28, starting transfers between devices, exchange(): return lax.ppermute(value, axis, [(i, i ^ distance) for i in range(n)])  28.1 us
    pallas_call x2, Pallas kernels, unpack(): pl.pallas_call(functools.partial(unpack_kernel, len(pieces), n_col, parts...  20.2 us
    unnamed x71, local copies, waits for them, and re-layouts  17 us
    pallas_call x4, Pallas kernels, join(): pl.pallas_call(functools.partial(join_kernel, len(parts)), in_specs=[whol...  11.9 us
  transfers between devices with their start and end apart: 34, of which 17 were waited for; matrix products, arithmetic and copies ran while one was open for 8% of the time, Pallas kernels for 49%

profile of v10, /device:TPU:25, one launch (start us, length us, event | category | flops | bytes accessed | tf_op | source)
XLA Modules:
  0.0 408.2 jit_solution(6734858469443604371)
XLA Ops:
  10.8 47.4 %front_products.2 = (bf16[4,3072,128]{2,1,0:T(8,128)(2,1)}, bf16[4,3072,128]{2,1,0:T(8,128)(2,1)}) custom-call(s32[3,192]{1,0:T(4,128)} %pad_add_fusion.meta_ref, bf16[192,128,128]{2,1,0:T(8,128)(2,1)} %tiles_ref.3, bf16[3072,6144]{1,0:T(8,128)(2,1)} %front_ref.3), custom_call_target="tpu_custom_call" | custom-call | bytes 1 | tf_op jit(solution)/shard_map/front_products/pallas_call | solution.py:171
  58.3 43.4 %front_products.3 = (bf16[3072,512]{1,0:T(8,128)(2,1)}, bf16[3072,512]{1,0:T(8,128)(2,1)}) custom-call(s32[3,192]{1,0:T(4,128)} %pad_add_fusion.meta_ref, bf16[192,128,128]{2,1,0:T(8,128)(2,1)} %tiles_ref.3, bf16[3072,6144]{1,0:T(8,128)(2,1)} %front_ref.3, bf16[4,3072,128]{2,1,0:T(8,128)(2,1)} %get-tuple-element.19.refs_0_), custom_call_target="tpu_custom_call" | custom-call | bytes 1 | tf_op jit(solution)/shard_map/front_products/pallas_call | solution.py:171
  101.8 1.1 slice.119
  103.5 2.4 reduce-window.16
  106.6 6.2 %select_reduce_fusion = s32[8,384]{1,0:T(8,128)S(1)} fusion(s32[8,2048]{1,0:T(8,128)S(1)} %subtract_add_fusion, s32[8,2048]{1,0:T(8,128)S(1)} %bitcast.55, pred[8,2048]{1,0:T(8,128)(4,1)S(1)} %get-tuple-element.34), kind=kLoop, calls=%fused_computation.1 | loop fusion | flops 25162752 | bytes 159744 | tf_op jit(solution)/shard_map/reduce_sum | solution.py:468
  112.8 1.7 copy.44
  114.5 13.9 %pack_rows.3 = (bf16[1536,512]{1,0:T(8,128)(2,1)}, bf16[1536,512]{1,0:T(8,128)(2,1)}) custom-call(s32[3072,1]{1,0:T(8,128)} %bitcast.48, bf16[3072,512]{1,0:T(8,128)(2,1)} %get-tuple-element.21.refs_0_), custom_call_target="tpu_custom_call" | custom-call | bytes 1 | tf_op jit(solution)/shard_map/pack_rows/pallas_call | solution.py:214
  130.6 1.6 collective-permute-done
  133.2 1.3 collective-permute-start.1
  135.4 1.2 collective-permute-start.2
  136.7 0.9 pad_maximum_fusion.3.refs_3_
  137.9 2.3 reduce-window.14
  141.9 1.2 fusion.3.index_ref
  143.2 13.4 %pack_rows.4 = (bf16[1536,512]{1,0:T(8,128)(2,1)}, bf16[1536,512]{1,0:T(8,128)(2,1)}) custom-call(s32[3072,1]{1,0:T(8,128)} %bitcast.49, bf16[3072,512]{1,0:T(8,128)(2,1)} %get-tuple-element.24.refs_0_, bf16[768,512]{1,0:T(8,128)(2,1)} %copy-done.6, bf16[768,512]{1,0:T(8,128)(2,1)} %pad_maximum_fusion.2.refs_2_, bf16[768,512]{1,0:T(8,128)(2,1)} %pad_maximum_fusion.3.refs_3_), custom_call_target="tpu_custom_call" | custom-call | bytes 1 | tf_op jit(solution)/shard_map/pack_rows/pallas_call | solution.py:214
  156.6 1.2 collective-permute-start.8
  157.8 13.2 %collective-permute-done.2.refs_3_ = bf16[768,512]{1,0:T(8,128)(2,1)} collective-permute-done((bf16[768,512]{1,0:T(8,128)(2,1)}, bf16[768,512]{1,0:T(8,128)(2,1)}, u32[]{:S(2)}, u32[]{:S(2)}) %collective-permute-start.2) | collective-permute-done | bytes 786464 | tf_op jit(solution)/shard_map/ppermute | solution.py:435
  171.0 10.4 %unpack.2.refs_2_ = bf16[4,2048,128]{2,1,0:T(8,128)(2,1)} custom-call(s32[2048,1]{1,0:T(8,128)} %fusion.3.index_ref, bf16[384,512]{1,0:T(8,128)(2,1)} %get-tuple-element.46.refs_0_, bf16[384,512]{1,0:T(8,128)(2,1)} %get-tuple-element.50.refs_1_, bf16[768,512]{1,0:T(8,128)(2,1)} %collective-permute-done.1.refs_2_, ...), custom_call_target="tpu_custom_call" | custom-call | flops 38654705664 | bytes 1 | tf_op jit(solution)/shard_map/unpack/pallas_call | solution.py:359
  181.5 1.3 copy-done.11
  184.5 1.0 pad_maximum_fusion.4
  185.7 1.0 pad_maximum_fusion.5
  186.7 1.3 collective-permute-start.10
  188.0 0.9 pad_maximum_fusion.6
  189.0 1.1 collective-permute-start.11
  190.1 8.1 %pack_rows.5 = (bf16[1536,256]{1,0:T(8,128)(2,1)}, bf16[1536,256]{1,0:T(8,128)(2,1)}) custom-call(s32[3072,1]{1,0:T(8,128)} %bitcast.50, bf16[3072,128]{1,0:T(8,128)(2,1)} %bitcast.69, bf16[3072,128]{1,0:T(8,128)(2,1)} %bitcast.68, bf16[4,2048,128]{2,1,0:T(8,128)(2,1)} %unpack.2.refs_2_), custom_call_target="tpu_custom_call" | custom-call | flops 28991029248 | bytes 1 | tf_op jit(solution)/shard_map/pack_rows/pallas_call | solution.py:214
  198.2 2.4 collective-permute-start.4
  200.6 2.0 fusion.10
  204.3 16.9 %collective-permute-done.11.refs_4_ = bf16[768,512]{1,0:T(8,128)(2,1)S(1)} collective-permute-done((bf16[768,512]{1,0:T(8,128)(2,1)}, bf16[768,512]{1,0:T(8,128)(2,1)S(1)}, u32[]{:S(2)}, u32[]{:S(2)}) %collective-permute-start.11) | collective-permute-done | bytes 786464 | tf_op jit(solution)/shard_map/ppermute | solution.py:435
  222.1 9.8 %unpack.3 = (bf16[4,1024,128]{2,1,0:T(8,128)(2,1)}, bf16[4,1024,128]{2,1,0:T(8,128)(2,1)}) custom-call(s32[2048,1]{1,0:T(8,128)} %fusion.3.index_ref, bf16[384,512]{1,0:T(8,128)(2,1)} %get-tuple-element.38.refs_0_, bf16[384,512]{1,0:T(8,128)(2,1)} %get-tuple-element.42.refs_1_, bf16[768,512]{1,0:T(8,128)(2,1)} %copy-done.13, bf16[768,512]{1,0:T(8,128)(2,1)} %copy-done.14, ...), custom_call_target="tpu_custom_call" | custom-call | bytes 1 | tf_op jit(solution)/shard_map/unpack/pallas_call | solution.py:359
  233.6 2.2 collective-permute-start.7
  235.9 4.9 %collective-permute-done.5.refs_2_ = bf16[768,256]{1,0:T(8,128)(2,1)S(1)} collective-permute-done((bf16[768,256]{1,0:T(8,128)(2,1)S(1)}, bf16[768,256]{1,0:T(8,128)(2,1)S(1)}, u32[]{:S(2)}, u32[]{:S(2)}) %collective-permute-start.5) | collective-permute-done | bytes 393248 | tf_op jit(solution)/shard_map/ppermute | solution.py:435
  241.3 6.4 %collective-permute-done.7.refs_4_ = bf16[768,256]{1,0:T(8,128)(2,1)S(1)} collective-permute-done((bf16[768,256]{1,0:T(8,128)(2,1)S(1)}, bf16[768,256]{1,0:T(8,128)(2,1)S(1)}, u32[]{:S(2)}, u32[]{:S(2)}) %collective-permute-start.7) | collective-permute-done | bytes 393248 | tf_op jit(solution)/shard_map/ppermute | solution.py:435
  248.4 6.3 %assemble.1 = (bf16[1024,256]{1,0:T(8,128)(2,1)}, bf16[1024,256]{1,0:T(8,128)(2,1)}) custom-call(s32[2048,1]{1,0:T(8,128)} %fusion.3.index_ref, bf16[2,1024,512]{2,1,0:T(8,128)(2,1)} %bem_ref.7, bf16[384,256]{1,0:T(8,128)(2,1)} %get-tuple-element.54.refs_0_, bf16[384,256]{1,0:T(8,128)(2,1)} %get-tuple-element.58.refs_1_, bf16[768,256]{1,0:T(8,128)(2,1)} %copy-done.28, ...), custom_call_target="tpu_custom_call" | custom-call | flops 6442450944 | bytes 1 | tf_op jit(solution)/shard_map/assemble/pallas_call | solution.py:251
  254.7 1.7 collective-permute-start.14
  256.4 1.0 collective-permute-start.13
  257.4 1.2 collective-permute-start.12
  258.6 1.8 subtract.2.ready_ref
  260.4 1.2 reduce-scatter.12.cloned.1.call-done
  261.6 2.0 finish.1.refs_4_.refs_6_.refs_0_
  263.9 16.0 %collective-permute-done.13.refs_2_ = bf16[1024,256]{1,0:T(8,128)(2,1)S(1)} collective-permute-done((bf16[1024,256]{1,0:T(8,128)(2,1)}, bf16[1024,256]{1,0:T(8,128)(2,1)S(1)}, u32[]{:S(2)}, u32[]{:S(2)}) %collective-permute-start.13) | collective-permute-done | bytes 524320 | tf_op jit(solution)/shard_map/ppermute | solution.py:435
  281.6 3.0 join.4.refs_4_
  284.5 2.2 collective-permute-start.15
  288.3 1.0 collective-permute-start.17
  290.8 1.3 copy-done.9
  292.1 13.4 %product.4.refs_4_.refs_6_.refs_0_ = bf16[1024,256]{1,0:T(8,128)(2,1)} custom-call(s32[8]{0:T(128)} %add_xor_fusion.order_ref, bf16[1024,8192]{1,0:T(8,128)(2,1)} %refs_3_.5, bf16[1024,8192]{1,0:T(8,128)(2,1)} %refs_3_.5, bf16[1024,8192]{1,0:T(8,128)(2,1)} %refs_3_.5, bf16[1024,8192]{1,0:T(8,128)(2,1)} %refs_3_.5, bf16[4096,256]{1,0:T(8,128)(2,1)} %join.4.refs_4_, ...), custom_call_target="tpu_custom_call" | custom-call | flops 12884901888 | bytes 1 | tf_op jit(solution)/shard_map/product/pallas_call | solution.py:415
  305.5 7.8 %collective-permute-done.17.refs_2_ = bf16[1024,256]{1,0:T(8,128)(2,1)S(1)} collective-permute-done((bf16[1024,256]{1,0:T(8,128)(2,1)S(1)}, bf16[1024,256]{1,0:T(8,128)(2,1)S(1)}, u32[]{:S(2)}, u32[]{:S(2)}) %collective-permute-start.17) | collective-permute-done | bytes 524320 | tf_op jit(solution)/shard_map/ppermute | solution.py:435
  314.9 3.0 join.5.refs_4_
  318.4 1.0 collective-permute-start.22
  319.4 1.0 collective-permute-start.21
  321.2 1.2 collective-permute-done.19.refs_5_
  322.4 1.3 copy-done.7
  323.7 13.4 %product.5.refs_4_.refs_2_.refs_0_ = bf16[1024,256]{1,0:T(8,128)(2,1)} custom-call(s32[8]{0:T(128)} %add_xor_fusion.order_ref, bf16[1024,8192]{1,0:T(8,128)(2,1)} %refs_3_.5, bf16[1024,8192]{1,0:T(8,128)(2,1)} %refs_3_.5, bf16[1024,8192]{1,0:T(8,128)(2,1)} %refs_3_.5, bf16[1024,8192]{1,0:T(8,128)(2,1)} %refs_3_.5, bf16[4096,256]{1,0:T(8,128)(2,1)} %join.5.refs_4_, ...), custom_call_target="tpu_custom_call" | custom-call | flops 12884901888 | bytes 1 | tf_op jit(solution)/shard_map/product/pallas_call | solution.py:415
  337.2 7.3 %collective-permute-done.21.refs_2_ = bf16[1024,256]{1,0:T(8,128)(2,1)S(1)} collective-permute-done((bf16[1024,256]{1,0:T(8,128)(2,1)S(1)}, bf16[1024,256]{1,0:T(8,128)(2,1)S(1)}, u32[]{:S(2)}, u32[]{:S(2)}) %collective-permute-start.21) | collective-permute-done | bytes 524320 | tf_op jit(solution)/shard_map/ppermute | solution.py:435
  346.1 3.0 join.6.refs_4_
  350.4 1.0 collective-permute-start.25
  352.2 2.1 subtract.3.refs_7_.refs_6_
  354.3 1.3 copy-done.8
  355.7 13.3 %product.6.refs_4_ = bf16[1024,256]{1,0:T(8,128)(2,1)} custom-call(s32[8]{0:T(128)} %add_xor_fusion.order_ref, bf16[1024,8192]{1,0:T(8,128)(2,1)} %refs_3_.7, bf16[1024,8192]{1,0:T(8,128)(2,1)} %refs_3_.7, bf16[1024,8192]{1,0:T(8,128)(2,1)} %refs_3_.7, bf16[1024,8192]{1,0:T(8,128)(2,1)} %refs_3_.7, bf16[4096,256]{1,0:T(8,128)(2,1)} %join.6.refs_4_, ...), custom_call_target="tpu_custom_call" | custom-call | flops 12884901888 | bytes 1 | tf_op jit(solution)/shard_map/product/pallas_call | solution.py:415
  369.0 6.6 %collective-permute-done.25.refs_2_ = bf16[1024,256]{1,0:T(8,128)(2,1)} collective-permute-done((bf16[1024,256]{1,0:T(8,128)(2,1)S(1)}, bf16[1024,256]{1,0:T(8,128)(2,1)}, u32[]{:S(2)}, u32[]{:S(2)}) %collective-permute-start.25) | collective-permute-done | bytes 524320 | tf_op jit(solution)/shard_map/ppermute | solution.py:435
  375.7 3.0 join.7.refs_4_
  379.2 3.9 collective-permute-done.27.refs_5_
  383.1 1.3 copy-done.10
  384.4 13.3 %product.7 = bf16[1024,256]{1,0:T(8,128)(2,1)} custom-call(s32[8]{0:T(128)} %add_xor_fusion.order_ref, bf16[1024,8192]{1,0:T(8,128)(2,1)} %refs_3_.7, bf16[1024,8192]{1,0:T(8,128)(2,1)} %refs_3_.7, bf16[1024,8192]{1,0:T(8,128)(2,1)} %refs_3_.7, bf16[1024,8192]{1,0:T(8,128)(2,1)} %refs_3_.7, bf16[4096,256]{1,0:T(8,128)(2,1)} %join.7.refs_4_, ...), custom_call_target="tpu_custom_call" | custom-call | flops 12884901888 | bytes 1 | tf_op jit(solution)/shard_map/product/pallas_call | solution.py:415
  397.8 1.1 maximum_bitcast_fusion.1
  398.9 1.5 pad_maximum_fusion
  (151 shorter events, 30.3 us)
Async XLA Ops:
  7.4 94.4 %all-gather.2.cloned.1.call-start = ((), (), s32[]{:S(2)}) async-start(), calls=%async_computation.5 | async-start | bytes 2359296 | tf_op jit(solution)/shard_map/all_gather | solution.py:461
  8.8 181.3 %reduce-scatter.8.cloned.1.call-start = ((), (), s32[]{:S(2)}) async-start(), calls=%async_computation.7 | async-start | bytes 3932160 | tf_op jit(solution)/shard_map/reduce_scatter | solution.py:507
  58.3 131.9 %reduce-scatter.6.cloned.1.call-start = ((), (), s32[]{:S(2)}) async-start(), calls=%async_computation.6 | async-start | bytes 3932160 | tf_op jit(solution)/shard_map/reduce_scatter | solution.py:507
  128.4 0.8 copy-start.27
  128.4 1.4 copy-start.12
  128.4 3.9 collective-permute-start
  129.1 129.6 %reduce-scatter.10.cloned.1.call-start = ((), (), s32[]{:S(2)}) async-start(), calls=%async_computation.8 | async-start | bytes 2621440 | tf_op jit(solution)/shard_map/reduce_scatter | solution.py:507
  133.2 8.4 %copy-start.6 = (bf16[768,512]{1,0:T(8,128)(2,1)}, bf16[768,512]{1,0:T(8,128)(2,1)S(1)}, u32[]{:S(2)}) copy-start(bf16[768,512]{1,0:T(8,128)(2,1)S(1)} %pad_maximum_fusion.1.refs_1_) | copy-start | bytes 2359300
  133.2 24.6 %collective-permute-start.1 = (bf16[768,512]{1,0:T(8,128)(2,1)S(1)}, bf16[768,512]{1,0:T(8,128)(2,1)}, u32[]{:S(2)}, u32[]{:S(2)}) collective-permute-start(bf16[768,512]{1,0:T(8,128)(2,1)S(1)} %pad_maximum_fusion.1.refs_1_), channel_id=1, source_target_pairs={{0,8},{4,12},{8,0},{12,4},{16,24},{20,28},{24,16},{28,20},{1,9},{5... | collective-permute-start | bytes 2359304 | tf_op jit(solution)/shard_map/ppermute | solution.py:435
  135.4 35.6 %collective-permute-start.2 = (bf16[768,512]{1,0:T(8,128)(2,1)}, bf16[768,512]{1,0:T(8,128)(2,1)}, u32[]{:S(2)}, u32[]{:S(2)}) collective-permute-start(bf16[768,512]{1,0:T(8,128)(2,1)} %pad_maximum_fusion.2.refs_2_), channel_id=1, source_target_pairs={{0,16},{4,20},{8,24},{12,28},{16,0},{20,4},{24,8},{28,12},{1,17},{... | collective-permute-start | bytes 2359304 | tf_op jit(solution)/shard_map/ppermute | solution.py:435
  137.6 33.4 %collective-permute-start.3 = (bf16[768,512]{1,0:T(8,128)(2,1)}, bf16[768,512]{1,0:T(8,128)(2,1)}, u32[]{:S(2)}, u32[]{:S(2)}) collective-permute-start(bf16[768,512]{1,0:T(8,128)(2,1)} %pad_maximum_fusion.3.refs_3_), channel_id=1, source_target_pairs={{0,24},{4,28},{8,16},{12,20},{16,8},{20,12},{24,0},{28,4},{1,25},{... | collective-permute-start | bytes 2359304 | tf_op jit(solution)/shard_map/ppermute | solution.py:435
  156.6 27.0 %collective-permute-start.8 = (bf16[1536,512]{1,0:T(8,128)(2,1)}, bf16[1536,512]{1,0:T(8,128)(2,1)S(1)}, u32[]{:S(2)}, u32[]{:S(2)}) collective-permute-start(bf16[1536,512]{1,0:T(8,128)(2,1)} %get-tuple-element.28), channel_id=1, source_target_pairs={{0,4},{4,0},{8,12},{12,8},{16,20},{20,16},{24,28},{28,24},{1,5},{5... | collective-permute-start | bytes 4718600 | tf_op jit(solution)/shard_map/ppermute | solution.py:435
  181.4 1.4 copy-start.11
  181.4 80.2 %reduce-scatter.12.cloned.1.call-start = ((), (), s32[]{:S(2)}) async-start(), calls=%async_computation.9 | async-start | bytes 1310720 | tf_op jit(solution)/shard_map/reduce_scatter | solution.py:507
  185.5 17.8 %collective-permute-start.9 = (bf16[768,512]{1,0:T(8,128)(2,1)}, bf16[768,512]{1,0:T(8,128)(2,1)S(1)}, u32[]{:S(2)}, u32[]{:S(2)}) collective-permute-start(bf16[768,512]{1,0:T(8,128)(2,1)} %pad_maximum_fusion.4), channel_id=1, source_target_pairs={{0,8},{4,12},{8,0},{12,4},{16,24},{20,28},{24,16},{28,20},{1,9},{5... | collective-permute-start | bytes 2359304 | tf_op jit(solution)/shard_map/ppermute | solution.py:435
  186.7 17.5 %collective-permute-start.10 = (bf16[768,512]{1,0:T(8,128)(2,1)}, bf16[768,512]{1,0:T(8,128)(2,1)S(1)}, u32[]{:S(2)}, u32[]{:S(2)}) collective-permute-start(bf16[768,512]{1,0:T(8,128)(2,1)} %pad_maximum_fusion.5), channel_id=1, source_target_pairs={{0,16},{4,20},{8,24},{12,28},{16,0},{20,4},{24,8},{28,12},{1,17},{... | collective-permute-start | bytes 2359304 | tf_op jit(solution)/shard_map/ppermute | solution.py:435
  189.0 32.2 %collective-permute-start.11 = (bf16[768,512]{1,0:T(8,128)(2,1)}, bf16[768,512]{1,0:T(8,128)(2,1)S(1)}, u32[]{:S(2)}, u32[]{:S(2)}) collective-permute-start(bf16[768,512]{1,0:T(8,128)(2,1)} %pad_maximum_fusion.6), channel_id=1, source_target_pairs={{0,24},{4,28},{8,16},{12,20},{16,8},{20,12},{24,0},{28,4},{1,25},{... | collective-permute-start | bytes 2359304 | tf_op jit(solution)/shard_map/ppermute | solution.py:435
  198.2 34.0 %collective-permute-start.4 = (bf16[1536,256]{1,0:T(8,128)(2,1)}, bf16[1536,256]{1,0:T(8,128)(2,1)S(1)}, u32[]{:S(2)}, u32[]{:S(2)}) collective-permute-start(bf16[1536,256]{1,0:T(8,128)(2,1)} %get-tuple-element.27), channel_id=1, source_target_pairs={{0,4},{4,0},{8,12},{12,8},{16,20},{20,16},{24,28},{28,24},{1,5},{5... | collective-permute-start | bytes 2359304 | tf_op jit(solution)/shard_map/ppermute | solution.py:435
  203.3 17.9 %copy-start.13 = (bf16[768,512]{1,0:T(8,128)(2,1)}, bf16[768,512]{1,0:T(8,128)(2,1)S(1)}, u32[]{:S(2)}) copy-start(bf16[768,512]{1,0:T(8,128)(2,1)S(1)} %collective-permute-done.9.refs_2_) | copy-start | bytes 2359300
  204.3 16.9 %copy-start.14 = (bf16[768,512]{1,0:T(8,128)(2,1)}, bf16[768,512]{1,0:T(8,128)(2,1)S(1)}, u32[]{:S(2)}) copy-start(bf16[768,512]{1,0:T(8,128)(2,1)S(1)} %collective-permute-done.10.refs_3_) | copy-start | bytes 2359300
  221.2 0.9 copy-start.15
  231.9 1.0 copy-start.16
  231.9 120.3 %reduce-scatter.14.cloned.1.call-start = ((), (), s32[]{:S(2)}) async-start(), calls=%async_computation.10 | async-start | bytes 1310720 | tf_op jit(solution)/shard_map/reduce_scatter | solution.py:507
  233.0 7.8 %collective-permute-start.5 = (bf16[768,256]{1,0:T(8,128)(2,1)S(1)}, bf16[768,256]{1,0:T(8,128)(2,1)S(1)}, u32[]{:S(2)}, u32[]{:S(2)}) collective-permute-start(bf16[768,256]{1,0:T(8,128)(2,1)S(1)} %pad_maximum_fusion.7), channel_id=1, source_target_pairs={{0,8},{4,12},{8,0},{12,4},{16,24},{20,28},{24,16},{28,20},{1,9},{5... | collective-permute-start | bytes 1179656 | tf_op jit(solution)/shard_map/ppermute | solution.py:435
  233.3 8.0 %collective-permute-start.6 = (bf16[768,256]{1,0:T(8,128)(2,1)S(1)}, bf16[768,256]{1,0:T(8,128)(2,1)S(1)}, u32[]{:S(2)}, u32[]{:S(2)}) collective-permute-start(bf16[768,256]{1,0:T(8,128)(2,1)S(1)} %pad_maximum_fusion.8), channel_id=1, source_target_pairs={{0,16},{4,20},{8,24},{12,28},{16,0},{20,4},{24,8},{28,12},{1,17},{... | collective-permute-start | bytes 1179656 | tf_op jit(solution)/shard_map/ppermute | solution.py:435
  233.6 14.0 %collective-permute-start.7 = (bf16[768,256]{1,0:T(8,128)(2,1)S(1)}, bf16[768,256]{1,0:T(8,128)(2,1)S(1)}, u32[]{:S(2)}, u32[]{:S(2)}) collective-permute-start(bf16[768,256]{1,0:T(8,128)(2,1)S(1)} %pad_maximum_fusion.9), channel_id=1, source_target_pairs={{0,24},{4,28},{8,16},{12,20},{16,8},{20,12},{24,0},{28,4},{1,25},{... | collective-permute-start | bytes 1179656 | tf_op jit(solution)/shard_map/ppermute | solution.py:435
  240.8 6.9 %copy-start.28 = (bf16[768,256]{1,0:T(8,128)(2,1)}, bf16[768,256]{1,0:T(8,128)(2,1)S(1)}, u32[]{:S(2)}) copy-start(bf16[768,256]{1,0:T(8,128)(2,1)S(1)} %collective-permute-done.5.refs_2_) | copy-start | bytes 1179652
  241.3 6.4 %copy-start.29 = (bf16[768,256]{1,0:T(8,128)(2,1)}, bf16[768,256]{1,0:T(8,128)(2,1)S(1)}, u32[]{:S(2)}) copy-start(bf16[768,256]{1,0:T(8,128)(2,1)S(1)} %collective-permute-done.6.refs_3_) | copy-start | bytes 1179652
  254.7 9.2 %collective-permute-start.14 = (bf16[1024,256]{1,0:T(8,128)(2,1)}, bf16[1024,256]{1,0:T(8,128)(2,1)S(1)}, u32[]{:S(2)}, u32[]{:S(2)}) collective-permute-start(bf16[1024,256]{1,0:T(8,128)(2,1)} %get-tuple-element.30.refs_1_.refs_0_), channel_id=1, source_target_pairs={{0,24},{4,28},{8,16},{12,20},{16,8},{20,12},{24,0},{28,4},{1,25},{... | collective-permute-start | bytes 1572872 | tf_op jit(solution)/shard_map/ppermute | solution.py:435
  256.4 23.6 %collective-permute-start.13 = (bf16[1024,256]{1,0:T(8,128)(2,1)}, bf16[1024,256]{1,0:T(8,128)(2,1)S(1)}, u32[]{:S(2)}, u32[]{:S(2)}) collective-permute-start(bf16[1024,256]{1,0:T(8,128)(2,1)} %get-tuple-element.30.refs_1_.refs_0_), channel_id=1, source_target_pairs={{0,16},{4,20},{8,24},{12,28},{16,0},{20,4},{24,8},{28,12},{1,17},{... | collective-permute-start | bytes 1572872 | tf_op jit(solution)/shard_map/ppermute | solution.py:435
  257.4 22.5 %collective-permute-start.12 = (bf16[1024,256]{1,0:T(8,128)(2,1)}, bf16[1024,256]{1,0:T(8,128)(2,1)S(1)}, u32[]{:S(2)}, u32[]{:S(2)}) collective-permute-start(bf16[1024,256]{1,0:T(8,128)(2,1)} %get-tuple-element.30.refs_1_.refs_0_), channel_id=1, source_target_pairs={{0,8},{4,12},{8,0},{12,4},{16,24},{20,28},{24,16},{28,20},{1,9},{5... | collective-permute-start | bytes 1572872 | tf_op jit(solution)/shard_map/ppermute | solution.py:435
  263.6 23.8 %copy-start.4 = (bf16[1024,256]{1,0:T(8,128)(2,1)S(1)}, bf16[1024,256]{1,0:T(8,128)(2,1)}, u32[]{:S(2)}) copy-start(bf16[1024,256]{1,0:T(8,128)(2,1)} %finish.1.refs_4_.refs_6_.refs_0_) | copy-start | bytes 1572868
  263.9 16.1 %copy-start.18 = (bf16[1024,256]{1,0:T(8,128)(2,1)}, bf16[1024,256]{1,0:T(8,128)(2,1)S(1)}, u32[]{:S(2)}) copy-start(bf16[1024,256]{1,0:T(8,128)(2,1)S(1)} %collective-permute-done.14.refs_3_) | copy-start | bytes 1572868
  280.0 0.8 copy-start.19
  280.8 0.8 copy-start.20
  284.5 6.2 %collective-permute-start.15 = (bf16[4096,256]{1,0:T(8,128)(2,1)}, bf16[4096,256]{1,0:T(8,128)(2,1)S(1)}, u32[]{:S(2)}, u32[]{:S(2)}) collective-permute-start(bf16[4096,256]{1,0:T(8,128)(2,1)} %join.4.refs_4_), channel_id=1, source_target_pairs={{0,4},{4,0},{8,12},{12,8},{16,20},{20,16},{24,28},{28,24},{1,5},{5... | collective-permute-start | bytes 6291464 | tf_op jit(solution)/shard_map/ppermute | solution.py:435
  287.4 18.1 %collective-permute-start.18 = (bf16[1024,256]{1,0:T(8,128)(2,1)S(1)}, bf16[1024,256]{1,0:T(8,128)(2,1)S(1)}, u32[]{:S(2)}, u32[]{:S(2)}) collective-permute-start(bf16[1024,256]{1,0:T(8,128)(2,1)S(1)} %copy-done.4), channel_id=1, source_target_pairs={{0,24},{4,28},{8,16},{12,20},{16,8},{20,12},{24,0},{28,4},{1,25},{... | collective-permute-start | bytes 1572872 | tf_op jit(solution)/shard_map/ppermute | solution.py:435
  288.3 25.1 %collective-permute-start.17 = (bf16[1024,256]{1,0:T(8,128)(2,1)S(1)}, bf16[1024,256]{1,0:T(8,128)(2,1)S(1)}, u32[]{:S(2)}, u32[]{:S(2)}) collective-permute-start(bf16[1024,256]{1,0:T(8,128)(2,1)S(1)} %copy-done.4), channel_id=1, source_target_pairs={{0,16},{4,20},{8,24},{12,28},{16,0},{20,4},{24,8},{28,12},{1,17},{... | collective-permute-start | bytes 1572872 | tf_op jit(solution)/shard_map/ppermute | solution.py:435
  289.3 24.0 %collective-permute-start.16 = (bf16[1024,256]{1,0:T(8,128)(2,1)S(1)}, bf16[1024,256]{1,0:T(8,128)(2,1)S(1)}, u32[]{:S(2)}, u32[]{:S(2)}) collective-permute-start(bf16[1024,256]{1,0:T(8,128)(2,1)S(1)} %copy-done.4), channel_id=1, source_target_pairs={{0,8},{4,12},{8,0},{12,4},{16,24},{20,28},{24,16},{28,20},{1,9},{5... | collective-permute-start | bytes 1572872 | tf_op jit(solution)/shard_map/ppermute | solution.py:435
  290.8 1.3 copy-start.9
  305.5 12.9 %copy-start = (bf16[1024,256]{1,0:T(8,128)(2,1)S(1)}, bf16[1024,256]{1,0:T(8,128)(2,1)}, u32[]{:S(2)}) copy-start(bf16[1024,256]{1,0:T(8,128)(2,1)} %product.4.refs_4_.refs_6_.refs_0_) | copy-start | bytes 1572868
  305.5 7.8 %copy-start.21 = (bf16[1024,256]{1,0:T(8,128)(2,1)}, bf16[1024,256]{1,0:T(8,128)(2,1)S(1)}, u32[]{:S(2)}) copy-start(bf16[1024,256]{1,0:T(8,128)(2,1)S(1)} %collective-permute-done.18.refs_3_) | copy-start | bytes 1572868
  313.3 0.8 copy-start.23
  314.1 0.8 copy-start.25
  317.9 4.5 %collective-permute-start.19 = (bf16[4096,256]{1,0:T(8,128)(2,1)}, bf16[4096,256]{1,0:T(8,128)(2,1)S(1)}, u32[]{:S(2)}, u32[]{:S(2)}) collective-permute-start(bf16[4096,256]{1,0:T(8,128)(2,1)} %join.5.refs_4_), channel_id=1, source_target_pairs={{0,4},{4,0},{8,12},{12,8},{16,20},{20,16},{24,28},{28,24},{1,5},{5... | collective-permute-start | bytes 6291464 | tf_op jit(solution)/shard_map/ppermute | solution.py:435
  318.4 18.8 %collective-permute-start.22 = (bf16[1024,256]{1,0:T(8,128)(2,1)S(1)}, bf16[1024,256]{1,0:T(8,128)(2,1)S(1)}, u32[]{:S(2)}, u32[]{:S(2)}) collective-permute-start(bf16[1024,256]{1,0:T(8,128)(2,1)S(1)} %copy-done), channel_id=1, source_target_pairs={{0,24},{4,28},{8,16},{12,20},{16,8},{20,12},{24,0},{28,4},{1,25},{... | collective-permute-start | bytes 1572872 | tf_op jit(solution)/shard_map/ppermute | solution.py:435
  319.4 25.1 %collective-permute-start.21 = (bf16[1024,256]{1,0:T(8,128)(2,1)S(1)}, bf16[1024,256]{1,0:T(8,128)(2,1)S(1)}, u32[]{:S(2)}, u32[]{:S(2)}) collective-permute-start(bf16[1024,256]{1,0:T(8,128)(2,1)S(1)} %copy-done), channel_id=1, source_target_pairs={{0,16},{4,20},{8,24},{12,28},{16,0},{20,4},{24,8},{28,12},{1,17},{... | collective-permute-start | bytes 1572872 | tf_op jit(solution)/shard_map/ppermute | solution.py:435
  320.4 24.1 %collective-permute-start.20 = (bf16[1024,256]{1,0:T(8,128)(2,1)S(1)}, bf16[1024,256]{1,0:T(8,128)(2,1)S(1)}, u32[]{:S(2)}, u32[]{:S(2)}) collective-permute-start(bf16[1024,256]{1,0:T(8,128)(2,1)S(1)} %copy-done), channel_id=1, source_target_pairs={{0,8},{4,12},{8,0},{12,4},{16,24},{20,28},{24,16},{28,20},{1,9},{5... | collective-permute-start | bytes 1572872 | tf_op jit(solution)/shard_map/ppermute | solution.py:435
  322.4 1.3 copy-start.7
  337.2 12.3 %copy-start.2 = (bf16[1024,256]{1,0:T(8,128)(2,1)S(1)}, bf16[1024,256]{1,0:T(8,128)(2,1)}, u32[]{:S(2)}) copy-start(bf16[1024,256]{1,0:T(8,128)(2,1)} %product.5.refs_4_.refs_2_.refs_0_) | copy-start | bytes 1572868
  337.2 7.3 %copy-start.22 = (bf16[1024,256]{1,0:T(8,128)(2,1)}, bf16[1024,256]{1,0:T(8,128)(2,1)S(1)}, u32[]{:S(2)}) copy-start(bf16[1024,256]{1,0:T(8,128)(2,1)S(1)} %collective-permute-done.22.refs_3_) | copy-start | bytes 1572868
  344.5 0.8 copy-start.24
  345.3 0.8 copy-start.26
  349.1 5.3 %collective-permute-start.23 = (bf16[4096,256]{1,0:T(8,128)(2,1)}, bf16[4096,256]{1,0:T(8,128)(2,1)S(1)}, u32[]{:S(2)}, u32[]{:S(2)}) collective-permute-start(bf16[4096,256]{1,0:T(8,128)(2,1)} %join.6.refs_4_), channel_id=1, source_target_pairs={{0,4},{4,0},{8,12},{12,8},{16,20},{20,16},{24,28},{28,24},{1,5},{5... | collective-permute-start | bytes 6291464 | tf_op jit(solution)/shard_map/ppermute | solution.py:435
  349.5 19.4 %collective-permute-start.26 = (bf16[1024,256]{1,0:T(8,128)(2,1)S(1)}, bf16[1024,256]{1,0:T(8,128)(2,1)S(1)}, u32[]{:S(2)}, u32[]{:S(2)}) collective-permute-start(bf16[1024,256]{1,0:T(8,128)(2,1)S(1)} %copy-done.2), channel_id=1, source_target_pairs={{0,24},{4,28},{8,16},{12,20},{16,8},{20,12},{24,0},{28,4},{1,25},{... | collective-permute-start | bytes 1572872 | tf_op jit(solution)/shard_map/ppermute | solution.py:435
  350.4 25.2 %collective-permute-start.25 = (bf16[1024,256]{1,0:T(8,128)(2,1)S(1)}, bf16[1024,256]{1,0:T(8,128)(2,1)}, u32[]{:S(2)}, u32[]{:S(2)}) collective-permute-start(bf16[1024,256]{1,0:T(8,128)(2,1)S(1)} %copy-done.2), channel_id=1, source_target_pairs={{0,16},{4,20},{8,24},{12,28},{16,0},{20,4},{24,8},{28,12},{1,17},{... | collective-permute-start | bytes 1572872 | tf_op jit(solution)/shard_map/ppermute | solution.py:435
  351.5 24.2 %collective-permute-start.24 = (bf16[1024,256]{1,0:T(8,128)(2,1)S(1)}, bf16[1024,256]{1,0:T(8,128)(2,1)}, u32[]{:S(2)}, u32[]{:S(2)}) collective-permute-start(bf16[1024,256]{1,0:T(8,128)(2,1)S(1)} %copy-done.2), channel_id=1, source_target_pairs={{0,8},{4,12},{8,0},{12,4},{16,24},{20,28},{24,16},{28,20},{1,9},{5... | collective-permute-start | bytes 1572872 | tf_op jit(solution)/shard_map/ppermute | solution.py:435
  354.3 1.3 copy-start.8
  369.0 10.1 %copy-start.1 = (bf16[1024,256]{1,0:T(8,128)(2,1)S(1)}, bf16[1024,256]{1,0:T(8,128)(2,1)}, u32[]{:S(2)}) copy-start(bf16[1024,256]{1,0:T(8,128)(2,1)} %product.4.refs_4_.refs_6_.refs_0_) | copy-start | bytes 1572868
  369.0 10.1 %copy-start.3 = (bf16[1024,256]{1,0:T(8,128)(2,1)S(1)}, bf16[1024,256]{1,0:T(8,128)(2,1)}, u32[]{:S(2)}) copy-start(bf16[1024,256]{1,0:T(8,128)(2,1)} %product.5.refs_4_.refs_2_.refs_0_) | copy-start | bytes 1572868
  369.0 6.7 %copy-start.17 = (bf16[1024,256]{1,0:T(8,128)(2,1)}, bf16[1024,256]{1,0:T(8,128)(2,1)S(1)}, u32[]{:S(2)}) copy-start(bf16[1024,256]{1,0:T(8,128)(2,1)S(1)} %collective-permute-done.26.refs_3_) | copy-start | bytes 1572868
  378.6 4.5 %collective-permute-start.27 = (bf16[4096,256]{1,0:T(8,128)(2,1)}, bf16[4096,256]{1,0:T(8,128)(2,1)S(1)}, u32[]{:S(2)}, u32[]{:S(2)}) collective-permute-start(bf16[4096,256]{1,0:T(8,128)(2,1)} %join.7.refs_4_), channel_id=1, source_target_pairs={{0,4},{4,0},{8,12},{12,8},{16,20},{20,16},{24,28},{28,24},{1,5},{5... | collective-permute-start | bytes 6291464 | tf_op jit(solution)/shard_map/ppermute | solution.py:435
  379.2 18.6 %copy-start.5 = (bf16[1024,256]{1,0:T(8,128)(2,1)S(1)}, bf16[1024,256]{1,0:T(8,128)(2,1)}, u32[]{:S(2)}) copy-start(bf16[1024,256]{1,0:T(8,128)(2,1)} %product.6.refs_4_) | copy-start | bytes 1572868
  383.1 1.3 copy-start.10
  (1 other events, 0.8 us)
Sparse Core Ops, SparseCore 0:
  10.1 29.2 all-gather.1
Sparse Core Ops, SparseCore 1:
  58.3 60.1 reduce-scatter.7
  129.1 59.5 reduce-scatter.5
  190.9 43.2 reduce-scatter.9
  236.6 25.0 reduce-scatter.11
  318.5 23.7 reduce-scatter.13
